TPU v7x, 32 devices: a whole 2x2x4 slice. The times are simulated.
32 devices in a mesh: dp: 4 (over y, x), seq: 4 (over z), head: 2 (over core).
Axes of the slice: x: 2, y: 2, z: 4, core: 2. Of those that a mesh axis runs over, the one named last changes fastest.
Arguments:
- dec_input: bfloat16 [96, 128, 768], P(('dp', 'seq'), 'head'), may hold values from -6 to 6
- enc_states: bfloat16 [96, 1296, 768], P('dp', 'seq'), may hold values from -6 to 6
- page_group: int32 [96], P(('dp', 'seq')), may hold values from 0 to 1, as said below
- target_mask: int32 [96, 128], P(('dp', 'seq')), may hold values from 0 to 1, as said below
- rel_buckets: int32 [96, 128, 128], P(('dp', 'seq')), may hold values from 0 to 31, as said below
- self_gain: float32 [768], replicated, may hold values from 0.5 to 1.5
- cross_gain: float32 [768], replicated, may hold values from 0.5 to 1.5
- ffn_gain: float32 [768], replicated, may hold values from 0.5 to 1.5
- self_q: bfloat16 [768, 768], P(None, 'head'), may hold values from -0.21875 to 0.21875
- self_k: bfloat16 [768, 768], P(None, 'head'), may hold values from -0.21875 to 0.21875
- self_v: bfloat16 [768, 768], P(None, 'head'), may hold values from -0.21875 to 0.21875
- self_o: bfloat16 [768, 768], P('head'), may hold values from -0.625 to 0.625
- rel_table: float32 [32, 12], P(None, 'head'), may hold values from -4 to 4
- cross_q: bfloat16 [768, 768], P(None, 'head'), may hold values from -0.21875 to 0.21875
- cross_k: bfloat16 [768, 768], P(None, 'head'), may hold values from -0.21875 to 0.21875
- cross_v: bfloat16 [768, 768], P(None, 'head'), may hold values from -0.21875 to 0.21875
- cross_o: bfloat16 [768, 768], P('head'), may hold values from -1 to 1
- ff_in: bfloat16 [768, 3072], P(None, 'head'), may hold values from -0.21875 to 0.21875
- ff_out: bfloat16 [3072, 768], P('head'), may hold values from -0.15625 to 0.15625
- cotangent: bfloat16 [96, 128, 768], P(('dp', 'seq'), 'head'), may hold values from -6 to 6
Outputs:
- dec_output: bfloat16 [96, 128, 768], P(('dp', 'seq'), 'head')
- input_grad: float32 [96, 128, 768], P(('dp', 'seq'), 'head')
- enc_grad: float32 [96, 1296, 768], P('dp', 'seq', 'head')
- self_gain_grad: float32 [768], replicated
- cross_gain_grad: float32 [768], replicated
- ffn_gain_grad: float32 [768], replicated
- self_q_grad: float32 [768, 768], P(None, 'head')
- self_k_grad: float32 [768, 768], P(None, 'head')
- self_v_grad: float32 [768, 768], P(None, 'head')
- self_o_grad: float32 [768, 768], P('head')
- rel_table_grad: float32 [32, 12], P(None, 'head')
- cross_q_grad: float32 [768, 768], P(None, 'head')
- cross_k_grad: float32 [768, 768], P(None, 'head')
- cross_v_grad: float32 [768, 768], P(None, 'head')
- cross_o_grad: float32 [768, 768], P('head')
- ff_in_grad: float32 [768, 3072], P(None, 'head')
- ff_out_grad: float32 [3072, 768], P('head')
- rms_stats: float32 [96, 4], P(('dp', 'seq'))
Inputs may be any that keep to these rules, and one draw needn't show every extreme that they name: `page_group`: 1 marks a page with 784 patches, 0 one with 196; every aligned block of 24 pages holds a page of group 1. `target_mask`: each page's row is ones followed by zeros, with 32 ones or more. `rel_buckets`: the T5 unidirectional bucket (32 buckets, exact up to 16, logarithmic up to distance 128) of the distance from key j to query i between increasing token positions of the page; 0 where j > i.
All inputs are finite; a program needn't handle non-finite values.
Results may differ from a plain program's by a relative error of at most 0.017.
Values may be sent and summed in bfloat16 or wider, within the bound.
No kernel may reach another device: no remote copies, remote signals or barrier semaphores. Data moves between devices by JAX's collectives and lax.ppermute only.
A program may use at most 256 MiB of HBM per device.

v0:
```python
import jax
import jax.numpy as jnp
from jax import lax
from jax.sharding import PartitionSpec as P

HEAD_DIM = 64
OCR = 512
PATCH_SMALL = 196
PATCH_LARGE = 784


EPSILON = 1e-06
MASKED = -1000000000.0


def normalize(tensor, gain_vec):
    inv_rms = lax.rsqrt(jnp.mean(tensor * tensor, axis=-1, keepdims=True) + EPSILON)
    return (tensor * inv_rms * gain_vec, inv_rms)


def norm_back(tensor, inv_rms, gain_vec, incoming):
    weighted = incoming * gain_vec
    inner_mean = jnp.mean(weighted * tensor, axis=-1, keepdims=True)
    gain_grad = jnp.sum(incoming * tensor * inv_rms, axis=(0, 1))
    return (gain_grad, inv_rms * weighted - tensor * inv_rms * inv_rms * inv_rms * inner_mean)


def project(row_data, weight):
    return jnp.einsum("pld,dw->plw", row_data, weight, preferred_element_type=jnp.float32)


def back_project(incoming, weight):
    return jnp.einsum("plw,dw->pld", incoming, weight, preferred_element_type=jnp.float32)


def weight_grad(row_data, incoming):
    return jnp.einsum("pld,plw->dw", row_data, incoming, preferred_element_type=jnp.float32)


def spread(row_share):
    return lax.all_gather(row_share, "head", axis=1, tiled=True)


def collect(full_rows):
    return lax.psum_scatter(full_rows, "head", scatter_dimension=1, tiled=True)


def split_heads(tensor):
    return tensor.reshape(tensor.shape[0], tensor.shape[1], tensor.shape[2] // HEAD_DIM, HEAD_DIM)


def attend_forward(queries, key_rows, value_rows, score_bias, allowed):
    scores = (
        jnp.einsum(
            "pqhd,pkhd->phqk",
            split_heads(queries),
            split_heads(key_rows),
            preferred_element_type=jnp.float32,
        )
        * HEAD_DIM ** (-0.5)
        + score_bias
    )
    scores = jnp.where(allowed, scores, MASKED)
    attn_probs = jax.nn.softmax(scores, axis=-1)
    attn_out = jnp.einsum(
        "phqk,pkhd->pqhd",
        attn_probs.astype(jnp.bfloat16),
        split_heads(value_rows),
        preferred_element_type=jnp.float32,
    )
    return (attn_probs, attn_out.reshape(queries.shape).astype(jnp.bfloat16))


def attend_back(queries, key_rows, value_rows, attn_probs, out_grad):
    grad_heads = split_heads(out_grad)
    value_grad = jnp.einsum(
        "phqk,pqhd->pkhd",
        attn_probs.astype(jnp.bfloat16),
        grad_heads,
        preferred_element_type=jnp.float32,
    )
    prob_grad = jnp.einsum(
        "pqhd,pkhd->phqk", grad_heads, split_heads(value_rows), preferred_element_type=jnp.float32
    )
    score_grad = attn_probs * (prob_grad - jnp.sum(attn_probs * prob_grad, axis=-1, keepdims=True))
    score_grad = score_grad.astype(jnp.bfloat16)
    query_grad = jnp.einsum(
        "phqk,pkhd->pqhd", score_grad, split_heads(key_rows), preferred_element_type=jnp.float32
    ) * HEAD_DIM ** (-0.5)
    key_grad = jnp.einsum(
        "phqk,pqhd->pkhd", score_grad, split_heads(queries), preferred_element_type=jnp.float32
    ) * HEAD_DIM ** (-0.5)
    return (
        score_grad,
        query_grad.reshape(queries.shape).astype(jnp.bfloat16),
        key_grad.reshape(key_rows.shape).astype(jnp.bfloat16),
        value_grad.reshape(value_rows.shape).astype(jnp.bfloat16),
    )


def per_device(
    dec_input,
    enc_states,
    page_group,
    target_mask,
    rel_buckets,
    self_gain,
    cross_gain,
    ffn_gain,
    self_q,
    self_k,
    self_v,
    self_o,
    rel_table,
    cross_q,
    cross_k,
    cross_v,
    cross_o,
    ff_in,
    ff_out,
    cotangent,
):
    row_share = dec_input.shape[1]
    row_width = dec_input.shape[2]
    length = target_mask.shape[1]
    row_start = lax.axis_index("head") * row_share
    valid_rows = lax.dynamic_slice_in_dim(target_mask, row_start, row_share, 1).astype(jnp.float32)[
        ..., None
    ]
    positions = jnp.arange(length, dtype=jnp.int32)
    causal = positions[None, :] <= positions[:, None]
    self_allowed = causal[None, None] & (target_mask[:, None, None, :] == 1)
    bucket_hot = (rel_buckets[..., None] == jnp.arange(rel_table.shape[0], dtype=jnp.int32)).astype(
        jnp.float32
    )
    score_bias = jnp.einsum("pqkb,bh->phqk", bucket_hot, rel_table, precision=lax.Precision.HIGHEST)
    enc_len = OCR + PATCH_SMALL + page_group * (PATCH_LARGE - PATCH_SMALL)
    enc_cap = OCR + PATCH_LARGE
    cross_allowed = (jnp.arange(enc_cap, dtype=jnp.int32)[None, :] < enc_len[:, None])[
        :, None, None, :
    ]
    stream = dec_input.astype(jnp.float32)
    normed_one, inv_one = normalize(stream, self_gain)
    rows_self = spread(normed_one.astype(jnp.bfloat16))
    query_self = project(rows_self, self_q).astype(jnp.bfloat16)
    key_self = project(rows_self, self_k).astype(jnp.bfloat16)
    value_self = project(rows_self, self_v).astype(jnp.bfloat16)
    probs_self, mixed_self = attend_forward(
        query_self, key_self, value_self, score_bias, self_allowed
    )
    branch_self = collect(project(mixed_self, self_o))
    hidden_one = stream + branch_self
    normed_two, inv_two = normalize(hidden_one, cross_gain)
    rows_cross = spread(normed_two.astype(jnp.bfloat16))
    query_cross = project(rows_cross, cross_q).astype(jnp.bfloat16)
    enc_keys = project(enc_states, cross_k).astype(jnp.bfloat16)
    enc_values = project(enc_states, cross_v).astype(jnp.bfloat16)
    key_cross, value_cross = (
        lax.all_to_all(enc_keys, "seq", split_axis=0, concat_axis=1, tiled=True),
        lax.all_to_all(enc_values, "seq", split_axis=0, concat_axis=1, tiled=True),
    )
    probs_cross, mixed_cross = attend_forward(
        query_cross, key_cross, value_cross, 0.0, cross_allowed
    )
    branch_cross = collect(project(mixed_cross, cross_o))
    hidden_two = hidden_one + branch_cross
    normed_three, inv_three = normalize(hidden_two, ffn_gain)
    rows_ffn = spread(normed_three.astype(jnp.bfloat16))
    ffn_inner = project(rows_ffn, ff_in)
    activated, gelu_back = jax.vjp(jax.nn.gelu, ffn_inner)
    act_low = activated.astype(jnp.bfloat16)
    branch_ffn = collect(project(act_low, ff_out))
    output = hidden_two + branch_ffn

    def squares(tensor):
        return jnp.sum(tensor * tensor * valid_rows, axis=(1, 2))

    square_sums = jnp.stack(
        [squares(output), squares(branch_self), squares(branch_cross), squares(branch_ffn)], axis=1
    )
    counts = jnp.sum(target_mask, axis=1).astype(jnp.float32) * row_width
    grad_out = cotangent.astype(jnp.float32)
    grad_rows_ffn = spread(cotangent)
    ff_out_grad = weight_grad(act_low, grad_rows_ffn)
    inner_grad = gelu_back(back_project(grad_rows_ffn, ff_out))[0].astype(jnp.bfloat16)
    ff_in_grad = weight_grad(rows_ffn, inner_grad)
    ffn_gain_grad, stream_grad = norm_back(
        hidden_two, inv_three, ffn_gain, collect(back_project(inner_grad, ff_in))
    )
    grad_two = grad_out + stream_grad
    grad_rows_cross = spread(grad_two.astype(jnp.bfloat16))
    cross_o_grad = weight_grad(mixed_cross, grad_rows_cross)
    mixed_cross_grad = back_project(grad_rows_cross, cross_o).astype(jnp.bfloat16)
    score_cross, query_cross_grad, key_cross_grad, value_cross_grad = attend_back(
        query_cross, key_cross, value_cross, probs_cross, mixed_cross_grad
    )
    cross_q_grad = weight_grad(rows_cross, query_cross_grad)
    enc_keys_grad, enc_values_grad = (
        lax.all_to_all(key_cross_grad, "seq", split_axis=1, concat_axis=0, tiled=True),
        lax.all_to_all(value_cross_grad, "seq", split_axis=1, concat_axis=0, tiled=True),
    )
    cross_k_grad = weight_grad(enc_states, enc_keys_grad)
    cross_v_grad = weight_grad(enc_states, enc_values_grad)
    enc_term = back_project(enc_keys_grad, cross_k) + back_project(enc_values_grad, cross_v)
    enc_grad = lax.psum_scatter(
        enc_term.astype(jnp.bfloat16), "head", scatter_dimension=2, tiled=True
    ).astype(jnp.float32)
    cross_gain_grad, stream_grad = norm_back(
        hidden_one, inv_two, cross_gain, collect(back_project(query_cross_grad, cross_q))
    )
    grad_one = grad_two + stream_grad
    grad_rows_self = spread(grad_one.astype(jnp.bfloat16))
    self_o_grad = weight_grad(mixed_self, grad_rows_self)
    mixed_self_grad = back_project(grad_rows_self, self_o).astype(jnp.bfloat16)
    score_self, query_self_grad, key_self_grad, value_self_grad = attend_back(
        query_self, key_self, value_self, probs_self, mixed_self_grad
    )
    rel_table_grad = jnp.einsum(
        "pqkb,phqk->bh", bucket_hot, score_self.astype(jnp.float32), precision=lax.Precision.HIGHEST
    )
    self_q_grad = weight_grad(rows_self, query_self_grad)
    self_k_grad = weight_grad(rows_self, key_self_grad)
    self_v_grad = weight_grad(rows_self, value_self_grad)
    input_parts = (
        back_project(query_self_grad, self_q)
        + back_project(key_self_grad, self_k)
        + back_project(value_self_grad, self_v)
    )
    self_gain_grad, stream_grad = norm_back(stream, inv_one, self_gain, collect(input_parts))
    input_grad = grad_one + stream_grad
    (
        self_gain_grad,
        cross_gain_grad,
        ffn_gain_grad,
        self_q_grad,
        self_k_grad,
        self_v_grad,
        self_o_grad,
        rel_table_grad,
        cross_q_grad,
        cross_k_grad,
        cross_v_grad,
        cross_o_grad,
        ff_in_grad,
        ff_out_grad,
    ) = lax.psum(
        (
            self_gain_grad,
            cross_gain_grad,
            ffn_gain_grad,
            self_q_grad,
            self_k_grad,
            self_v_grad,
            self_o_grad,
            rel_table_grad,
            cross_q_grad,
            cross_k_grad,
            cross_v_grad,
            cross_o_grad,
            ff_in_grad,
            ff_out_grad,
        ),
        ("dp", "seq"),
    )
    square_sums, self_gain_grad, cross_gain_grad, ffn_gain_grad = lax.psum(
        (square_sums, self_gain_grad, cross_gain_grad, ffn_gain_grad), "head"
    )
    rms_stats = jnp.sqrt(square_sums / counts[:, None])
    return (
        output.astype(jnp.bfloat16),
        input_grad,
        enc_grad,
        self_gain_grad,
        cross_gain_grad,
        ffn_gain_grad,
        self_q_grad,
        self_k_grad,
        self_v_grad,
        self_o_grad,
        rel_table_grad,
        cross_q_grad,
        cross_k_grad,
        cross_v_grad,
        cross_o_grad,
        ff_in_grad,
        ff_out_grad,
        rms_stats,
    )


def solution(mesh):
    placed = (
        P(("dp", "seq"), "head", None),
        P("dp", "seq", None),
        P(("dp", "seq")),
        P(("dp", "seq"), None),
        P(("dp", "seq"), None, None),
        P(),
        P(),
        P(),
        P(None, "head"),
        P(None, "head"),
        P(None, "head"),
        P("head", None),
        P(None, "head"),
        P(None, "head"),
        P(None, "head"),
        P(None, "head"),
        P("head", None),
        P(None, "head"),
        P("head", None),
        P(("dp", "seq"), "head", None),
    )
    return jax.shard_map(
        per_device,
        mesh=mesh,
        in_specs=placed,
        out_specs=(
            P(("dp", "seq"), "head", None),
            P(("dp", "seq"), "head", None),
            P("dp", "seq", "head"),
            P(),
            P(),
            P(),
            P(None, "head"),
            P(None, "head"),
            P(None, "head"),
            P("head", None),
            P(None, "head"),
            P(None, "head"),
            P(None, "head"),
            P(None, "head"),
            P("head", None),
            P(None, "head"),
            P("head", None),
            P(("dp", "seq"), None),
        ),
        check_vma=False,
    )
```

profile of v0, /device:TPU:0, one launch (start us, length us, event | category | flops | bytes accessed | tf_op | source)
XLA Modules:
  0.0 1491.3 jit_solution(11005721902567365984)
XLA Ops:
  7.2 12.1 fusion.30
  19.3 6.5 all-to-all-start
  29.3 5.5 fusion.3
  34.9 12.2 fusion.33
  47.0 112.2 %all-to-all-done = bf16[24,324,384]{2,1,0:T(8,128)(2,1)} async-done(((bf16[24,324,384]{2,1,0:T(8,128)(2,1)}), bf16[24,324,384]{2,1,0:T(8,128)(2,1)}, u32[]{:S(2)}, u32[]{:S(2)}) %all-to-all-start) | async-done | bytes 5972000 | tf_op jit(solution)/shard_map/all_to_all | solution.py:160
  159.2 5.2 all-to-all-start.1
  164.7 3.1 convolution_convert_fusion.7
  169.9 2.7 convolution_convert_fusion.6
  174.7 2.7 convolution_convert_fusion.5
  178.7 3.1 fusion.43
  181.8 2.8 fusion.103
  184.6 3.3 convolution_convert_fusion.4
  190.3 11.4 reduce-scatter.10.cloned.1.call-done
  205.7 9.8 all-gather.9.cloned.1.call-done
  215.5 3.0 convolution_convert_fusion.3
  220.6 13.4 copy.127
  234.0 12.7 reshape.175
  246.7 50.3 %all-to-all-done.1 = bf16[24,324,384]{2,1,0:T(8,128)(2,1)} async-done(((bf16[24,324,384]{2,1,0:T(8,128)(2,1)}), bf16[24,324,384]{2,1,0:T(8,128)(2,1)}, u32[]{:S(2)}, u32[]{:S(2)}) %all-to-all-start.1) | async-done | bytes 5972000 | tf_op jit(solution)/shard_map/all_to_all | solution.py:159
  297.0 13.4 copy.130
  310.4 12.7 reshape.177
  323.0 15.6 %fusion.104 = (f32[6,6,128]{2,1,0:T(8,128)}, f32[6,6,128,1296]{2,3,1,0:T(8,128)}) fusion(pred[6,1296]{1,0:T(8,128)(4,1)} %iota_compare_fusion.2, bf16[6,128,6,64]{1,3,2,0:T(8,128)(2,1)} %bitcast.226, bf16[6,1296,6,64]{1,3,2,0:T(8,128)(2,1)} %reshape.177), kind=kOutput, calls=%fused_computation.160 | convolution fusion | flops 788301056 | bytes 30475872 | tf_op jit(solution)/shard_map/sub | solution.py:64
  338.7 14.6 fusion.59
  353.3 3.5 fusion.75
  356.8 8.9 reduce-scatter.12.cloned.1.call-done
  370.1 9.7 all-gather.11.cloned.1.call-done
  379.8 4.0 fusion.41
  386.0 4.3 fusion.37
  391.6 6.5 fusion.29
  399.5 3.4 fusion.39
  405.6 14.0 reduce-scatter.16.cloned.1.call-done
  419.6 4.7 multiply_reduce_fusion.5
  426.6 10.6 all-gather.15.cloned.1.call-done
  437.2 3.0 convolution_convert_fusion.2
  442.3 19.8 %multiply_reduce_fusion = (f32[6,6,128]{2,1,0:T(8,128)}, f32[6,6,128,1296]{2,3,1,0:T(8,128)}) fusion(f32[6,6,128,1296]{2,3,1,0:T(8,128)} %get-tuple-element.112, f32[6,6,128]{2,1,0:T(8,128)} %get-tuple-element.111, bf16[6,128,6,64]{1,3,2,0:T(8,128)(2,1)} %bitcast.238, bf16[6,1296,6,64]{1,3,2,0:T(8,128)(2,1)} %reshape.175), kind=kOutput, calls=%fused_computation.4 | convolution fusion | flops 782323200 | bytes 54374400 | tf_op jit(solution)/shard_map/pqhd,pkhd->phqk/dot_general | solution.py:82
  462.1 20.3 %multiply_convert_fusion = bf16[6,6,128,1296]{2,3,1,0:T(8,128)(2,1)} fusion(f32[6,6,128,1296]{2,3,1,0:T(8,128)} %get-tuple-element.114, f32[6,6,128]{2,1,0:T(8,128)} %get-tuple-element.113, f32[6,6,128,1296]{2,3,1,0:T(8,128)} %get-tuple-element.112, f32[6,6,128]{2,1,0:T(8,128)} %get-tuple-element.111), kind=kLoop, calls=%fused_computation.3 | loop fusion | flops 23887872 | bytes 59756544 | tf_op jit(solution)/shard_map/convert_element_type | solution.py:86
  482.5 11.3 multiply_convert_fusion.1
  493.8 11.3 copy.141
  505.1 5.6 all-to-all-start.2
  510.9 8.9 fusion.58
  522.9 15.7 %fusion.20 = bf16[6,6,64,1296]{3,2,1,0:T(8,128)(2,1)} fusion(bf16[6,128,6,64]{1,3,2,0:T(8,128)(2,1)} %bitcast.239, f32[6,6,128]{2,1,0:T(8,128)} %get-tuple-element.111, pred[6,1296]{1,0:T(8,128)(4,1)} %iota_compare_fusion.2, bf16[6,128,6,64]{1,3,2,0:T(8,128)(2,1)} %bitcast.229, bf16[6,1296,6,64]{1,3,2,0:T(8,128)(2,1)} %reshape.177), kind=kOutput, calls=%fused_computation.30 | convolution fusion | flops 1561675520 | bytes 13149792 | tf_op jit(solution)/shard_map/phqk,pqhd->pkhd/dot_general | solution.py:76
  538.6 11.3 copy.144
  549.9 135.5 %all-to-all-done.2 = bf16[6,1296,384]{2,0,1:T(8,128)(2,1)} async-done(((bf16[6,1296,384]{2,0,1:T(8,128)(2,1)}), bf16[6,1296,384]{2,0,1:T(8,128)(2,1)}, u32[]{:S(2)}, u32[]{:S(2)}) %all-to-all-start.2) | async-done | bytes 5972000 | tf_op jit(solution)/shard_map/all_to_all | solution.py:199
  685.4 5.6 all-to-all-start.3
  695.7 7.7 convolution_bitcast_fusion
  703.4 3.0 all-gather.17.cloned.1.call-done
  709.5 3.6 convolution_convert_fusion
  722.6 6.3 convolution_bitcast_fusion.1
  739.8 6.7 copy.143
  746.5 118.4 %all-to-all-done.3 = bf16[6,1296,384]{2,0,1:T(8,128)(2,1)} async-done(((bf16[6,1296,384]{2,0,1:T(8,128)(2,1)}), bf16[6,1296,384]{2,0,1:T(8,128)(2,1)}, u32[]{:S(2)}, u32[]{:S(2)}) %all-to-all-start.3) | async-done | bytes 5972000 | tf_op jit(solution)/shard_map/all_to_all | solution.py:200
  864.9 4.2 copy.146
  869.9 13.8 fusion.50
  883.7 12.5 fusion.53
  897.3 14.1 fusion.77
  911.4 18.0 %add_convert_fusion = bf16[24,324,768]{2,1,0:T(8,128)(2,1)} fusion(f32[24,324,768]{2,1,0:T(8,128)} %fusion.77, bf16[24,324,384]{2,1,0:T(8,128)(2,1)} %bitcast.210, bf16[768,384]{1,0:T(8,128)(2,1)S(1)} %copy-done.46), kind=kOutput, calls=%fused_computation.2 | convolution fusion | flops 4598415360 | bytes 42393600 | tf_op jit(solution)/shard_map/plw,dw->pld/dot_general | solution.py:33
  929.4 18.6 %copy.179 = bf16[24,324,768]{1,0,2:T(8,128)(2,1)} copy(bf16[24,324,768]{2,1,0:T(8,128)(2,1)} %add_convert_fusion) | data formatting | bytes 23887872
  948.0 22.5 %reshape.202 = bf16[768,7776]{1,0:T(8,128)(2,1)} reshape(bf16[768,24,324]{2,1,0:T(8,128)(2,1)} %bitcast.202) | data formatting | bytes 23887872
  975.8 80.3 %all-reduce = (f32[768]{0:T(1024)S(1)}, f32[768]{0:T(1024)S(1)}, f32[768]{0:T(1024)S(1)}, f32[32,6]{0,1:T(8,128)}) all-reduce(f32[768]{0:T(1024)S(1)} %get-tuple-element.76, f32[768]{0:T(1024)S(1)} %copy-done.64, f32[768]{0:T(1024)S(1)} %copy-done.65, f32[32,6]{0,1:T(8,128)S(1)} %fusion.71), channel_id=1, replica_groups=mesh['dp'=4,'seq'=4,'head'=2] {'dp','seq'}, use_global_device_ids=true, to_apply=%region_20.21 | all-reduce | flops 2496 | bytes 19968 | tf_op jit(solution)/shard_map/psum | solution.py:246
  1056.1 3.9 all-reduce.2
  1061.9 355.2 %all-reduce.5.cloned.1.call-done = (f32[768,384]{1,0:T(8,128)}, f32[768,384]{1,0:T(8,128)}, f32[768,384]{1,0:T(8,128)}, f32[384,768]{1,0:T(8,128)}, f32[768,384]...) async-done(((f32[768,384]{1,0:T(8,128)}, f32[768,384]{1,0:T(8,128)}, ...) | async-done | bytes 18874384 | tf_op jit(solution)/shard_map/psum | solution.py:246
  1417.1 2.7 copy.156
  1421.3 17.6 %reduce-scatter.22.cloned.1.call-done = bf16[384,7776]{1,0:T(8,128)(2,1)} async-done(((bf16[768,7776]{1,0:T(8,128)(2,1)}), bf16[384,7776]{1,0:T(8,128)(2,1)}) %reduce-scatter.22.cloned.1.call-update) | async-done | bytes 5971984
  1438.9 13.9 reshape.203
  1452.7 9.9 copy.180
  1462.7 8.2 copy.155
  (251 shorter events, 89.4 us)
Async XLA Ops:
  7.2 378.8 %copy-start = (bf16[1536,768]{1,0:T(8,128)(2,1)S(1)}, bf16[1536,768]{1,0:T(8,128)(2,1)}, u32[]{:S(2)}) copy-start(bf16[1536,768]{1,0:T(8,128)(2,1)} %param.38) | copy-start | bytes 7077892
  19.3 7.0 copy-start.6
  19.3 7.8 copy-start.58
  19.3 139.9 %all-to-all-start = ((bf16[24,324,384]{2,1,0:T(8,128)(2,1)}), bf16[24,324,384]{2,1,0:T(8,128)(2,1)}, u32[]{:S(2)}, u32[]{:S(2)}) async-start(bf16[24,324,384]{2,1,0:T(8,128)(2,1)} %fusion.30), calls=%async_computation.1 | async-start | bytes 12091392 | tf_op jit(solution)/shard_map/all_to_all | solution.py:160
  25.8 2.4 copy-start.49
  25.8 2.7 copy-start.60
  25.8 3.6 copy-start.71
  25.8 138.9 %all-gather.7.cloned.1.call-start = ((), (), s32[]{:S(2)}) async-start(), calls=%async_computation.11 | async-start | bytes 1769472 | tf_op jit(solution)/shard_map/all_gather | solution.py:41
  28.4 6.4 copy-start.47
  29.3 5.5 copy-start.44
  159.2 137.8 %all-to-all-start.1 = ((bf16[24,324,384]{2,1,0:T(8,128)(2,1)}), bf16[24,324,384]{2,1,0:T(8,128)(2,1)}, u32[]{:S(2)}, u32[]{:S(2)}) async-start(bf16[24,324,384]{2,1,0:T(8,128)(2,1)} %fusion.33), calls=%async_computation.2 | async-start | bytes 12091392 | tf_op jit(solution)/shard_map/all_to_all | solution.py:159
  164.4 37.3 %reduce-scatter.10.cloned.1.call-start = ((), (), s32[]{:S(2)}) async-start(), calls=%async_computation.12 | async-start | bytes 3538944 | tf_op jit(solution)/shard_map/reduce_scatter | solution.py:45
  164.7 5.2 copy-start.8
  178.7 3.1 copy-start.17
  181.8 2.8 copy-start.13
  184.6 3.4 copy-start.39
  190.2 13.8 copy-start.56
  190.2 14.8 copy-start.72
  190.2 25.3 %all-gather.9.cloned.1.call-start = ((), (), s32[]{:S(2)}) async-start(), calls=%async_computation.13 | async-start | bytes 1769472 | tf_op jit(solution)/shard_map/all_gather | solution.py:41
  205.0 160.8 %reduce-scatter.12.cloned.1.call-start = ((), (), s32[]{:S(2)}) async-start(), calls=%async_computation.14 | async-start | bytes 3538944 | tf_op jit(solution)/shard_map/reduce_scatter | solution.py:45
  356.8 11.5 copy-start.55
  356.8 23.0 %all-gather.11.cloned.1.call-start = ((), (), s32[]{:S(2)}) async-start(), calls=%async_computation.15 | async-start | bytes 1769472 | tf_op jit(solution)/shard_map/all_gather | solution.py:41
  369.3 22.4 %all-gather.13.cloned.1.call-start = ((), (), s32[]{:S(2)}) async-start(), calls=%async_computation.17 | async-start | bytes 1769472 | tf_op jit(solution)/shard_map/all_gather | solution.py:41
  369.9 35.7 %reduce-scatter.14.cloned.1.call-start = ((), (), s32[]{:S(2)}) async-start(), calls=%async_computation.16 | async-start | bytes 3538944 | tf_op jit(solution)/shard_map/reduce_scatter | solution.py:45
  390.3 29.2 %reduce-scatter.16.cloned.1.call-start = ((), (), s32[]{:S(2)}) async-start(), calls=%async_computation.18 | async-start | bytes 3538944 | tf_op jit(solution)/shard_map/reduce_scatter | solution.py:45
  391.6 7.9 copy-start.70
  403.0 16.6 %copy-start.4 = (f32[6,64,768]{2,1,0:T(8,128)S(1)}, f32[6,64,768]{2,1,0:T(8,128)}, u32[]{:S(2)}) copy-start(f32[6,64,768]{2,1,0:T(8,128)} %copy-done.3) | copy-start | bytes 3538948
  403.0 34.2 %all-gather.15.cloned.1.call-start = ((), (), s32[]{:S(2)}) async-start(), calls=%async_computation.19 | async-start | bytes 1769472 | tf_op jit(solution)/shard_map/all_gather | solution.py:41
  419.6 4.7 copy-start.10
  424.3 15.9 %copy-start.62 = (f32[6,64]{1,0:T(8,128)}, f32[6,64]{1,0:T(8,128)S(1)}, u32[]{:S(2)}) copy-start(f32[6,64]{1,0:T(8,128)S(1)} %broadcast_multiply_fusion.2) | copy-start | bytes 4612
  505.1 180.3 %all-to-all-start.2 = ((bf16[6,1296,384]{2,0,1:T(8,128)(2,1)}), bf16[6,1296,384]{2,0,1:T(8,128)(2,1)}, u32[]{:S(2)}, u32[]{:S(2)}) async-start(bf16[6,1296,384]{2,0,1:T(8,128)(2,1)} %copy.141), calls=%async_computation.8 | async-start | bytes 15925248 | tf_op jit(solution)/shard_map/all_to_all | solution.py:199
  510.7 180.4 %reduce-scatter.18.cloned.1.call-start = ((), (), s32[]{:S(2)}) async-start(), calls=%async_computation.20 | async-start | bytes 3538944 | tf_op jit(solution)/shard_map/reduce_scatter | solution.py:45
  510.9 9.7 copy-start.38
  549.9 141.2 %copy-start.54 = (f32[6,64]{1,0:T(8,128)S(1)}, f32[6,64]{1,0:T(8,128)}, u32[]{:S(2)}) copy-start(f32[6,64]{1,0:T(8,128)} %copy-done.53) | copy-start | bytes 4612
  549.9 141.2 %copy-start.57 = (f32[768]{0:T(1024)S(1)}, f32[768]{0:T(1024)}, u32[]{:S(2)}) copy-start(f32[768]{0:T(1024)} %param.26) | copy-start | bytes 9220
  685.4 179.5 %all-to-all-start.3 = ((bf16[6,1296,384]{2,0,1:T(8,128)(2,1)}), bf16[6,1296,384]{2,0,1:T(8,128)(2,1)}, u32[]{:S(2)}, u32[]{:S(2)}) async-start(bf16[6,1296,384]{2,0,1:T(8,128)(2,1)} %copy.144), calls=%async_computation.9 | async-start | bytes 15925248 | tf_op jit(solution)/shard_map/all_to_all | solution.py:200
  691.0 15.4 %all-gather.17.cloned.1.call-start = ((), (), s32[]{:S(2)}) async-start(), calls=%async_computation.21 | async-start | bytes 1769472 | tf_op jit(solution)/shard_map/all_gather | solution.py:41
  691.1 2.4 copy-start.19
  695.5 10.9 copy-start.40
  695.5 278.4 %reduce-scatter.20.cloned.1.call-start = ((), (), s32[]{:S(2)}) async-start(), calls=%async_computation.22 | async-start | bytes 3538944 | tf_op jit(solution)/shard_map/reduce_scatter | solution.py:45
  709.5 3.6 copy-start.11
  709.5 3.6 copy-start.43
  722.3 6.7 copy-start.15
  722.3 694.8 %all-reduce.5.cloned.1.call-start = ((), (), s32[]{:S(2)}) async-start(), calls=%async_computation.24 | async-start | bytes 37748736 | tf_op jit(solution)/shard_map/psum | solution.py:246
  722.6 6.3 copy-start.34
  729.0 3.7 copy-start.9
  734.5 3.7 copy-start.24
  734.5 3.7 copy-start.36
  864.9 5.0 copy-start.2
  869.1 14.6 copy-start.5
  896.3 15.1 %copy-start.46 = (bf16[768,384]{1,0:T(8,128)(2,1)S(1)}, bf16[768,384]{1,0:T(8,128)(2,1)}, u32[]{:S(2)}) copy-start(bf16[768,384]{1,0:T(8,128)(2,1)} %param.35) | copy-start | bytes 1769476
  896.3 542.6 %reduce-scatter.22.cloned.1.call-start = ((), (), s32[]{:S(2)}) async-start(), calls=%async_computation.23 | async-start | bytes 17989632
  971.6 4.2 copy-start.64
  971.6 4.2 copy-start.65
  971.6 88.9 %copy-start.21 = (f32[6,64,768]{2,1,0:T(8,128)S(1)}, f32[6,64,768]{2,1,0:T(8,128)}, u32[]{:S(2)}) copy-start(f32[6,64,768]{2,1,0:T(8,128)} %get-tuple-element.103) | copy-start | bytes 3538948
  973.9 86.6 %copy-start.20 = (f32[6,64,768]{2,1,0:T(8,128)S(1)}, f32[6,64,768]{2,1,0:T(8,128)}, u32[]{:S(2)}) copy-start(f32[6,64,768]{2,1,0:T(8,128)} %reduce-scatter.20.cloned.1.call-done) | copy-start | bytes 3538948
  1417.1 2.8 copy-start.33
  1452.7 24.9 %slice-start.2 = ((s8[4718592]{0:T(1024)(128)(4,1)}), s8[524288]{0:T(1024)(128)(4,1)S(1)}, s32[]{:S(2)}) async-start(s8[4718592]{0:T(1024)(128)(4,1)} %bitcast.224), calls=%async_computation.27 | async-start | bytes 1048576
  1462.7 8.2 copy-start.32
  1462.7 15.0 %slice-start.3 = ((s8[4718592]{0:T(1024)(128)(4,1)}), s8[4194304]{0:T(1024)(128)(4,1)S(1)}, s32[]{:S(2)}) async-start(s8[4718592]{0:T(1024)(128)(4,1)} %bitcast.224), calls=%async_computation.28 | async-start | bytes 8388608
  1470.9 2.7 copy-start.30
  1476.6 4.2 slice-start
  1477.7 3.5 slice-start.1
  1481.2 3.4 copy-start.1
  (32 other events, 48.4 us)
Sparse Core Ops, SparseCore 0:
  28.7 11.0 all-gather.6
  190.3 11.3 reduce-scatter.9
  205.1 10.3 all-gather.8
  356.9 8.8 reduce-scatter.11
  369.4 10.3 all-gather.10
  381.2 10.3 all-gather.12
  394.5 11.0 reduce-scatter.13
  408.5 11.0 reduce-scatter.15
  426.7 10.3 all-gather.14
  523.0 11.4 reduce-scatter.17
  695.6 10.7 all-gather.16
  722.4 11.0 reduce-scatter.19
  896.4 520.7 all-reduce.4
  1419.4 19.3 reduce-scatter.21
where the time goes:
time: 1500 us; the launch traced here: 1490 us
  waiting for transfers between devices  861 us (57%)
  matrix products  261 us (17%)
  local copies, waits for them, and re-layouts  199 us (13%)
  blocking collectives  84.2 us (6%)
  other arithmetic  47 us (3%)
  starting transfers between devices  25.3 us (2%)
    psum x1, waiting for transfers between devices, per_device(): lax.psum((self_gain_grad, cross_gain_grad, ffn_gain_grad, self_q_grad, se...  355 us
    all_to_all x1, waiting for transfers between devices, per_device(): lax.all_to_all(key_cross_grad, 'seq', split_axis=1, concat_axis=0, tiled=...  136 us
    all_to_all x1, waiting for transfers between devices, per_device(): lax.all_to_all(value_cross_grad, 'seq', split_axis=1, concat_axis=0, tile...  118 us
    all_to_all x1, waiting for transfers between devices, per_device(): lax.all_to_all(enc_values, 'seq', split_axis=0, concat_axis=1, tiled=True)  112 us
    unnamed x172, local copies, waits for them, and re-layouts  102 us
    psum x1, blocking collectives, per_device(): lax.psum((self_gain_grad, cross_gain_grad, ffn_gain_grad, self_q_grad, se...  80.3 us
    dot_general x10, matrix products, back_project(): jnp.einsum('plw,dw->pld', incoming, weight, preferred_element_type=jnp.fl...  53.2 us
    dot_general x10, matrix products, weight_grad(): jnp.einsum('pld,plw->dw', row_data, incoming, preferred_element_type=jnp....  51 us
  transfers between devices with their start and end apart: 18, of which 15 were waited for; matrix products, arithmetic and copies ran while one was open for 20% of the time, Pallas kernels for 0%

commit v1 on v0

v1 whole, which is shorter than its diff:
```python
import functools

import jax
import jax.numpy as jnp
from jax import lax
from jax.experimental import pallas as pl
from jax.experimental.pallas import tpu as pltpu
from jax.sharding import PartitionSpec as P

HEAD_DIM = 64
OCR = 512
PATCH_SMALL = 196
PATCH_LARGE = 784
EPSILON = 1e-06
MASKED = -1000000000.0
BF = jnp.bfloat16
F32 = jnp.float32
SCALE = HEAD_DIM ** (-0.5)
VMEM = 56 * 1024 * 1024
PAIR = 2 * HEAD_DIM


def nn(a, b):
    return lax.dot_general(a, b, (((1,), (0,)), ((), ())), preferred_element_type=F32)


def nt(a, b):
    return lax.dot_general(a, b, (((1,), (1,)), ((), ())), preferred_element_type=F32)


def tn(a, b):
    return lax.dot_general(a, b, (((0,), (0,)), ((), ())), preferred_element_type=F32)


def call(body, grid, ins, outs, *, scalars=(), scratch=(), flops=0, nbytes=0, exps=0, aliases={}):
    spec = pltpu.PrefetchScalarGridSpec(
        num_scalar_prefetch=len(scalars),
        grid=grid,
        in_specs=[pl.BlockSpec(b, m) for _, b, m in ins],
        out_specs=[pl.BlockSpec(b, m) for _, _, b, m in outs],
        scratch_shapes=list(scratch),
    )
    return pl.pallas_call(
        body,
        grid_spec=spec,
        out_shape=[jax.ShapeDtypeStruct(s, d) for s, d, _, _ in outs],
        compiler_params=pltpu.CompilerParams(
            vmem_limit_bytes=VMEM, dimension_semantics=("arbitrary",) * len(grid)
        ),
        cost_estimate=pl.CostEstimate(flops=flops, bytes_accessed=nbytes, transcendentals=exps),
        input_output_aliases=aliases,
    )(*scalars, *[a for a, _, _ in ins])


def whole(a):
    n = a.ndim
    return (a, a.shape, lambda *_: (0,) * n)


def paged(a, k=1):
    n = a.ndim
    return (a, (k,) + a.shape[1:], lambda i, *_: (i,) + (0,) * (n - 1))


def out_paged(shape, dtype, k=1):
    n = len(shape)
    return (shape, dtype, (k,) + tuple(shape[1:]), lambda i, *_: (i,) + (0,) * (n - 1))


def out_whole(shape, dtype):
    n = len(shape)
    return (shape, dtype, tuple(shape), lambda *_: (0,) * n)


def inv_rms(v):
    return lax.rsqrt(jnp.mean(v * v, axis=-1, keepdims=True) + EPSILON)


def pair_rows(block):
    lane = lax.broadcasted_iota(jnp.int32, (1, PAIR), 1)
    low = (lane < HEAD_DIM).astype(F32).astype(block.dtype)
    return jnp.concatenate([block * low, block * (1 - low)], axis=0)


def two_rows(ref_rows, t):
    return jnp.concatenate([ref_rows[2 * t : 2 * t + 1, :], ref_rows[2 * t + 1 : 2 * t + 2, :]], axis=1)


def norm_back(v, gain, dn):
    inv = inv_rms(v)
    weighted = dn * gain
    inner = jnp.mean(weighted * v, axis=-1, keepdims=True)
    return dn * v * inv, inv * weighted - v * (inv * inv * inv * inner)


def fold8(v):
    return jnp.sum(v.reshape(v.shape[0] // 8, 8, v.shape[1]), axis=0)


def self_bias(buckets_ref, table_ref, heads):
    idx = jnp.transpose(buckets_ref[0])
    rows = []
    for h in range(heads):
        tab = jnp.broadcast_to(table_ref[h : h + 1, :], idx.shape)
        rows.append(jnp.take_along_axis(tab, idx, axis=1))
    return rows


def self_allowed(length, rows):
    key = lax.broadcasted_iota(jnp.int32, (rows, rows), 0)
    query = lax.broadcasted_iota(jnp.int32, (rows, rows), 1)
    ok = (key <= query) & (key < length)
    return jnp.concatenate([ok, ok], axis=1)


def self_fwd_kernel(
    head, lens, xo, xr, gain, wq, wk, wv, wo, buckets, table, xf, n1, qkv, o1, lse, a_part
):
    page = pl.program_id(0)
    first = head[0] == 0
    own, rec = xo[0].astype(F32), xr[0].astype(F32)
    x = jnp.concatenate([jnp.where(first, own, rec), jnp.where(first, rec, own)], axis=0)
    xf[0] = x.astype(BF)
    n = (x * inv_rms(x) * gain[...]).astype(BF)
    n1[0] = n
    w = wq.shape[1]
    q = (nn(n, wq[...]).astype(BF).astype(F32) * SCALE).astype(BF)
    k = nn(n, wk[...]).astype(BF)
    v = nn(n, wv[...]).astype(BF)
    qkv[0, :, 0:w] = q
    qkv[0, :, w : 2 * w] = k
    qkv[0, :, 2 * w : 3 * w] = v
    rows = x.shape[0]
    bias = self_bias(buckets, table, w // HEAD_DIM)
    ok = self_allowed(lens[page], rows)
    lses, outs = [], []
    for t in range(w // PAIR):
        c = slice(t * PAIR, (t + 1) * PAIR)
        s = nt(k[:, c], pair_rows(q[:, c])) + jnp.concatenate(bias[2 * t : 2 * t + 2], axis=1)
        s = jnp.where(ok, s, MASKED)
        m = jnp.max(s, axis=0, keepdims=True)
        e = jnp.exp(s - m)
        total = jnp.sum(e, axis=0, keepdims=True)
        p = e * (1.0 / total)
        o = tn(p.astype(BF), v[:, c])
        lane = lax.broadcasted_iota(jnp.int32, (rows, PAIR), 1)
        outs.append(jnp.where(lane < HEAD_DIM, o[:rows], o[rows:]))
        row = m + jnp.log(total)
        lses += [row[:, :rows], row[:, rows:]]
    lses += [jnp.zeros((1, rows), F32)] * (8 - len(lses))
    lse[0] = jnp.concatenate(lses, axis=0)
    o = jnp.concatenate(outs, axis=1).astype(BF)
    o1[0] = o
    a_part[0] = nn(o, wo[...]).astype(BF)


def self_fwd(head, lens, xo, xr, gain, wq, wk, wv, wo, buckets, table):
    pages, half, d = xo.shape
    rows, w = 2 * half, wq.shape[1]
    return call(
        self_fwd_kernel,
        (pages,),
        [
            paged(xo), paged(xr), whole(gain), whole(wq), whole(wk), whole(wv), whole(wo),
            paged(buckets), whole(table),
        ],
        [
            out_paged((pages, rows, d), BF), out_paged((pages, rows, d), BF),
            out_paged((pages, rows, 3 * w), BF), out_paged((pages, rows, w), BF),
            out_paged((pages, 8, rows), F32), out_paged((pages, rows, d), BF),
        ],
        scalars=(head, lens),
        flops=8 * pages * rows * d * w + 8 * pages * rows * rows * w,
        nbytes=pages * rows * (8 * d + 8 * w) + 8 * d * w,
        exps=pages * rows * rows * w // HEAD_DIM,
    )


def self_bwd_kernel(
    head, lens, h1, dn_a, dn_b, dh2, gain, wq, wk, wv, wo, buckets, table, qkv, lse,
    dh1, dar_out, dqkv, ds_out, dn_keep, dn_send, gain_grad,
):
    page = pl.program_id(0)
    first = head[0] == 0
    v1 = h1[0]
    rows = v1.shape[0]
    half = rows // 2
    gg, dv = norm_back(v1, gain[...], dn_a[0].astype(F32) + dn_b[0].astype(F32))
    d1 = dh2[0] + dv
    gpart = fold8(jnp.where(first, gg[:half], gg[half:]))

    @pl.when(page == 0)
    def _():
        gain_grad[...] = gpart

    @pl.when(page != 0)
    def _():
        gain_grad[...] += gpart

    dh1[0] = jnp.where(first, d1[:half], d1[half:])
    dar = d1.astype(BF)
    dar_out[0] = dar
    w = wo.shape[0]
    do = nt(dar, wo[...]).astype(BF)
    bias = self_bias(buckets, table, w // HEAD_DIM)
    ok = self_allowed(lens[page], rows)
    lane = lax.broadcasted_iota(jnp.int32, (rows, PAIR), 1)
    dqs, dks, dvs = [], [], []
    for t in range(w // PAIR):
        c = slice(t * PAIR, (t + 1) * PAIR)
        q = pair_rows(qkv[0, :, t * PAIR : (t + 1) * PAIR])
        k = qkv[0, :, w + t * PAIR : w + (t + 1) * PAIR]
        v = qkv[0, :, 2 * w + t * PAIR : 2 * w + (t + 1) * PAIR]
        g = pair_rows(do[:, c])
        s = nt(k, q) + jnp.concatenate(bias[2 * t : 2 * t + 2], axis=1)
        s = jnp.where(ok, s, MASKED)
        p = jnp.exp(s - two_rows(lse[0], t))
        dp = nt(v, g)
        ds = (p * (dp - jnp.sum(p * dp, axis=0, keepdims=True))).astype(BF)
        ds_out[0, 2 * t] = ds[:, :rows]
        ds_out[0, 2 * t + 1] = ds[:, rows:]
        dq = tn(ds, k) * SCALE
        dqs.append(jnp.where(lane < HEAD_DIM, dq[:rows], dq[rows:]).astype(BF))
        dks.append(nn(ds, q).astype(BF))
        dvs.append(nn(p.astype(BF), g).astype(BF))
    dq, dk, dvv = (jnp.concatenate(a, axis=1) for a in (dqs, dks, dvs))
    dqkv[0, :, 0:w] = dq
    dqkv[0, :, w : 2 * w] = dk
    dqkv[0, :, 2 * w : 3 * w] = dvv
    dn = (nt(dq, wq[...]) + nt(dk, wk[...]) + nt(dvv, wv[...])).astype(BF).astype(F32)
    dn_keep[0] = jnp.where(first, dn[:half], dn[half:]).astype(BF)
    dn_send[0] = jnp.where(first, dn[half:], dn[:half]).astype(BF)


def self_bwd(head, lens, h1, dn_a, dn_b, dh2, gain, wq, wk, wv, wo, buckets, table, qkv, lse):
    pages, rows, d = h1.shape
    w = wq.shape[1]
    heads = w // HEAD_DIM
    return call(
        self_bwd_kernel,
        (pages,),
        [
            paged(h1), paged(dn_a), paged(dn_b), paged(dh2), whole(gain), whole(wq), whole(wk),
            whole(wv), whole(wo), paged(buckets), whole(table), paged(qkv), paged(lse),
        ],
        [
            out_paged((pages, rows // 2, d), F32), out_paged((pages, rows, d), BF),
            out_paged((pages, rows, 3 * w), BF), out_paged((pages, heads, rows, rows), BF),
            out_paged((pages, rows // 2, d), BF), out_paged((pages, rows // 2, d), BF),
            out_whole((8, d), F32),
        ],
        scalars=(head, lens),
        flops=8 * pages * rows * d * w + 20 * pages * rows * rows * w,
        nbytes=pages * rows * (16 * d + 12 * w) + 8 * d * w,
        exps=pages * rows * rows * heads,
    )


def table_grad_kernel(ds, buckets, out):
    page = pl.program_id(0)
    idx = jnp.transpose(buckets[0])
    heads = ds.shape[1]
    dsf = [ds[0, h].astype(F32) for h in range(heads)]
    rows = [[] for _ in range(heads)]
    for b in range(32):
        hit = idx == b
        for h in range(heads):
            rows[h].append(jnp.sum(jnp.where(hit, dsf[h], 0.0), axis=0, keepdims=True))
    for h in range(heads):
        part = jnp.concatenate(rows[h], axis=0)

        @pl.when(page == 0)
        def _():
            out[h] = part

        @pl.when(page != 0)
        def _():
            out[h] += part


def table_grad(ds, buckets):
    pages, heads, rows, _ = ds.shape
    (out,) = call(
        table_grad_kernel,
        (pages,),
        [paged(ds), paged(buckets)],
        [out_whole((heads, 32, rows), F32)],
        flops=64 * pages * heads * rows * rows,
        nbytes=pages * rows * rows * (4 + 2 * heads),
    )
    return jnp.sum(out, axis=-1)


def cross_q_kernel(xf, a_a, a_b, gain, wq, h1, n2, q2):
    k, rows, d = xf.shape
    h = xf[...].astype(F32) + a_a[...].astype(F32) + a_b[...].astype(F32)
    h1[...] = h
    h = h.reshape(k * rows, d)
    n = (h * inv_rms(h) * gain[...]).astype(BF)
    n2[...] = n.reshape(k, rows, d)
    q = nn(n, wq[...]).astype(BF).astype(F32) * SCALE
    q2[...] = q.astype(BF).reshape(k, rows, wq.shape[1])


def cross_q(xf, a_a, a_b, gain, wq, k):
    pages, rows, d = xf.shape
    w = wq.shape[1]
    return call(
        cross_q_kernel,
        (pages // k,),
        [paged(xf, k), paged(a_a, k), paged(a_b, k), whole(gain), whole(wq)],
        [
            out_paged((pages, rows, d), F32, k), out_paged((pages, rows, d), BF, k),
            out_paged((pages, rows, w), BF, k),
        ],
        flops=2 * pages * rows * d * w,
        nbytes=pages * rows * (12 * d + 2 * w) + 2 * d * w,
    )


def combine_kernel(nparts, *refs):
    os, ls = refs[:nparts], refs[nparts : 2 * nparts]
    wo, o2, o2t, lse, c_part = refs[2 * nparts :]
    k, w, rows = o2t.shape
    heads = w // HEAD_DIM
    flat = []
    for i in range(k):
        m = ls[0][i]
        for l in ls[1:]:
            m = jnp.maximum(m, l[i])
        es = [jnp.exp(l[i] - m) for l in ls]
        total = sum(es[1:], es[0])
        lse[i] = m + jnp.log(total)
        inv = 1.0 / total
        ws = [e * inv for e in es]
        pieces = []
        for h in range(heads):
            r = slice(h * HEAD_DIM, (h + 1) * HEAD_DIM)
            acc = os[0][i, r, :].astype(F32) * ws[0][h : h + 1, :]
            for o, ww in zip(os[1:], ws[1:]):
                acc = acc + o[i, r, :].astype(F32) * ww[h : h + 1, :]
            pieces.append(acc)
        ot = jnp.concatenate(pieces, axis=0)
        o2t[i] = ot.astype(BF)
        o = jnp.transpose(ot).astype(BF)
        o2[i] = o
        flat.append(o)
    c = nn(jnp.concatenate(flat, axis=0), wo[...])
    c_part[...] = c.astype(BF).reshape(c_part.shape)


def combine(os, ls, wo, k):
    pages, w, rows = os[0].shape
    d = wo.shape[1]
    return call(
        functools.partial(combine_kernel, len(os)),
        (pages // k,),
        [paged(o, k) for o in os] + [paged(l, k) for l in ls] + [whole(wo)],
        [
            out_paged((pages, rows, w), BF, k), out_paged((pages, w, rows), BF, k),
            out_paged((pages, 8, rows), F32, k), out_paged((pages, rows, d), BF, k),
        ],
        flops=2 * pages * rows * d * w,
        nbytes=pages * rows * (2 * d + 8 * w) + 2 * d * w,
    )


def ffn_kernel(h1, c_a, c_b, cot, gain, w_in, w_out, h2, n3, act_out, du_out, dn3):
    k, rows, d = h1.shape
    h = (h1[...] + c_a[...].astype(F32) + c_b[...].astype(F32)).reshape(k * rows, d)
    h2[...] = h.reshape(k, rows, d)
    n = (h * inv_rms(h) * gain[...]).astype(BF)
    n3[...] = n.reshape(k, rows, d)
    g = cot[...].reshape(k * rows, d)
    units = w_in.shape[1]
    step = units // 3
    root = 0.7978845608028654
    total = None
    for j in range(0, units, step):
        c = slice(j, j + step)
        u = nn(n, w_in[:, c])
        da = nt(g, w_out[c, :])
        u2 = u * u
        th = jnp.tanh(root * u * (1.0 + 0.044715 * u2))
        half = 0.5 + 0.5 * th
        act_out[:, :, c] = (u * half).astype(BF).reshape(k, rows, step)
        slope = half + (0.5 * root) * u * (1.0 - th * th) * (1.0 + (3 * 0.044715) * u2)
        du = (da * slope).astype(BF)
        du_out[:, :, c] = du.reshape(k, rows, step)
        part = nt(du, w_in[:, c])
        total = part if total is None else total + part
    dn3[...] = total.astype(BF).reshape(k, rows, d)


def ffn(h1, c_a, c_b, cot, gain, w_in, w_out, k):
    pages, rows, d = h1.shape
    units = w_in.shape[1]
    return call(
        ffn_kernel,
        (pages // k,),
        [
            paged(h1, k), paged(c_a, k), paged(c_b, k), paged(cot, k), whole(gain), whole(w_in),
            whole(w_out),
        ],
        [
            out_paged((pages, rows, d), F32, k), out_paged((pages, rows, d), BF, k),
            out_paged((pages, rows, units), BF, k), out_paged((pages, rows, units), BF, k),
            out_paged((pages, rows, d), BF, k),
        ],
        flops=6 * pages * rows * d * units,
        nbytes=pages * rows * (18 * d + 4 * units) + 4 * d * units,
        exps=pages * rows * units,
    )


def grad_two_kernel(head, h2, dn_a, dn_b, cot, gain, wo, o2t, dh2, dcr_out, do2, delta, gain_grad):
    step = pl.program_id(0)
    k, rows, d = h2.shape
    half = rows // 2
    w = wo.shape[0]
    first = head[0] == 0
    gacc = None
    flat = []
    for i in range(k):
        gg, dv = norm_back(h2[i], gain[...], dn_a[i].astype(F32) + dn_b[i].astype(F32))
        part = fold8(jnp.where(first, gg[:half], gg[half:]))
        gacc = part if gacc is None else gacc + part
        g = cot[i].astype(F32) + dv
        dh2[i] = g
        dcr = g.astype(BF)
        dcr_out[i] = dcr
        flat.append(dcr)
        dot = nt(wo[...], dcr).astype(BF).astype(F32) * o2t[i].astype(F32)
        sums = [
            jnp.sum(dot[a : a + HEAD_DIM], axis=0, keepdims=True) for a in range(0, w, HEAD_DIM)
        ]
        sums += [jnp.zeros((1, rows), F32)] * (8 - len(sums))
        delta[i] = jnp.concatenate(sums, axis=0)
    do2[...] = nt(jnp.concatenate(flat, axis=0), wo[...]).astype(BF).reshape(k, rows, w)

    @pl.when(step == 0)
    def _():
        gain_grad[...] = gacc

    @pl.when(step != 0)
    def _():
        gain_grad[...] += gacc


def grad_two(head, h2, dn_a, dn_b, cot, gain, wo, o2t, k):
    pages, rows, d = h2.shape
    w = wo.shape[0]
    return call(
        grad_two_kernel,
        (pages // k,),
        [
            paged(h2, k), paged(dn_a, k), paged(dn_b, k), paged(cot, k), whole(gain), whole(wo),
            paged(o2t, k),
        ],
        [
            out_paged((pages, rows, d), F32, k), out_paged((pages, rows, d), BF, k),
            out_paged((pages, rows, w), BF, k), out_paged((pages, 8, rows), F32, k),
            out_whole((8, d), F32),
        ],
        scalars=(head,),
        flops=4 * pages * rows * d * w,
        nbytes=pages * rows * (18 * d + 4 * w) + 2 * d * w,
    )


def grad_q_kernel(nparts, *refs):
    parts = refs[:nparts]
    wq, dq2, dn2 = refs[nparts:]
    k, w, rows = parts[0].shape
    flat = []
    for i in range(k):
        acc = parts[0][i].astype(F32)
        for p in parts[1:]:
            acc = acc + p[i].astype(F32)
        dq = jnp.transpose(acc).astype(BF)
        dq2[i] = dq
        flat.append(dq)
    dn = nt(jnp.concatenate(flat, axis=0), wq[...])
    dn2[...] = dn.astype(BF).reshape(dn2.shape)


def grad_q(parts, wq, k):
    pages, w, rows = parts[0].shape
    d = wq.shape[0]
    return call(
        functools.partial(grad_q_kernel, len(parts)),
        (pages // k,),
        [paged(p, k) for p in parts] + [whole(wq)],
        [out_paged((pages, rows, w), BF, k), out_paged((pages, rows, d), BF, k)],
        flops=2 * pages * rows * d * w,
        nbytes=pages * rows * (2 * d + 8 * w) + 2 * d * w,
    )


def last_kernel(xo, dn_a, dn_b, dh1, gain, out, gain_grad):
    page = pl.program_id(0)
    gg, dv = norm_back(
        xo[0].astype(F32), gain[...], dn_a[0].astype(F32) + dn_b[0].astype(F32)
    )
    out[0] = dh1[0] + dv
    part = fold8(gg)

    @pl.when(page == 0)
    def _():
        gain_grad[...] = part

    @pl.when(page != 0)
    def _():
        gain_grad[...] += part


def last(xo, dn_a, dn_b, dh1, gain):
    pages, half, d = xo.shape
    return call(
        last_kernel,
        (pages,),
        [paged(xo), paged(dn_a), paged(dn_b), paged(dh1), whole(gain)],
        [out_paged((pages, half, d), F32), out_whole((8, d), F32)],
        flops=20 * pages * half * d,
        nbytes=pages * half * d * 14,
    )


def branch_ffn_kernel(head, act, w_out, keep, send):
    k, rows, units = act.shape
    half = rows // 2
    first = head[0] == 0
    f = nn(act[...].reshape(k * rows, units), w_out[...])
    f = f.reshape(k, rows, f.shape[1])
    keep[...] = jnp.where(first, f[:, :half], f[:, half:]).astype(BF)
    send[...] = jnp.where(first, f[:, half:], f[:, :half]).astype(BF)


def branch_ffn(head, act, w_out, k):
    pages, rows, units = act.shape
    d = w_out.shape[1]
    return call(
        branch_ffn_kernel,
        (pages // k,),
        [paged(act, k), whole(w_out)],
        [out_paged((pages, rows // 2, d), BF, k), out_paged((pages, rows // 2, d), BF, k)],
        scalars=(head,),
        flops=2 * pages * rows * d * units,
        nbytes=pages * rows * (2 * d + 2 * units) + 2 * d * units,
    )


def output_kernel(head, lens, h2, f_a, f_b, a_a, a_b, c_a, c_b, out, stats):
    page = pl.program_id(0)
    first = head[0] == 0
    half = f_a.shape[1]

    def mine(ref):
        v = ref[0].astype(F32)
        return jnp.where(first, v[:half], v[half:])

    f = f_a[0].astype(F32) + f_b[0].astype(F32)
    y = mine(h2) + f
    out[0] = y.astype(BF)
    a = mine(a_a) + mine(a_b)
    c = mine(c_a) + mine(c_b)
    row = lax.broadcasted_iota(jnp.int32, (half, 1), 0) + head[0] * half
    valid = (row < lens[page]).astype(F32)
    stats[0] = jnp.concatenate(
        [jnp.sum(v * v * valid, axis=0, keepdims=True) for v in (y, a, c, f)]
        + [jnp.zeros((4, y.shape[1]), F32)],
        axis=0,
    )


def output_rows(head, lens, h2, f_a, f_b, a_a, a_b, c_a, c_b):
    pages, rows, d = h2.shape
    return call(
        output_kernel,
        (pages,),
        [paged(a) for a in (h2, f_a, f_b, a_a, a_b, c_a, c_b)],
        [out_paged((pages, rows // 2, d), BF), out_paged((pages, 8, d), F32)],
        scalars=(head, lens),
        flops=10 * pages * rows * d,
        nbytes=pages * rows * d * 16,
    )


def kv_own_kernel(table, enc, w, kv):
    kv[0] = nn(enc[0], w[...]).astype(BF)


def kv_own(table, enc, w, slots):
    pages, n, d = enc.shape
    return call(
        kv_own_kernel,
        (slots,),
        [(enc, (1, n, d), lambda i, t: (t[i], 0, 0)), whole(w)],
        [out_paged((slots, n, w.shape[1]), BF)],
        scalars=(table,),
        flops=2 * slots * n * d * w.shape[1],
        nbytes=4 * slots * n * d + 2 * d * d,
    )[0]


def kv_rec_kernel(split, table, enc_a, enc_b, w, kv):
    i = pl.program_id(0)

    @pl.when(table[i] < split)
    def _():
        kv[0] = nn(enc_a[0], w[...]).astype(BF)

    @pl.when(table[i] >= split)
    def _():
        kv[0] = nn(enc_b[0], w[...]).astype(BF)


def rec_blocks(enc_a, enc_b):
    split, n, d = enc_a.shape
    return [
        (enc_a, (1, n, d), lambda i, t: (jnp.minimum(t[i], split - 1), 0, 0)),
        (enc_b, (1, n, d), lambda i, t: (jnp.maximum(t[i] - split, 0), 0, 0)),
    ]


def kv_rec(table, enc_a, enc_b, w):
    split, n, d = enc_a.shape
    slots = 2 * split
    return call(
        functools.partial(kv_rec_kernel, split),
        (slots,),
        rec_blocks(enc_a, enc_b) + [whole(w)],
        [out_paged((slots, n, w.shape[1]), BF)],
        scalars=(table,),
        flops=2 * slots * n * d * w.shape[1],
        nbytes=4 * slots * n * d + 2 * d * d,
    )[0]


def cross_fwd_kernel(lims, q, kv_a, kv_b, o, lse):
    slot = pl.program_id(0)
    rows, w = q.shape[1:]
    n = kv_a.shape[1]

    def run(masked):
        rowsum = []
        for t in range(w // PAIR):
            c = slice(t * PAIR, (t + 1) * PAIR)
            cv = slice(w + t * PAIR, w + (t + 1) * PAIR)
            qm = pair_rows(q[0, :, c])
            ss = []
            for j, kv in enumerate((kv_a, kv_b)):
                s = nt(kv[0, :, c], qm)
                if masked:
                    pos = lax.broadcasted_iota(jnp.int32, s.shape, 0)
                    s = jnp.where(pos < lims[j, slot], s, MASKED)
                ss.append(s)
            m = jnp.maximum(*[jnp.max(s, axis=0, keepdims=True) for s in ss])
            es = [jnp.exp(s - m) for s in ss]
            total = sum(jnp.sum(e, axis=0, keepdims=True) for e in es)
            acc = tn(kv_a[0, :, cv], es[0].astype(BF)) + tn(kv_b[0, :, cv], es[1].astype(BF))
            inv = 1.0 / total
            o[0, t * PAIR : t * PAIR + HEAD_DIM, :] = (
                acc[:HEAD_DIM, :rows] * inv[:, :rows]
            ).astype(BF)
            o[0, t * PAIR + HEAD_DIM : (t + 1) * PAIR, :] = (
                acc[HEAD_DIM:, rows:] * inv[:, rows:]
            ).astype(BF)
            row = m + jnp.log(total)
            rowsum += [row[:, :rows], row[:, rows:]]
        rowsum += [jnp.zeros((1, rows), F32)] * (8 - len(rowsum))
        lse[0] = jnp.concatenate(rowsum, axis=0)

    full = (lims[0, slot] >= n) & (lims[1, slot] >= n)
    pl.when(full)(lambda: run(False))
    pl.when(jnp.logical_not(full))(lambda: run(True))


def cross_fwd(lims, q, kv_a, kv_b):
    slots, rows, w = q.shape
    n = kv_a.shape[1]
    return call(
        cross_fwd_kernel,
        (slots,),
        [paged(q), paged(kv_a), paged(kv_b)],
        [out_paged((slots, w, rows), BF), out_paged((slots, 8, rows), F32)],
        scalars=(lims,),
        flops=32 * slots * rows * n * w,
        nbytes=slots * (8 * n * w + 4 * rows * w),
        exps=2 * slots * rows * n * w // HEAD_DIM,
    )


def cross_bwd_kernel(lims, q, do, lse, delta, kv_a, kv_b, dq, dkv_a, dkv_b):
    slot = pl.program_id(0)
    rows, w = q.shape[1:]
    n = kv_a.shape[1]

    def run(masked):
        for t in range(w // PAIR):
            c = slice(t * PAIR, (t + 1) * PAIR)
            cv = slice(w + t * PAIR, w + (t + 1) * PAIR)
            qm = pair_rows(q[0, :, c])
            gm = pair_rows(do[0, :, c])
            ls, dl = two_rows(lse[0], t), two_rows(delta[0], t)
            acc = None
            for j, (kv, dkv) in enumerate(((kv_a, dkv_a), (kv_b, dkv_b))):
                k = kv[0, :, c]
                s = nt(k, qm)
                if masked:
                    pos = lax.broadcasted_iota(jnp.int32, s.shape, 0)
                    s = jnp.where(pos < lims[j, slot], s, MASKED)
                p = jnp.exp(s - ls)
                ds = (p * (nt(kv[0, :, cv], gm) - dl)).astype(BF)
                dkv[0, :, c] = nn(ds, qm).astype(BF)
                dkv[0, :, cv] = nn(p.astype(BF), gm).astype(BF)
                part = tn(k, ds)
                acc = part if acc is None else acc + part
            dq[0, t * PAIR : t * PAIR + HEAD_DIM, :] = (acc[:HEAD_DIM, :rows] * SCALE).astype(BF)
            dq[0, t * PAIR + HEAD_DIM : (t + 1) * PAIR, :] = (
                acc[HEAD_DIM:, rows:] * SCALE
            ).astype(BF)

    full = (lims[0, slot] >= n) & (lims[1, slot] >= n)
    pl.when(full)(lambda: run(False))
    pl.when(jnp.logical_not(full))(lambda: run(True))


def cross_bwd(lims, q, do, lse, delta, kv_a, kv_b):
    slots, rows, w = q.shape
    n = kv_a.shape[1]
    return call(
        cross_bwd_kernel,
        (slots,),
        [paged(a) for a in (q, do, lse, delta, kv_a, kv_b)],
        [
            out_paged((slots, w, rows), BF), out_paged((slots, n, 2 * w), BF),
            out_paged((slots, n, 2 * w), BF),
        ],
        scalars=(lims,),
        flops=80 * slots * rows * n * w,
        nbytes=slots * (16 * n * w + 8 * rows * w),
        exps=2 * slots * rows * n * w // HEAD_DIM,
    )


def enc_terms(step, dkv, enc, wk_keep, wv_keep, wk_send, wv_send, keep, send, dw):
    w = wk_keep.shape[1]
    dk, dv = dkv[0, :, :w], dkv[0, :, w:]
    send[0] = (nt(dk, wk_send[...]) + nt(dv, wv_send[...])).astype(BF)
    keep[0] = (nt(dk, wk_keep[...]) + nt(dv, wv_keep[...])).astype(BF)
    part = tn(dkv[0], enc)

    @pl.when(step == 0)
    def _():
        dw[...] = part

    @pl.when(step != 0)
    def _():
        dw[...] += part


def enc_own_kernel(table, head, dkv, enc, wkk, wvk, wks, wvs, keep, send, dw):
    enc_terms(pl.program_id(0), dkv, enc[0], wkk, wvk, wks, wvs, keep, send, dw)


def enc_rec_kernel(split, table, head, dkv, enc_a, enc_b, wkk, wvk, wks, wvs, keep, send, dw):
    i = pl.program_id(0)

    @pl.when(table[i] < split)
    def _():
        enc_terms(i, dkv, enc_a[0], wkk, wvk, wks, wvs, keep, send, dw)

    @pl.when(table[i] >= split)
    def _():
        enc_terms(i, dkv, enc_b[0], wkk, wvk, wks, wvs, keep, send, dw)


def enc_back(table, head, dkv, encs, wk, wv):
    slots, n, w2 = dkv.shape
    d, w = wk.shape
    part = d // 2
    if len(encs) == 1:
        body = enc_own_kernel
        blocks = [(encs[0], (1, n, d), lambda i, t, h: (t[i], 0, 0))]
    else:
        split = encs[0].shape[0]
        body = functools.partial(enc_rec_kernel, split)
        blocks = [
            (encs[0], (1, n, d), lambda i, t, h: (jnp.minimum(t[i], split - 1), 0, 0)),
            (encs[1], (1, n, d), lambda i, t, h: (jnp.maximum(t[i] - split, 0), 0, 0)),
        ]
    mine = lambda i, t, h: (h[0], 0)
    other = lambda i, t, h: (1 - h[0], 0)
    return call(
        body,
        (slots,),
        [paged(dkv)]
        + blocks
        + [
            (wk, (part, w), mine), (wv, (part, w), mine), (wk, (part, w), other),
            (wv, (part, w), other),
        ],
        [
            out_paged((slots, n, part), BF), out_paged((slots, n, part), BF),
            out_whole((w2, d), F32),
        ],
        scalars=(table, head),
        flops=4 * slots * n * d * w2,
        nbytes=slots * n * (2 * w2 + 4 * d),
    )


def add_pages_kernel(a, b, out):
    out[0] = (a[0].astype(F32) + b[0].astype(F32)).astype(out.dtype)


def add_pages(a, b):
    return call(
        add_pages_kernel,
        (a.shape[0],),
        [paged(a), paged(b)],
        [out_paged(a.shape, BF)],
        flops=a.size,
        nbytes=6 * a.size,
    )[0]


def enc_first_kernel(table, a, b, out):
    out[0] = a[0].astype(F32) + b[0].astype(F32)


def enc_first(table, a, b, pages):
    slots, n, c = a.shape
    return call(
        enc_first_kernel,
        (slots,),
        [paged(a), paged(b)],
        [((pages, n, c), F32, (1, n, c), lambda i, t: (t[i], 0, 0))],
        scalars=(table,),
        flops=a.size,
        nbytes=8 * a.size,
    )[0]


def enc_second_kernel(table, a, _, out):
    out[0] = a[0].astype(F32)


def enc_second(table, a, so_far):
    slots, n, c = a.shape
    return call(
        enc_second_kernel,
        (slots,),
        [paged(a), (so_far, (1, 8, 128), lambda i, t: (0, 0, 0))],
        [(so_far.shape, F32, (1, n, c), lambda i, t: (t[i], 0, 0))],
        scalars=(table,),
        flops=a.size,
        nbytes=6 * a.size,
        aliases={2: 0},
    )[0]


def swap(x, axis, mask, size):
    return lax.ppermute(x, axis, [(i, i ^ mask) for i in range(size)])


def bit_of(axis, mask):
    return (lax.axis_index(axis) // mask) % 2


def reduce_rows(x, steps, sizes):
    for axis, mask in steps:
        half = x.shape[0] // 2
        b = bit_of(axis, mask)
        keep = lax.dynamic_slice_in_dim(x, b * half, half, 0)
        send = lax.dynamic_slice_in_dim(x, (1 - b) * half, half, 0)
        got = swap(send, axis, mask, sizes[axis])
        x = (keep.astype(F32) + got.astype(F32)).astype(x.dtype)
    for axis, mask in reversed(steps):
        b = bit_of(axis, mask)
        got = swap(x, axis, mask, sizes[axis])
        x = jnp.concatenate([jnp.where(b == 0, x, got), jnp.where(b == 0, got, x)], axis=0)
    return x


def reduce_bucket(x, sizes):
    dp = [("dp", 1 << i) for i in range(sizes["dp"].bit_length() - 1)]
    seq = [("seq", 1 << i) for i in range(sizes["seq"].bit_length() - 1)]
    half = x.shape[0] // 2
    return jnp.concatenate(
        [
            reduce_rows(x[:half], dp + seq, sizes),
            reduce_rows(x[half:], dp[::-1] + seq, sizes),
        ],
        axis=0,
    )


def reduce_small(x, sizes):
    x = x + swap(x, "head", 1, sizes["head"])
    for axis in ("dp", "seq"):
        for i in range(sizes[axis].bit_length() - 1):
            x = x + swap(x, axis, 1 << i, sizes[axis])
    return x


def rows_grad(a, b):
    a = a.reshape(-1, a.shape[-1])
    b = b.reshape(-1, b.shape[-1])
    return lax.dot_general(a, b, (((0,), (0,)), ((), ())), preferred_element_type=F32).astype(BF)


def per_device(
    sizes,
    dec_input,
    enc_states,
    page_group,
    target_mask,
    rel_buckets,
    self_gain,
    cross_gain,
    ffn_gain,
    self_q,
    self_k,
    self_v,
    self_o,
    rel_table,
    cross_q_w,
    cross_k,
    cross_v,
    cross_o,
    ff_in,
    ff_out,
    cotangent,
):
    n_seq = sizes["seq"]
    pages, half, d = dec_input.shape
    n = enc_states.shape[1]
    w = self_q.shape[1]
    nb = n_seq // 2
    slots = nb * pages
    s = lax.axis_index("seq")
    h = lax.axis_index("head")
    block, par = s // 2, s % 2
    head = h.reshape(1).astype(jnp.int32)

    kk = jnp.arange(slots, dtype=jnp.int32) // pages
    pg = jnp.arange(slots, dtype=jnp.int32) % pages
    owner = (block + kk) % nb
    own_table = ((owner * 2 + par) * pages + pg).astype(jnp.int32)
    away_table = ((owner * 2 + 1 - par) * pages + pg).astype(jnp.int32)
    rec_table = (((owner - h * (nb // 2)) % nb) * pages + pg).astype(jnp.int32)

    def head_swap(x):
        return swap(x, "head", 1, 2)

    def owners(x):
        got = [x]
        for step in range(1, nb):
            perm = [
                (2 * b + r, 2 * ((b - step) % nb) + r) for b in range(nb) for r in range(2)
            ]
            got.append(lax.ppermute(x, "seq", perm))
        return got

    def returned(x):
        got = [x[:pages]]
        for step in range(1, nb):
            perm = [
                (2 * b + r, 2 * ((b + step) % nb) + r) for b in range(nb) for r in range(2)
            ]
            got.append(lax.ppermute(x[step * pages : (step + 1) * pages], "seq", perm))
        return got

    x_other = head_swap(dec_input)
    away = lax.dynamic_slice(
        enc_states.reshape(nb, 2, pages, n, d),
        (h * (nb // 2), 1 - par, 0, 0, 0),
        (nb // 2, 1, pages, n, d),
    ).reshape(slots // 2, n, d)
    enc_a = swap(away, "seq", 1, n_seq)
    cot_other = head_swap(cotangent)
    cot = jnp.concatenate(
        [jnp.where(h == 0, cotangent, cot_other), jnp.where(h == 0, cot_other, cotangent)], axis=1
    )
    groups = jnp.concatenate(owners(page_group))
    enc_len = OCR + PATCH_SMALL + groups * (PATCH_LARGE - PATCH_SMALL)
    lims = jnp.stack([enc_len - s * n, enc_len - (s + 1 - 2 * par) * n]).astype(jnp.int32)
    lens = jnp.sum(target_mask, axis=1).astype(jnp.int32)
    table = jnp.pad(rel_table.T, ((0, 8 - rel_table.shape[1]), (0, 128 - rel_table.shape[0])))
    gains = [g.reshape(1, d) for g in (self_gain, cross_gain, ffn_gain)]
    w_kv = jnp.concatenate([cross_k, cross_v], axis=1)

    xf, n1, qkv, o1, lse1, a_part = self_fwd(
        head, lens, dec_input, x_other, gains[0], self_q, self_k, self_v, self_o, rel_buckets, table
    )
    a_other = head_swap(a_part)
    kv_a = kv_own(own_table, enc_states, w_kv, slots)
    h1, n2, q2 = cross_q(xf, a_part, a_other, gains[1], cross_q_w, 2)
    q_all = jnp.concatenate(owners(q2), axis=0)
    enc_b = head_swap(enc_a)
    kv_b = kv_rec(rec_table, enc_a, enc_b, w_kv)
    o_all, lse_all = cross_fwd(lims, q_all, kv_a, kv_b)
    o2, o2t, lse2, c_part = combine(returned(o_all), returned(lse_all), cross_o, 2)
    c_other = head_swap(c_part)
    h2, n3, act, du, dn3 = ffn(h1, c_part, c_other, cot, gains[2], ff_in, ff_out, 2)
    dn3_other = head_swap(dn3)
    dh2, dcr, do2, delta, ffn_gain_part = grad_two(
        head, h2, dn3, dn3_other, cot, gains[2], cross_o, o2t, 2
    )
    do_all = jnp.concatenate(owners(do2), axis=0)
    lse_back = jnp.concatenate(owners(lse2), axis=0)
    delta_all = jnp.concatenate(owners(delta), axis=0)

    f_keep, f_send = branch_ffn(head, act, ff_out, 2)
    f_other = head_swap(f_send)
    output, squares = output_rows(
        head, lens, h2, f_keep, f_other, a_part, a_other, c_part, c_other
    )
    bucket_ffn = jnp.concatenate([rows_grad(act, cot), rows_grad(du, n3)], axis=0)
    sum_ffn = reduce_bucket(bucket_ffn, sizes)

    dq_all, dkv_a, dkv_b = cross_bwd(lims, q_all, do_all, lse_back, delta_all, kv_a, kv_b)
    dq2, dn2 = grad_q(returned(dq_all), cross_q_w, 2)
    dn2_other = head_swap(dn2)
    keep_b, send_b, dw_b = enc_back(rec_table, head, dkv_b, [enc_a, enc_b], cross_k, cross_v)
    back_b = add_pages(keep_b, head_swap(send_b))
    enc_away = swap(back_b, "seq", 1, n_seq)
    keep_a, send_a, dw_a = enc_back(own_table, head, dkv_a, [enc_states], cross_k, cross_v)
    enc_grad = enc_first(own_table, keep_a, head_swap(send_a), enc_states.shape[0])

    dh1, dar, dqkv, ds1, dn1_keep, dn1_send, cross_gain_part = self_bwd(
        head, lens, h1, dn2, dn2_other, dh2, gains[1], self_q, self_k, self_v, self_o,
        rel_buckets, table, qkv, lse1,
    )
    dn1_other = head_swap(dn1_send)
    bucket_cross = jnp.concatenate(
        [rows_grad(dq2, n2), (dw_a + dw_b).astype(BF), rows_grad(o2, dcr)], axis=0
    )
    sum_cross = reduce_bucket(bucket_cross, sizes)
    bucket_self = jnp.concatenate([rows_grad(dqkv, n1), rows_grad(o1, dar)], axis=0)
    sum_self = reduce_bucket(bucket_self, sizes)
    input_grad, self_gain_part = last(dec_input, dn1_keep, dn1_other, dh1, gains[0])
    table_part = table_grad(ds1, rel_buckets)
    enc_grad = enc_second(away_table, enc_away, enc_grad)

    small = jnp.stack([jnp.sum(g, axis=0) for g in (self_gain_part, cross_gain_part, ffn_gain_part)])
    squares = jnp.sum(squares[:, :4], axis=-1)
    squares = squares + head_swap(squares)
    counts = lens.astype(F32) * d
    rms_stats = jnp.sqrt(squares / counts[:, None])
    small = reduce_small(small, sizes)
    for axis in ("dp", "seq"):
        for i in range(sizes[axis].bit_length() - 1):
            table_part = table_part + swap(table_part, axis, 1 << i, sizes[axis])

    def turned(x):
        return jnp.transpose(x.astype(F32))

    units = ff_in.shape[1]
    return (
        output,
        input_grad,
        enc_grad,
        small[0],
        small[1],
        small[2],
        turned(sum_self[:w]),
        turned(sum_self[w : 2 * w]),
        turned(sum_self[2 * w : 3 * w]),
        sum_self[3 * w :].astype(F32),
        table_part.T,
        turned(sum_cross[:w]),
        turned(sum_cross[w : 2 * w]),
        turned(sum_cross[2 * w : 3 * w]),
        sum_cross[3 * w :].astype(F32),
        turned(sum_ffn[units:]),
        sum_ffn[:units].astype(F32),
        rms_stats,
    )


def solution(mesh):
    sizes = dict(mesh.shape)
    rows = P(("dp", "seq"), "head", None)
    cols, tall = P(None, "head"), P("head", None)
    placed = (
        rows, P("dp", "seq", None), P(("dp", "seq")), P(("dp", "seq"), None),
        P(("dp", "seq"), None, None), P(), P(), P(), cols, cols, cols, tall, cols, cols, cols, cols,
        tall, cols, tall, rows,
    )
    return jax.shard_map(
        functools.partial(per_device, sizes),
        mesh=mesh,
        in_specs=placed,
        out_specs=(
            rows, rows, P("dp", "seq", "head"), P(), P(), P(), cols, cols, cols, tall, cols, cols,
            cols, cols, tall, cols, tall, P(("dp", "seq"), None),
        ),
        check_vma=False,
    )
```

time: 1500 us -> 802 us (0.53)
  waiting for transfers between devices: 861 us -> 345 us
  matrix products: 261 us -> 13.6 us
  Pallas kernels: 0 us -> 237 us
  local copies, waits for them, and re-layouts: 199 us -> 61.9 us
  blocking collectives: 84.2 us -> 0 us
  starting transfers between devices: 25.3 us -> 78.7 us
    all_to_all x4 -> x0, waiting for transfers between devices: 416 us -> none  [the longest x1 136 us: per_device(): lax.all_to_all(key_cross_grad, 'seq', split_axis=1, concat_axis=0, tiled=...]
    psum x1 -> x0, waiting for transfers between devices: 355 us -> none  [per_device(): lax.psum((self_gain_grad, cross_gain_grad, ffn_gain_grad, self_q_grad, se...]
    ppermute x0 -> x79, waiting for transfers between devices: none -> 345 us  [the longest x71 289 us: swap(): return lax.ppermute(x, axis, [(i, i ^ mask) for i in range(size)])]
    pallas_call x0 -> x20, Pallas kernels: none -> 237 us  [call(): pl.pallas_call(body, grid_spec=spec, out_shape=[jax.ShapeDtypeStruct(s, d...]
    dot_general x43 -> x6, matrix products: 245 us -> 13.6 us  [rows_grad(): lax.dot_general(a, b, (((0,), (0,)), ((), ())), preferred_element_type=F32)]
    psum x2 -> x0, blocking collectives: 84.2 us -> none  [the longest x1 80.3 us: per_device(): lax.psum((self_gain_grad, cross_gain_grad, ffn_gain_grad, self_q_grad, se...]
    ppermute x0 -> x79, starting transfers between devices: none -> 78.7 us  [the longest x71 68.7 us: swap(): return lax.ppermute(x, axis, [(i, i ^ mask) for i in range(size)])]
    unnamed x172 -> x122, local copies, waits for them, and re-layouts: 102 us -> 48.2 us
  transfers between devices with their start and end apart: 18 -> 79, of which waited for: 15 -> 44; matrix products, arithmetic and copies ran while one was open for 20% -> 11% of each run, Pallas kernels for 0% -> 22%
where the time goes in v1:
time: 802 us; the launch traced here: 791 us
  waiting for transfers between devices  345 us (43%)
  Pallas kernels  237 us (30%)
  starting transfers between devices  78.7 us (10%)
  local copies, waits for them, and re-layouts  61.9 us (8%)
  other arithmetic  53 us (7%)
  matrix products  13.6 us (2%)
    ppermute x71, waiting for transfers between devices, swap(): return lax.ppermute(x, axis, [(i, i ^ mask) for i in range(size)])  289 us
    pallas_call x20, Pallas kernels, call(): pl.pallas_call(body, grid_spec=spec, out_shape=[jax.ShapeDtypeStruct(s, d...  237 us
    ppermute x71, starting transfers between devices, swap(): return lax.ppermute(x, axis, [(i, i ^ mask) for i in range(size)])  68.7 us
    unnamed x122, local copies, waits for them, and re-layouts  48.2 us
    ppermute x5, waiting for transfers between devices, owners(): got.append(lax.ppermute(x, 'seq', perm))  30.5 us
    ppermute x3, waiting for transfers between devices, returned(): got.append(lax.ppermute(x[step * pages:(step + 1) * pages], 'seq', perm))  25.4 us
  transfers between devices with their start and end apart: 79, of which 44 were waited for; matrix products, arithmetic and copies ran while one was open for 11% of the time, Pallas kernels for 22%

profile of v1, /device:TPU:0, one launch (start us, length us, event | category | flops | bytes accessed | tf_op | source)
XLA Modules:
  0.0 791.2 jit_solution(8686335670911111126)
XLA Ops:
  0.7 11.3 %copy.73.enc = bf16[24,324,768]{2,1,0:T(8,128)(2,1)} copy(bf16[24,324,768]{2,0,1:T(8,128)(2,1)} %param.21) | data formatting | bytes 23887872 | tf_op args[1]
  14.2 3.1 collective-permute-start.4
  17.2 65.6 %collective-permute-done.4.enc_a = bf16[6,324,768]{2,1,0:T(8,128)(2,1)} collective-permute-done((bf16[6,324,768]{2,1,0:T(8,128)(2,1)S(1)}, bf16[6,324,768]{2,1,0:T(8,128)(2,1)}, u32[]{:S(2)}, u32[]{:S(2)}) %collective-permute-start.4) | collective-permute-done | bytes 2986016 | tf_op jit(solution)/shard_map/ppermute | solution.py:865
  85.1 3.6 collective-permute-done.xr
  89.6 10.6 %shard_map.331 = (bf16[6,128,768]{2,1,0:T(8,128)(2,1)}, bf16[6,128,768]{2,1,0:T(8,128)(2,1)}, bf16[6,128,1152]{2,1,0:T(8,128)(2,1)}, bf16[6,128,384]{2,1,0:T(8,1...) custom-call(s32[1]{0:T(128)} %bitcast.head, s32[6]{0:T(128)} %reduce_sum.54.lens, bf16[6,64,768]{2,1,0:T(8,128)(2,1)} %xo.3, ...), custom_call_target="tpu_custom_call" | custom-call | flops 2113929216 | bytes 9437184 | tf_op jit(solution)/shard_map/pallas_call | solution.py:43
  100.6 2.8 collective-permute-start.2
  105.8 5.2 shard_map.332
  112.3 13.4 %shard_map.333.kv_a = bf16[12,324,768]{2,1,0:T(8,128)(2,1)} custom-call(s32[12]{0:T(128)} %get-tuple-element.236.table, bf16[24,324,768]{2,1,0:T(8,128)(2,1)} %copy.73.enc, bf16[768,768]{1,0:T(8,128)(2,1)} %copy-done.5), custom_call_target="tpu_custom_call" | custom-call | flops 4586471424 | bytes 13123584 | tf_op jit(solution)/shard_map/pallas_call | solution.py:43
  126.4 13.4 %collective-permute-done.3 = bf16[6,128,384]{2,1,0:T(8,128)(2,1)S(1)} collective-permute-done((bf16[6,128,384]{2,1,0:T(8,128)(2,1)}, bf16[6,128,384]{2,1,0:T(8,128)(2,1)S(1)}, u32[]{:S(2)}, u32[]{:S(2)}) %collective-permute-start.3) | collective-permute-done | bytes 589856 | tf_op jit(solution)/shard_map/ppermute | solution.py:964
  139.9 13.5 %shard_map.334.kv_b = bf16[12,324,768]{2,1,0:T(8,128)(2,1)} custom-call(s32[12]{0:T(128)} %get-tuple-element.235.table, bf16[6,324,768]{2,1,0:T(8,128)(2,1)} %collective-permute-done.4.enc_a, bf16[6,324,768]{2,1,0:T(8,128)(2,1)} %collective-permute-done.5.enc_b, bf16[768,768]{1,0:T(8,128)(2,1)} %copy-done.5), custom_call_target="tpu_custom_call" | custom-call | flops 4586471424 | bytes 13123584 | tf_op jit(solution)/shard_map/pallas_call | solution.py:43
  153.4 16.9 %shard_map.335 = (bf16[12,384,128]{2,1,0:T(8,128)(2,1)}, f32[12,8,128]{2,1,0:T(8,128)}) custom-call(s32[2,12]{1,0:T(2,128)} %pad_add_fusion.lims, bf16[12,128,384]{2,1,0:T(8,128)(2,1)} %copy-done.34, bf16[12,324,768]{2,1,0:T(8,128)(2,1)} %shard_map.333.kv_a, bf16[12,324,768]{2,1,0:T(8,128)(2,1)} %shard_map.334.kv_b), custom_call_target="tpu_custom_call" | custom-call | flops 6115295232 | bytes 14303232 | tf_op jit(solution)/shard_map/pallas_call | solution.py:43
  173.1 2.9 collective-permute-start.7
  176.0 25.4 %collective-permute-done.7.refs_3_ = f32[6,8,128]{2,1,0:T(8,128)S(1)} collective-permute-done((f32[6,8,128]{2,1,0:T(8,128)S(1)}, f32[6,8,128]{2,1,0:T(8,128)S(1)}, u32[]{:S(2)}, u32[]{:S(2)}) %collective-permute-start.7) | collective-permute-done | bytes 24608 | tf_op jit(solution)/shard_map/ppermute | solution.py:973
  202.2 4.5 shard_map.336
  207.8 2.6 collective-permute-done.9
  212.6 12.1 %shard_map.337 = (f32[6,128,768]{2,1,0:T(8,128)}, bf16[6,128,768]{2,1,0:T(8,128)(2,1)}, bf16[6,128,1536]{2,1,0:T(8,128)(2,1)}, bf16[6,128,1536]{2,1,0:T(8,128)(2,1)}, bf16[6,128,768]{2,1,0:T(8,128)(2,1)}) custom-call(f32[6,128,768]{2,1,0:T(8,128)} %get-tuple-element.69.h1, bf16[6,128,768]{2,1,0:T(8,128)(2,1)} %get-tuple-element.73.c_a, ...), custom_call_target="tpu_custom_call" | custom-call | flops 5435817984 | bytes 20054016 | tf_op jit(solution)/shard_map/pallas_call | solution.py:43
  224.7 3.7 bitcast_convert_fusion
  228.4 5.6 shard_map.338
  242.7 6.7 shard_map.339
  252.5 10.1 %collective-permute-done.70 = bf16[768,768]{1,0:T(8,128)(2,1)} collective-permute-done((bf16[768,768]{1,0:T(8,128)(2,1)S(1)}, bf16[768,768]{1,0:T(8,128)(2,1)}, u32[]{:S(2)}, u32[]{:S(2)}) %collective-permute-start.70) | collective-permute-done | bytes 1179680 | tf_op jit(solution)/shard_map/ppermute | solution.py:865
  266.0 2.8 collective-permute-done.62
  271.9 7.3 shard_map.340
  280.0 2.9 collective-permute-start.12
  285.1 9.2 %collective-permute-done.14 = f32[6,8,128]{2,1,0:T(8,128)S(1)} collective-permute-done((f32[6,8,128]{2,1,0:T(8,128)}, f32[6,8,128]{2,1,0:T(8,128)S(1)}, u32[]{:S(2)}, u32[]{:S(2)}) %collective-permute-start.14) | collective-permute-done | bytes 24608 | tf_op jit(solution)/shard_map/ppermute | solution.py:964
  300.2 7.9 collective-permute-done.12
  309.2 26.2 %shard_map.341 = (bf16[12,384,128]{2,1,0:T(8,128)(2,1)}, bf16[12,324,768]{2,1,0:T(8,128)(2,1)}, bf16[12,324,768]{2,1,0:T(8,128)(2,1)}) custom-call(s32[2,12]{1,0:T(2,128)} %pad_add_fusion.lims, bf16[12,128,384]{2,1,0:T(8,128)(2,1)} %copy-done.34, bf16[12,128,384]{2,1,0:T(8,128)(2,1)} %pad_maximum_fusion.1.do, f32[12,8,128]{2,1,0:T(8,128)} %pad_maximum_fusion.20.lse, ...), custom_call_target="tpu_custom_call" | custom-call | flops 15288238080 | bytes 28606464 | tf_op jit(solution)/shard_map/pallas_call | solution.py:43
  335.5 25.1 %shard_map.347 = (bf16[12,324,384]{2,1,0:T(8,128)(2,1)}, bf16[12,324,384]{2,1,0:T(8,128)(2,1)}, f32[768,768]{1,0:T(8,128)}) custom-call(s32[12]{0:T(128)} %get-tuple-element.236.table, s32[1]{0:T(128)} %bitcast.head, bf16[12,324,768]{2,1,0:T(8,128)(2,1)} %get-tuple-element.96.dkv, bf16[24,324,768]{2,1,0:T(8,128)(2,1)} %copy.73.enc, bf16[768,384]{1,0:T(8,128)(2,1)} %wks.3, ...), custom_call_target="tpu_custom_call" | custom-call | flops 9172942848 | bytes 17915904 | tf_op jit(solution)/shard_map/pallas_call | solution.py:43
  361.5 25.9 %shard_map.345 = (bf16[12,324,384]{2,1,0:T(8,128)(2,1)}, bf16[12,324,384]{2,1,0:T(8,128)(2,1)}, f32[768,768]{1,0:T(8,128)}) custom-call(s32[12]{0:T(128)} %get-tuple-element.235.table, s32[1]{0:T(128)} %bitcast.head, bf16[12,324,768]{2,1,0:T(8,128)(2,1)} %get-tuple-element.93.dkv, bf16[6,324,768]{2,1,0:T(8,128)(2,1)} %collective-permute-done.4.enc_a, ...), custom_call_target="tpu_custom_call" | custom-call | flops 9172942848 | bytes 17915904 | tf_op jit(solution)/shard_map/pallas_call | solution.py:43
  390.0 2.8 collective-permute-start.73
  393.1 10.8 %collective-permute-done.73 = bf16[96,768]{1,0:T(8,128)(2,1)S(1)} collective-permute-done((bf16[96,768]{1,0:T(8,128)(2,1)S(1)}, bf16[96,768]{1,0:T(8,128)(2,1)S(1)}, u32[]{:S(2)}, u32[]{:S(2)}) %collective-permute-start.73) | collective-permute-done | bytes 147488 | tf_op jit(solution)/shard_map/ppermute | solution.py:865
  404.1 7.8 collective-permute-done.65
  412.0 4.6 collective-permute-done.74
  420.1 4.3 shard_map.342
  433.3 10.9 %collective-permute-done.54 = bf16[384,768]{1,0:T(8,128)(2,1)S(1)} collective-permute-done((bf16[384,768]{1,0:T(8,128)(2,1)S(1)}, bf16[384,768]{1,0:T(8,128)(2,1)S(1)}, u32[]{:S(2)}, u32[]{:S(2)}) %collective-permute-start.54) | collective-permute-done | bytes 589856 | tf_op jit(solution)/shard_map/ppermute | solution.py:865
  446.6 8.4 %collective-permute-done.76 = bf16[384,768]{1,0:T(8,128)(2,1)S(1)} collective-permute-done((bf16[384,768]{1,0:T(8,128)(2,1)S(1)}, bf16[384,768]{1,0:T(8,128)(2,1)S(1)}, u32[]{:S(2)}, u32[]{:S(2)}) %collective-permute-start.76) | collective-permute-done | bytes 589856 | tf_op jit(solution)/shard_map/ppermute | solution.py:865
  456.7 3.1 collective-permute-done.68
  464.6 3.9 collective-permute-done.55
  470.6 3.0 collective-permute-done.48
  475.7 3.1 collective-permute-done.56
  481.0 3.1 collective-permute-done.49
  484.1 2.6 collective-permute-start.57
  489.3 2.9 collective-permute-start.50
  493.9 16.7 %shard_map.343 = (f32[6,64,768]{2,1,0:T(8,128)}, bf16[6,128,768]{2,1,0:T(8,128)(2,1)}, bf16[6,128,1152]{2,1,0:T(8,128)(2,1)}, bf16[6,6,128,128]{3,2,1,0:T(8,128)...) custom-call(s32[1]{0:T(128)} %bitcast.head, s32[6]{0:T(128)} %reduce_sum.54.lens, ...), custom_call_target="tpu_custom_call" | custom-call | flops 2566914048 | bytes 15335424 | tf_op jit(solution)/shard_map/pallas_call | solution.py:43
  511.4 8.9 %shard_map.350 = f32[6,32,128]{2,1,0:T(8,128)} custom-call(bf16[6,6,128,128]{3,2,1,0:T(8,128)(2,1)} %get-tuple-element.106.ds, s32[6,128,128]{2,1,0:T(8,128)} %buckets.5), custom_call_target="tpu_custom_call" | custom-call | flops 37748736 | bytes 1572864 | tf_op jit(solution)/shard_map/pallas_call | solution.py:43
  521.3 3.4 fusion
  538.9 3.3 collective-permute-done.44
  544.6 2.8 collective-permute-done.59
  550.2 3.9 collective-permute-done.52
  559.0 5.2 shard_map.344
  567.9 3.3 collective-permute-done.34
  573.6 9.4 %collective-permute-done.22 = f32[3,768]{1,0:T(4,128)S(1)} collective-permute-done((f32[3,768]{1,0:T(4,128)S(1)}, f32[3,768]{1,0:T(4,128)S(1)}, u32[]{:S(2)}, u32[]{:S(2)}) %collective-permute-start.22) | collective-permute-done | bytes 9248 | tf_op jit(solution)/shard_map/ppermute | solution.py:865
  592.8 2.9 collective-permute-done.25
  603.3 6.1 copy.89
  609.4 2.7 collective-permute-done.77
  615.7 13.8 %collective-permute-done.35 = bf16[192,768]{1,0:T(8,128)(2,1)S(1)} collective-permute-done((bf16[192,768]{1,0:T(8,128)(2,1)S(1)}, bf16[192,768]{1,0:T(8,128)(2,1)S(1)}, u32[]{:S(2)}, u32[]{:S(2)}) %collective-permute-start.35) | collective-permute-done | bytes 294944 | tf_op jit(solution)/shard_map/ppermute | solution.py:865
  631.1 5.8 collective-permute-done.27
  637.8 5.3 collective-permute-done.36
  643.7 5.9 collective-permute-done.28
  661.3 9.1 %shard_map.346 = bf16[12,324,384]{2,1,0:T(8,128)(2,1)} custom-call(bf16[12,324,384]{2,1,0:T(8,128)(2,1)} %get-tuple-element.94.a, bf16[12,324,384]{2,1,0:T(8,128)(2,1)} %collective-permute-done.18.b), custom_call_target="tpu_custom_call" | custom-call | flops 1492992 | bytes 8957952 | tf_op jit(solution)/shard_map/pallas_call | solution.py:43
  673.3 61.1 %collective-permute-done.39 = bf16[96,768]{1,0:T(8,128)(2,1)S(1)} collective-permute-done((bf16[96,768]{1,0:T(8,128)(2,1)S(1)}, bf16[96,768]{1,0:T(8,128)(2,1)S(1)}, u32[]{:S(2)}, u32[]{:S(2)}) %collective-permute-start.39) | collective-permute-done | bytes 147488 | tf_op jit(solution)/shard_map/ppermute | solution.py:865
  737.5 6.9 collective-permute-done.40
  752.4 10.2 %shard_map.348._ = f32[24,324,384]{2,1,0:T(8,128)} custom-call(s32[12]{0:T(128)} %get-tuple-element.236.table, bf16[12,324,384]{2,1,0:T(8,128)(2,1)} %get-tuple-element.97.a, bf16[12,324,384]{2,1,0:T(8,128)(2,1)} %collective-permute-done.20.b), custom_call_target="tpu_custom_call" | custom-call | flops 1492992 | bytes 11943936 | tf_op jit(solution)/shard_map/pallas_call | solution.py:43
  770.2 9.2 %shard_map.349 = f32[24,324,384]{2,1,0:T(8,128)} custom-call(s32[12]{0:T(128)} %multiply_add_fusion.table, bf16[12,324,384]{2,1,0:T(8,128)(2,1)} %collective-permute-done.19.a, f32[24,324,384]{2,1,0:T(8,128)} %shard_map.348._), custom_call_target="tpu_custom_call", output_to_operand_aliasing={{}: (2, {})} | custom-call | flops 1492992 | bytes 8957952 | tf_op jit(solution)/shard_map/pallas_call | solution.py:43
  779.5 11.3 %copy.82 = f32[24,324,384]{2,0,1:T(8,128)} copy(f32[24,324,384]{2,1,0:T(8,128)} %shard_map.349) | data formatting | bytes 23887872
  (375 shorter events, 170.2 us)
Async XLA Ops:
  14.2 68.7 %collective-permute-start.4 = (bf16[6,324,768]{2,1,0:T(8,128)(2,1)S(1)}, bf16[6,324,768]{2,1,0:T(8,128)(2,1)}, u32[]{:S(2)}, u32[]{:S(2)}) collective-permute-start(bf16[6,324,768]{2,1,0:T(8,128)(2,1)S(1)} %dynamic-slice_bitcast_fusion), channel_id=1, source_target_pairs={{0,2},{2,0},{4,6},{6,4},{1,3},{3,1},{5,7},{7,5},{8,10},{10,8},{12,... | collective-permute-start | bytes 8957960 | tf_op jit(solution)/shard_map/ppermute | solution.py:865
  82.8 57.1 %collective-permute-start.5 = (bf16[6,324,768]{2,1,0:T(8,128)(2,1)}, bf16[6,324,768]{2,1,0:T(8,128)(2,1)}, u32[]{:S(2)}, u32[]{:S(2)}) collective-permute-start(bf16[6,324,768]{2,1,0:T(8,128)(2,1)} %collective-permute-done.4.enc_a), channel_id=1, source_target_pairs={{0,1},{1,0},{2,3},{3,2},{4,5},{5,4},{6,7},{7,6},{8,9},{9,8},{10,11... | collective-permute-start | bytes 8957960 | tf_op jit(solution)/shard_map/ppermute | solution.py:865
  82.8 6.0 collective-permute-start
  100.6 25.1 %collective-permute-start.2 = (s32[6]{0:T(128)S(1)}, s32[6]{0:T(128)S(1)}, u32[]{:S(2)}, u32[]{:S(2)}) collective-permute-start(s32[6]{0:T(128)S(1)} %copy-done.47), channel_id=1, source_target_pairs={{0,4},{2,6},{4,0},{6,2},{1,5},{3,7},{5,1},{7,3},{8,12},{10,14},{12... | collective-permute-start | bytes 80 | tf_op jit(solution)/shard_map/ppermute | solution.py:964
  111.0 28.8 %collective-permute-start.3 = (bf16[6,128,384]{2,1,0:T(8,128)(2,1)}, bf16[6,128,384]{2,1,0:T(8,128)(2,1)S(1)}, u32[]{:S(2)}, u32[]{:S(2)}) collective-permute-start(bf16[6,128,384]{2,1,0:T(8,128)(2,1)} %get-tuple-element.70), channel_id=1, source_target_pairs={{0,4},{2,6},{4,0},{6,2},{1,5},{3,7},{5,1},{7,3},{8,12},{10,14},{12... | collective-permute-start | bytes 1769480 | tf_op jit(solution)/shard_map/ppermute | solution.py:964
  172.4 29.0 %collective-permute-start.6 = (bf16[6,384,128]{2,1,0:T(8,128)(2,1)S(1)}, bf16[6,384,128]{2,1,0:T(8,128)(2,1)S(1)}, u32[]{:S(2)}, u32[]{:S(2)}) collective-permute-start(bf16[6,384,128]{2,1,0:T(8,128)(2,1)S(1)} %get-tuple-element.197), channel_id=1, source_target_pairs={{0,4},{2,6},{4,0},{6,2},{1,5},{3,7},{5,1},{7,3},{8,12},{10,14},{12... | collective-permute-start | bytes 1769480 | tf_op jit(solution)/shard_map/ppermute | solution.py:973
  173.1 28.3 %collective-permute-start.7 = (f32[6,8,128]{2,1,0:T(8,128)S(1)}, f32[6,8,128]{2,1,0:T(8,128)S(1)}, u32[]{:S(2)}, u32[]{:S(2)}) collective-permute-start(f32[6,8,128]{2,1,0:T(8,128)S(1)} %get-tuple-element.231), channel_id=1, source_target_pairs={{0,4},{2,6},{4,0},{6,2},{1,5},{3,7},{5,1},{7,3},{8,12},{10,14},{12... | collective-permute-start | bytes 73736 | tf_op jit(solution)/shard_map/ppermute | solution.py:973
  234.0 7.8 collective-permute-start.10
  234.2 28.4 %collective-permute-start.70 = (bf16[768,768]{1,0:T(8,128)(2,1)S(1)}, bf16[768,768]{1,0:T(8,128)(2,1)}, u32[]{:S(2)}, u32[]{:S(2)}) collective-permute-start(bf16[768,768]{1,0:T(8,128)(2,1)S(1)} %constant_dynamic-slice_fusion.3), channel_id=1, source_target_pairs={{0,8},{8,0},{16,24},{24,16},{1,9},{9,1},{17,25},{25,17},{2,10},{10... | collective-permute-start | bytes 3538952 | tf_op jit(solution)/shard_map/ppermute | solution.py:865
  239.7 29.1 %collective-permute-start.62 = (bf16[768,768]{1,0:T(8,128)(2,1)}, bf16[768,768]{1,0:T(8,128)(2,1)}, u32[]{:S(2)}, u32[]{:S(2)}) collective-permute-start(bf16[768,768]{1,0:T(8,128)(2,1)} %constant_dynamic-slice_fusion.7), channel_id=1, source_target_pairs={{0,16},{8,24},{16,0},{24,8},{1,17},{9,25},{17,1},{25,9},{2,18},{10... | collective-permute-start | bytes 3538952 | tf_op jit(solution)/shard_map/ppermute | solution.py:865
  241.7 9.2 %collective-permute-start.13 = (f32[6,8,128]{2,1,0:T(8,128)S(1)}, f32[6,8,128]{2,1,0:T(8,128)S(1)}, u32[]{:S(2)}, u32[]{:S(2)}) collective-permute-start(f32[6,8,128]{2,1,0:T(8,128)S(1)} %copy-done.39), channel_id=1, source_target_pairs={{0,4},{2,6},{4,0},{6,2},{1,5},{3,7},{5,1},{7,3},{8,12},{10,14},{12... | collective-permute-start | bytes 73736 | tf_op jit(solution)/shard_map/ppermute | solution.py:964
  241.8 30.1 %collective-permute-start.11 = (bf16[6,128,768]{2,1,0:T(8,128)(2,1)}, bf16[6,128,768]{2,1,0:T(8,128)(2,1)}, u32[]{:S(2)}, u32[]{:S(2)}) collective-permute-start(bf16[6,128,768]{2,1,0:T(8,128)(2,1)} %get-tuple-element.79.dn_a), channel_id=1, source_target_pairs={{0,1},{1,0},{2,3},{3,2},{4,5},{5,4},{6,7},{7,6},{8,9},{9,8},{10,11... | collective-permute-start | bytes 3538952 | tf_op jit(solution)/shard_map/ppermute | solution.py:865
  264.4 30.5 %collective-permute-start.71 = (bf16[384,768]{1,0:T(8,128)(2,1)S(1)}, bf16[384,768]{1,0:T(8,128)(2,1)}, u32[]{:S(2)}, u32[]{:S(2)}) collective-permute-start(bf16[384,768]{1,0:T(8,128)(2,1)S(1)} %constant_dynamic-slice_fusion.2), channel_id=1, source_target_pairs={{0,16},{8,24},{16,0},{24,8},{1,17},{9,25},{17,1},{25,9},{2,18},{10... | collective-permute-start | bytes 1769480 | tf_op jit(solution)/shard_map/ppermute | solution.py:865
  270.5 26.4 %collective-permute-start.63 = (bf16[384,768]{1,0:T(8,128)(2,1)S(1)}, bf16[384,768]{1,0:T(8,128)(2,1)}, u32[]{:S(2)}, u32[]{:S(2)}) collective-permute-start(bf16[384,768]{1,0:T(8,128)(2,1)S(1)} %constant_dynamic-slice_fusion.6), channel_id=1, source_target_pairs={{0,8},{8,0},{16,24},{24,16},{1,9},{9,1},{17,25},{25,17},{2,10},{10... | collective-permute-start | bytes 1769480 | tf_op jit(solution)/shard_map/ppermute | solution.py:865
  280.0 14.3 %collective-permute-start.14 = (f32[6,8,128]{2,1,0:T(8,128)}, f32[6,8,128]{2,1,0:T(8,128)S(1)}, u32[]{:S(2)}, u32[]{:S(2)}) collective-permute-start(f32[6,8,128]{2,1,0:T(8,128)} %get-tuple-element.83), channel_id=1, source_target_pairs={{0,4},{2,6},{4,0},{6,2},{1,5},{3,7},{5,1},{7,3},{8,12},{10,14},{12... | collective-permute-start | bytes 73736 | tf_op jit(solution)/shard_map/ppermute | solution.py:964
  280.0 28.0 %collective-permute-start.12 = (bf16[6,128,384]{2,1,0:T(8,128)(2,1)}, bf16[6,128,384]{2,1,0:T(8,128)(2,1)S(1)}, u32[]{:S(2)}, u32[]{:S(2)}) collective-permute-start(bf16[6,128,384]{2,1,0:T(8,128)(2,1)} %get-tuple-element.81), channel_id=1, source_target_pairs={{0,4},{2,6},{4,0},{6,2},{1,5},{3,7},{5,1},{7,3},{8,12},{10,14},{12... | collective-permute-start | bytes 1769480 | tf_op jit(solution)/shard_map/ppermute | solution.py:964
  296.9 93.0 %collective-permute-start.72 = (bf16[192,768]{1,0:T(8,128)(2,1)}, bf16[192,768]{1,0:T(8,128)(2,1)S(1)}, u32[]{:S(2)}, u32[]{:S(2)}) collective-permute-start(bf16[192,768]{1,0:T(8,128)(2,1)} %constant_dynamic-slice_fusion.1), channel_id=1, source_target_pairs={{0,2},{2,0},{4,6},{6,4},{1,3},{3,1},{5,7},{7,5},{8,10},{10,8},{12,... | collective-permute-start | bytes 884744 | tf_op jit(solution)/shard_map/ppermute | solution.py:865
  298.2 94.6 %collective-permute-start.64 = (bf16[192,768]{1,0:T(8,128)(2,1)S(1)}, bf16[192,768]{1,0:T(8,128)(2,1)S(1)}, u32[]{:S(2)}, u32[]{:S(2)}) collective-permute-start(bf16[192,768]{1,0:T(8,128)(2,1)S(1)} %constant_dynamic-slice_fusion.5), channel_id=1, source_target_pairs={{0,2},{2,0},{4,6},{6,4},{1,3},{3,1},{5,7},{7,5},{8,10},{10,8},{12,... | collective-permute-start | bytes 884744 | tf_op jit(solution)/shard_map/ppermute | solution.py:865
  361.5 57.8 %collective-permute-start.15 = (bf16[6,384,128]{2,1,0:T(8,128)(2,1)S(1)}, bf16[6,384,128]{2,1,0:T(8,128)(2,1)S(1)}, u32[]{:S(2)}, u32[]{:S(2)}) collective-permute-start(bf16[6,384,128]{2,1,0:T(8,128)(2,1)S(1)} %get-tuple-element.193), channel_id=1, source_target_pairs={{0,4},{2,6},{4,0},{6,2},{1,5},{3,7},{5,1},{7,3},{8,12},{10,14},{12... | collective-permute-start | bytes 1769480 | tf_op jit(solution)/shard_map/ppermute | solution.py:973
  387.4 273.9 %collective-permute-start.18 = (bf16[12,324,384]{2,1,0:T(8,128)(2,1)}, bf16[12,324,384]{2,1,0:T(8,128)(2,1)}, u32[]{:S(2)}, u32[]{:S(2)}) collective-permute-start(bf16[12,324,384]{2,1,0:T(8,128)(2,1)} %get-tuple-element.95), channel_id=1, source_target_pairs={{0,1},{1,0},{2,3},{3,2},{4,5},{5,4},{6,7},{7,6},{8,9},{9,8},{10,11... | collective-permute-start | bytes 8957960 | tf_op jit(solution)/shard_map/ppermute | solution.py:865
  387.5 365.0 %collective-permute-start.20 = (bf16[12,324,384]{2,1,0:T(8,128)(2,1)}, bf16[12,324,384]{2,1,0:T(8,128)(2,1)}, u32[]{:S(2)}, u32[]{:S(2)}) collective-permute-start(bf16[12,324,384]{2,1,0:T(8,128)(2,1)} %get-tuple-element.98), channel_id=1, source_target_pairs={{0,1},{1,0},{2,3},{3,2},{4,5},{5,4},{6,7},{7,6},{8,9},{9,8},{10,11... | collective-permute-start | bytes 8957960 | tf_op jit(solution)/shard_map/ppermute | solution.py:865
  390.0 14.0 %collective-permute-start.73 = (bf16[96,768]{1,0:T(8,128)(2,1)S(1)}, bf16[96,768]{1,0:T(8,128)(2,1)S(1)}, u32[]{:S(2)}, u32[]{:S(2)}) collective-permute-start(bf16[96,768]{1,0:T(8,128)(2,1)S(1)} %constant_dynamic-slice_fusion), channel_id=1, source_target_pairs={{0,4},{2,6},{4,0},{6,2},{1,5},{3,7},{5,1},{7,3},{8,12},{10,14},{12... | collective-permute-start | bytes 442376 | tf_op jit(solution)/shard_map/ppermute | solution.py:865
  392.9 18.9 %collective-permute-start.65 = (bf16[96,768]{1,0:T(8,128)(2,1)S(1)}, bf16[96,768]{1,0:T(8,128)(2,1)S(1)}, u32[]{:S(2)}, u32[]{:S(2)}) collective-permute-start(bf16[96,768]{1,0:T(8,128)(2,1)S(1)} %constant_dynamic-slice_fusion.4), channel_id=1, source_target_pairs={{0,4},{2,6},{4,0},{6,2},{1,5},{3,7},{5,1},{7,3},{8,12},{10,14},{12... | collective-permute-start | bytes 442376 | tf_op jit(solution)/shard_map/ppermute | solution.py:865
  404.0 12.6 %collective-permute-start.74 = (bf16[96,768]{1,0:T(8,128)(2,1)S(1)}, bf16[96,768]{1,0:T(8,128)(2,1)S(1)}, u32[]{:S(2)}, u32[]{:S(2)}) collective-permute-start(bf16[96,768]{1,0:T(8,128)(2,1)S(1)} %add_convert_fusion.15), channel_id=1, source_target_pairs={{0,4},{2,6},{4,0},{6,2},{1,5},{3,7},{5,1},{7,3},{8,12},{10,14},{12... | collective-permute-start | bytes 442376 | tf_op jit(solution)/shard_map/ppermute | solution.py:865
  411.9 7.2 collective-permute-start.66
  416.6 12.7 %collective-permute-start.75 = (bf16[192,768]{1,0:T(8,128)(2,1)S(1)}, bf16[192,768]{1,0:T(8,128)(2,1)S(1)}, u32[]{:S(2)}, u32[]{:S(2)}) collective-permute-start(bf16[192,768]{1,0:T(8,128)(2,1)S(1)} %pad_maximum_fusion.15), channel_id=1, source_target_pairs={{0,2},{2,0},{4,6},{6,4},{1,3},{3,1},{5,7},{7,5},{8,10},{10,8},{12,... | collective-permute-start | bytes 884744 | tf_op jit(solution)/shard_map/ppermute | solution.py:865
  419.2 12.5 %collective-permute-start.67 = (bf16[192,768]{1,0:T(8,128)(2,1)S(1)}, bf16[192,768]{1,0:T(8,128)(2,1)S(1)}, u32[]{:S(2)}, u32[]{:S(2)}) collective-permute-start(bf16[192,768]{1,0:T(8,128)(2,1)S(1)} %pad_maximum_fusion.14), channel_id=1, source_target_pairs={{0,2},{2,0},{4,6},{6,4},{1,3},{3,1},{5,7},{7,5},{8,10},{10,8},{12,... | collective-permute-start | bytes 884744 | tf_op jit(solution)/shard_map/ppermute | solution.py:865
  427.8 16.3 %collective-permute-start.54 = (bf16[384,768]{1,0:T(8,128)(2,1)S(1)}, bf16[384,768]{1,0:T(8,128)(2,1)S(1)}, u32[]{:S(2)}, u32[]{:S(2)}) collective-permute-start(bf16[384,768]{1,0:T(8,128)(2,1)S(1)} %get-tuple-element.185), channel_id=1, source_target_pairs={{0,16},{8,24},{16,0},{24,8},{1,17},{9,25},{17,1},{25,9},{2,18},{10... | collective-permute-start | bytes 1769480 | tf_op jit(solution)/shard_map/ppermute | solution.py:865
  429.3 14.8 %collective-permute-start.46 = (bf16[384,768]{1,0:T(8,128)(2,1)S(1)}, bf16[384,768]{1,0:T(8,128)(2,1)S(1)}, u32[]{:S(2)}, u32[]{:S(2)}) collective-permute-start(bf16[384,768]{1,0:T(8,128)(2,1)S(1)} %get-tuple-element.186), channel_id=1, source_target_pairs={{0,8},{8,0},{16,24},{24,16},{1,9},{9,1},{17,25},{25,17},{2,10},{10... | collective-permute-start | bytes 1769480 | tf_op jit(solution)/shard_map/ppermute | solution.py:865
  431.6 23.4 %collective-permute-start.76 = (bf16[384,768]{1,0:T(8,128)(2,1)S(1)}, bf16[384,768]{1,0:T(8,128)(2,1)S(1)}, u32[]{:S(2)}, u32[]{:S(2)}) collective-permute-start(bf16[384,768]{1,0:T(8,128)(2,1)S(1)} %pad_maximum_fusion.9), channel_id=1, source_target_pairs={{0,16},{8,24},{16,0},{24,8},{1,17},{9,25},{17,1},{25,9},{2,18},{10... | collective-permute-start | bytes 1769480 | tf_op jit(solution)/shard_map/ppermute | solution.py:865
  444.1 48.8 %collective-permute-start.16 = (bf16[6,128,768]{2,1,0:T(8,128)(2,1)S(1)}, bf16[6,128,768]{2,1,0:T(8,128)(2,1)S(1)}, u32[]{:S(2)}, u32[]{:S(2)}) collective-permute-start(bf16[6,128,768]{2,1,0:T(8,128)(2,1)S(1)} %copy-done.21), channel_id=1, source_target_pairs={{0,1},{1,0},{2,3},{3,2},{4,5},{5,4},{6,7},{7,6},{8,9},{9,8},{10,11... | collective-permute-start | bytes 3538952 | tf_op jit(solution)/shard_map/ppermute | solution.py:865
  444.1 15.7 %collective-permute-start.68 = (bf16[384,768]{1,0:T(8,128)(2,1)S(1)}, bf16[384,768]{1,0:T(8,128)(2,1)S(1)}, u32[]{:S(2)}, u32[]{:S(2)}) collective-permute-start(bf16[384,768]{1,0:T(8,128)(2,1)S(1)} %pad_maximum_fusion.8), channel_id=1, source_target_pairs={{0,8},{8,0},{16,24},{24,16},{1,9},{9,1},{17,25},{25,17},{2,10},{10... | collective-permute-start | bytes 1769480 | tf_op jit(solution)/shard_map/ppermute | solution.py:865
  455.0 8.0 %collective-permute-start.47 = (bf16[192,768]{1,0:T(8,128)(2,1)S(1)}, bf16[192,768]{1,0:T(8,128)(2,1)S(1)}, u32[]{:S(2)}, u32[]{:S(2)}) collective-permute-start(bf16[192,768]{1,0:T(8,128)(2,1)S(1)} %constant_dynamic-slice_fusion.13), channel_id=1, source_target_pairs={{0,16},{8,24},{16,0},{24,8},{1,17},{9,25},{17,1},{25,9},{2,18},{10... | collective-permute-start | bytes 884744 | tf_op jit(solution)/shard_map/ppermute | solution.py:865
  459.9 8.6 %collective-permute-start.55 = (bf16[192,768]{1,0:T(8,128)(2,1)S(1)}, bf16[192,768]{1,0:T(8,128)(2,1)S(1)}, u32[]{:S(2)}, u32[]{:S(2)}) collective-permute-start(bf16[192,768]{1,0:T(8,128)(2,1)S(1)} %constant_dynamic-slice_fusion.10), channel_id=1, source_target_pairs={{0,8},{8,0},{16,24},{24,16},{1,9},{9,1},{17,25},{25,17},{2,10},{10... | collective-permute-start | bytes 884744 | tf_op jit(solution)/shard_map/ppermute | solution.py:865
  463.0 134.8 %collective-permute-start.69 = (bf16[768,768]{1,0:T(8,128)(2,1)}, bf16[768,768]{1,0:T(8,128)(2,1)}, u32[]{:S(2)}, u32[]{:S(2)}) collective-permute-start(bf16[768,768]{1,0:T(8,128)(2,1)} %pad_maximum_fusion.2), channel_id=1, source_target_pairs={{0,16},{8,24},{16,0},{24,8},{1,17},{9,25},{17,1},{25,9},{2,18},{10... | collective-permute-start | bytes 3538952 | tf_op jit(solution)/shard_map/ppermute | solution.py:865
  478.7 5.3 collective-permute-start.49
  484.1 5.3 collective-permute-start.57
  489.3 40.3 %collective-permute-start.50 = (bf16[48,768]{1,0:T(8,128)(2,1)}, bf16[48,768]{1,0:T(8,128)(2,1)}, u32[]{:S(2)}, u32[]{:S(2)}) collective-permute-start(bf16[48,768]{1,0:T(8,128)(2,1)} %add_convert_fusion.22), channel_id=1, source_target_pairs={{0,4},{2,6},{4,0},{6,2},{1,5},{3,7},{5,1},{7,3},{8,12},{10,14},{12... | collective-permute-start | bytes 221192 | tf_op jit(solution)/shard_map/ppermute | solution.py:865
  492.9 42.1 %collective-permute-start.58 = (bf16[48,768]{1,0:T(8,128)(2,1)}, bf16[48,768]{1,0:T(8,128)(2,1)}, u32[]{:S(2)}, u32[]{:S(2)}) collective-permute-start(bf16[48,768]{1,0:T(8,128)(2,1)} %add_convert_fusion.21), channel_id=1, source_target_pairs={{0,4},{2,6},{4,0},{6,2},{1,5},{3,7},{5,1},{7,3},{8,12},{10,14},{12... | collective-permute-start | bytes 221192 | tf_op jit(solution)/shard_map/ppermute | solution.py:865
  533.3 9.3 %collective-permute-start.51 = (bf16[96,768]{1,0:T(8,128)(2,1)S(1)}, bf16[96,768]{1,0:T(8,128)(2,1)S(1)}, u32[]{:S(2)}, u32[]{:S(2)}) collective-permute-start(bf16[96,768]{1,0:T(8,128)(2,1)S(1)} %pad_maximum_fusion.18), channel_id=1, source_target_pairs={{0,2},{2,0},{4,6},{6,4},{1,3},{3,1},{5,7},{7,5},{8,10},{10,8},{12,... | collective-permute-start | bytes 442376 | tf_op jit(solution)/shard_map/ppermute | solution.py:865
  542.5 6.5 collective-permute-start.45
  547.4 6.7 collective-permute-start.52
  549.0 6.8 collective-permute-start.60
  555.8 15.4 %collective-permute-start.34 = (bf16[384,768]{1,0:T(8,128)(2,1)}, bf16[384,768]{1,0:T(8,128)(2,1)}, u32[]{:S(2)}, u32[]{:S(2)}) collective-permute-start(bf16[384,768]{1,0:T(8,128)(2,1)} %fusion.4), channel_id=1, source_target_pairs={{0,16},{8,24},{16,0},{24,8},{1,17},{9,25},{17,1},{25,9},{2,18},{10... | collective-permute-start | bytes 1769480 | tf_op jit(solution)/shard_map/ppermute | solution.py:865
  567.2 16.4 %collective-permute-start.26 = (bf16[384,768]{1,0:T(8,128)(2,1)S(1)}, bf16[384,768]{1,0:T(8,128)(2,1)S(1)}, u32[]{:S(2)}, u32[]{:S(2)}) collective-permute-start(bf16[384,768]{1,0:T(8,128)(2,1)S(1)} %copy-done.29), channel_id=1, source_target_pairs={{0,8},{8,0},{16,24},{24,16},{1,9},{9,1},{17,25},{25,17},{2,10},{10... | collective-permute-start | bytes 1769480 | tf_op jit(solution)/shard_map/ppermute | solution.py:865
  571.1 11.9 %collective-permute-start.22 = (f32[3,768]{1,0:T(4,128)S(1)}, f32[3,768]{1,0:T(4,128)S(1)}, u32[]{:S(2)}, u32[]{:S(2)}) collective-permute-start(f32[3,768]{1,0:T(4,128)S(1)} %fusion.16), channel_id=1, source_target_pairs={{0,8},{8,0},{16,24},{24,16},{1,9},{9,1},{17,25},{25,17},{2,10},{10... | collective-permute-start | bytes 27656 | tf_op jit(solution)/shard_map/ppermute | solution.py:865
  583.0 29.1 %collective-permute-start.77 = (bf16[768,768]{1,0:T(8,128)(2,1)}, bf16[768,768]{1,0:T(8,128)(2,1)S(1)}, u32[]{:S(2)}, u32[]{:S(2)}) collective-permute-start(bf16[768,768]{1,0:T(8,128)(2,1)} %pad_maximum_fusion.3), channel_id=1, source_target_pairs={{0,8},{8,0},{16,24},{24,16},{1,9},{9,1},{17,25},{25,17},{2,10},{10... | collective-permute-start | bytes 3538952 | tf_op jit(solution)/shard_map/ppermute | solution.py:865
  595.7 152.7 %collective-permute-start.53 = (bf16[384,768]{1,0:T(8,128)(2,1)}, bf16[384,768]{1,0:T(8,128)(2,1)}, u32[]{:S(2)}, u32[]{:S(2)}) collective-permute-start(bf16[384,768]{1,0:T(8,128)(2,1)} %pad_maximum_fusion.6), channel_id=1, source_target_pairs={{0,8},{8,0},{16,24},{24,16},{1,9},{9,1},{17,25},{25,17},{2,10},{10... | collective-permute-start | bytes 1769480 | tf_op jit(solution)/shard_map/ppermute | solution.py:865
  597.8 52.9 %collective-permute-start.61 = (bf16[384,768]{1,0:T(8,128)(2,1)}, bf16[384,768]{1,0:T(8,128)(2,1)}, u32[]{:S(2)}, u32[]{:S(2)}) collective-permute-start(bf16[384,768]{1,0:T(8,128)(2,1)} %pad_maximum_fusion.7), channel_id=1, source_target_pairs={{0,16},{8,24},{16,0},{24,8},{1,17},{9,25},{17,1},{25,9},{2,18},{10... | collective-permute-start | bytes 1769480 | tf_op jit(solution)/shard_map/ppermute | solution.py:865
  612.1 17.4 %collective-permute-start.35 = (bf16[192,768]{1,0:T(8,128)(2,1)S(1)}, bf16[192,768]{1,0:T(8,128)(2,1)S(1)}, u32[]{:S(2)}, u32[]{:S(2)}) collective-permute-start(bf16[192,768]{1,0:T(8,128)(2,1)S(1)} %copy-done.36), channel_id=1, source_target_pairs={{0,8},{8,0},{16,24},{24,16},{1,9},{9,1},{17,25},{25,17},{2,10},{10... | collective-permute-start | bytes 884744 | tf_op jit(solution)/shard_map/ppermute | solution.py:865
  629.5 7.4 collective-permute-start.27
  636.9 6.2 collective-permute-start.36
  643.1 6.6 collective-permute-start.28
  649.6 8.6 %collective-permute-start.37 = (bf16[48,768]{1,0:T(8,128)(2,1)S(1)}, bf16[48,768]{1,0:T(8,128)(2,1)S(1)}, u32[]{:S(2)}, u32[]{:S(2)}) collective-permute-start(bf16[48,768]{1,0:T(8,128)(2,1)S(1)} %constant_dynamic-slice_fusion.14), channel_id=1, source_target_pairs={{0,4},{2,6},{4,0},{6,2},{1,5},{3,7},{5,1},{7,3},{8,12},{10,14},{12... | collective-permute-start | bytes 221192 | tf_op jit(solution)/shard_map/ppermute | solution.py:865
  650.7 8.8 %collective-permute-start.29 = (bf16[48,768]{1,0:T(8,128)(2,1)S(1)}, bf16[48,768]{1,0:T(8,128)(2,1)S(1)}, u32[]{:S(2)}, u32[]{:S(2)}) collective-permute-start(bf16[48,768]{1,0:T(8,128)(2,1)S(1)} %constant_dynamic-slice_fusion.17), channel_id=1, source_target_pairs={{0,4},{2,6},{4,0},{6,2},{1,5},{3,7},{5,1},{7,3},{8,12},{10,14},{12... | collective-permute-start | bytes 221192 | tf_op jit(solution)/shard_map/ppermute | solution.py:865
  658.2 12.8 %collective-permute-start.38 = (bf16[48,768]{1,0:T(8,128)(2,1)S(1)}, bf16[48,768]{1,0:T(8,128)(2,1)S(1)}, u32[]{:S(2)}, u32[]{:S(2)}) collective-permute-start(bf16[48,768]{1,0:T(8,128)(2,1)S(1)} %add_convert_fusion.23), channel_id=1, source_target_pairs={{0,4},{2,6},{4,0},{6,2},{1,5},{3,7},{5,1},{7,3},{8,12},{10,14},{12... | collective-permute-start | bytes 221192 | tf_op jit(solution)/shard_map/ppermute | solution.py:865
  659.5 13.1 %collective-permute-start.30 = (bf16[48,768]{1,0:T(8,128)(2,1)S(1)}, bf16[48,768]{1,0:T(8,128)(2,1)S(1)}, u32[]{:S(2)}, u32[]{:S(2)}) collective-permute-start(bf16[48,768]{1,0:T(8,128)(2,1)S(1)} %add_convert_fusion.24), channel_id=1, source_target_pairs={{0,4},{2,6},{4,0},{6,2},{1,5},{3,7},{5,1},{7,3},{8,12},{10,14},{12... | collective-permute-start | bytes 221192 | tf_op jit(solution)/shard_map/ppermute | solution.py:865
  670.5 99.8 %collective-permute-start.19 = (bf16[12,324,384]{2,1,0:T(8,128)(2,1)}, bf16[12,324,384]{2,1,0:T(8,128)(2,1)}, u32[]{:S(2)}, u32[]{:S(2)}) collective-permute-start(bf16[12,324,384]{2,1,0:T(8,128)(2,1)} %shard_map.346), channel_id=1, source_target_pairs={{0,2},{2,0},{4,6},{6,4},{1,3},{3,1},{5,7},{7,5},{8,10},{10,8},{12,... | collective-permute-start | bytes 8957960 | tf_op jit(solution)/shard_map/ppermute | solution.py:865
  671.1 63.3 %collective-permute-start.39 = (bf16[96,768]{1,0:T(8,128)(2,1)S(1)}, bf16[96,768]{1,0:T(8,128)(2,1)S(1)}, u32[]{:S(2)}, u32[]{:S(2)}) collective-permute-start(bf16[96,768]{1,0:T(8,128)(2,1)S(1)} %pad_maximum_fusion.17), channel_id=1, source_target_pairs={{0,2},{2,0},{4,6},{6,4},{1,3},{3,1},{5,7},{7,5},{8,10},{10,8},{12,... | collective-permute-start | bytes 442376 | tf_op jit(solution)/shard_map/ppermute | solution.py:865
  672.7 63.3 %collective-permute-start.31 = (bf16[96,768]{1,0:T(8,128)(2,1)S(1)}, bf16[96,768]{1,0:T(8,128)(2,1)S(1)}, u32[]{:S(2)}, u32[]{:S(2)}) collective-permute-start(bf16[96,768]{1,0:T(8,128)(2,1)S(1)} %pad_maximum_fusion.16), channel_id=1, source_target_pairs={{0,2},{2,0},{4,6},{6,4},{1,3},{3,1},{5,7},{7,5},{8,10},{10,8},{12,... | collective-permute-start | bytes 442376 | tf_op jit(solution)/shard_map/ppermute | solution.py:865
  734.5 10.0 %collective-permute-start.40 = (bf16[192,768]{1,0:T(8,128)(2,1)S(1)}, bf16[192,768]{1,0:T(8,128)(2,1)S(1)}, u32[]{:S(2)}, u32[]{:S(2)}) collective-permute-start(bf16[192,768]{1,0:T(8,128)(2,1)S(1)} %pad_maximum_fusion.11), channel_id=1, source_target_pairs={{0,8},{8,0},{16,24},{24,16},{1,9},{9,1},{17,25},{25,17},{2,10},{10... | collective-permute-start | bytes 884744 | tf_op jit(solution)/shard_map/ppermute | solution.py:865
  736.0 10.8 %collective-permute-start.32 = (bf16[192,768]{1,0:T(8,128)(2,1)S(1)}, bf16[192,768]{1,0:T(8,128)(2,1)S(1)}, u32[]{:S(2)}, u32[]{:S(2)}) collective-permute-start(bf16[192,768]{1,0:T(8,128)(2,1)S(1)} %pad_maximum_fusion.10), channel_id=1, source_target_pairs={{0,16},{8,24},{16,0},{24,8},{1,17},{9,25},{17,1},{25,9},{2,18},{10... | collective-permute-start | bytes 884744 | tf_op jit(solution)/shard_map/ppermute | solution.py:865
  745.4 17.2 %collective-permute-start.41 = (bf16[384,768]{1,0:T(8,128)(2,1)}, bf16[384,768]{1,0:T(8,128)(2,1)}, u32[]{:S(2)}, u32[]{:S(2)}) collective-permute-start(bf16[384,768]{1,0:T(8,128)(2,1)} %pad_maximum_fusion.5), channel_id=1, source_target_pairs={{0,16},{8,24},{16,0},{24,8},{1,17},{9,25},{17,1},{25,9},{2,18},{10... | collective-permute-start | bytes 1769480 | tf_op jit(solution)/shard_map/ppermute | solution.py:865
  747.8 18.4 %collective-permute-start.33 = (bf16[384,768]{1,0:T(8,128)(2,1)}, bf16[384,768]{1,0:T(8,128)(2,1)}, u32[]{:S(2)}, u32[]{:S(2)}) collective-permute-start(bf16[384,768]{1,0:T(8,128)(2,1)} %pad_maximum_fusion.4), channel_id=1, source_target_pairs={{0,8},{8,0},{16,24},{24,16},{1,9},{9,1},{17,25},{25,17},{2,10},{10... | collective-permute-start | bytes 1769480 | tf_op jit(solution)/shard_map/ppermute | solution.py:865
  (70 other events, 795.1 us)

commit v2 on v1

v2 whole, which is shorter than its diff:
```python
import functools

import jax
import jax.numpy as jnp
from jax import lax
from jax.experimental import pallas as pl
from jax.experimental.layout import Layout, with_layout_constraint
from jax.experimental.pallas import tpu as pltpu
from jax.sharding import PartitionSpec as P

HEAD_DIM = 64
OCR = 512
PATCH_SMALL = 196
PATCH_LARGE = 784
EPSILON = 1e-06
MASKED = -1000000000.0
BF = jnp.bfloat16
F32 = jnp.float32
SCALE = HEAD_DIM ** (-0.5)
VMEM = 56 * 1024 * 1024
PAIR = 2 * HEAD_DIM


def nn(a, b):
    return lax.dot_general(a, b, (((1,), (0,)), ((), ())), preferred_element_type=F32)


def nt(a, b):
    return lax.dot_general(a, b, (((1,), (1,)), ((), ())), preferred_element_type=F32)


def tn(a, b):
    return lax.dot_general(a, b, (((0,), (0,)), ((), ())), preferred_element_type=F32)


ORDER = []


def call(body, grid, ins, outs, *, us, scalars=(), scratch=(), after=(), aliases={}):
    held = [a for a, _, _ in ins]
    after = [t for t in [*after, *ORDER] if not any(t is a for a in held)]
    first, last = len(scalars) + len(ins), len(scalars) + len(ins) + len(after)

    def run(*refs):
        body(*refs[:first], *refs[last:])

    spec = pltpu.PrefetchScalarGridSpec(
        num_scalar_prefetch=len(scalars),
        grid=grid,
        in_specs=[pl.BlockSpec(b, m) for _, b, m in ins]
        + [pl.BlockSpec(memory_space=pl.ANY)] * len(after),
        out_specs=[pl.BlockSpec(b, m) for _, _, b, m in outs],
        scratch_shapes=list(scratch),
    )
    results = pl.pallas_call(
        run,
        grid_spec=spec,
        out_shape=[jax.ShapeDtypeStruct(s, d) for s, d, _, _ in outs],
        compiler_params=pltpu.CompilerParams(
            vmem_limit_bytes=VMEM, dimension_semantics=("arbitrary",) * len(grid)
        ),
        cost_estimate=pl.CostEstimate(flops=int(us * 1e10), bytes_accessed=0, transcendentals=0),
        input_output_aliases=aliases,
    )(*scalars, *[a for a, _, _ in ins], *after)
    ORDER[:] = [min(results, key=lambda r: r.size)]
    return results


def whole(a):
    n = a.ndim
    return (a, a.shape, lambda *_: (0,) * n)


def paged(a, k=1):
    a, at = a if isinstance(a, tuple) else (a, 0)
    n = a.ndim
    return (a, (k,) + a.shape[1:], lambda i, *_: (i + at // k,) + (0,) * (n - 1))


def kept(a):
    n = a.ndim
    return (a, (1,) * (n - 2) + (8, 128), lambda *_: (0,) * n)


def out_paged(shape, dtype, k=1):
    n = len(shape)
    return (shape, dtype, (k,) + tuple(shape[1:]), lambda i, *_: (i,) + (0,) * (n - 1))


def out_whole(shape, dtype):
    n = len(shape)
    return (shape, dtype, tuple(shape), lambda *_: (0,) * n)


def inv_rms(v):
    return lax.rsqrt(jnp.mean(v * v, axis=-1, keepdims=True) + EPSILON)


def pair_rows(block):
    lane = lax.broadcasted_iota(jnp.int32, (1, PAIR), 1)
    low = (lane < HEAD_DIM).astype(F32).astype(block.dtype)
    return jnp.concatenate([block * low, block * (1 - low)], axis=0)


def thirds(v):
    hi = v.astype(BF)
    rest = v - hi.astype(F32)
    mid = rest.astype(BF)
    return [hi, mid, (rest - mid.astype(F32)).astype(BF)]


def joined(hi, mid, lo):
    return hi.astype(F32) + mid.astype(F32) + lo.astype(F32)


STATS = 32
MORE = 32


def two_rows(ref_rows, t):
    return jnp.concatenate([ref_rows[2 * t : 2 * t + 1, :], ref_rows[2 * t + 1 : 2 * t + 2, :]], axis=1)


def norm_back(v, gain, dn):
    inv = inv_rms(v)
    weighted = dn * gain
    inner = jnp.mean(weighted * v, axis=-1, keepdims=True)
    return dn * v * inv, inv * weighted - v * (inv * inv * inv * inner)


def fold8(v):
    return jnp.sum(v.reshape(v.shape[0] // 8, 8, v.shape[1]), axis=0)


def self_bias(buckets_ref, table_ref, heads):
    idx = jnp.transpose(buckets_ref[0])
    rows = []
    for h in range(heads):
        tab = jnp.broadcast_to(table_ref[h : h + 1, :], idx.shape)
        rows.append(jnp.take_along_axis(tab, idx, axis=1))
    return rows


def self_allowed(length, rows):
    key = lax.broadcasted_iota(jnp.int32, (rows, rows), 0)
    query = lax.broadcasted_iota(jnp.int32, (rows, rows), 1)
    ok = (key <= query) & (key < length)
    return jnp.concatenate([ok, ok], axis=1)


def self_fwd_kernel(
    head, lens, xo, xr, gain, wq, wk, wv, wo, buckets, table, xf, n1, qkv, o1, lse, a_part
):
    page = pl.program_id(0)
    first = head[0] == 0
    own, rec = xo[0].astype(F32), xr[0].astype(F32)
    x = jnp.concatenate([jnp.where(first, own, rec), jnp.where(first, rec, own)], axis=0)
    xf[0] = x.astype(BF)
    n = (x * inv_rms(x) * gain[...]).astype(BF)
    n1[0] = n
    w = wq.shape[1]
    q = (nn(n, wq[...]).astype(BF).astype(F32) * SCALE).astype(BF)
    k = nn(n, wk[...]).astype(BF)
    v = nn(n, wv[...]).astype(BF)
    qkv[0, :, 0:w] = q
    qkv[0, :, w : 2 * w] = k
    qkv[0, :, 2 * w : 3 * w] = v
    rows = x.shape[0]
    bias = self_bias(buckets, table, w // HEAD_DIM)
    ok = self_allowed(lens[page], rows)
    lses, outs = [], []
    for t in range(w // PAIR):
        c = slice(t * PAIR, (t + 1) * PAIR)
        s = nt(k[:, c], pair_rows(q[:, c])) + jnp.concatenate(bias[2 * t : 2 * t + 2], axis=1)
        s = jnp.where(ok, s, MASKED)
        m = jnp.max(s, axis=0, keepdims=True)
        e = jnp.exp(s - m)
        total = jnp.sum(e, axis=0, keepdims=True)
        p = e * (1.0 / total)
        o = tn(p.astype(BF), v[:, c])
        lane = lax.broadcasted_iota(jnp.int32, (rows, PAIR), 1)
        outs.append(jnp.where(lane < HEAD_DIM, o[:rows], o[rows:]))
        row = m + jnp.log(total)
        lses += [row[:, :rows], row[:, rows:]]
    lses += [jnp.zeros((1, rows), F32)] * (8 - len(lses))
    lse[0] = jnp.concatenate(lses, axis=0)
    o = jnp.concatenate(outs, axis=1).astype(BF)
    o1[0] = o
    a_part[0] = nn(o, wo[...]).astype(BF)


def self_fwd(head, lens, xo, xr, gain, wq, wk, wv, wo, buckets, table, after=()):
    pages, half, d = xo.shape
    rows, w = 2 * half, wq.shape[1]
    return call(
        self_fwd_kernel,
        (pages,),
        [
            paged(xo), paged(xr), whole(gain), whole(wq), whole(wk), whole(wv), whole(wo),
            paged(buckets), whole(table),
        ],
        [
            out_paged((pages, rows, d), BF), out_paged((pages, rows, d), BF),
            out_paged((pages, rows, 3 * w), BF), out_paged((pages, rows, w), BF),
            out_paged((pages, 8, rows), F32), out_paged((pages, rows, d), BF),
        ],
        scalars=(head, lens),
        us=10, after=after,
    )


def self_bwd_kernel(
    at, head, lens, h1, dn_a, dn_b, dh2, gain, wq, wk, wv, wo, buckets, table, qkv, lse,
    dh1, dar_out, dq_out, dk_out, dv_out, ds_out, dn_keep, dn_send, gain_grad,
):
    page = pl.program_id(0)
    first = head[0] == 0
    v1 = h1[0]
    rows = v1.shape[0]
    half = rows // 2
    gg, dv = norm_back(v1, gain[...], dn_a[0].astype(F32) + dn_b[0].astype(F32))
    d1 = dh2[0] + dv
    gpart = fold8(jnp.where(first, gg[:half], gg[half:]))

    @pl.when(page == 0)
    def _():
        gain_grad[...] = gpart

    @pl.when(page != 0)
    def _():
        gain_grad[...] += gpart

    dh1[0] = jnp.where(first, d1[:half], d1[half:])
    dar = d1.astype(BF)
    dar_out[0] = dar
    w = wo.shape[0]
    do = nt(dar, wo[...]).astype(BF)
    bias = self_bias(buckets, table, w // HEAD_DIM)
    ok = self_allowed(lens[page + at], rows)
    lane = lax.broadcasted_iota(jnp.int32, (rows, PAIR), 1)
    dqs, dks, dvs = [], [], []
    for t in range(w // PAIR):
        c = slice(t * PAIR, (t + 1) * PAIR)
        q = pair_rows(qkv[0, :, t * PAIR : (t + 1) * PAIR])
        k = qkv[0, :, w + t * PAIR : w + (t + 1) * PAIR]
        v = qkv[0, :, 2 * w + t * PAIR : 2 * w + (t + 1) * PAIR]
        g = pair_rows(do[:, c])
        s = nt(k, q) + jnp.concatenate(bias[2 * t : 2 * t + 2], axis=1)
        s = jnp.where(ok, s, MASKED)
        p = jnp.exp(s - two_rows(lse[0], t))
        dp = nt(v, g)
        ds = (p * (dp - jnp.sum(p * dp, axis=0, keepdims=True))).astype(BF)
        ds_out[0, 2 * t] = ds[:, :rows]
        ds_out[0, 2 * t + 1] = ds[:, rows:]
        dq = tn(ds, k) * SCALE
        dqs.append(jnp.where(lane < HEAD_DIM, dq[:rows], dq[rows:]).astype(BF))
        dks.append(nn(ds, q).astype(BF))
        dvs.append(nn(p.astype(BF), g).astype(BF))
    dq, dk, dvv = (jnp.concatenate(a, axis=1) for a in (dqs, dks, dvs))
    dq_out[0] = dq
    dk_out[0] = dk
    dv_out[0] = dvv
    dn = (nt(dq, wq[...]) + nt(dk, wk[...]) + nt(dvv, wv[...])).astype(BF).astype(F32)
    dn_keep[0] = jnp.where(first, dn[:half], dn[half:]).astype(BF)
    dn_send[0] = jnp.where(first, dn[half:], dn[:half]).astype(BF)


def self_bwd(at, head, lens, h1, dn_a, dn_b, dh2, gain, wq, wk, wv, wo, buckets, table, qkv, lse, after=()):
    pages, rows, d = dh2.shape
    w = wq.shape[1]
    heads = w // HEAD_DIM
    return call(
        functools.partial(self_bwd_kernel, at),
        (pages,),
        [
            paged((h1, at)), paged(dn_a), paged(dn_b), paged(dh2), whole(gain), whole(wq),
            whole(wk), whole(wv), whole(wo), paged((buckets, at)), whole(table), paged((qkv, at)),
            paged((lse, at)),
        ],
        [
            out_paged((pages, rows // 2, d), F32), out_paged((pages, rows, d), BF),
            out_paged((pages, rows, w), BF), out_paged((pages, rows, w), BF),
            out_paged((pages, rows, w), BF), out_paged((pages, heads, rows, rows), BF),
            out_paged((pages, rows // 2, d), BF), out_paged((pages, rows // 2, d), BF),
            out_whole((8, d), F32),
        ],
        scalars=(head, lens),
        us=2.8 * pages,
        after=after,
    )


def table_grad_kernel(ds, buckets, out):
    page = pl.program_id(0)
    idx = jnp.transpose(buckets[0])
    heads = ds.shape[1]
    dsf = [ds[0, h].astype(F32) for h in range(heads)]
    rows = [[] for _ in range(heads)]
    for b in range(32):
        hit = idx == b
        for h in range(heads):
            rows[h].append(jnp.sum(jnp.where(hit, dsf[h], 0.0), axis=0, keepdims=True))
    for h in range(heads):
        part = jnp.concatenate(rows[h], axis=0)

        @pl.when(page == 0)
        def _():
            out[h] = part

        @pl.when(page != 0)
        def _():
            out[h] += part


def table_grad(ds, buckets, at, after=()):
    pages, heads, rows, _ = ds.shape
    (out,) = call(
        table_grad_kernel,
        (pages,),
        [paged(ds), paged((buckets, at))],
        [out_whole((heads, 32, rows), F32)],
        us=9, after=after,
    )
    return jnp.sum(out, axis=-1)


def cross_q_kernel(xf, a_a, a_b, gain, wq, h1, n2, q2):
    k, rows, d = xf.shape
    h = xf[...].astype(F32) + a_a[...].astype(F32) + a_b[...].astype(F32)
    h1[...] = h
    h = h.reshape(k * rows, d)
    n = (h * inv_rms(h) * gain[...]).astype(BF)
    n2[...] = n.reshape(k, rows, d)
    q = nn(n, wq[...]).astype(BF).astype(F32) * SCALE
    q2[...] = q.astype(BF).reshape(k, rows, wq.shape[1])


def cross_q(xf, a_a, a_b, gain, wq, k, after=()):
    pages, rows, d = xf.shape
    w = wq.shape[1]
    return call(
        cross_q_kernel,
        (pages // k,),
        [paged(xf, k), paged(a_a, k), paged(a_b, k), whole(gain), whole(wq)],
        [
            out_paged((pages, rows, d), F32, k), out_paged((pages, rows, d), BF, k),
            out_paged((pages, rows, w), BF, k),
        ],
        us=5, after=after,
    )


def combine_kernel(nparts, *refs):
    os = refs[:nparts]
    wo, o2, o2t, lse, c_part = refs[nparts:]
    k, w, rows = o2t.shape
    heads = w // HEAD_DIM
    flat = []
    for i in range(k):
        terms = [o[i, w:, :].astype(F32) for o in os]
        ls = [t[:8] + t[8:16] + t[16:24] for t in terms]
        m = ls[0]
        for l in ls[1:]:
            m = jnp.maximum(m, l)
        es = [jnp.exp(l - m) for l in ls]
        total = sum(es[1:], es[0])
        lse[i] = m + jnp.log(total)
        inv = 1.0 / total
        ws = [e * inv for e in es]
        pieces = []
        for h in range(heads):
            r = slice(h * HEAD_DIM, (h + 1) * HEAD_DIM)
            acc = os[0][i, r, :].astype(F32) * ws[0][h : h + 1, :]
            for o, ww in zip(os[1:], ws[1:]):
                acc = acc + o[i, r, :].astype(F32) * ww[h : h + 1, :]
            pieces.append(acc)
        ot = jnp.concatenate(pieces, axis=0)
        o2t[i] = ot.astype(BF)
        o = jnp.transpose(ot).astype(BF)
        o2[i] = o
        flat.append(o)
    c = nn(jnp.concatenate(flat, axis=0), wo[...])
    c_part[...] = c.astype(BF).reshape(c_part.shape)


def combine(os, wo, k, after=()):
    pages, _, rows = os[0].shape
    w, d = wo.shape
    return call(
        functools.partial(combine_kernel, len(os)),
        (pages // k,),
        [paged(o, k) for o in os] + [whole(wo)],
        [
            out_paged((pages, rows, w), BF, k), out_paged((pages, w, rows), BF, k),
            out_paged((pages, 8, rows), F32, k), out_paged((pages, rows, d), BF, k),
        ],
        us=4.5,
        after=after,
    )


def ffn_kernel(h1, c_a, c_b, cot, gain, w_in, w_out, h2, n3, act_out, du_out, dn3):
    k, rows, d = h1.shape
    h = (h1[...] + c_a[...].astype(F32) + c_b[...].astype(F32)).reshape(k * rows, d)
    h2[...] = h.reshape(k, rows, d)
    n = (h * inv_rms(h) * gain[...]).astype(BF)
    n3[...] = n.reshape(k, rows, d)
    g = cot[...].reshape(k * rows, d)
    units = w_in.shape[1]
    step = units // 3
    root = 0.7978845608028654
    total = None
    for j in range(0, units, step):
        c = slice(j, j + step)
        u = nn(n, w_in[:, c])
        da = nt(g, w_out[c, :])
        u2 = u * u
        th = jnp.tanh(root * u * (1.0 + 0.044715 * u2))
        half = 0.5 + 0.5 * th
        act_out[:, :, c] = (u * half).astype(BF).reshape(k, rows, step)
        slope = half + (0.5 * root) * u * (1.0 - th * th) * (1.0 + (3 * 0.044715) * u2)
        du = (da * slope).astype(BF)
        du_out[:, :, c] = du.reshape(k, rows, step)
        part = nt(du, w_in[:, c])
        total = part if total is None else total + part
    dn3[...] = total.astype(BF).reshape(k, rows, d)


def ffn(at, h1, c_a, c_b, cot, gain, w_in, w_out, k, after=()):
    pages, rows, d = c_a.shape
    units = w_in.shape[1]
    return call(
        ffn_kernel,
        (pages // k,),
        [
            paged((h1, at), k), paged(c_a, k), paged(c_b, k), paged((cot, at), k), whole(gain), whole(w_in),
            whole(w_out),
        ],
        [
            out_paged((pages, rows, d), F32, k), out_paged((pages, rows, d), BF, k),
            out_paged((pages, rows, units), BF, k), out_paged((pages, rows, units), BF, k),
            out_paged((pages, rows, d), BF, k),
        ],
        us=12, after=after,
    )


def grad_two_kernel(head, h2, dn_a, dn_b, cot, gain, wo, o2t, lse, dh2, dcr_out, do2, gain_grad):
    step = pl.program_id(0)
    k, rows, d = h2.shape
    half = rows // 2
    w = wo.shape[0]
    first = head[0] == 0
    gacc = None
    flat = []
    for i in range(k):
        gg, dv = norm_back(h2[i], gain[...], dn_a[i].astype(F32) + dn_b[i].astype(F32))
        part = fold8(jnp.where(first, gg[:half], gg[half:]))
        gacc = part if gacc is None else gacc + part
        g = cot[i].astype(F32) + dv
        dh2[i] = g
        dcr = g.astype(BF)
        dcr_out[i] = dcr
        flat.append(dcr)
        dot = nt(wo[...], dcr).astype(BF).astype(F32) * o2t[i].astype(F32)
        sums = [
            jnp.sum(dot[a : a + HEAD_DIM], axis=0, keepdims=True) for a in range(0, w, HEAD_DIM)
        ]
        sums += [jnp.zeros((1, rows), F32)] * (8 - len(sums))
        terms = thirds(lse[i]) + thirds(jnp.concatenate(sums, axis=0))
        stats = jnp.concatenate([t.astype(F32) for t in terms], axis=0)
        per = w // rows
        lines = [
            jnp.concatenate([stats[r + p : r + p + 1] for p in range(per)], axis=1)
            for t in range(6)
            for r in range(8 * t, 8 * t + w // HEAD_DIM, per)
        ]
        lines.append(jnp.zeros((MORE - len(lines), w), F32))
        do2[i, rows:, :] = jnp.concatenate(lines, axis=0).astype(BF)
    g2 = nt(jnp.concatenate(flat, axis=0), wo[...]).astype(BF)
    do2[:, :rows, :] = g2.reshape(k, rows, w)

    @pl.when(step == 0)
    def _():
        gain_grad[...] = gacc

    @pl.when(step != 0)
    def _():
        gain_grad[...] += gacc


def grad_two(at, head, h2, dn_a, dn_b, cot, gain, wo, o2t, lse, k, after=()):
    pages, rows, d = h2.shape
    w = wo.shape[0]
    return call(
        grad_two_kernel,
        (pages // k,),
        [
            paged(h2, k), paged(dn_a, k), paged(dn_b, k), paged((cot, at), k), whole(gain), whole(wo),
            paged(o2t, k), paged(lse, k),
        ],
        [
            out_paged((pages, rows, d), F32, k), out_paged((pages, rows, d), BF, k),
            out_paged((pages, rows + MORE, w), BF, k), out_whole((8, d), F32),
        ],
        scalars=(head,),
        us=5.6, after=after,
    )


def grad_q_kernel(nparts, *refs):
    parts = refs[:nparts]
    wq, dq2, dn2 = refs[nparts:]
    k, w, rows = parts[0].shape
    flat = []
    for i in range(k):
        acc = parts[0][i].astype(F32)
        for p in parts[1:]:
            acc = acc + p[i].astype(F32)
        dq = jnp.transpose(acc).astype(BF)
        dq2[i] = dq
        flat.append(dq)
    dn = nt(jnp.concatenate(flat, axis=0), wq[...])
    dn2[...] = dn.astype(BF).reshape(dn2.shape)


def grad_q(parts, wq, k, after=()):
    pages, w, rows = parts[0].shape
    d = wq.shape[0]
    return call(
        functools.partial(grad_q_kernel, len(parts)),
        (pages // k,),
        [paged(p, k) for p in parts] + [whole(wq)],
        [out_paged((pages, rows, w), BF, k), out_paged((pages, rows, d), BF, k)],
        us=4, after=after,
    )


def last_kernel(xo, dn_a, dn_b, dh1, gain, out, gain_grad):
    page = pl.program_id(0)
    gg, dv = norm_back(
        xo[0].astype(F32), gain[...], dn_a[0].astype(F32) + dn_b[0].astype(F32)
    )
    out[0] = dh1[0] + dv
    part = fold8(gg)

    @pl.when(page == 0)
    def _():
        gain_grad[...] = part

    @pl.when(page != 0)
    def _():
        gain_grad[...] += part


def last(at, xo, dn_a, dn_b, dh1, gain, after=()):
    pages, half, d = dh1.shape
    return call(
        last_kernel,
        (pages,),
        [paged((xo, at)), paged(dn_a), paged(dn_b), paged(dh1), whole(gain)],
        [out_paged((pages, half, d), F32), out_whole((8, d), F32)],
        us=0.9 * pages,
        after=after,
    )


def branch_ffn_kernel(head, act, w_out, keep, send):
    k, rows, units = act.shape
    half = rows // 2
    first = head[0] == 0
    f = nn(act[...].reshape(k * rows, units), w_out[...])
    f = f.reshape(k, rows, f.shape[1])
    keep[...] = jnp.where(first, f[:, :half], f[:, half:]).astype(BF)
    send[...] = jnp.where(first, f[:, half:], f[:, :half]).astype(BF)


def branch_ffn(head, act, w_out, k, after=()):
    pages, rows, units = act.shape
    d = w_out.shape[1]
    return call(
        branch_ffn_kernel,
        (pages // k,),
        [paged(act, k), whole(w_out)],
        [out_paged((pages, rows // 2, d), BF, k), out_paged((pages, rows // 2, d), BF, k)],
        scalars=(head,),
        us=6.8, after=after,
    )


def output_kernel(at, head, lens, h2, f_a, f_b, a_a, a_b, c_a, c_b, out, stats):
    page = pl.program_id(0)
    first = head[0] == 0
    half = f_a.shape[1]

    def mine(ref):
        v = ref[0].astype(F32)
        return jnp.where(first, v[:half], v[half:])

    f = f_a[0].astype(F32) + f_b[0].astype(F32)
    y = mine(h2) + f
    out[0] = y.astype(BF)
    a = mine(a_a) + mine(a_b)
    c = mine(c_a) + mine(c_b)
    row = lax.broadcasted_iota(jnp.int32, (half, 1), 0) + head[0] * half
    valid = (row < lens[page + at]).astype(F32)
    stats[0] = jnp.concatenate(
        [jnp.sum(v * v * valid, axis=0, keepdims=True) for v in (y, a, c, f)]
        + [jnp.zeros((4, y.shape[1]), F32)],
        axis=0,
    )


def output_rows(at, head, lens, h2, f_a, f_b, a_a, a_b, c_a, c_b, after=()):
    pages, rows, d = h2.shape
    return call(
        functools.partial(output_kernel, at),
        (pages,),
        [paged(a) for a in (h2, f_a, f_b, (a_a, at), (a_b, at), c_a, c_b)],
        [out_paged((pages, rows // 2, d), BF), out_paged((pages, 8, d), F32)],
        scalars=(head, lens),
        us=7.4, after=after,
    )


def gate(x):
    return pl.pallas_call(
        lambda *refs: None,
        out_shape=jax.ShapeDtypeStruct(x.shape, x.dtype),
        in_specs=[pl.BlockSpec(memory_space=pl.ANY)] * (1 + len(ORDER)),
        out_specs=pl.BlockSpec(memory_space=pl.ANY),
        input_output_aliases={0: 0},
        cost_estimate=pl.CostEstimate(flops=0, bytes_accessed=0, transcendentals=0),
    )(x, *ORDER)


def kv_kernel(copied, src, dst, enc, w, *refs):
    if copied:
        kv, copy = refs[-2:]
        copy[...] = enc[...]
    else:
        kv = refs[-1]
    for i in range(enc.shape[0]):
        kv[i] = nn(enc[i], w[...]).astype(BF)


def kv_project(src, dst, enc, w, slots, k, copied=False, prev=None, after=()):
    n, d = enc.shape[1:]
    ins = [(enc, (k, n, d), lambda i, a, b: (a[i], 0, 0)), whole(w)]
    if prev is not None:
        ins += [kept(p) for p in prev]
    widths = [w.shape[1]] + [d] * copied
    return call(
        functools.partial(kv_kernel, copied),
        (src.shape[0],),
        ins,
        [((slots, n, c), BF, (k, n, c), lambda i, a, b: (b[i], 0, 0)) for c in widths],
        scalars=(src, dst),
        us=0.9 * k * src.shape[0],
        after=after,
        aliases={} if prev is None else {4 + i: i for i in range(len(prev))},
    )


def cross_fwd_kernel(lims, q, kv_a, kv_b, o):
    slot = pl.program_id(0)
    rows, w = q.shape[1:]
    n = kv_a.shape[1]

    def run(masked):
        rowsum = []
        for t in range(w // PAIR):
            c = slice(t * PAIR, (t + 1) * PAIR)
            cv = slice(w + t * PAIR, w + (t + 1) * PAIR)
            qm = pair_rows(q[0, :, c])
            ss = []
            for j, kv in enumerate((kv_a, kv_b)):
                s = nt(kv[0, :, c], qm)
                if masked:
                    pos = lax.broadcasted_iota(jnp.int32, s.shape, 0)
                    s = jnp.where(pos < lims[j, slot], s, MASKED)
                ss.append(s)
            m = jnp.maximum(*[jnp.max(s, axis=0, keepdims=True) for s in ss])
            es = [jnp.exp(s - m) for s in ss]
            total = sum(jnp.sum(e, axis=0, keepdims=True) for e in es)
            acc = tn(kv_a[0, :, cv], es[0].astype(BF)) + tn(kv_b[0, :, cv], es[1].astype(BF))
            inv = 1.0 / total
            o[0, t * PAIR : t * PAIR + HEAD_DIM, :] = (
                acc[:HEAD_DIM, :rows] * inv[:, :rows]
            ).astype(BF)
            o[0, t * PAIR + HEAD_DIM : (t + 1) * PAIR, :] = (
                acc[HEAD_DIM:, rows:] * inv[:, rows:]
            ).astype(BF)
            row = m + jnp.log(total)
            rowsum += [row[:, :rows], row[:, rows:]]
        rowsum += [jnp.zeros((1, rows), F32)] * (8 - len(rowsum))
        terms = thirds(jnp.concatenate(rowsum, axis=0)) + [jnp.zeros((STATS - 24, rows), BF)]
        o[0, w:, :] = jnp.concatenate([t.astype(F32) for t in terms], axis=0).astype(BF)

    full = (lims[0, slot] >= n) & (lims[1, slot] >= n)
    pl.when(full)(lambda: run(False))
    pl.when(jnp.logical_not(full))(lambda: run(True))


def cross_fwd(lims, q, kv_a, kv_b, at, pages, after=()):
    rows, w = q[0].shape[1:]
    return call(
        cross_fwd_kernel,
        (pages,),
        [paged(q), paged((kv_a, at)), paged((kv_b, at))],
        [out_paged((pages, w + STATS, rows), BF)],
        scalars=(lims,),
        us=1.6 * pages,
        after=after,
    )[0]


def cross_bwd_kernel(lims, q, do, kv_a, kv_b, *refs):
    dq, dkv_a, dkv_b = refs[-3:]
    slot = pl.program_id(0)
    rows, w = q.shape[1:]
    n = kv_a.shape[1]
    per = w // rows
    lines = w // HEAD_DIM // per
    stats = do[0, rows:, :].astype(F32)

    def line(first, head):
        at = [first + t * lines + head // per for t in range(3)]
        c = slice(head % per * rows, (head % per + 1) * rows)
        return sum(stats[a : a + 1, c] for a in at)

    def both(first, t):
        return jnp.concatenate([line(first, 2 * t), line(first, 2 * t + 1)], axis=1)

    def run(masked):
        for t in range(w // PAIR):
            c = slice(t * PAIR, (t + 1) * PAIR)
            cv = slice(w + t * PAIR, w + (t + 1) * PAIR)
            qm = pair_rows(q[0, :, c])
            gm = pair_rows(do[0, :rows, c])
            ls, dl = both(0, t), both(3 * lines, t)
            acc = None
            for j, (kv, dkv) in enumerate(((kv_a, dkv_a), (kv_b, dkv_b))):
                k = kv[0, :, c]
                s = nt(k, qm)
                if masked:
                    pos = lax.broadcasted_iota(jnp.int32, s.shape, 0)
                    s = jnp.where(pos < lims[j, slot], s, MASKED)
                p = jnp.exp(s - ls)
                ds = (p * (nt(kv[0, :, cv], gm) - dl)).astype(BF)
                dkv[0, :, c] = nn(ds, qm).astype(BF)
                dkv[0, :, cv] = nn(p.astype(BF), gm).astype(BF)
                part = tn(k, ds)
                acc = part if acc is None else acc + part
            dq[0, t * PAIR : t * PAIR + HEAD_DIM, :] = (acc[:HEAD_DIM, :rows] * SCALE).astype(BF)
            dq[0, t * PAIR + HEAD_DIM : (t + 1) * PAIR, :] = (
                acc[HEAD_DIM:, rows:] * SCALE
            ).astype(BF)

    full = (lims[0, slot] >= n) & (lims[1, slot] >= n)
    pl.when(full)(lambda: run(False))
    pl.when(jnp.logical_not(full))(lambda: run(True))


def cross_bwd(lims, q, do, kv_a, kv_b, at, prev=None, after=()):
    pages, _, w = do.shape
    rows = q[0].shape[1]
    n = kv_a.shape[1]
    ins = [paged(a) for a in (q, do, (kv_a, at), (kv_b, at))]
    if prev is not None:
        ins += [kept(p) for p in prev]

    def out(v):
        return (v.shape, BF, (1,) + v.shape[1:], lambda i, *_: (i + at, 0, 0))

    return call(
        cross_bwd_kernel,
        (pages,),
        ins,
        [out_paged((pages, w, rows), BF), out(kv_a), out(kv_b)],
        scalars=(lims,),
        us=2.4 * pages,
        after=after,
        aliases={} if prev is None else {5: 1, 6: 2},
    )


def enc_back_kernel(src, head, dkv, enc, w, prev, keep, send, dw):
    low = head[0] == 0
    part = keep.shape[-1]

    @pl.when(pl.program_id(0) == 0)
    def _():
        dw[...] = prev[...]

    for j in range(dkv.shape[0]):
        term = nt(dkv[j], w[...])
        lo, hi = term[:, :part], term[:, part:]
        keep[j] = jnp.where(low, lo, hi).astype(BF)
        send[j] = jnp.where(low, hi, lo).astype(BF)
        dw[...] += tn(enc[j], dkv[j])


def enc_back(src, head, dkv, enc, w, prev, k, after=()):
    slots, n, w2 = dkv.shape
    d = w.shape[0]
    part = d // 2
    return call(
        enc_back_kernel,
        (slots // k,),
        [paged(dkv, k), (enc, (k, n, d), lambda i, t, h: (t[i], 0, 0)), whole(w), whole(prev)],
        [
            out_paged((slots, n, part), BF, k), out_paged((slots, n, part), BF, k),
            out_whole((d, w2), F32),
        ],
        scalars=(src, head),
        us=1.7 * slots,
        after=after,
    )


def add_pages_kernel(a, b, out):
    out[...] = (a[...].astype(F32) + b[...].astype(F32)).astype(BF)


def add_pages(at, pages, a, b, after=()):
    return call(
        add_pages_kernel,
        (pages,),
        [paged((a, at)), paged((b, at))],
        [out_paged((pages,) + a.shape[1:], BF)],
        us=0.7 * pages,
        after=after,
    )[0]


def swap(x, axis, mask, size):
    return lax.ppermute(x, axis, [(i, i ^ mask) for i in range(size)])


def pick(bit, a, b):
    return jnp.where(bit == 0, b, a), jnp.where(bit == 0, a, b)


def rows_of(refs):
    return jnp.concatenate([r[...] for r in refs], axis=0) if len(refs) > 1 else refs[0][...]


def grads_wide_kernel(nc, bits, *refs):
    act, n3, du = (refs[j * nc : (j + 1) * nc] for j in range(3))
    cot, send_a, keep_a, send_b, keep_b = refs[3 * nc :]
    i = pl.program_id(0)
    for lo, out in ((0, send_a), (2, keep_a)):

        @pl.when((i >= lo) & (i < lo + 2))
        def _():
            out[...] = tn(rows_of(act), cot[...]).astype(BF)

    for lo, out in ((4, send_b), (6, keep_b)):

        @pl.when((i >= lo) & (i < lo + 2))
        def _():
            out[...] = tn(rows_of(n3), rows_of(du)).astype(BF)


def flat_rows(v):
    return v.reshape(-1, v.shape[-1])


def grads_wide(bits, act, cot, n3, du, after=()):
    act, n3, du = ([flat_rows(v) for v in c] for c in (act, n3, du))
    cot = flat_rows(cot)
    rows, units, d = act[0].shape[0], act[0].shape[1], cot.shape[1]
    blk = units // 4

    def quarter_a(i, t):
        j = jnp.minimum(i, 3)
        side = jnp.where(j < 2, 1 - t[0], t[0])
        return (0, 2 * side + j % 2)

    def side_b(i, t):
        return (0, jnp.where(jnp.maximum(i, 4) < 6, 1 - t[1], t[1]))

    def out(lo):
        return ((2 * blk, d), BF, (blk, d), lambda i, t: (jnp.clip(i - lo, 0, 1), 0))

    return call(
        functools.partial(grads_wide_kernel, len(act)),
        (8,),
        [(v, (rows, blk), quarter_a) for v in act]
        + [(v, (rows, d // 2), lambda i, t: (0, jnp.maximum(i, 4) % 2)) for v in n3]
        + [(v, (rows, units // 2), side_b) for v in du]
        + [whole(cot)],
        [out(0), out(2), out(4), out(6)],
        scalars=(bits,),
        us=10,
        after=after,
    )


def grads_self_kernel(nc, bits, n, o, *refs):
    dq, dk, dv, g = (rows_of(refs[j * nc : (j + 1) * nc]) for j in range(4))
    send_a, keep_a, send_b, keep_b = refs[4 * nc :]
    d = n.shape[1]
    turned = jnp.transpose(n[...])
    send_a[...], keep_a[...] = pick(bits[0], nn(turned, dq).astype(BF), nn(turned, dk).astype(BF))
    ot = tn(o[...], g).astype(BF)
    ot = jnp.concatenate([ot[:, : d // 2], ot[:, d // 2 :]], axis=0)
    send_b[...], keep_b[...] = pick(bits[1], nn(turned, dv).astype(BF), ot)


def grads_cross_kernel(nc, bits, n, dw, *refs):
    dq, o, g = (rows_of(refs[j * nc : (j + 1) * nc]) for j in range(3))
    send_a, keep_a, send_b, keep_b = refs[3 * nc :]
    d = n.shape[1]
    w = dq.shape[1]
    send_a[...], keep_a[...] = pick(bits[0], tn(n[...], dq).astype(BF), dw[:, :w].astype(BF))
    ot = tn(o, g).astype(BF)
    ot = jnp.concatenate([ot[:, : d // 2], ot[:, d // 2 :]], axis=0)
    send_b[...], keep_b[...] = pick(bits[1], dw[:, w:].astype(BF), ot)


def grads_tall(kernel, bits, arrays, chunked, d, w, us, after=()):
    flat = [flat_rows(v) for v in arrays] + [flat_rows(v) for c in chunked for v in c]
    return call(
        functools.partial(kernel, len(chunked[0])),
        (1,),
        [whole(v) for v in flat],
        [out_whole((d, w), BF)] * 4,
        scalars=(bits,),
        us=us,
        after=after,
    )


def sum_one_kernel(bits, keep_a, got_a, keep_b, got_b, send_a, next_a, send_b, next_b):
    blk = send_a.shape[0]
    for keep, got, send, nxt, bit in (
        (keep_a, got_a, send_a, next_a, bits[1]), (keep_b, got_b, send_b, next_b, bits[0])
    ):
        lo = keep[:blk].astype(F32) + got[:blk].astype(F32)
        hi = keep[blk:].astype(F32) + got[blk:].astype(F32)
        s, k = pick(bit, lo, hi)
        send[...] = s.astype(BF)
        nxt[...] = k.astype(BF)


def sum_two_kernel(nz, place, keep_a, got_a, keep_b, got_b, *rest):
    outs, (sum_a, sum_b) = rest[:nz], rest[nz:]
    part = keep_a.shape[0] // nz
    sum_a[...] = keep_a[...].astype(F32) + got_a[...].astype(F32)
    sum_b[...] = keep_b[...].astype(F32) + got_b[...].astype(F32)
    for k in range(nz):
        z = lax.rem(place[0] + k, nz)
        at = pl.ds(pl.multiple_of(z * part, part), part)
        outs[k][:part] = sum_a[at, :].astype(BF)
        outs[k][part:] = sum_b[at, :].astype(BF)


def sum_three_kernel(*refs):
    acc = refs[0][...].astype(F32)
    for r in refs[1:-1]:
        acc = acc + r[...].astype(F32)
    refs[-1][...] = acc.astype(BF)


def join_kernel(nz, place, *refs):
    pieces, (out_a, out_b, all_a, all_b) = refs[:nz], refs[nz:]
    part = pieces[0].shape[0] // 2
    for k in range(nz):
        z = lax.rem(place[0] + k, nz)
        at = pl.ds(pl.multiple_of(z * part, part), part)
        all_a[at, :] = pieces[k][:part].astype(F32)
        all_b[at, :] = pieces[k][part:].astype(F32)
    out_a[...] = all_a[...].astype(BF)
    out_b[...] = all_b[...].astype(BF)


def reduce_bucket(parts, bits, place, nz):
    send_a, keep_a, send_b, keep_b = parts
    blk, c = send_a.shape[0] // 2, send_a.shape[1]
    piece = (2 * blk // nz, c)
    fast = c / 384

    def x(v):
        return swap(v, "dp", 1, 4)

    def y(v):
        return swap(v, "dp", 2, 4)

    def shift(v, k):
        return lax.ppermute(v, "seq", [((i + k) % nz, i) for i in range(nz)])

    got_a, got_b = x(send_a), y(send_b)
    yield
    send_a, keep_a, send_b, keep_b = call(
        sum_one_kernel, (1,), [whole(v) for v in (keep_a, got_a, keep_b, got_b)],
        [out_whole((blk, c), BF)] * 4, scalars=(bits,), us=2 * fast,
    )
    got_a, got_b = y(send_a), x(send_b)
    yield
    outs = call(
        functools.partial(sum_two_kernel, nz), (1,),
        [whole(v) for v in (keep_a, got_a, keep_b, got_b)], [out_whole(piece, BF)] * nz,
        scalars=(place,), scratch=[pltpu.VMEM((blk, c), F32)] * 2, us=1.5 * fast,
    )
    got = [shift(outs[k], -k) for k in range(1, nz)]
    yield
    (mine,) = call(
        sum_three_kernel, (1,), [whole(v) for v in [outs[0]] + got], [out_whole(piece, BF)],
        us=1.5,
    )
    pieces = [mine] + [shift(mine, k) for k in range(1, nz)]
    yield
    a0, b0 = call(
        functools.partial(join_kernel, nz), (1,), [whole(v) for v in pieces],
        [out_whole((blk, c), BF)] * 2, scalars=(place,),
        scratch=[pltpu.VMEM((blk, c), F32)] * 2, us=1.5 * fast,
    )
    a1, b1 = y(a0), x(b0)
    a2, b2 = x(a0), y(b0)
    a3, b3 = x(a1), y(b1)
    yield [a0, a1, a2, a3, b0, b1, b2, b3]


def final_kernel(outs, bits, *refs):
    pieces, results = refs[:8], refs[8:]
    t = pl.program_id(0)
    for half, (hi, lo) in enumerate(((bits[0], bits[1]), (bits[1], bits[0]))):
        rel = (t // 2 + hi) % 2 * 2 + (t % 2 + lo) % 2
        for j in range(4):
            for r, (at, first, count) in zip(results, outs):
                if at != half:
                    continue

                @pl.when((rel == j) & (t >= first) & (t < first + count))
                def _():
                    r[...] = pieces[4 * half + j][...].astype(F32)


def final(pieces, bits, outs, us, after=()):
    blk, c = pieces[0].shape

    def index(first, count, where):
        return lambda t, *_: where(jnp.clip(t - first, 0, count - 1))

    return call(
        functools.partial(final_kernel, [(o[1], o[2], o[3]) for o in outs]),
        (4,),
        [whole(p) for p in pieces],
        [(o[0], F32, (blk, c), index(o[2], o[3], o[4])) for o in outs],
        scalars=(bits,),
        us=us,
        after=after,
    )


def per_device(
    sizes,
    dec_input,
    enc_states,
    page_group,
    target_mask,
    rel_buckets,
    self_gain,
    cross_gain,
    ffn_gain,
    self_q,
    self_k,
    self_v,
    self_o,
    rel_table,
    cross_q_w,
    cross_k,
    cross_v,
    cross_o,
    ff_in,
    ff_out,
    cotangent,
):
    n_seq = sizes["seq"]
    pages, half, d = dec_input.shape
    n = enc_states.shape[1]
    w = self_q.shape[1]
    nb = n_seq // 2
    slots = nb * pages
    k = 3
    chunks = pages // k
    ORDER.clear()
    s = lax.axis_index("seq")
    h = lax.axis_index("head")
    dp = lax.axis_index("dp")
    block, par = s // 2, s % 2
    head = h.reshape(1).astype(jnp.int32)
    bits = jnp.stack([dp % 2, dp // 2]).astype(jnp.int32)
    place = s.reshape(1).astype(jnp.int32)

    kk = jnp.arange(nb * chunks, dtype=jnp.int32) // chunks
    cc = jnp.arange(nb * chunks, dtype=jnp.int32) % chunks
    ident = jnp.arange(nb * chunks, dtype=jnp.int32)
    own_groups = ((((block + kk) % nb) * 2 + par) * chunks + cc).astype(jnp.int32)
    jl = jnp.arange(nb, dtype=jnp.int32)
    arrived = ((jl + h * (nb // 2) - block) % nb * chunks).astype(jnp.int32)

    def head_swap(x):
        return swap(x, "head", 1, 2)

    def rolled(x, step):
        perm = [(2 * b + r, 2 * ((b - step) % nb) + r) for b in range(nb) for r in range(2)]
        return lax.ppermute(x, "seq", perm) if step % nb else x

    def owners(x):
        return [rolled(x, step) for step in range(nb)]

    others = list(range(1, nb))
    both = range(chunks)

    x_other = head_swap(dec_input)
    away = lax.dynamic_slice(
        enc_states.reshape(nb, 2, pages, n, d),
        (h * (nb // 2), 1 - par, 0, 0, 0),
        (nb // 2, 1, pages, n, d),
    ).reshape(nb // 2, pages, n, d)
    away = [away[:, c * k : (c + 1) * k].reshape(nb // 2 * k, n, d) for c in both]
    enc_in = [swap(away[0], "seq", 1, n_seq)]
    cot_other = head_swap(cotangent)
    cot = jnp.concatenate(
        [jnp.where(h == 0, cotangent, cot_other), jnp.where(h == 0, cot_other, cotangent)], axis=1
    )
    enc_len = [
        OCR + PATCH_SMALL + g * (PATCH_LARGE - PATCH_SMALL) for g in owners(page_group)
    ]
    lims = [
        jnp.stack([e - s * n, e - (s + 1 - 2 * par) * n]).astype(jnp.int32) for e in enc_len
    ]
    lens = jnp.sum(target_mask, axis=1).astype(jnp.int32)
    table = jnp.pad(rel_table.T, ((0, 8 - rel_table.shape[1]), (0, 128 - rel_table.shape[0])))
    gains = [g.reshape(1, d) for g in (self_gain, cross_gain, ffn_gain)]
    w_kv = jnp.concatenate([cross_k, cross_v], axis=1)

    xf, n1, qkv, o1, lse1, a_part = self_fwd(
        head, lens, dec_input, x_other, gains[0], self_q, self_k, self_v, self_o, rel_buckets, table,
        after=(away[0], *lims[1:]),
    )
    a_other = head_swap(a_part)
    h1, n2, q2 = cross_q(xf, a_part, a_other, gains[1], cross_q_w, k)
    qs = owners(q2)
    for c in both[1:]:
        enc_in.append(swap(gate(away[c]), "seq", 1, n_seq))
    (kv_a,) = kv_project(own_groups, ident, enc_states, w_kv, slots, k)
    os = [[None] * chunks for _ in range(nb)]
    rec = None

    def attend(j, c):
        o = cross_fwd(
            lims[j][:, c * k : (c + 1) * k], (qs[j], c * k), kv_a, kv_b, j * pages + c * k, k
        )
        os[j][c] = rolled(o, -j)

    for c in both:
        direct = gate(enc_in[c])
        for late, part in enumerate((direct, head_swap(direct))):
            rec = kv_project(
                ident[: nb // 2], arrived[late * (nb // 2) : (late + 1) * (nb // 2)] + c, part,
                w_kv, slots, k, copied=True, prev=rec,
            )
        kv_b, enc_rec = rec
        attend(0, c)
        if c:
            for e in range(c - 1, chunks if c == chunks - 1 else c):
                for j in others:
                    attend(j, e)

    o2, o2t, lse2, c_part, c_other = ([None] * chunks for _ in range(5))
    h2, n3, act, du, dn3, dn3_other = ([None] * chunks for _ in range(6))
    dh2, dcr, gain3, dos = ([None] * chunks for _ in range(4))
    dqs = [[None] * chunks for _ in range(nb)]
    dkv = None

    def mix(c):
        o2[c], o2t[c], lse2[c], c_part[c] = combine(
            [v[c] for v in os], cross_o, k
        )
        c_other[c] = head_swap(c_part[c])

    def feed(c):
        h2[c], n3[c], act[c], du[c], dn3[c] = ffn(
            c * k, h1, c_part[c], c_other[c], cot, gains[2], ff_in, ff_out, k
        )
        dn3_other[c] = head_swap(dn3[c])

    def turn(c):
        dh2[c], dcr[c], do2, gain3[c] = grad_two(
            c * k, head, h2[c], dn3[c], dn3_other[c], cot, gains[2], cross_o, o2t[c], lse2[c], k
        )
        dos[c] = owners(do2)

    def back(j, c):
        nonlocal dkv
        dqs[j][c], *dkv = cross_bwd(
            lims[j][:, c * k : (c + 1) * k], (qs[j], c * k), dos[c][j], kv_a, kv_b,
            j * pages + c * k, prev=dkv,
        )
        dqs[j][c] = rolled(dqs[j][c], -j)

    mix(0)
    feed(0)
    for c in both[1:]:
        mix(c)
        turn(c - 1)
        feed(c)
        back(0, c - 1)
    turn(chunks - 1)
    grads_ffn = reduce_bucket(grads_wide(bits, act, cot, n3, du), bits, place, n_seq)
    next(grads_ffn)
    for c in both[:-1]:
        for j in others:
            back(j, c)
    for j in [0] + others:
        back(j, chunks - 1)
    next(grads_ffn)

    keep_b, send_b, dw = enc_back(
        ident, head, dkv[1], enc_rec, w_kv, jnp.zeros((d, 2 * w), F32), k
    )
    send_b = head_swap(send_b)
    dq2, dn2, dn2_other = ([None] * chunks for _ in range(3))
    for c in both:
        dq2[c], dn2[c] = grad_q([v[c] for v in dqs], cross_q_w, k)
        dn2_other[c] = head_swap(dn2[c])
        if c == 0:
            next(grads_ffn)
    quarter = slots // 4
    enc_away = []

    def send_away(*parts):
        for i in parts:
            enc_away.append(
                swap(add_pages(i * quarter, quarter, keep_b, send_b), "seq", 1, n_seq)
            )

    backs = []
    dn1_other = []
    for c in both:
        backs.append(
            self_bwd(
                c * k, head, lens, h1, dn2[c], dn2_other[c], dh2[c], gains[1], self_q, self_k,
                self_v, self_o, rel_buckets, table, qkv, lse1,
            )
        )
        dn1_other.append(head_swap(backs[c][7]))
        if c == 0:
            send_away(0)
    dh1, dar, dq1, dk1, dv1, ds1, dn1, _, gain2 = zip(*backs)
    grads_self = reduce_bucket(
        grads_tall(
            grads_self_kernel, bits, [n1, o1], [dq1, dk1, dv1, dar], d, w, 7
        ),
        bits, place, n_seq,
    )
    next(grads_self)
    next(grads_ffn)
    send_away(1)
    keep_a, send_a, dw = enc_back(own_groups, head, dkv[0], enc_states, w_kv, dw, k)
    send_a = head_swap(send_a)
    next(grads_self)
    grads_cross = reduce_bucket(
        grads_tall(grads_cross_kernel, bits, [n2, dw], [dq2, o2, dcr], d, w, 6),
        bits, place, n_seq,
    )
    next(grads_cross)
    sums_ffn = next(grads_ffn)
    next(grads_self)
    lasts = [last(c * k, dec_input, dn1[c], dn1_other[c], dh1[c], gains[0]) for c in both]
    next(grads_cross)
    send_away(2)
    next(grads_self)
    branches = [branch_ffn(head, act[c], ff_out, k) for c in both]
    f_other = [head_swap(f[1]) for f in branches]
    next(grads_cross)
    sums_self = next(grads_self)
    send_away(3)
    tables = [table_grad(ds1[c], rel_buckets, c * k) for c in both]
    next(grads_cross)
    outputs = [
        output_rows(
            c * k, head, lens, h2[c], branches[c][0], f_other[c], a_part, a_other, c_part[c],
            c_other[c],
        )
        for c in both
    ]
    sums_cross = next(grads_cross)

    units = ff_in.shape[1]
    row, col = (lambda v: (v, 0)), (lambda v: (0, v))
    ff_out_grad, ff_in_grad = final(
        sums_ffn, bits,
        [((units, d), 0, 0, 4, row), ((d, units), 1, 0, 4, lambda v: (v % 2, v // 2))], 6,
    )
    four = [
        ((d, w), 0, 0, 2, row), ((d, w), 0, 2, 2, row), ((d, w), 1, 0, 2, row), ((w, d), 1, 2, 2, col)
    ]
    sq, sk, sv, so = final(sums_self, bits, four, 4)

    back_a = (keep_a.astype(F32) + send_a.astype(F32)).astype(BF)
    enc_away = jnp.concatenate(enc_away, axis=0)
    pieces = []
    for j in range(nb):
        at = (j - block) % nb * pages
        mine, theirs = (
            lax.dynamic_slice_in_dim(v, at, pages, 0) for v in (back_a, enc_away)
        )
        pieces += [jnp.where(par == 0, mine, theirs), jnp.where(par == 0, theirs, mine)]
    enc_t = jnp.transpose(jnp.concatenate(pieces, axis=0), (1, 0, 2)).astype(F32)
    enc_grad = jnp.transpose(with_layout_constraint(enc_t, Layout((0, 1, 2))), (1, 0, 2))
    cq, ck, cv, co = final(sums_cross, bits, four, 4)

    output = jnp.concatenate([o[0] for o in outputs], axis=0)
    input_grad = jnp.concatenate([o[0] for o in lasts], axis=0)
    squares = jnp.sum(jnp.concatenate([o[1] for o in outputs], axis=0)[:, :4], axis=-1)
    squares = squares + head_swap(squares)
    counts = lens.astype(F32) * d
    rms_stats = jnp.sqrt(squares / counts[:, None])
    small = jnp.stack(
        [jnp.sum(sum(g), axis=0) for g in ([o[1] for o in lasts], gain2, gain3)]
    )
    small = small + head_swap(small)
    table_part = sum(tables)
    line = jnp.pad(table_part.reshape(1, -1), ((0, 0), (0, d - table_part.size)))
    small = jnp.concatenate([small, line], axis=0)
    for axis in ("dp", "seq"):
        for i in range(sizes[axis].bit_length() - 1):
            small = small + swap(small, axis, 1 << i, sizes[axis])
    table_sum = small[3, : table_part.size].reshape(table_part.shape)

    return (
        output, input_grad, enc_grad, small[0], small[1], small[2], sq, sk, sv, so, table_sum.T,
        cq, ck, cv, co, ff_in_grad, ff_out_grad, rms_stats,
    )


def solution(mesh):
    sizes = dict(mesh.shape)
    rows = P(("dp", "seq"), "head", None)
    cols, tall = P(None, "head"), P("head", None)
    placed = (
        rows, P("dp", "seq", None), P(("dp", "seq")), P(("dp", "seq"), None),
        P(("dp", "seq"), None, None), P(), P(), P(), cols, cols, cols, tall, cols, cols, cols, cols,
        tall, cols, tall, rows,
    )
    return jax.shard_map(
        functools.partial(per_device, sizes),
        mesh=mesh,
        in_specs=placed,
        out_specs=(
            rows, rows, P("dp", "seq", "head"), P(), P(), P(), cols, cols, cols, tall, cols, cols,
            cols, cols, tall, cols, tall, P(("dp", "seq"), None),
        ),
        check_vma=False,
    )
```

time: 802 us -> 630 us (0.79)
  waiting for transfers between devices: 345 us -> 128 us
  Pallas kernels: 237 us -> 322 us
  other arithmetic: 53 us -> 32.9 us
  local copies, waits for them, and re-layouts: 61.9 us -> 47.6 us
  matrix products: 13.6 us -> 0 us
    ppermute x71 -> x59, waiting for transfers between devices: 289 us -> 66.5 us  [swap(): return lax.ppermute(x, axis, [(i, i ^ mask) for i in range(size)])]
    pallas_call x20 -> x60, Pallas kernels: 237 us -> 322 us  [the longest x57 322 us: call(): pl.pallas_call(run, grid_spec=spec, out_shape=[jax.ShapeDtypeStruct(s, d)...]
    ppermute x8 -> x26, starting transfers between devices: 10.1 us -> 39.5 us  [the longest x18 29.1 us: shift(): return lax.ppermute(v, 'seq', [((i + k) % nz, i) for i in range(nz)])]
    ppermute x71 -> x59, starting transfers between devices: 68.7 us -> 45.1 us  [swap(): return lax.ppermute(x, axis, [(i, i ^ mask) for i in range(size)])]
    unnamed x122 -> x203, local copies, waits for them, and re-layouts: 48.2 us -> 27.9 us
    dot_general x6 -> x0, matrix products: 13.6 us -> none  [rows_grad(): lax.dot_general(a, b, (((0,), (0,)), ((), ())), preferred_element_type=F32)]
    convert_element_type x27 -> x3, other arithmetic: 20.5 us -> 12.7 us  [the longest x1 6.4 us: per_device(): jnp.transpose(jnp.concatenate(pieces, axis=0), (1, 0, 2)).astype(F32)]
    ppermute x8 -> x26, waiting for transfers between devices: 55.9 us -> 61.9 us  [the longest x18 43.5 us: shift(): return lax.ppermute(v, 'seq', [((i + k) % nz, i) for i in range(nz)])]
  transfers between devices with their start and end apart: 79 -> 85, of which waited for: 44 -> 23; matrix products, arithmetic and copies ran while one was open for 11% -> 8% of each run, Pallas kernels for 22% -> 51%
where the time goes in v2:
time: 630 us; the launch traced here: 619 us
  Pallas kernels  322 us (51%)
  waiting for transfers between devices  128 us (20%)
  starting transfers between devices  84.6 us (13%)
  local copies, waits for them, and re-layouts  47.6 us (8%)
  other arithmetic  32.9 us (5%)
    pallas_call x57, Pallas kernels, call(): pl.pallas_call(run, grid_spec=spec, out_shape=[jax.ShapeDtypeStruct(s, d)...  322 us
    ppermute x59, waiting for transfers between devices, swap(): return lax.ppermute(x, axis, [(i, i ^ mask) for i in range(size)])  66.5 us
    ppermute x59, starting transfers between devices, swap(): return lax.ppermute(x, axis, [(i, i ^ mask) for i in range(size)])  45.1 us
    ppermute x18, waiting for transfers between devices, shift(): return lax.ppermute(v, 'seq', [((i + k) % nz, i) for i in range(nz)])  43.5 us
    ppermute x18, starting transfers between devices, shift(): return lax.ppermute(v, 'seq', [((i + k) % nz, i) for i in range(nz)])  29.1 us
    unnamed x203, local copies, waits for them, and re-layouts  27.9 us
    ppermute x8, waiting for transfers between devices, rolled(): return lax.ppermute(x, 'seq', perm) if step % nb else x  18.4 us
  transfers between devices with their start and end apart: 85, of which 23 were waited for; matrix products, arithmetic and copies ran while one was open for 8% of the time, Pallas kernels for 51%

profile of v2, /device:TPU:0, one launch (start us, length us, event | category | flops | bytes accessed | tf_op | source)
XLA Modules:
  0.0 618.8 jit_solution(11450932063157847866)
XLA Ops:
  0.7 4.1 collective-permute-start.1
  4.8 11.3 %copy.81.refs_2_.refs_3_ = bf16[24,324,768]{2,1,0:T(8,128)(2,1)} copy(bf16[24,324,768]{2,0,1:T(8,128)(2,1)} %param.21) | data formatting | bytes 23887872 | tf_op args[1]
  25.1 10.7 %shard_map.331 = (bf16[6,128,768]{2,1,0:T(8,128)(2,1)}, bf16[6,128,768]{2,1,0:T(8,128)(2,1)}, bf16[6,128,1152]{2,1,0:T(8,128)(2,1)}, bf16[6,128,384]{2,1,0:T(8,1...) custom-call(s32[1]{0:T(128)} %bitcast.refs_0_.refs_1_, s32[6]{0:T(128)} %reduce_sum.63.refs_1_, ...), custom_call_target="tpu_custom_call" | custom-call | flops 99999997952 | tf_op jit(solution)/shard_map/pallas_call | solution.py:55
  41.8 4.1 shard_map.332
  46.8 9.8 %shard_map.333.refs_1_.refs_4_.refs_2_.refs_3_ = bf16[12,324,768]{2,1,0:T(8,128)(2,1)} custom-call(s32[4]{0:T(128)} %fusion.2.refs_0_, s32[4]{0:T(128)} %iota.23.refs_1_, bf16[24,324,768]{2,1,0:T(8,128)(2,1)} %copy.81.refs_2_.refs_3_, bf16[768,768]{1,0:T(8,128)(2,1)} %copy-done.9, bf16[6,128,384]{2,1,0:T(8,128)(2,1)} %get-tuple-element.169.refs_4_.refs_1_), custom_call_target="tpu_custom_call" | custom-call | flops 108000002048 | tf_op jit(solution)/shard_map/pallas_call | solution.py:55
  56.6 4.6 collective-permute-done.3.refs_0_
  61.7 6.0 shard_map.335
  68.8 6.1 shard_map.336
  74.9 6.1 shard_map.337.refs_1_.refs_6_.refs_0_
  81.0 23.1 %collective-permute-done.6.refs_0_ = bf16[3,324,768]{2,1,0:T(8,128)(2,1)S(1)} collective-permute-done((bf16[3,324,768]{2,1,0:T(8,128)(2,1)}, bf16[3,324,768]{2,1,0:T(8,128)(2,1)S(1)}, u32[]{:S(2)}, u32[]{:S(2)}) %collective-permute-start.6) | collective-permute-done | bytes 1493024 | tf_op jit(solution)/shard_map/ppermute | solution.py:838
  105.2 5.5 shard_map.340
  111.8 5.4 shard_map.341
  117.2 6.4 %shard_map.342.refs_4_.refs_0_ = bf16[3,416,128]{2,1,0:T(8,128)(2,1)} custom-call(s32[2,3]{1,0:T(2,128)} %get-tuple-element.362.refs_0_, bf16[6,128,384]{2,1,0:T(8,128)(2,1)} %get-tuple-element.169.refs_4_.refs_1_, bf16[12,324,768]{2,1,0:T(8,128)(2,1)} %shard_map.333.refs_1_.refs_4_.refs_2_.refs_3_, bf16[12,324,768]{2,1,0:T(8,128)(2,1)} %get-tuple-element.176.refs_3_.refs_4_), custom_call_target="tpu_custom_call" | custom-call | flops 48000000000 | tf_op jit(solution)/shard_map/pallas_call | solution.py:55
  123.7 6.1 shard_map.343.refs_4_
  129.8 6.1 shard_map.344.refs_3_
  135.9 10.9 %collective-permute-done.8.refs_1_ = bf16[3,416,128]{2,1,0:T(8,128)(2,1)S(1)} collective-permute-done((bf16[3,416,128]{2,1,0:T(8,128)(2,1)}, bf16[3,416,128]{2,1,0:T(8,128)(2,1)S(1)}, u32[]{:S(2)}, u32[]{:S(2)}) %collective-permute-start.8) | collective-permute-done | bytes 319520 | tf_op jit(solution)/shard_map/ppermute | solution.py:1110
  154.7 8.3 %shard_map.346 = (f32[3,128,768]{2,1,0:T(8,128)}, bf16[3,128,768]{2,1,0:T(8,128)(2,1)}, bf16[3,128,1536]{2,1,0:T(8,128)(2,1)}, bf16[3,128,1536]{2,1,0:T(8,128)(2,1)}, bf16[3,128,768]{2,1,0:T(8,128)(2,1)}) custom-call(f32[6,128,768]{2,1,0:T(8,128)} %get-tuple-element.168.refs_0_.refs_2_, bf16[3,128,768]{2,1,0:T(8,128)(2,1)} %get-tuple-element.177.refs_1_.refs_7_, ...), custom_call_target="tpu_custom_call" | custom-call | flops 120000004096 | tf_op jit(solution)/shard_map/pallas_call | solution.py:55
  163.4 7.5 %collective-permute-done.12.refs_1_ = bf16[3,416,128]{2,1,0:T(8,128)(2,1)S(1)} collective-permute-done((bf16[3,416,128]{2,1,0:T(8,128)(2,1)S(1)}, bf16[3,416,128]{2,1,0:T(8,128)(2,1)S(1)}, u32[]{:S(2)}, u32[]{:S(2)}) %collective-permute-start.12) | collective-permute-done | bytes 319520 | tf_op jit(solution)/shard_map/ppermute | solution.py:1110
  175.2 4.2 shard_map.348
  180.2 8.3 %shard_map.349 = (f32[3,128,768]{2,1,0:T(8,128)}, bf16[3,128,768]{2,1,0:T(8,128)(2,1)}, bf16[3,128,1536]{2,1,0:T(8,128)(2,1)}, bf16[3,128,1536]{2,1,0:T(8,128)(2,1)}, bf16[3,128,768]{2,1,0:T(8,128)(2,1)}) custom-call(f32[6,128,768]{2,1,0:T(8,128)} %get-tuple-element.168.refs_0_.refs_2_, bf16[3,128,768]{2,1,0:T(8,128)(2,1)} %get-tuple-element.187.refs_1_.refs_7_, ...), custom_call_target="tpu_custom_call" | custom-call | flops 120000004096 | tf_op jit(solution)/shard_map/pallas_call | solution.py:55
  188.9 8.8 %shard_map.350 = (bf16[3,384,128]{2,1,0:T(8,128)(2,1)}, bf16[12,324,768]{2,1,0:T(8,128)(2,1)}, bf16[12,324,768]{2,1,0:T(8,128)(2,1)}) custom-call(s32[2,3]{1,0:T(2,128)} %get-tuple-element.361.refs_0_, bf16[6,128,384]{2,1,0:T(8,128)(2,1)} %get-tuple-element.169.refs_4_.refs_1_, bf16[3,160,384]{2,1,0:T(8,128)(2,1)} %get-tuple-element.186.refs_2_, ...), custom_call_target="tpu_custom_call" | custom-call | flops 71999995904 | tf_op jit(solution)/shard_map/pallas_call | solution.py:55
  198.6 4.2 shard_map.351
  205.7 11.9 %shard_map.352 = (bf16[768,768]{1,0:T(8,128)(2,1)}, bf16[768,768]{1,0:T(8,128)(2,1)}, bf16[768,768]{1,0:T(8,128)(2,1)}, bf16[768,768]{1,0:T(8,128)(2,1)}) custom-call(s32[2]{0:T(128)} %pad_add_fusion.2.refs_0_, bf16[384,1536]{1,0:T(8,128)(2,1)} %bitcast.56, bf16[384,1536]{1,0:T(8,128)(2,1)} %bitcast.57, bf16[384,768]{1,0:T(8,128)(2,1)} %bitcast.64, ...), custom_call_target="tpu_custom_call" | custom-call | flops 99999997952 | tf_op jit(solution)/shard_map/pallas_call | solution.py:55
  220.5 8.8 %shard_map.353 = (bf16[3,384,128]{2,1,0:T(8,128)(2,1)}, bf16[12,324,768]{2,1,0:T(8,128)(2,1)}, bf16[12,324,768]{2,1,0:T(8,128)(2,1)}) custom-call(s32[2,3]{1,0:T(2,128)} %get-tuple-element.359.refs_0_, bf16[6,128,384]{2,1,0:T(8,128)(2,1)} %collective-permute-done.5.refs_1_, ...), custom_call_target="tpu_custom_call", output_to_operand_aliasing={{1}: (5, {}), {2}: (6, {})} | custom-call | flops 71999995904 | tf_op jit(solution)/shard_map/pallas_call | solution.py:55
  229.3 9.1 %shard_map.354 = (bf16[3,384,128]{2,1,0:T(8,128)(2,1)}, bf16[12,324,768]{2,1,0:T(8,128)(2,1)}, bf16[12,324,768]{2,1,0:T(8,128)(2,1)}) custom-call(s32[2,3]{1,0:T(2,128)} %get-tuple-element.362.refs_0_, bf16[6,128,384]{2,1,0:T(8,128)(2,1)} %get-tuple-element.169.refs_4_.refs_1_, ...), custom_call_target="tpu_custom_call", output_to_operand_aliasing={{1}: (5, {}), {2}: (6, {})} | custom-call | flops 71999995904 | tf_op jit(solution)/shard_map/pallas_call | solution.py:55
  239.0 8.7 %shard_map.355 = (bf16[3,384,128]{2,1,0:T(8,128)(2,1)}, bf16[12,324,768]{2,1,0:T(8,128)(2,1)}, bf16[12,324,768]{2,1,0:T(8,128)(2,1)}) custom-call(s32[2,3]{1,0:T(2,128)} %get-tuple-element.360.refs_0_, bf16[6,128,384]{2,1,0:T(8,128)(2,1)} %collective-permute-done.5.refs_1_, ...), custom_call_target="tpu_custom_call", output_to_operand_aliasing={{1}: (5, {}), {2}: (6, {})} | custom-call | flops 71999995904 | tf_op jit(solution)/shard_map/pallas_call | solution.py:55
  250.7 4.7 shard_map.356
  258.5 18.9 %shard_map.357 = (bf16[12,324,384]{2,1,0:T(8,128)(2,1)}, bf16[12,324,384]{2,1,0:T(8,128)(2,1)}, f32[768,768]{1,0:T(8,128)}) custom-call(s32[4]{0:T(128)} %iota.26.refs_0_, s32[1]{0:T(128)} %bitcast.refs_0_.refs_1_, bf16[12,324,768]{2,1,0:T(8,128)(2,1)} %get-tuple-element.209.refs_2_, bf16[12,324,768]{2,1,0:T(8,128)(2,1)} %get-tuple-element.210.refs_3_, ...), custom_call_target="tpu_custom_call" | custom-call | flops 204000002048 | tf_op jit(solution)/shard_map/pallas_call | solution.py:55
  280.5 3.1 shard_map.359
  290.1 10.3 %shard_map.361 = (f32[3,64,768]{2,1,0:T(8,128)}, bf16[3,128,768]{2,1,0:T(8,128)(2,1)}, bf16[3,128,384]{2,1,0:T(8,128)(2,1)}, bf16[3,128,384]{2,1,0:T(8,128)(2,1)...) custom-call(s32[1]{0:T(128)} %bitcast.refs_0_.refs_1_, ...), custom_call_target="tpu_custom_call" | custom-call | flops 83999997952 | tf_op jit(solution)/shard_map/pallas_call | solution.py:55
  300.5 3.1 shard_map.362.refs_15_
  304.4 10.3 %shard_map.363 = (f32[3,64,768]{2,1,0:T(8,128)}, bf16[3,128,768]{2,1,0:T(8,128)(2,1)}, bf16[3,128,384]{2,1,0:T(8,128)(2,1)}, bf16[3,128,384]{2,1,0:T(8,128)(2,1)...) custom-call(s32[1]{0:T(128)} %bitcast.refs_0_.refs_1_, ...), custom_call_target="tpu_custom_call" | custom-call | flops 83999997952 | tf_op jit(solution)/shard_map/pallas_call | solution.py:55
  314.7 6.5 %shard_map.364 = (bf16[768,384]{1,0:T(8,128)(2,1)}, bf16[768,384]{1,0:T(8,128)(2,1)}, bf16[768,384]{1,0:T(8,128)(2,1)}, bf16[768,384]{1,0:T(8,128)(2,1)}) custom-call(s32[2]{0:T(128)} %pad_add_fusion.2.refs_0_, bf16[768,768]{1,0:T(8,128)(2,1)} %bitcast.58, bf16[768,384]{1,0:T(8,128)(2,1)} %bitcast.61, bf16[384,384]{1,0:T(8,128)(2,1)} %bitcast.72, ...), custom_call_target="tpu_custom_call" | custom-call | flops 70000001024 | tf_op jit(solution)/shard_map/pallas_call | solution.py:55
  329.1 3.2 shard_map.366.refs_6_
  332.3 18.6 %shard_map.367 = (bf16[12,324,384]{2,1,0:T(8,128)(2,1)}, bf16[12,324,384]{2,1,0:T(8,128)(2,1)}, f32[768,768]{1,0:T(8,128)}) custom-call(s32[4]{0:T(128)} %fusion.2.refs_0_, s32[1]{0:T(128)} %bitcast.refs_0_.refs_1_, bf16[12,324,768]{2,1,0:T(8,128)(2,1)} %get-tuple-element.244.refs_2_, bf16[24,324,768]{2,1,0:T(8,128)(2,1)} %copy.81.refs_2_.refs_3_, ...), custom_call_target="tpu_custom_call" | custom-call | flops 204000002048 | tf_op jit(solution)/shard_map/pallas_call | solution.py:55
  352.9 3.4 shard_map.368
  356.4 5.9 shard_map.369
  367.4 4.4 collective-permute-done.31.refs_2_
  375.6 3.3 shard_map.372
  379.0 3.4 shard_map.373
  390.3 3.4 shard_map.374
  393.7 3.2 shard_map.375.refs_4_
  396.9 26.4 %collective-permute-done.36.refs_1_ = bf16[192,384]{1,0:T(8,128)(2,1)S(1)} collective-permute-done((bf16[192,384]{1,0:T(8,128)(2,1)S(1)}, bf16[192,384]{1,0:T(8,128)(2,1)S(1)}, u32[]{:S(2)}, u32[]{:S(2)}) %collective-permute-start.36) | collective-permute-done | bytes 147488 | tf_op jit(solution)/shard_map/ppermute | solution.py:992
  424.8 3.7 collective-permute-done.38.refs_3_
  431.0 4.0 shard_map.377
  435.0 4.8 collective-permute-start.49
  440.4 3.9 shard_map.378
  456.2 3.2 shard_map.381.refs_2_
  459.4 5.1 shard_map.382.refs_2_
  464.5 5.3 shard_map.383.refs_4_
  479.1 3.0 convert_element_type.26
  506.5 3.2 collective-permute-start.75
  509.7 4.5 shard_map.385
  514.9 4.7 shard_map.386
  527.3 7.8 %collective-permute-done.76.refs_3_ = bf16[192,384]{1,0:T(8,128)(2,1)S(1)} collective-permute-done((bf16[192,384]{1,0:T(8,128)(2,1)S(1)}, bf16[192,384]{1,0:T(8,128)(2,1)S(1)}, u32[]{:S(2)}, u32[]{:S(2)}) %collective-permute-start.76) | collective-permute-done | bytes 147488 | tf_op jit(solution)/shard_map/ppermute | solution.py:992
  543.3 15.5 %collective-permute-done.63.refs_2_ = bf16[384,384]{1,0:T(8,128)(2,1)S(1)} collective-permute-done((bf16[384,384]{1,0:T(8,128)(2,1)S(1)}, bf16[384,384]{1,0:T(8,128)(2,1)S(1)}, u32[]{:S(2)}, u32[]{:S(2)}) %collective-permute-start.63) | collective-permute-done | bytes 294944 | tf_op jit(solution)/shard_map/ppermute | solution.py:838
  562.9 7.1 %shard_map.388 = (f32[1536,768]{1,0:T(8,128)}, f32[768,1536]{1,0:T(8,128)}) custom-call(s32[2]{0:T(128)} %pad_add_fusion.2.refs_0_, bf16[384,768]{1,0:T(8,128)(2,1)} %get-tuple-element.259.refs_5_.refs_1_, bf16[384,768]{1,0:T(8,128)(2,1)} %collective-permute-done.69.refs_2_, bf16[384,768]{1,0:T(8,128)(2,1)} %collective-permute-done.70.refs_3_, ...), custom_call_target="tpu_custom_call" | custom-call | flops 60000002048 | tf_op jit(solution)/shard_map/pallas_call | solution.py:55
  575.8 5.6 shard_map.389
  582.8 6.0 collective-permute-done.81.refs_6_
  591.6 5.1 pad_maximum_fusion
  599.9 5.6 shard_map.390
  605.5 3.2 fusion
  608.8 3.2 broadcast_select_fusion.3
  612.0 6.4 %maximum_convert_fusion = f32[24,324,384]{2,0,1:T(8,128)} fusion(bf16[6,324,384]{2,0,1:T(8,128)(2,1)S(1)} %get-tuple-element.354, bf16[6,324,384]{2,0,1:T(8,128)(2,1)S(1)} %get-tuple-element.353, bf16[6,324,384]{2,0,1:T(8,128)(2,1)S(1)} %get-tuple-element.352, bf16[6,324,384]{2,0,1:T(8,128)(2,1)S(1)} %get-tuple-element.351), kind=kLoop, calls=%fused_computation.2 | loop fusion | flops 23887872 | bytes 17915904 | tf_op jit(solution)/shard_map/convert_element_type | solution.py:1314
  (428 shorter events, 166.7 us)
Async XLA Ops:
  0.7 23.0 %collective-permute-start.1 = (s32[6]{0:T(128)}, s32[6]{0:T(128)S(1)}, u32[]{:S(2)}, u32[]{:S(2)}) collective-permute-start(s32[6]{0:T(128)} %param.22), channel_id=1, source_target_pairs={{0,4},{2,6},{4,0},{6,2},{1,5},{3,7},{5,1},{7,3},{8,12},{10,14},{12... | collective-permute-start | bytes 80 | tf_op jit(solution)/shard_map/ppermute | solution.py:1110
  4.8 19.5 %collective-permute-start = (bf16[6,64,768]{2,1,0:T(8,128)(2,1)}, bf16[6,64,768]{2,1,0:T(8,128)(2,1)S(1)}, u32[]{:S(2)}, u32[]{:S(2)}) collective-permute-start(bf16[6,64,768]{2,1,0:T(8,128)(2,1)} %refs_0_.3), channel_id=1, source_target_pairs={{0,1},{1,0},{2,3},{3,2},{4,5},{5,4},{6,7},{7,6},{8,9},{9,8},{10,11... | collective-permute-start | bytes 1769480 | tf_op jit(solution)/shard_map/ppermute | solution.py:838
  20.0 41.2 %collective-permute-start.3 = (bf16[3,324,768]{2,1,0:T(8,128)(2,1)}, bf16[3,324,768]{2,1,0:T(8,128)(2,1)}, u32[]{:S(2)}, u32[]{:S(2)}) collective-permute-start(bf16[3,324,768]{2,1,0:T(8,128)(2,1)} %get-tuple-element.356.refs_11_), channel_id=1, source_target_pairs={{0,2},{2,0},{4,6},{6,4},{1,3},{3,1},{5,7},{7,5},{8,10},{10,8},{12,... | collective-permute-start | bytes 4478984 | tf_op jit(solution)/shard_map/ppermute | solution.py:838
  21.5 129.8 %collective-permute-start.10 = (bf16[6,64,768]{2,1,0:T(8,128)(2,1)}, bf16[6,64,768]{2,1,0:T(8,128)(2,1)}, u32[]{:S(2)}, u32[]{:S(2)}) collective-permute-start(bf16[6,64,768]{2,1,0:T(8,128)(2,1)} %param.39), channel_id=1, source_target_pairs={{0,1},{1,0},{2,3},{3,2},{4,5},{5,4},{6,7},{7,6},{8,9},{9,8},{10,11... | collective-permute-start | bytes 1769480 | tf_op jit(solution)/shard_map/ppermute | solution.py:838
  45.9 77.7 %collective-permute-start.5 = (bf16[6,128,384]{2,1,0:T(8,128)(2,1)}, bf16[6,128,384]{2,1,0:T(8,128)(2,1)}, u32[]{:S(2)}, u32[]{:S(2)}) collective-permute-start(bf16[6,128,384]{2,1,0:T(8,128)(2,1)} %get-tuple-element.169.refs_4_.refs_1_), channel_id=1, source_target_pairs={{0,4},{2,6},{4,0},{6,2},{1,5},{3,7},{5,1},{7,3},{8,12},{10,14},{12... | collective-permute-start | bytes 1769480 | tf_op jit(solution)/shard_map/ppermute | solution.py:1110
  61.2 42.9 %collective-permute-start.6 = (bf16[3,324,768]{2,1,0:T(8,128)(2,1)}, bf16[3,324,768]{2,1,0:T(8,128)(2,1)S(1)}, u32[]{:S(2)}, u32[]{:S(2)}) collective-permute-start(bf16[3,324,768]{2,1,0:T(8,128)(2,1)} %shard_map.338), channel_id=1, source_target_pairs={{0,2},{2,0},{4,6},{6,4},{1,3},{3,1},{5,7},{7,5},{8,10},{10,8},{12,... | collective-permute-start | bytes 4478984 | tf_op jit(solution)/shard_map/ppermute | solution.py:838
  129.8 17.0 %collective-permute-start.8 = (bf16[3,416,128]{2,1,0:T(8,128)(2,1)}, bf16[3,416,128]{2,1,0:T(8,128)(2,1)S(1)}, u32[]{:S(2)}, u32[]{:S(2)}) collective-permute-start(bf16[3,416,128]{2,1,0:T(8,128)(2,1)} %shard_map.343.refs_4_), channel_id=1, source_target_pairs={{0,4},{2,6},{4,0},{6,2},{1,5},{3,7},{5,1},{7,3},{8,12},{10,14},{12... | collective-permute-start | bytes 958472 | tf_op jit(solution)/shard_map/ppermute | solution.py:1110
  153.9 17.1 %collective-permute-start.12 = (bf16[3,416,128]{2,1,0:T(8,128)(2,1)S(1)}, bf16[3,416,128]{2,1,0:T(8,128)(2,1)S(1)}, u32[]{:S(2)}, u32[]{:S(2)}) collective-permute-start(bf16[3,416,128]{2,1,0:T(8,128)(2,1)S(1)} %copy-done.48), channel_id=1, source_target_pairs={{0,4},{2,6},{4,0},{6,2},{1,5},{3,7},{5,1},{7,3},{8,12},{10,14},{12... | collective-permute-start | bytes 958472 | tf_op jit(solution)/shard_map/ppermute | solution.py:1110
  163.0 11.4 %collective-permute-start.11 = (bf16[3,128,768]{2,1,0:T(8,128)(2,1)}, bf16[3,128,768]{2,1,0:T(8,128)(2,1)S(1)}, u32[]{:S(2)}, u32[]{:S(2)}) collective-permute-start(bf16[3,128,768]{2,1,0:T(8,128)(2,1)} %get-tuple-element.183.refs_2_), channel_id=1, source_target_pairs={{0,1},{1,0},{2,3},{3,2},{4,5},{5,4},{6,7},{7,6},{8,9},{9,8},{10,11... | collective-permute-start | bytes 1769480 | tf_op jit(solution)/shard_map/ppermute | solution.py:838
  188.9 31.6 %collective-permute-start.14 = (bf16[3,160,384]{2,1,0:T(8,128)(2,1)}, bf16[3,160,384]{2,1,0:T(8,128)(2,1)}, u32[]{:S(2)}, u32[]{:S(2)}) collective-permute-start(bf16[3,160,384]{2,1,0:T(8,128)(2,1)} %get-tuple-element.186.refs_2_), channel_id=1, source_target_pairs={{0,4},{2,6},{4,0},{6,2},{1,5},{3,7},{5,1},{7,3},{8,12},{10,14},{12... | collective-permute-start | bytes 1105928 | tf_op jit(solution)/shard_map/ppermute | solution.py:1110
  202.7 36.3 %collective-permute-start.17 = (bf16[3,160,384]{2,1,0:T(8,128)(2,1)}, bf16[3,160,384]{2,1,0:T(8,128)(2,1)}, u32[]{:S(2)}, u32[]{:S(2)}) collective-permute-start(bf16[3,160,384]{2,1,0:T(8,128)(2,1)} %get-tuple-element.203.refs_2_), channel_id=1, source_target_pairs={{0,4},{2,6},{4,0},{6,2},{1,5},{3,7},{5,1},{7,3},{8,12},{10,14},{12... | collective-permute-start | bytes 1105928 | tf_op jit(solution)/shard_map/ppermute | solution.py:1110
  217.5 33.1 %collective-permute-start.18 = (bf16[768,768]{1,0:T(8,128)(2,1)}, bf16[768,768]{1,0:T(8,128)(2,1)}, u32[]{:S(2)}, u32[]{:S(2)}) collective-permute-start(bf16[768,768]{1,0:T(8,128)(2,1)} %get-tuple-element.201.refs_7_), channel_id=1, source_target_pairs={{0,8},{8,0},{16,24},{24,16},{1,9},{9,1},{17,25},{25,17},{2,10},{10... | collective-permute-start | bytes 3538952 | tf_op jit(solution)/shard_map/ppermute | solution.py:838
  219.0 31.7 %collective-permute-start.19 = (bf16[768,768]{1,0:T(8,128)(2,1)}, bf16[768,768]{1,0:T(8,128)(2,1)}, u32[]{:S(2)}, u32[]{:S(2)}) collective-permute-start(bf16[768,768]{1,0:T(8,128)(2,1)} %get-tuple-element.213), channel_id=1, source_target_pairs={{0,16},{8,24},{16,0},{24,8},{1,17},{9,25},{17,1},{25,9},{2,18},{10... | collective-permute-start | bytes 3538952 | tf_op jit(solution)/shard_map/ppermute | solution.py:838
  229.3 48.1 %collective-permute-start.16 = (bf16[3,384,128]{2,1,0:T(8,128)(2,1)}, bf16[3,384,128]{2,1,0:T(8,128)(2,1)}, u32[]{:S(2)}, u32[]{:S(2)}) collective-permute-start(bf16[3,384,128]{2,1,0:T(8,128)(2,1)} %get-tuple-element.202.refs_7_), channel_id=1, source_target_pairs={{0,4},{2,6},{4,0},{6,2},{1,5},{3,7},{5,1},{7,3},{8,12},{10,14},{12... | collective-permute-start | bytes 884744 | tf_op jit(solution)/shard_map/ppermute | solution.py:1110
  247.8 35.8 %collective-permute-start.21 = (bf16[3,384,128]{2,1,0:T(8,128)(2,1)}, bf16[3,384,128]{2,1,0:T(8,128)(2,1)}, u32[]{:S(2)}, u32[]{:S(2)}) collective-permute-start(bf16[3,384,128]{2,1,0:T(8,128)(2,1)} %get-tuple-element.214.refs_5_), channel_id=1, source_target_pairs={{0,4},{2,6},{4,0},{6,2},{1,5},{3,7},{5,1},{7,3},{8,12},{10,14},{12... | collective-permute-start | bytes 884744 | tf_op jit(solution)/shard_map/ppermute | solution.py:1110
  255.4 25.1 %collective-permute-start.22 = (bf16[384,768]{1,0:T(8,128)(2,1)}, bf16[384,768]{1,0:T(8,128)(2,1)}, u32[]{:S(2)}, u32[]{:S(2)}) collective-permute-start(bf16[384,768]{1,0:T(8,128)(2,1)} %get-tuple-element.215.refs_6_), channel_id=1, source_target_pairs={{0,16},{8,24},{16,0},{24,8},{1,17},{9,25},{17,1},{25,9},{2,18},{10... | collective-permute-start | bytes 1769480 | tf_op jit(solution)/shard_map/ppermute | solution.py:838
  255.9 24.6 %collective-permute-start.23 = (bf16[384,768]{1,0:T(8,128)(2,1)}, bf16[384,768]{1,0:T(8,128)(2,1)}, u32[]{:S(2)}, u32[]{:S(2)}) collective-permute-start(bf16[384,768]{1,0:T(8,128)(2,1)} %get-tuple-element.222), channel_id=1, source_target_pairs={{0,8},{8,0},{16,24},{24,16},{1,9},{9,1},{17,25},{25,17},{2,10},{10... | collective-permute-start | bytes 1769480 | tf_op jit(solution)/shard_map/ppermute | solution.py:838
  280.0 20.4 %collective-permute-start.25 = (bf16[12,324,384]{2,1,0:T(8,128)(2,1)}, bf16[12,324,384]{2,1,0:T(8,128)(2,1)}, u32[]{:S(2)}, u32[]{:S(2)}) collective-permute-start(bf16[12,324,384]{2,1,0:T(8,128)(2,1)} %get-tuple-element.230), channel_id=1, source_target_pairs={{0,1},{1,0},{2,3},{3,2},{4,5},{5,4},{6,7},{7,6},{8,9},{9,8},{10,11... | collective-permute-start | bytes 8957960 | tf_op jit(solution)/shard_map/ppermute | solution.py:838
  286.2 17.4 %collective-permute-start.24 = (bf16[3,128,768]{2,1,0:T(8,128)(2,1)}, bf16[3,128,768]{2,1,0:T(8,128)(2,1)S(1)}, u32[]{:S(2)}, u32[]{:S(2)}) collective-permute-start(bf16[3,128,768]{2,1,0:T(8,128)(2,1)} %get-tuple-element.227.refs_3_), channel_id=1, source_target_pairs={{0,1},{1,0},{2,3},{3,2},{4,5},{5,4},{6,7},{7,6},{8,9},{9,8},{10,11... | collective-permute-start | bytes 1769480 | tf_op jit(solution)/shard_map/ppermute | solution.py:838
  286.2 36.6 %collective-permute-start.28 = (bf16[192,768]{1,0:T(8,128)(2,1)}, bf16[192,768]{1,0:T(8,128)(2,1)}, u32[]{:S(2)}, u32[]{:S(2)}) collective-permute-start(bf16[192,768]{1,0:T(8,128)(2,1)} %get-tuple-element.245), channel_id=1, source_target_pairs={{6,0},{0,2},{2,4},{4,6},{7,1},{1,3},{3,5},{5,7},{14,8},{8,10},{10,... | collective-permute-start | bytes 884744 | tf_op jit(solution)/shard_map/ppermute | solution.py:992
  286.2 36.6 %collective-permute-start.29 = (bf16[192,768]{1,0:T(8,128)(2,1)}, bf16[192,768]{1,0:T(8,128)(2,1)}, u32[]{:S(2)}, u32[]{:S(2)}) collective-permute-start(bf16[192,768]{1,0:T(8,128)(2,1)} %get-tuple-element.246), channel_id=1, source_target_pairs={{4,0},{6,2},{0,4},{2,6},{5,1},{7,3},{1,5},{3,7},{12,8},{14,10},{8,... | collective-permute-start | bytes 884744 | tf_op jit(solution)/shard_map/ppermute | solution.py:992
  288.5 34.3 %collective-permute-start.30 = (bf16[192,768]{1,0:T(8,128)(2,1)}, bf16[192,768]{1,0:T(8,128)(2,1)}, u32[]{:S(2)}, u32[]{:S(2)}) collective-permute-start(bf16[192,768]{1,0:T(8,128)(2,1)} %get-tuple-element.247), channel_id=1, source_target_pairs={{2,0},{4,2},{6,4},{0,6},{3,1},{5,3},{7,5},{1,7},{10,8},{12,10},{14... | collective-permute-start | bytes 884744 | tf_op jit(solution)/shard_map/ppermute | solution.py:992
  300.4 75.3 %collective-permute-start.42 = (bf16[3,64,768]{2,1,0:T(8,128)(2,1)}, bf16[3,64,768]{2,1,0:T(8,128)(2,1)}, u32[]{:S(2)}, u32[]{:S(2)}) collective-permute-start(bf16[3,64,768]{2,1,0:T(8,128)(2,1)} %get-tuple-element.271), channel_id=1, source_target_pairs={{0,1},{1,0},{2,3},{3,2},{4,5},{5,4},{6,7},{7,6},{8,9},{9,8},{10,11... | collective-permute-start | bytes 884744 | tf_op jit(solution)/shard_map/ppermute | solution.py:838
  321.3 30.3 %collective-permute-start.26 = (bf16[768,384]{1,0:T(8,128)(2,1)}, bf16[768,384]{1,0:T(8,128)(2,1)}, u32[]{:S(2)}, u32[]{:S(2)}) collective-permute-start(bf16[768,384]{1,0:T(8,128)(2,1)} %get-tuple-element.241.refs_4_), channel_id=1, source_target_pairs={{0,8},{8,0},{16,24},{24,16},{1,9},{9,1},{17,25},{25,17},{2,10},{10... | collective-permute-start | bytes 1769480 | tf_op jit(solution)/shard_map/ppermute | solution.py:838
  324.9 37.4 %collective-permute-start.33 = (bf16[192,768]{1,0:T(8,128)(2,1)}, bf16[192,768]{1,0:T(8,128)(2,1)}, u32[]{:S(2)}, u32[]{:S(2)}) collective-permute-start(bf16[192,768]{1,0:T(8,128)(2,1)} %shard_map.365.refs_2_.refs_1_), channel_id=1, source_target_pairs={{2,0},{4,2},{6,4},{0,6},{3,1},{5,3},{7,5},{1,7},{10,8},{12,10},{14... | collective-permute-start | bytes 884744 | tf_op jit(solution)/shard_map/ppermute | solution.py:992
  325.8 37.0 %collective-permute-start.34 = (bf16[192,768]{1,0:T(8,128)(2,1)}, bf16[192,768]{1,0:T(8,128)(2,1)}, u32[]{:S(2)}, u32[]{:S(2)}) collective-permute-start(bf16[192,768]{1,0:T(8,128)(2,1)} %shard_map.365.refs_2_.refs_1_), channel_id=1, source_target_pairs={{4,0},{6,2},{0,4},{2,6},{5,1},{7,3},{1,5},{3,7},{12,8},{14,10},{8,... | collective-permute-start | bytes 884744 | tf_op jit(solution)/shard_map/ppermute | solution.py:992
  327.6 25.3 %collective-permute-start.27 = (bf16[768,384]{1,0:T(8,128)(2,1)}, bf16[768,384]{1,0:T(8,128)(2,1)}, u32[]{:S(2)}, u32[]{:S(2)}) collective-permute-start(bf16[768,384]{1,0:T(8,128)(2,1)} %get-tuple-element.243), channel_id=1, source_target_pairs={{0,16},{8,24},{16,0},{24,8},{1,17},{9,25},{17,1},{25,9},{2,18},{10... | collective-permute-start | bytes 1769480 | tf_op jit(solution)/shard_map/ppermute | solution.py:838
  351.5 11.9 %collective-permute-start.35 = (bf16[192,768]{1,0:T(8,128)(2,1)S(1)}, bf16[192,768]{1,0:T(8,128)(2,1)S(1)}, u32[]{:S(2)}, u32[]{:S(2)}) collective-permute-start(bf16[192,768]{1,0:T(8,128)(2,1)S(1)} %copy-done.59), channel_id=1, source_target_pairs={{6,0},{0,2},{2,4},{4,6},{7,1},{1,3},{3,5},{5,7},{14,8},{8,10},{10,... | collective-permute-start | bytes 884744 | tf_op jit(solution)/shard_map/ppermute | solution.py:992
  352.9 26.0 %collective-permute-start.41 = (bf16[3,64,768]{2,1,0:T(8,128)(2,1)}, bf16[3,64,768]{2,1,0:T(8,128)(2,1)}, u32[]{:S(2)}, u32[]{:S(2)}) collective-permute-start(bf16[3,64,768]{2,1,0:T(8,128)(2,1)} %get-tuple-element.268), channel_id=1, source_target_pairs={{0,1},{1,0},{2,3},{3,2},{4,5},{5,4},{6,7},{7,6},{8,9},{9,8},{10,11... | collective-permute-start | bytes 884744 | tf_op jit(solution)/shard_map/ppermute | solution.py:838
  362.3 9.5 %collective-permute-start.31 = (bf16[384,384]{1,0:T(8,128)(2,1)S(1)}, bf16[384,384]{1,0:T(8,128)(2,1)S(1)}, u32[]{:S(2)}, u32[]{:S(2)}) collective-permute-start(bf16[384,384]{1,0:T(8,128)(2,1)S(1)} %copy-done.69), channel_id=1, source_target_pairs={{0,16},{8,24},{16,0},{24,8},{1,17},{9,25},{17,1},{25,9},{2,18},{10... | collective-permute-start | bytes 884744 | tf_op jit(solution)/shard_map/ppermute | solution.py:838
  362.9 9.8 %collective-permute-start.32 = (bf16[384,384]{1,0:T(8,128)(2,1)S(1)}, bf16[384,384]{1,0:T(8,128)(2,1)S(1)}, u32[]{:S(2)}, u32[]{:S(2)}) collective-permute-start(bf16[384,384]{1,0:T(8,128)(2,1)S(1)} %copy-done.68), channel_id=1, source_target_pairs={{0,8},{8,0},{16,24},{24,16},{1,9},{9,1},{17,25},{25,17},{2,10},{10... | collective-permute-start | bytes 884744 | tf_op jit(solution)/shard_map/ppermute | solution.py:838
  363.4 23.1 %collective-permute-start.39 = (bf16[768,384]{1,0:T(8,128)(2,1)}, bf16[768,384]{1,0:T(8,128)(2,1)S(1)}, u32[]{:S(2)}, u32[]{:S(2)}) collective-permute-start(bf16[768,384]{1,0:T(8,128)(2,1)} %get-tuple-element.258.refs_5_), channel_id=1, source_target_pairs={{0,8},{8,0},{16,24},{24,16},{1,9},{9,1},{17,25},{25,17},{2,10},{10... | collective-permute-start | bytes 1769480 | tf_op jit(solution)/shard_map/ppermute | solution.py:838
  371.8 17.5 %collective-permute-start.40 = (bf16[768,384]{1,0:T(8,128)(2,1)S(1)}, bf16[768,384]{1,0:T(8,128)(2,1)S(1)}, u32[]{:S(2)}, u32[]{:S(2)}) collective-permute-start(bf16[768,384]{1,0:T(8,128)(2,1)S(1)} %copy-done.37), channel_id=1, source_target_pairs={{0,16},{8,24},{16,0},{24,8},{1,17},{9,25},{17,1},{25,9},{2,18},{10... | collective-permute-start | bytes 1769480 | tf_op jit(solution)/shard_map/ppermute | solution.py:838
  383.3 101.5 %collective-permute-start.55 = (bf16[3,324,384]{2,1,0:T(8,128)(2,1)}, bf16[3,324,384]{2,1,0:T(8,128)(2,1)}, u32[]{:S(2)}, u32[]{:S(2)}) collective-permute-start(bf16[3,324,384]{2,1,0:T(8,128)(2,1)} %shard_map.366.refs_6_), channel_id=1, source_target_pairs={{0,2},{2,0},{4,6},{6,4},{1,3},{3,1},{5,7},{7,5},{8,10},{10,8},{12,... | collective-permute-start | bytes 2239496 | tf_op jit(solution)/shard_map/ppermute | solution.py:838
  383.8 103.4 %collective-permute-start.54 = (bf16[3,324,384]{2,1,0:T(8,128)(2,1)}, bf16[3,324,384]{2,1,0:T(8,128)(2,1)}, u32[]{:S(2)}, u32[]{:S(2)}) collective-permute-start(bf16[3,324,384]{2,1,0:T(8,128)(2,1)} %shard_map.362.refs_15_), channel_id=1, source_target_pairs={{0,2},{2,0},{4,6},{6,4},{1,3},{3,1},{5,7},{7,5},{8,10},{10,8},{12,... | collective-permute-start | bytes 2239496 | tf_op jit(solution)/shard_map/ppermute | solution.py:838
  385.4 37.9 %collective-permute-start.36 = (bf16[192,384]{1,0:T(8,128)(2,1)S(1)}, bf16[192,384]{1,0:T(8,128)(2,1)S(1)}, u32[]{:S(2)}, u32[]{:S(2)}) collective-permute-start(bf16[192,384]{1,0:T(8,128)(2,1)S(1)} %copy-done.85), channel_id=1, source_target_pairs={{6,0},{0,2},{2,4},{4,6},{7,1},{1,3},{3,5},{5,7},{14,8},{8,10},{10,... | collective-permute-start | bytes 442376 | tf_op jit(solution)/shard_map/ppermute | solution.py:992
  386.5 38.3 %collective-permute-start.37 = (bf16[192,384]{1,0:T(8,128)(2,1)S(1)}, bf16[192,384]{1,0:T(8,128)(2,1)S(1)}, u32[]{:S(2)}, u32[]{:S(2)}) collective-permute-start(bf16[192,384]{1,0:T(8,128)(2,1)S(1)} %copy-done.84), channel_id=1, source_target_pairs={{4,0},{6,2},{0,4},{2,6},{5,1},{7,3},{1,5},{3,7},{12,8},{14,10},{8,... | collective-permute-start | bytes 442376 | tf_op jit(solution)/shard_map/ppermute | solution.py:992
  389.3 39.2 %collective-permute-start.38 = (bf16[192,384]{1,0:T(8,128)(2,1)S(1)}, bf16[192,384]{1,0:T(8,128)(2,1)S(1)}, u32[]{:S(2)}, u32[]{:S(2)}) collective-permute-start(bf16[192,384]{1,0:T(8,128)(2,1)S(1)} %copy-done.83), channel_id=1, source_target_pairs={{2,0},{4,2},{6,4},{0,6},{3,1},{5,3},{7,5},{1,7},{10,8},{12,10},{14... | collective-permute-start | bytes 442376 | tf_op jit(solution)/shard_map/ppermute | solution.py:992
  423.3 21.0 %collective-permute-start.44 = (bf16[384,384]{1,0:T(8,128)(2,1)}, bf16[384,384]{1,0:T(8,128)(2,1)}, u32[]{:S(2)}, u32[]{:S(2)}) collective-permute-start(bf16[384,384]{1,0:T(8,128)(2,1)} %get-tuple-element.275.refs_2_), channel_id=1, source_target_pairs={{0,16},{8,24},{16,0},{24,8},{1,17},{9,25},{17,1},{25,9},{2,18},{10... | collective-permute-start | bytes 884744 | tf_op jit(solution)/shard_map/ppermute | solution.py:838
  435.0 14.5 %collective-permute-start.49 = (bf16[192,384]{1,0:T(8,128)(2,1)S(1)}, bf16[192,384]{1,0:T(8,128)(2,1)S(1)}, u32[]{:S(2)}, u32[]{:S(2)}) collective-permute-start(bf16[192,384]{1,0:T(8,128)(2,1)S(1)} %copy-done.86), channel_id=1, source_target_pairs={{2,0},{4,2},{6,4},{0,6},{3,1},{5,3},{7,5},{1,7},{10,8},{12,10},{14... | collective-permute-start | bytes 442376 | tf_op jit(solution)/shard_map/ppermute | solution.py:992
  478.5 11.3 %collective-permute-start.61 = (f32[4,768]{1,0:T(4,128)S(1)}, f32[4,768]{1,0:T(4,128)S(1)}, u32[]{:S(2)}, u32[]{:S(2)}) collective-permute-start(f32[4,768]{1,0:T(4,128)S(1)} %add.162), channel_id=1, source_target_pairs={{0,2},{2,0},{4,6},{6,4},{1,3},{3,1},{5,7},{7,5},{8,10},{10,8},{12,... | collective-permute-start | bytes 36872 | tf_op jit(solution)/shard_map/ppermute | solution.py:838
  482.1 40.5 %collective-permute-start.69 = (bf16[384,768]{1,0:T(8,128)(2,1)}, bf16[384,768]{1,0:T(8,128)(2,1)}, u32[]{:S(2)}, u32[]{:S(2)}) collective-permute-start(bf16[384,768]{1,0:T(8,128)(2,1)} %get-tuple-element.259.refs_5_.refs_1_), channel_id=1, source_target_pairs={{0,16},{8,24},{16,0},{24,8},{1,17},{9,25},{17,1},{25,9},{2,18},{10... | collective-permute-start | bytes 1769480 | tf_op jit(solution)/shard_map/ppermute | solution.py:838
  483.3 41.8 %collective-permute-start.70 = (bf16[384,768]{1,0:T(8,128)(2,1)}, bf16[384,768]{1,0:T(8,128)(2,1)}, u32[]{:S(2)}, u32[]{:S(2)}) collective-permute-start(bf16[384,768]{1,0:T(8,128)(2,1)} %get-tuple-element.259.refs_5_.refs_1_), channel_id=1, source_target_pairs={{0,8},{8,0},{16,24},{24,16},{1,9},{9,1},{17,25},{25,17},{2,10},{10... | collective-permute-start | bytes 1769480 | tf_op jit(solution)/shard_map/ppermute | solution.py:838
  493.6 10.3 %collective-permute-start.47 = (bf16[192,384]{1,0:T(8,128)(2,1)S(1)}, bf16[192,384]{1,0:T(8,128)(2,1)S(1)}, u32[]{:S(2)}, u32[]{:S(2)}) collective-permute-start(bf16[192,384]{1,0:T(8,128)(2,1)S(1)} %copy-done.80), channel_id=1, source_target_pairs={{4,0},{6,2},{0,4},{2,6},{5,1},{7,3},{1,5},{3,7},{12,8},{14,10},{8,... | collective-permute-start | bytes 442376 | tf_op jit(solution)/shard_map/ppermute | solution.py:992
  500.8 24.1 %collective-permute-start.72 = (bf16[384,768]{1,0:T(8,128)(2,1)}, bf16[384,768]{1,0:T(8,128)(2,1)}, u32[]{:S(2)}, u32[]{:S(2)}) collective-permute-start(bf16[384,768]{1,0:T(8,128)(2,1)} %get-tuple-element.298.refs_5_), channel_id=1, source_target_pairs={{0,8},{8,0},{16,24},{24,16},{1,9},{9,1},{17,25},{25,17},{2,10},{10... | collective-permute-start | bytes 1769480 | tf_op jit(solution)/shard_map/ppermute | solution.py:838
  504.0 10.2 %collective-permute-start.52 = (bf16[3,64,768]{2,1,0:T(8,128)(2,1)S(1)}, bf16[3,64,768]{2,1,0:T(8,128)(2,1)S(1)}, u32[]{:S(2)}, u32[]{:S(2)}) collective-permute-start(bf16[3,64,768]{2,1,0:T(8,128)(2,1)S(1)} %copy-done.53), channel_id=1, source_target_pairs={{0,1},{1,0},{2,3},{3,2},{4,5},{5,4},{6,7},{7,6},{8,9},{9,8},{10,11... | collective-permute-start | bytes 884744 | tf_op jit(solution)/shard_map/ppermute | solution.py:838
  506.5 20.1 %collective-permute-start.75 = (bf16[192,384]{1,0:T(8,128)(2,1)}, bf16[192,384]{1,0:T(8,128)(2,1)}, u32[]{:S(2)}, u32[]{:S(2)}) collective-permute-start(bf16[192,384]{1,0:T(8,128)(2,1)} %shard_map.384.refs_9_.refs_1_), channel_id=1, source_target_pairs={{2,0},{4,2},{6,4},{0,6},{3,1},{5,3},{7,5},{1,7},{10,8},{12,10},{14... | collective-permute-start | bytes 442376 | tf_op jit(solution)/shard_map/ppermute | solution.py:992
  522.6 12.5 %collective-permute-start.76 = (bf16[192,384]{1,0:T(8,128)(2,1)S(1)}, bf16[192,384]{1,0:T(8,128)(2,1)S(1)}, u32[]{:S(2)}, u32[]{:S(2)}) collective-permute-start(bf16[192,384]{1,0:T(8,128)(2,1)S(1)} %copy-done.82), channel_id=1, source_target_pairs={{4,0},{6,2},{0,4},{2,6},{5,1},{7,3},{1,5},{3,7},{12,8},{14,10},{8,... | collective-permute-start | bytes 442376 | tf_op jit(solution)/shard_map/ppermute | solution.py:992
  523.0 12.6 %collective-permute-start.77 = (bf16[192,384]{1,0:T(8,128)(2,1)S(1)}, bf16[192,384]{1,0:T(8,128)(2,1)S(1)}, u32[]{:S(2)}, u32[]{:S(2)}) collective-permute-start(bf16[192,384]{1,0:T(8,128)(2,1)S(1)} %copy-done.82), channel_id=1, source_target_pairs={{6,0},{0,2},{2,4},{4,6},{7,1},{1,3},{3,5},{5,7},{14,8},{8,10},{10,... | collective-permute-start | bytes 442376 | tf_op jit(solution)/shard_map/ppermute | solution.py:992
  524.9 16.5 %collective-permute-start.73 = (bf16[384,768]{1,0:T(8,128)(2,1)}, bf16[384,768]{1,0:T(8,128)(2,1)S(1)}, u32[]{:S(2)}, u32[]{:S(2)}) collective-permute-start(bf16[384,768]{1,0:T(8,128)(2,1)} %get-tuple-element.298.refs_5_), channel_id=1, source_target_pairs={{0,16},{8,24},{16,0},{24,8},{1,17},{9,25},{17,1},{25,9},{2,18},{10... | collective-permute-start | bytes 1769480 | tf_op jit(solution)/shard_map/ppermute | solution.py:838
  525.1 35.8 %collective-permute-start.71 = (bf16[384,768]{1,0:T(8,128)(2,1)}, bf16[384,768]{1,0:T(8,128)(2,1)S(1)}, u32[]{:S(2)}, u32[]{:S(2)}) collective-permute-start(bf16[384,768]{1,0:T(8,128)(2,1)} %collective-permute-done.69.refs_2_), channel_id=1, source_target_pairs={{0,8},{8,0},{16,24},{24,16},{1,9},{9,1},{17,25},{25,17},{2,10},{10... | collective-permute-start | bytes 1769480 | tf_op jit(solution)/shard_map/ppermute | solution.py:838
  526.6 34.9 %collective-permute-start.74 = (bf16[384,768]{1,0:T(8,128)(2,1)}, bf16[384,768]{1,0:T(8,128)(2,1)S(1)}, u32[]{:S(2)}, u32[]{:S(2)}) collective-permute-start(bf16[384,768]{1,0:T(8,128)(2,1)} %collective-permute-done.72.refs_6_), channel_id=1, source_target_pairs={{0,16},{8,24},{16,0},{24,8},{1,17},{9,25},{17,1},{25,9},{2,18},{10... | collective-permute-start | bytes 1769480 | tf_op jit(solution)/shard_map/ppermute | solution.py:838
  535.1 23.7 %collective-permute-start.63 = (bf16[384,384]{1,0:T(8,128)(2,1)S(1)}, bf16[384,384]{1,0:T(8,128)(2,1)S(1)}, u32[]{:S(2)}, u32[]{:S(2)}) collective-permute-start(bf16[384,384]{1,0:T(8,128)(2,1)S(1)} %copy-done.51), channel_id=1, source_target_pairs={{0,16},{8,24},{16,0},{24,8},{1,17},{9,25},{17,1},{25,9},{2,18},{10... | collective-permute-start | bytes 884744 | tf_op jit(solution)/shard_map/ppermute | solution.py:838
  535.6 24.0 %collective-permute-start.66 = (bf16[384,384]{1,0:T(8,128)(2,1)S(1)}, bf16[384,384]{1,0:T(8,128)(2,1)S(1)}, u32[]{:S(2)}, u32[]{:S(2)}) collective-permute-start(bf16[384,384]{1,0:T(8,128)(2,1)S(1)} %copy-done.52), channel_id=1, source_target_pairs={{0,8},{8,0},{16,24},{24,16},{1,9},{9,1},{17,25},{25,17},{2,10},{10... | collective-permute-start | bytes 884744 | tf_op jit(solution)/shard_map/ppermute | solution.py:838
  541.4 28.6 %collective-permute-start.56 = (bf16[3,324,384]{2,1,0:T(8,128)(2,1)S(1)}, bf16[3,324,384]{2,1,0:T(8,128)(2,1)S(1)}, u32[]{:S(2)}, u32[]{:S(2)}) collective-permute-start(bf16[3,324,384]{2,1,0:T(8,128)(2,1)S(1)} %copy-done.33), channel_id=1, source_target_pairs={{0,2},{2,0},{4,6},{6,4},{1,3},{3,1},{5,7},{7,5},{8,10},{10,8},{12,... | collective-permute-start | bytes 2239496 | tf_op jit(solution)/shard_map/ppermute | solution.py:838
  558.8 11.7 %collective-permute-start.64 = (bf16[384,384]{1,0:T(8,128)(2,1)S(1)}, bf16[384,384]{1,0:T(8,128)(2,1)S(1)}, u32[]{:S(2)}, u32[]{:S(2)}) collective-permute-start(bf16[384,384]{1,0:T(8,128)(2,1)S(1)} %copy-done.51), channel_id=1, source_target_pairs={{0,8},{8,0},{16,24},{24,16},{1,9},{9,1},{17,25},{25,17},{2,10},{10... | collective-permute-start | bytes 884744 | tf_op jit(solution)/shard_map/ppermute | solution.py:838
  559.6 13.2 %collective-permute-start.67 = (bf16[384,384]{1,0:T(8,128)(2,1)S(1)}, bf16[384,384]{1,0:T(8,128)(2,1)S(1)}, u32[]{:S(2)}, u32[]{:S(2)}) collective-permute-start(bf16[384,384]{1,0:T(8,128)(2,1)S(1)} %copy-done.52), channel_id=1, source_target_pairs={{0,16},{8,24},{16,0},{24,8},{1,17},{9,25},{17,1},{25,9},{2,18},{10... | collective-permute-start | bytes 884744 | tf_op jit(solution)/shard_map/ppermute | solution.py:838
  560.9 12.8 %collective-permute-start.65 = (bf16[384,384]{1,0:T(8,128)(2,1)S(1)}, bf16[384,384]{1,0:T(8,128)(2,1)S(1)}, u32[]{:S(2)}, u32[]{:S(2)}) collective-permute-start(bf16[384,384]{1,0:T(8,128)(2,1)S(1)} %collective-permute-done.63.refs_2_), channel_id=1, source_target_pairs={{0,8},{8,0},{16,24},{24,16},{1,9},{9,1},{17,25},{25,17},{2,10},{10... | collective-permute-start | bytes 884744 | tf_op jit(solution)/shard_map/ppermute | solution.py:838
  561.5 13.5 %collective-permute-start.68 = (bf16[384,384]{1,0:T(8,128)(2,1)S(1)}, bf16[384,384]{1,0:T(8,128)(2,1)S(1)}, u32[]{:S(2)}, u32[]{:S(2)}) collective-permute-start(bf16[384,384]{1,0:T(8,128)(2,1)S(1)} %collective-permute-done.66.refs_6_), channel_id=1, source_target_pairs={{0,16},{8,24},{16,0},{24,8},{1,17},{9,25},{17,1},{25,9},{2,18},{10... | collective-permute-start | bytes 884744 | tf_op jit(solution)/shard_map/ppermute | solution.py:838
  570.1 35.4 %collective-permute-start.53 = (bf16[12,324,384]{2,1,0:T(8,128)(2,1)}, bf16[12,324,384]{2,1,0:T(8,128)(2,1)}, u32[]{:S(2)}, u32[]{:S(2)}) collective-permute-start(bf16[12,324,384]{2,1,0:T(8,128)(2,1)} %get-tuple-element.296), channel_id=1, source_target_pairs={{0,1},{1,0},{2,3},{3,2},{4,5},{5,4},{6,7},{7,6},{8,9},{9,8},{10,11... | collective-permute-start | bytes 8957960 | tf_op jit(solution)/shard_map/ppermute | solution.py:838
  570.6 19.8 %collective-permute-start.57 = (bf16[3,324,384]{2,1,0:T(8,128)(2,1)S(1)}, bf16[3,324,384]{2,1,0:T(8,128)(2,1)S(1)}, u32[]{:S(2)}, u32[]{:S(2)}) collective-permute-start(bf16[3,324,384]{2,1,0:T(8,128)(2,1)S(1)} %copy-done.34), channel_id=1, source_target_pairs={{0,2},{2,0},{4,6},{6,4},{1,3},{3,1},{5,7},{7,5},{8,10},{10,8},{12,... | collective-permute-start | bytes 2239496 | tf_op jit(solution)/shard_map/ppermute | solution.py:838
  573.7 23.0 %collective-permute-start.79 = (bf16[384,384]{1,0:T(8,128)(2,1)S(1)}, bf16[384,384]{1,0:T(8,128)(2,1)S(1)}, u32[]{:S(2)}, u32[]{:S(2)}) collective-permute-start(bf16[384,384]{1,0:T(8,128)(2,1)S(1)} %copy-done.55), channel_id=1, source_target_pairs={{0,8},{8,0},{16,24},{24,16},{1,9},{9,1},{17,25},{25,17},{2,10},{10... | collective-permute-start | bytes 884744 | tf_op jit(solution)/shard_map/ppermute | solution.py:838
  575.0 13.9 %collective-permute-start.81 = (bf16[384,384]{1,0:T(8,128)(2,1)S(1)}, bf16[384,384]{1,0:T(8,128)(2,1)S(1)}, u32[]{:S(2)}, u32[]{:S(2)}) collective-permute-start(bf16[384,384]{1,0:T(8,128)(2,1)S(1)} %copy-done.56), channel_id=1, source_target_pairs={{0,8},{8,0},{16,24},{24,16},{1,9},{9,1},{17,25},{25,17},{2,10},{10... | collective-permute-start | bytes 884744 | tf_op jit(solution)/shard_map/ppermute | solution.py:838
  582.0 14.7 %collective-permute-start.82 = (bf16[384,384]{1,0:T(8,128)(2,1)S(1)}, bf16[384,384]{1,0:T(8,128)(2,1)S(1)}, u32[]{:S(2)}, u32[]{:S(2)}) collective-permute-start(bf16[384,384]{1,0:T(8,128)(2,1)S(1)} %copy-done.56), channel_id=1, source_target_pairs={{0,16},{8,24},{16,0},{24,8},{1,17},{9,25},{17,1},{25,9},{2,18},{10... | collective-permute-start | bytes 884744 | tf_op jit(solution)/shard_map/ppermute | solution.py:838
  (121 other events, 767.2 us)

commit v3 on v2

--- a/solution.py
+++ b/solution.py
@@ -156,7 +156,7 @@
     own, rec = xo[0].astype(F32), xr[0].astype(F32)
     x = jnp.concatenate([jnp.where(first, own, rec), jnp.where(first, rec, own)], axis=0)
     xf[0] = x.astype(BF)
-    n = (x * inv_rms(x) * gain[...]).astype(BF)
+    n = (x * inv_rms(x) * gain[0:1]).astype(BF)
     n1[0] = n
     w = wq.shape[1]
     q = (nn(n, wq[...]).astype(BF).astype(F32) * SCALE).astype(BF)
@@ -218,7 +218,7 @@
     v1 = h1[0]
     rows = v1.shape[0]
     half = rows // 2
-    gg, dv = norm_back(v1, gain[...], dn_a[0].astype(F32) + dn_b[0].astype(F32))
+    gg, dv = norm_back(v1, gain[1:2], dn_a[0].astype(F32) + dn_b[0].astype(F32))
     d1 = dh2[0] + dv
     gpart = fold8(jnp.where(first, gg[:half], gg[half:]))
 
@@ -324,12 +324,13 @@
     return jnp.sum(out, axis=-1)
 
 
-def cross_q_kernel(xf, a_a, a_b, gain, wq, h1, n2, q2):
+def cross_q_kernel(xf, a_a, a_b, gain, wq, h1, n2, q2, zero):
+    zero[...] = jnp.zeros_like(zero)
     k, rows, d = xf.shape
     h = xf[...].astype(F32) + a_a[...].astype(F32) + a_b[...].astype(F32)
     h1[...] = h
     h = h.reshape(k * rows, d)
-    n = (h * inv_rms(h) * gain[...]).astype(BF)
+    n = (h * inv_rms(h) * gain[1:2]).astype(BF)
     n2[...] = n.reshape(k, rows, d)
     q = nn(n, wq[...]).astype(BF).astype(F32) * SCALE
     q2[...] = q.astype(BF).reshape(k, rows, wq.shape[1])
@@ -344,9 +345,9 @@
         [paged(xf, k), paged(a_a, k), paged(a_b, k), whole(gain), whole(wq)],
         [
             out_paged((pages, rows, d), F32, k), out_paged((pages, rows, d), BF, k),
-            out_paged((pages, rows, w), BF, k),
+            out_paged((pages, rows, w), BF, k), out_whole((8, 128), jnp.int32),
         ],
-        us=5, after=after,
+        us=4, after=after,
     )
 
 
@@ -394,7 +395,7 @@
             out_paged((pages, rows, w), BF, k), out_paged((pages, w, rows), BF, k),
             out_paged((pages, 8, rows), F32, k), out_paged((pages, rows, d), BF, k),
         ],
-        us=4.5,
+        us=2.7,
         after=after,
     )
 
@@ -403,7 +404,7 @@
     k, rows, d = h1.shape
     h = (h1[...] + c_a[...].astype(F32) + c_b[...].astype(F32)).reshape(k * rows, d)
     h2[...] = h.reshape(k, rows, d)
-    n = (h * inv_rms(h) * gain[...]).astype(BF)
+    n = (h * inv_rms(h) * gain[2:3]).astype(BF)
     n3[...] = n.reshape(k, rows, d)
     g = cot[...].reshape(k * rows, d)
     units = w_in.shape[1]
@@ -454,7 +455,7 @@
     gacc = None
     flat = []
     for i in range(k):
-        gg, dv = norm_back(h2[i], gain[...], dn_a[i].astype(F32) + dn_b[i].astype(F32))
+        gg, dv = norm_back(h2[i], gain[2:3], dn_a[i].astype(F32) + dn_b[i].astype(F32))
         part = fold8(jnp.where(first, gg[:half], gg[half:]))
         gacc = part if gacc is None else gacc + part
         g = cot[i].astype(F32) + dv
@@ -536,59 +537,68 @@
     )
 
 
-def last_kernel(xo, dn_a, dn_b, dh1, gain, out, gain_grad):
-    page = pl.program_id(0)
-    gg, dv = norm_back(
-        xo[0].astype(F32), gain[...], dn_a[0].astype(F32) + dn_b[0].astype(F32)
-    )
-    out[0] = dh1[0] + dv
-    part = fold8(gg)
-
-    @pl.when(page == 0)
-    def _():
-        gain_grad[...] = part
-
-    @pl.when(page != 0)
-    def _():
-        gain_grad[...] += part
-
-
-def last(at, xo, dn_a, dn_b, dh1, gain, after=()):
+def last_kernel(xo, dn_a, dn_b, dh1, gain, *refs):
+    out, gain_grad = refs[-2:]
+    acc = None
+    for i in range(dh1.shape[0]):
+        gg, dv = norm_back(
+            xo[i].astype(F32), gain[0:1], dn_a[i].astype(F32) + dn_b[i].astype(F32)
+        )
+        out[i] = dh1[i] + dv
+        part = fold8(gg)
+        acc = part if acc is None else acc + part
+    gain_grad[...] = acc
+
+
+def last(at, xo, dn_a, dn_b, dh1, gain, prev=None, after=()):
     pages, half, d = dh1.shape
     return call(
         last_kernel,
-        (pages,),
-        [paged((xo, at)), paged(dn_a), paged(dn_b), paged(dh1), whole(gain)],
-        [out_paged((pages, half, d), F32), out_whole((8, d), F32)],
-        us=0.9 * pages,
+        (1,),
+        [paged((xo, at), pages), paged(dn_a, pages), paged(dn_b, pages), paged(dh1, pages), whole(gain)]
+        + ([] if prev is None else [kept(prev)]),
+        [
+            (xo.shape, F32, (pages, half, d), lambda i, *_: (at // pages, 0, 0)),
+            out_whole((8, d), F32),
+        ],
+        us=3,
         after=after,
-    )
-
-
-def branch_ffn_kernel(head, act, w_out, keep, send):
-    k, rows, units = act.shape
-    half = rows // 2
+        aliases={} if prev is None else {5: 0},
+    )
+
+
+def branch_ffn_kernel(nc, head, *refs):
+    acts, (w_out, keep, send) = refs[:nc], refs[nc:]
     first = head[0] == 0
-    f = nn(act[...].reshape(k * rows, units), w_out[...])
-    f = f.reshape(k, rows, f.shape[1])
-    keep[...] = jnp.where(first, f[:, :half], f[:, half:]).astype(BF)
-    send[...] = jnp.where(first, f[:, half:], f[:, :half]).astype(BF)
-
-
-def branch_ffn(head, act, w_out, k, after=()):
-    pages, rows, units = act.shape
+    for c, act in enumerate(acts):
+
+        @pl.when(pl.program_id(0) == c)
+        def _():
+            k, rows, units = act.shape
+            half = rows // 2
+            f = nn(act[...].reshape(k * rows, units), w_out[...])
+            f = f.reshape(k, rows, f.shape[1])
+            keep[...] = jnp.where(first, f[:, :half], f[:, half:]).astype(BF)
+            send[...] = jnp.where(first, f[:, half:], f[:, :half]).astype(BF)
+
+
+def branch_ffn(head, acts, w_out, after=()):
+    k, rows, units = acts[0].shape
     d = w_out.shape[1]
-    return call(
-        branch_ffn_kernel,
-        (pages // k,),
-        [paged(act, k), whole(w_out)],
+    pages = k * len(acts)
+    return call(
+        functools.partial(branch_ffn_kernel, len(acts)),
+        (len(acts),),
+        [whole(a) for a in acts] + [whole(w_out)],
         [out_paged((pages, rows // 2, d), BF, k), out_paged((pages, rows // 2, d), BF, k)],
         scalars=(head,),
-        us=6.8, after=after,
-    )
-
-
-def output_kernel(at, head, lens, h2, f_a, f_b, a_a, a_b, c_a, c_b, out, stats):
+        us=7,
+        after=after,
+    )
+
+
+def output_kernel(at, head, lens, h2, f_a, f_b, a_a, a_b, c_a, c_b, *refs):
+    out, stats = refs[-2:]
     page = pl.program_id(0)
     first = head[0] == 0
     half = f_a.shape[1]
@@ -611,15 +621,24 @@
     )
 
 
-def output_rows(at, head, lens, h2, f_a, f_b, a_a, a_b, c_a, c_b, after=()):
+def output_rows(at, head, lens, h2, f_a, f_b, a_a, a_b, c_a, c_b, prev=None, after=()):
     pages, rows, d = h2.shape
     return call(
         functools.partial(output_kernel, at),
         (pages,),
-        [paged(a) for a in (h2, f_a, f_b, (a_a, at), (a_b, at), c_a, c_b)],
-        [out_paged((pages, rows // 2, d), BF), out_paged((pages, 8, d), F32)],
+        [paged(a) for a in (h2, (f_a, at), (f_b, at), (a_a, at), (a_b, at), c_a, c_b)]
+        + ([] if prev is None else [kept(prev)]),
+        [
+            (
+                (a_a.shape[0], rows // 2, d), BF, (1, rows // 2, d),
+                lambda i, *_: (i + at, 0, 0),
+            ),
+            out_paged((pages, 8, d), F32),
+        ],
         scalars=(head, lens),
-        us=7.4, after=after,
+        us=1.5 * pages,
+        after=after,
+        aliases={} if prev is None else {9: 0},
     )
 
 
@@ -634,7 +653,7 @@
     )(x, *ORDER)
 
 
-def kv_kernel(copied, src, dst, enc, w, *refs):
+def kv_kernel(copied, pos, enc, w, *refs):
     if copied:
         kv, copy = refs[-2:]
         copy[...] = enc[...]
@@ -644,28 +663,33 @@
         kv[i] = nn(enc[i], w[...]).astype(BF)
 
 
-def kv_project(src, dst, enc, w, slots, k, copied=False, prev=None, after=()):
+def kv_project(pos, enc, w, slots, k, where, copied=False, prev=None, after=()):
     n, d = enc.shape[1:]
-    ins = [(enc, (k, n, d), lambda i, a, b: (a[i], 0, 0)), whole(w)]
+    ins = [paged(enc, k), whole(w)]
     if prev is not None:
         ins += [kept(p) for p in prev]
     widths = [w.shape[1]] + [d] * copied
     return call(
         functools.partial(kv_kernel, copied),
-        (src.shape[0],),
+        (enc.shape[0] // k,),
         ins,
-        [((slots, n, c), BF, (k, n, c), lambda i, a, b: (b[i], 0, 0)) for c in widths],
-        scalars=(src, dst),
-        us=0.9 * k * src.shape[0],
+        [((slots, n, c), BF, (k, n, c), lambda i, p: (where(i, p), 0, 0)) for c in widths],
+        scalars=(pos,),
+        us=0.9 * enc.shape[0],
         after=after,
-        aliases={} if prev is None else {4 + i: i for i in range(len(prev))},
-    )
-
-
-def cross_fwd_kernel(lims, q, kv_a, kv_b, o):
-    slot = pl.program_id(0)
+        aliases={} if prev is None else {3 + i: i for i in range(len(prev))},
+    )
+
+
+def limits(pos, group, n):
+    length = OCR + PATCH_SMALL + group * (PATCH_LARGE - PATCH_SMALL)
+    return length - pos[1] * n, length - (pos[1] + 1 - 2 * pos[6]) * n
+
+
+def cross_fwd_kernel(at, pos, group, q, kv_a, kv_b, o):
     rows, w = q.shape[1:]
     n = kv_a.shape[1]
+    lims = limits(pos, group[pl.program_id(0) + at], n)
 
     def run(masked):
         rowsum = []
@@ -678,7 +702,7 @@
                 s = nt(kv[0, :, c], qm)
                 if masked:
                     pos = lax.broadcasted_iota(jnp.int32, s.shape, 0)
-                    s = jnp.where(pos < lims[j, slot], s, MASKED)
+                    s = jnp.where(pos < lims[j], s, MASKED)
                 ss.append(s)
             m = jnp.maximum(*[jnp.max(s, axis=0, keepdims=True) for s in ss])
             es = [jnp.exp(s - m) for s in ss]
@@ -697,29 +721,29 @@
         terms = thirds(jnp.concatenate(rowsum, axis=0)) + [jnp.zeros((STATS - 24, rows), BF)]
         o[0, w:, :] = jnp.concatenate([t.astype(F32) for t in terms], axis=0).astype(BF)
 
-    full = (lims[0, slot] >= n) & (lims[1, slot] >= n)
+    full = (lims[0] >= n) & (lims[1] >= n)
     pl.when(full)(lambda: run(False))
     pl.when(jnp.logical_not(full))(lambda: run(True))
 
 
-def cross_fwd(lims, q, kv_a, kv_b, at, pages, after=()):
+def cross_fwd(pos, group, q, kv_a, kv_b, at, pages, after=()):
     rows, w = q[0].shape[1:]
     return call(
-        cross_fwd_kernel,
+        functools.partial(cross_fwd_kernel, q[1]),
         (pages,),
         [paged(q), paged((kv_a, at)), paged((kv_b, at))],
         [out_paged((pages, w + STATS, rows), BF)],
-        scalars=(lims,),
+        scalars=(pos, group),
         us=1.6 * pages,
         after=after,
     )[0]
 
 
-def cross_bwd_kernel(lims, q, do, kv_a, kv_b, *refs):
+def cross_bwd_kernel(at, pos, group, q, do, kv_a, kv_b, *refs):
     dq, dkv_a, dkv_b = refs[-3:]
-    slot = pl.program_id(0)
     rows, w = q.shape[1:]
     n = kv_a.shape[1]
+    lims = limits(pos, group[pl.program_id(0) + at], n)
     per = w // rows
     lines = w // HEAD_DIM // per
     stats = do[0, rows:, :].astype(F32)
@@ -745,7 +769,7 @@
                 s = nt(k, qm)
                 if masked:
                     pos = lax.broadcasted_iota(jnp.int32, s.shape, 0)
-                    s = jnp.where(pos < lims[j, slot], s, MASKED)
+                    s = jnp.where(pos < lims[j], s, MASKED)
                 p = jnp.exp(s - ls)
                 ds = (p * (nt(kv[0, :, cv], gm) - dl)).astype(BF)
                 dkv[0, :, c] = nn(ds, qm).astype(BF)
@@ -757,12 +781,12 @@
                 acc[HEAD_DIM:, rows:] * SCALE
             ).astype(BF)
 
-    full = (lims[0, slot] >= n) & (lims[1, slot] >= n)
+    full = (lims[0] >= n) & (lims[1] >= n)
     pl.when(full)(lambda: run(False))
     pl.when(jnp.logical_not(full))(lambda: run(True))
 
 
-def cross_bwd(lims, q, do, kv_a, kv_b, at, prev=None, after=()):
+def cross_bwd(pos, group, q, do, kv_a, kv_b, at, prev=None, after=()):
     pages, _, w = do.shape
     rows = q[0].shape[1]
     n = kv_a.shape[1]
@@ -774,18 +798,18 @@
         return (v.shape, BF, (1,) + v.shape[1:], lambda i, *_: (i + at, 0, 0))
 
     return call(
-        cross_bwd_kernel,
+        functools.partial(cross_bwd_kernel, q[1]),
         (pages,),
         ins,
         [out_paged((pages, w, rows), BF), out(kv_a), out(kv_b)],
-        scalars=(lims,),
+        scalars=(pos, group),
         us=2.4 * pages,
         after=after,
-        aliases={} if prev is None else {5: 1, 6: 2},
-    )
-
-
-def enc_back_kernel(src, head, dkv, enc, w, prev, keep, send, dw):
+        aliases={} if prev is None else {6: 1, 7: 2},
+    )
+
+
+def enc_back_kernel(head, dkv, enc, w, prev, keep, send, dw):
     low = head[0] == 0
     part = keep.shape[-1]
 
@@ -801,19 +825,19 @@
         dw[...] += tn(enc[j], dkv[j])
 
 
-def enc_back(src, head, dkv, enc, w, prev, k, after=()):
+def enc_back(head, dkv, enc, w, prev, k, after=()):
     slots, n, w2 = dkv.shape
     d = w.shape[0]
     part = d // 2
     return call(
         enc_back_kernel,
         (slots // k,),
-        [paged(dkv, k), (enc, (k, n, d), lambda i, t, h: (t[i], 0, 0)), whole(w), whole(prev)],
+        [paged(dkv, k), paged(enc, k), whole(w), whole(prev)],
         [
             out_paged((slots, n, part), BF, k), out_paged((slots, n, part), BF, k),
             out_whole((d, w2), F32),
         ],
-        scalars=(src, head),
+        scalars=(head,),
         us=1.7 * slots,
         after=after,
     )
@@ -823,12 +847,12 @@
     out[...] = (a[...].astype(F32) + b[...].astype(F32)).astype(BF)
 
 
-def add_pages(at, pages, a, b, after=()):
+def add_pages(at, pages, a, b, k, after=()):
     return call(
         add_pages_kernel,
-        (pages,),
-        [paged((a, at)), paged((b, at))],
-        [out_paged((pages,) + a.shape[1:], BF)],
+        (pages // k,),
+        [paged((a, at), k), paged((b, at), k)],
+        [out_paged((pages,) + a.shape[1:], BF, k)],
         us=0.7 * pages,
         after=after,
     )[0]
@@ -875,11 +899,11 @@
 
     def quarter_a(i, t):
         j = jnp.minimum(i, 3)
-        side = jnp.where(j < 2, 1 - t[0], t[0])
+        side = jnp.where(j < 2, 1 - t[2], t[2])
         return (0, 2 * side + j % 2)
 
     def side_b(i, t):
-        return (0, jnp.where(jnp.maximum(i, 4) < 6, 1 - t[1], t[1]))
+        return (0, jnp.where(jnp.maximum(i, 4) < 6, 1 - t[3], t[3]))
 
     def out(lo):
         return ((2 * blk, d), BF, (blk, d), lambda i, t: (jnp.clip(i - lo, 0, 1), 0))
@@ -898,26 +922,27 @@
     )
 
 
+def stacked(v):
+    c = v.shape[1] // 2
+    return jnp.concatenate([v[:, :c], v[:, c:]], axis=0)
+
+
 def grads_self_kernel(nc, bits, n, o, *refs):
     dq, dk, dv, g = (rows_of(refs[j * nc : (j + 1) * nc]) for j in range(4))
-    send_a, keep_a, send_b, keep_b = refs[4 * nc :]
-    d = n.shape[1]
+    send_a, keep_a, send_b, keep_b = refs[-4:]
     turned = jnp.transpose(n[...])
-    send_a[...], keep_a[...] = pick(bits[0], nn(turned, dq).astype(BF), nn(turned, dk).astype(BF))
-    ot = tn(o[...], g).astype(BF)
-    ot = jnp.concatenate([ot[:, : d // 2], ot[:, d // 2 :]], axis=0)
-    send_b[...], keep_b[...] = pick(bits[1], nn(turned, dv).astype(BF), ot)
+    send_a[...], keep_a[...] = pick(bits[2], nn(turned, dq).astype(BF), nn(turned, dk).astype(BF))
+    ot = stacked(tn(o[...], g).astype(BF))
+    send_b[...], keep_b[...] = pick(bits[3], nn(turned, dv).astype(BF), ot)
 
 
 def grads_cross_kernel(nc, bits, n, dw, *refs):
     dq, o, g = (rows_of(refs[j * nc : (j + 1) * nc]) for j in range(3))
-    send_a, keep_a, send_b, keep_b = refs[3 * nc :]
-    d = n.shape[1]
+    send_a, keep_a, send_b, keep_b = refs[-4:]
     w = dq.shape[1]
-    send_a[...], keep_a[...] = pick(bits[0], tn(n[...], dq).astype(BF), dw[:, :w].astype(BF))
-    ot = tn(o, g).astype(BF)
-    ot = jnp.concatenate([ot[:, : d // 2], ot[:, d // 2 :]], axis=0)
-    send_b[...], keep_b[...] = pick(bits[1], dw[:, w:].astype(BF), ot)
+    send_a[...], keep_a[...] = pick(bits[2], tn(n[...], dq).astype(BF), dw[:, :w].astype(BF))
+    ot = stacked(tn(o, g).astype(BF))
+    send_b[...], keep_b[...] = pick(bits[3], dw[:, w:].astype(BF), ot)
 
 
 def grads_tall(kernel, bits, arrays, chunked, d, w, us, after=()):
@@ -936,7 +961,7 @@
 def sum_one_kernel(bits, keep_a, got_a, keep_b, got_b, send_a, next_a, send_b, next_b):
     blk = send_a.shape[0]
     for keep, got, send, nxt, bit in (
-        (keep_a, got_a, send_a, next_a, bits[1]), (keep_b, got_b, send_b, next_b, bits[0])
+        (keep_a, got_a, send_a, next_a, bits[3]), (keep_b, got_b, send_b, next_b, bits[2])
     ):
         lo = keep[:blk].astype(F32) + got[:blk].astype(F32)
         hi = keep[blk:].astype(F32) + got[blk:].astype(F32)
@@ -945,41 +970,34 @@
         nxt[...] = k.astype(BF)
 
 
-def sum_two_kernel(nz, place, keep_a, got_a, keep_b, got_b, *rest):
-    outs, (sum_a, sum_b) = rest[:nz], rest[nz:]
-    part = keep_a.shape[0] // nz
-    sum_a[...] = keep_a[...].astype(F32) + got_a[...].astype(F32)
-    sum_b[...] = keep_b[...].astype(F32) + got_b[...].astype(F32)
-    for k in range(nz):
-        z = lax.rem(place[0] + k, nz)
-        at = pl.ds(pl.multiple_of(z * part, part), part)
-        outs[k][:part] = sum_a[at, :].astype(BF)
-        outs[k][part:] = sum_b[at, :].astype(BF)
-
-
-def sum_three_kernel(*refs):
-    acc = refs[0][...].astype(F32)
-    for r in refs[1:-1]:
-        acc = acc + r[...].astype(F32)
-    refs[-1][...] = acc.astype(BF)
-
-
-def join_kernel(nz, place, *refs):
-    pieces, (out_a, out_b, all_a, all_b) = refs[:nz], refs[nz:]
-    part = pieces[0].shape[0] // 2
-    for k in range(nz):
-        z = lax.rem(place[0] + k, nz)
-        at = pl.ds(pl.multiple_of(z * part, part), part)
-        all_a[at, :] = pieces[k][:part].astype(F32)
-        all_b[at, :] = pieces[k][part:].astype(F32)
-    out_a[...] = all_a[...].astype(BF)
-    out_b[...] = all_b[...].astype(BF)
-
-
-def reduce_bucket(parts, bits, place, nz):
+def sum_two_kernel(keep_a, got_a, keep_b, got_b, out):
+    nz, part = out.shape[0], out.shape[1] // 2
+    sides = ((0, keep_a, got_a), (part, keep_b, got_b))
+    for first, keep, got in sides:
+        total = keep[...].astype(F32) + got[...].astype(F32)
+        for z in range(nz):
+            out[z, first : first + part] = total[z * part : (z + 1) * part].astype(BF)
+
+
+def sum_three_kernel(got, out):
+    nz = got.shape[0]
+    total = sum(got[z].astype(F32) for z in range(nz)).astype(BF)
+    for z in range(nz):
+        out[z] = total
+
+
+def join_kernel(got, out_a, out_b):
+    nz, part = got.shape[0], got.shape[1] // 2
+    for first, out in ((0, out_a), (part, out_b)):
+        out[...] = jnp.concatenate(
+            [got[z, first : first + part].astype(F32) for z in range(nz)], axis=0
+        ).astype(BF)
+
+
+def reduce_bucket(parts, bits, nz):
     send_a, keep_a, send_b, keep_b = parts
     blk, c = send_a.shape[0] // 2, send_a.shape[1]
-    piece = (2 * blk // nz, c)
+    piece = (nz, 2 * blk // nz, c)
     fast = c / 384
 
     def x(v):
@@ -988,8 +1006,8 @@
     def y(v):
         return swap(v, "dp", 2, 4)
 
-    def shift(v, k):
-        return lax.ppermute(v, "seq", [((i + k) % nz, i) for i in range(nz)])
+    def over_seq(v):
+        return lax.all_to_all(v, "seq", 0, 0, tiled=True)
 
     got_a, got_b = x(send_a), y(send_b)
     yield
@@ -999,34 +1017,25 @@
     )
     got_a, got_b = y(send_a), x(send_b)
     yield
-    outs = call(
-        functools.partial(sum_two_kernel, nz), (1,),
-        [whole(v) for v in (keep_a, got_a, keep_b, got_b)], [out_whole(piece, BF)] * nz,
-        scalars=(place,), scratch=[pltpu.VMEM((blk, c), F32)] * 2, us=1.5 * fast,
-    )
-    got = [shift(outs[k], -k) for k in range(1, nz)]
+    (out,) = call(
+        sum_two_kernel, (1,), [whole(v) for v in (keep_a, got_a, keep_b, got_b)],
+        [out_whole(piece, BF)], us=1.5 * fast,
+    )
+    got = over_seq(out)
     yield
-    (mine,) = call(
-        sum_three_kernel, (1,), [whole(v) for v in [outs[0]] + got], [out_whole(piece, BF)],
-        us=1.5,
-    )
-    pieces = [mine] + [shift(mine, k) for k in range(1, nz)]
+    (out,) = call(sum_three_kernel, (1,), [whole(got)], [out_whole(piece, BF)], us=1.5)
+    got = over_seq(out)
     yield
-    a0, b0 = call(
-        functools.partial(join_kernel, nz), (1,), [whole(v) for v in pieces],
-        [out_whole((blk, c), BF)] * 2, scalars=(place,),
-        scratch=[pltpu.VMEM((blk, c), F32)] * 2, us=1.5 * fast,
-    )
+    a0, b0 = call(join_kernel, (1,), [whole(got)], [out_whole((blk, c), BF)] * 2, us=1.5 * fast)
     a1, b1 = y(a0), x(b0)
     a2, b2 = x(a0), y(b0)
-    a3, b3 = x(a1), y(b1)
-    yield [a0, a1, a2, a3, b0, b1, b2, b3]
-
-
-def final_kernel(outs, bits, *refs):
+    yield [a0, a1, a2, x(a1), b0, b1, b2, y(b1)]
+
+
+def final_kernel(outs, pos, *refs):
     pieces, results = refs[:8], refs[8:]
     t = pl.program_id(0)
-    for half, (hi, lo) in enumerate(((bits[0], bits[1]), (bits[1], bits[0]))):
+    for half, (hi, lo) in enumerate(((pos[2], pos[3]), (pos[3], pos[2]))):
         rel = (t // 2 + hi) % 2 * 2 + (t % 2 + lo) % 2
         for j in range(4):
             for r, (at, first, count) in zip(results, outs):
@@ -1038,7 +1047,7 @@
                     r[...] = pieces[4 * half + j][...].astype(F32)
 
 
-def final(pieces, bits, outs, us, after=()):
+def final(pieces, pos, outs, us, after=()):
     blk, c = pieces[0].shape
 
     def index(first, count, where):
@@ -1049,10 +1058,51 @@
         (4,),
         [whole(p) for p in pieces],
         [(o[0], F32, (blk, c), index(o[2], o[3], o[4])) for o in outs],
-        scalars=(bits,),
+        scalars=(pos,),
         us=us,
         after=after,
     )
+
+
+def add_kernel(a, b, out):
+    out[...] = a[...] + b[...]
+
+
+def add_small(a, b):
+    return call(add_kernel, (1,), [whole(a), whole(b)], [out_whole(a.shape, F32)], us=1)[0]
+
+
+def place_kernel(pos, a, b, out):
+    out[...] = (a[...].astype(F32) + b[...].astype(F32)).astype(BF)
+
+
+def keep_kernel(pos, a, prev, out):
+    out[...] = a[...]
+
+
+def place_sum(pos, a, b, pages, k, where):
+    n, c = a.shape[1:]
+    return call(
+        place_kernel,
+        (a.shape[0] // k,),
+        [paged(a, k), paged(b, k)],
+        [((pages, n, c), BF, (k, n, c), lambda i, p: (where(i, p), 0, 0))],
+        scalars=(pos,),
+        us=1.2 * a.shape[0] // k,
+    )[0]
+
+
+def place_more(pos, a, so_far, k, where):
+    n, c = a.shape[1:]
+    return call(
+        keep_kernel,
+        (a.shape[0] // k,),
+        [paged(a, k), kept(so_far)],
+        [(so_far.shape, BF, (k, n, c), lambda i, p: (where(i, p), 0, 0))],
+        scalars=(pos,),
+        us=1.5 * a.shape[0] // k,
+        aliases={2: 0},
+    )[0]
 
 
 def per_device(
@@ -1091,16 +1141,23 @@
     h = lax.axis_index("head")
     dp = lax.axis_index("dp")
     block, par = s // 2, s % 2
-    head = h.reshape(1).astype(jnp.int32)
-    bits = jnp.stack([dp % 2, dp // 2]).astype(jnp.int32)
-    place = s.reshape(1).astype(jnp.int32)
-
-    kk = jnp.arange(nb * chunks, dtype=jnp.int32) // chunks
-    cc = jnp.arange(nb * chunks, dtype=jnp.int32) % chunks
-    ident = jnp.arange(nb * chunks, dtype=jnp.int32)
-    own_groups = ((((block + kk) % nb) * 2 + par) * chunks + cc).astype(jnp.int32)
-    jl = jnp.arange(nb, dtype=jnp.int32)
-    arrived = ((jl + h * (nb // 2) - block) % nb * chunks).astype(jnp.int32)
+    pos = jnp.stack(
+        [v.astype(jnp.int32) for v in (h, s, dp % 2, dp // 2, dp, block, par)]
+    )
+    head = bits = pos
+
+    def arrived(late, c):
+        return lambda i, p: (
+            (i // k + late * (nb // 2) + p[0] * (nb // 2) + nb - p[5]) % nb * pages + c * k + i % k
+        )
+
+    def out_group(first, other):
+        def where(i, p):
+            kk, c = (i + first) // chunks, (i + first) % chunks
+            side = 1 - p[6] if other else p[6]
+            return ((p[5] + kk) % nb * 2 + side) * chunks + c
+
+        return where
 
     def head_swap(x):
         return swap(x, "head", 1, 2)
@@ -1116,60 +1173,65 @@
     both = range(chunks)
 
     x_other = head_swap(dec_input)
-    away = lax.dynamic_slice(
-        enc_states.reshape(nb, 2, pages, n, d),
-        (h * (nb // 2), 1 - par, 0, 0, 0),
-        (nb // 2, 1, pages, n, d),
-    ).reshape(nb // 2, pages, n, d)
-    away = [away[:, c * k : (c + 1) * k].reshape(nb // 2 * k, n, d) for c in both]
-    enc_in = [swap(away[0], "seq", 1, n_seq)]
+    enc_t = jnp.transpose(enc_states, (1, 0, 2))
+
+    def some_pages(at):
+        return jnp.transpose(lax.dynamic_slice_in_dim(enc_t, at, pages, 1), (1, 0, 2))
+
+    away = [some_pages(((h * (nb // 2) + i) * 2 + 1 - par) * pages) for i in range(nb // 2)]
+    away = [
+        jnp.concatenate([v[c * k : (c + 1) * k] for v in away], axis=0) for c in both
+    ]
+    enc_in = [swap(v, "seq", 1, n_seq) for v in away]
     cot_other = head_swap(cotangent)
     cot = jnp.concatenate(
         [jnp.where(h == 0, cotangent, cot_other), jnp.where(h == 0, cot_other, cotangent)], axis=1
     )
-    enc_len = [
-        OCR + PATCH_SMALL + g * (PATCH_LARGE - PATCH_SMALL) for g in owners(page_group)
-    ]
-    lims = [
-        jnp.stack([e - s * n, e - (s + 1 - 2 * par) * n]).astype(jnp.int32) for e in enc_len
-    ]
+    page_groups = owners(page_group)
     lens = jnp.sum(target_mask, axis=1).astype(jnp.int32)
     table = jnp.pad(rel_table.T, ((0, 8 - rel_table.shape[1]), (0, 128 - rel_table.shape[0])))
-    gains = [g.reshape(1, d) for g in (self_gain, cross_gain, ffn_gain)]
+    gains = jnp.stack([self_gain, cross_gain, ffn_gain])
     w_kv = jnp.concatenate([cross_k, cross_v], axis=1)
 
     xf, n1, qkv, o1, lse1, a_part = self_fwd(
-        head, lens, dec_input, x_other, gains[0], self_q, self_k, self_v, self_o, rel_buckets, table,
-        after=(away[0], *lims[1:]),
+        head, lens, dec_input, x_other, gains, self_q, self_k, self_v, self_o, rel_buckets, table,
+        after=(*away, *page_groups[1:], cot_other),
     )
     a_other = head_swap(a_part)
-    h1, n2, q2 = cross_q(xf, a_part, a_other, gains[1], cross_q_w, k)
+    h1, n2, q2, zero = cross_q(xf, a_part, a_other, gains, cross_q_w, k)
     qs = owners(q2)
-    for c in both[1:]:
-        enc_in.append(swap(gate(away[c]), "seq", 1, n_seq))
-    (kv_a,) = kv_project(own_groups, ident, enc_states, w_kv, slots, k)
+    direct = gate(enc_in[0])
+    arriving = [[direct, head_swap(direct)]]
+    enc_own = jnp.concatenate(
+        [some_pages((((block + i) % nb) * 2 + par) * pages + zero[0, 0]) for i in range(nb)], axis=0
+    )
+    (kv_a,) = kv_project(pos, enc_own, w_kv, slots, k, lambda i, p: i)
     os = [[None] * chunks for _ in range(nb)]
     rec = None
 
     def attend(j, c):
         o = cross_fwd(
-            lims[j][:, c * k : (c + 1) * k], (qs[j], c * k), kv_a, kv_b, j * pages + c * k, k
+            pos, page_groups[j], (qs[j], c * k), kv_a, kv_b, j * pages + c * k, k
         )
         os[j][c] = rolled(o, -j)
 
     for c in both:
-        direct = gate(enc_in[c])
-        for late, part in enumerate((direct, head_swap(direct))):
+        if c:
+            direct = gate(enc_in[c])
+            arriving.append([direct, head_swap(direct)])
+        for late, part in enumerate(arriving[c]):
             rec = kv_project(
-                ident[: nb // 2], arrived[late * (nb // 2) : (late + 1) * (nb // 2)] + c, part,
-                w_kv, slots, k, copied=True, prev=rec,
+                pos, part, w_kv, slots, 1, arrived(late, c), copied=True, prev=rec
             )
         kv_b, enc_rec = rec
-        attend(0, c)
-        if c:
-            for e in range(c - 1, chunks if c == chunks - 1 else c):
+        if c == chunks - 1:
+            for e in range(max(c - 1, 0), chunks):
                 for j in others:
                     attend(j, e)
+        elif c:
+            for j in others:
+                attend(j, c - 1)
+        attend(0, c)
 
     o2, o2t, lse2, c_part, c_other = ([None] * chunks for _ in range(5))
     h2, n3, act, du, dn3, dn3_other = ([None] * chunks for _ in range(6))
@@ -1185,20 +1247,20 @@
 
     def feed(c):
         h2[c], n3[c], act[c], du[c], dn3[c] = ffn(
-            c * k, h1, c_part[c], c_other[c], cot, gains[2], ff_in, ff_out, k
+            c * k, h1, c_part[c], c_other[c], cot, gains, ff_in, ff_out, k
         )
         dn3_other[c] = head_swap(dn3[c])
 
     def turn(c):
         dh2[c], dcr[c], do2, gain3[c] = grad_two(
-            c * k, head, h2[c], dn3[c], dn3_other[c], cot, gains[2], cross_o, o2t[c], lse2[c], k
+            c * k, head, h2[c], dn3[c], dn3_other[c], cot, gains, cross_o, o2t[c], lse2[c], k
         )
         dos[c] = owners(do2)
 
     def back(j, c):
         nonlocal dkv
         dqs[j][c], *dkv = cross_bwd(
-            lims[j][:, c * k : (c + 1) * k], (qs[j], c * k), dos[c][j], kv_a, kv_b,
+            pos, page_groups[j], (qs[j], c * k), dos[c][j], kv_a, kv_b,
             j * pages + c * k, prev=dkv,
         )
         dqs[j][c] = rolled(dqs[j][c], -j)
@@ -1209,129 +1271,136 @@
         mix(c)
         turn(c - 1)
         feed(c)
+        if c == chunks - 1:
+            grads_ffn = reduce_bucket(grads_wide(bits, act, cot, n3, du), bits, n_seq)
+            next(grads_ffn)
+            turn(c)
         back(0, c - 1)
-    turn(chunks - 1)
-    grads_ffn = reduce_bucket(grads_wide(bits, act, cot, n3, du), bits, place, n_seq)
-    next(grads_ffn)
     for c in both[:-1]:
         for j in others:
             back(j, c)
     for j in [0] + others:
+        if j == nb - 1:
+            next(grads_ffn)
         back(j, chunks - 1)
-    next(grads_ffn)
 
     keep_b, send_b, dw = enc_back(
-        ident, head, dkv[1], enc_rec, w_kv, jnp.zeros((d, 2 * w), F32), k
+        head, dkv[1], enc_rec, w_kv, jnp.zeros((d, 2 * w), F32), k
     )
     send_b = head_swap(send_b)
     dq2, dn2, dn2_other = ([None] * chunks for _ in range(3))
     for c in both:
         dq2[c], dn2[c] = grad_q([v[c] for v in dqs], cross_q_w, k)
         dn2_other[c] = head_swap(dn2[c])
-        if c == 0:
+        if c == chunks - 1:
             next(grads_ffn)
     quarter = slots // 4
+    spans = [(0, 2 * quarter), (2 * quarter, quarter), (3 * quarter, quarter)]
     enc_away = []
 
-    def send_away(*parts):
-        for i in parts:
-            enc_away.append(
-                swap(add_pages(i * quarter, quarter, keep_b, send_b), "seq", 1, n_seq)
-            )
-
+    def send_away():
+        at, count = spans[len(enc_away)]
+        enc_away.append(
+            swap(add_pages(at, count, keep_b, send_b, k), "seq", 1, n_seq)
+        )
+
+    keep_a, send_a, dw = enc_back(head, dkv[0], enc_own, w_kv, dw, k, after=(send_b,))
+    send_away()
+    send_a = head_swap(send_a)
+    grads_cross = reduce_bucket(
+        grads_tall(grads_cross_kernel, bits, [n2, dw], [dq2, o2, dcr], d, w, 6), bits, n_seq
+    )
+    next(grads_cross)
+    next(grads_ffn)
     backs = []
     dn1_other = []
     for c in both:
         backs.append(
             self_bwd(
-                c * k, head, lens, h1, dn2[c], dn2_other[c], dh2[c], gains[1], self_q, self_k,
+                c * k, head, lens, h1, dn2[c], dn2_other[c], dh2[c], gains, self_q, self_k,
                 self_v, self_o, rel_buckets, table, qkv, lse1,
             )
         )
         dn1_other.append(head_swap(backs[c][7]))
         if c == 0:
-            send_away(0)
+            next(grads_cross)
     dh1, dar, dq1, dk1, dv1, ds1, dn1, _, gain2 = zip(*backs)
+    next(grads_cross)
+    send_away()
     grads_self = reduce_bucket(
         grads_tall(
-            grads_self_kernel, bits, [n1, o1], [dq1, dk1, dv1, dar], d, w, 7
+            grads_self_kernel, bits, [n1, o1], [dq1, dk1, dv1, dar], d, w, 7,
+            after=(*dn1_other[:1], send_a),
         ),
-        bits, place, n_seq,
+        bits, n_seq,
     )
     next(grads_self)
-    next(grads_ffn)
-    send_away(1)
-    keep_a, send_a, dw = enc_back(own_groups, head, dkv[0], enc_states, w_kv, dw, k)
-    send_a = head_swap(send_a)
+    f_keep, f_send = branch_ffn(head, act, ff_out, after=dn1_other)
+    f_other = head_swap(f_send)
+    enc_out = place_sum(pos, keep_a, send_a, 2 * slots, k, out_group(0, False))
+    enc_out = place_more(pos, enc_away[0], enc_out, k, out_group(0, True))
     next(grads_self)
-    grads_cross = reduce_bucket(
-        grads_tall(grads_cross_kernel, bits, [n2, dw], [dq2, o2, dcr], d, w, 6),
-        bits, place, n_seq,
-    )
+    sums_ffn = next(grads_ffn)
+    input_grad, gain1 = None, []
+    for c in both:
+        input_grad, g = last(
+            c * k, dec_input, dn1[c], dn1_other[c], dh1[c], gains, prev=input_grad
+        )
+        gain1.append(g)
+    next(grads_self)
     next(grads_cross)
-    sums_ffn = next(grads_ffn)
+    tables = [table_grad(ds1[c], rel_buckets, c * k) for c in both]
+    enc_out = place_more(pos, enc_away[1], enc_out, k, out_group(spans[1][0] // k, True))
     next(grads_self)
-    lasts = [last(c * k, dec_input, dn1[c], dn1_other[c], dh1[c], gains[0]) for c in both]
-    next(grads_cross)
-    send_away(2)
-    next(grads_self)
-    branches = [branch_ffn(head, act[c], ff_out, k) for c in both]
-    f_other = [head_swap(f[1]) for f in branches]
-    next(grads_cross)
-    sums_self = next(grads_self)
-    send_away(3)
-    tables = [table_grad(ds1[c], rel_buckets, c * k) for c in both]
-    next(grads_cross)
-    outputs = [
-        output_rows(
-            c * k, head, lens, h2[c], branches[c][0], f_other[c], a_part, a_other, c_part[c],
-            c_other[c],
+    send_away()
+    output, squares = None, []
+    for c in both:
+        output, sq = output_rows(
+            c * k, head, lens, h2[c], f_keep, f_other, a_part, a_other, c_part[c],
+            c_other[c], prev=output,
         )
-        for c in both
-    ]
-    sums_cross = next(grads_cross)
-
+        squares.append(sq)
     units = ff_in.shape[1]
     row, col = (lambda v: (v, 0)), (lambda v: (0, v))
     ff_out_grad, ff_in_grad = final(
-        sums_ffn, bits,
+        sums_ffn, pos,
         [((units, d), 0, 0, 4, row), ((d, units), 1, 0, 4, lambda v: (v % 2, v // 2))], 6,
     )
+    sums_cross = next(grads_cross)
+    sums_self = next(grads_self)
+
+    squares = jnp.sum(jnp.concatenate(squares, axis=0)[:, :4], axis=-1)
+
+    def line(v):
+        return jnp.pad(v.reshape(1, -1), ((0, 0), (0, d - v.size)))
+
+    small = jnp.concatenate(
+        [jnp.sum(sum(g), axis=0)[None] for g in (gain1, gain2, gain3)] + [line(squares)], axis=0
+    )
+    small_other = head_swap(small)
+    small = add_small(small, small_other)
+    rms_stats = jnp.sqrt(small[3, : pages * 4].reshape(pages, 4) / (lens.astype(F32) * d)[:, None])
+    table_part = sum(tables)
+    small = jnp.concatenate([small[:3], line(table_part)], axis=0)
+    steps = [(axis, 1 << i) for axis in ("dp", "seq") for i in range(sizes[axis].bit_length() - 1)]
     four = [
         ((d, w), 0, 0, 2, row), ((d, w), 0, 2, 2, row), ((d, w), 1, 0, 2, row), ((w, d), 1, 2, 2, col)
     ]
-    sq, sk, sv, so = final(sums_self, bits, four, 4)
-
-    back_a = (keep_a.astype(F32) + send_a.astype(F32)).astype(BF)
-    enc_away = jnp.concatenate(enc_away, axis=0)
-    pieces = []
-    for j in range(nb):
-        at = (j - block) % nb * pages
-        mine, theirs = (
-            lax.dynamic_slice_in_dim(v, at, pages, 0) for v in (back_a, enc_away)
-        )
-        pieces += [jnp.where(par == 0, mine, theirs), jnp.where(par == 0, theirs, mine)]
-    enc_t = jnp.transpose(jnp.concatenate(pieces, axis=0), (1, 0, 2)).astype(F32)
-    enc_grad = jnp.transpose(with_layout_constraint(enc_t, Layout((0, 1, 2))), (1, 0, 2))
-    cq, ck, cv, co = final(sums_cross, bits, four, 4)
-
-    output = jnp.concatenate([o[0] for o in outputs], axis=0)
-    input_grad = jnp.concatenate([o[0] for o in lasts], axis=0)
-    squares = jnp.sum(jnp.concatenate([o[1] for o in outputs], axis=0)[:, :4], axis=-1)
-    squares = squares + head_swap(squares)
-    counts = lens.astype(F32) * d
-    rms_stats = jnp.sqrt(squares / counts[:, None])
-    small = jnp.stack(
-        [jnp.sum(sum(g), axis=0) for g in ([o[1] for o in lasts], gain2, gain3)]
-    )
-    small = small + head_swap(small)
-    table_part = sum(tables)
-    line = jnp.pad(table_part.reshape(1, -1), ((0, 0), (0, d - table_part.size)))
-    small = jnp.concatenate([small, line], axis=0)
-    for axis in ("dp", "seq"):
-        for i in range(sizes[axis].bit_length() - 1):
-            small = small + swap(small, axis, 1 << i, sizes[axis])
+    for step, (axis, mask) in enumerate(steps):
+        other = swap(small, axis, mask, sizes[axis])
+        if step == 1:
+            enc_out = place_more(
+                pos, enc_away[2], enc_out, k, out_group(spans[2][0] // k, True)
+            )
+        if step == 2:
+            cq, ck, cv, co = final(sums_cross, pos, four, 5)
+        small = add_small(small, other)
     table_sum = small[3, : table_part.size].reshape(table_part.shape)
+    enc_grad = with_layout_constraint(
+        jnp.transpose(enc_out, (1, 0, 2)).astype(F32), Layout((0, 1, 2))
+    )
+    enc_grad = jnp.transpose(enc_grad, (1, 0, 2))
+    sq, sk, sv, so = final(sums_self, pos, four, 5)
 
     return (
         output, input_grad, enc_grad, small[0], small[1], small[2], sq, sk, sv, so, table_sum.T,

time: 630 us -> 554 us (0.88)
  waiting for transfers between devices: 128 us -> 47.7 us
  other arithmetic: 32.9 us -> 11.8 us
  local copies, waits for them, and re-layouts: 47.6 us -> 67.3 us
  Pallas kernels: 322 us -> 334 us
    ppermute x18 -> x0, waiting for transfers between devices: 43.5 us -> none  [shift(): return lax.ppermute(v, 'seq', [((i + k) % nz, i) for i in range(nz)])]
    ppermute x59 -> x56, waiting for transfers between devices: 66.5 us -> 25.7 us  [swap(): return lax.ppermute(x, axis, [(i, i ^ mask) for i in range(size)])]
    ppermute x18 -> x0, starting transfers between devices: 29.1 us -> none  [shift(): return lax.ppermute(v, 'seq', [((i + k) % nz, i) for i in range(nz)])]
    all_to_all x0 -> x6, starting transfers between devices: none -> 26.5 us  [over_seq(): return lax.all_to_all(v, 'seq', 0, 0, tiled=True)]
    pallas_call x57 -> x64, Pallas kernels: 322 us -> 334 us  [call(): pl.pallas_call(run, grid_spec=spec, out_shape=[jax.ShapeDtypeStruct(s, d)...]
    transpose x0 -> x1, local copies, waits for them, and re-layouts: none -> 11.2 us  [some_pages(): jnp.transpose(lax.dynamic_slice_in_dim(enc_t, at, pages, 1), (1, 0, 2))]
    all_to_all x0 -> x6, waiting for transfers between devices: none -> 9.74 us  [over_seq(): return lax.all_to_all(v, 'seq', 0, 0, tiled=True)]
    slice x3, local copies, waits for them, and re-layouts: 2.02 us -> 10 us  [the longest x1 8.14 us: per_device(): v[c * k:(c + 1) * k]]
  transfers between devices with their start and end apart: 85 -> 70, of which waited for: 23 -> 11; matrix products, arithmetic and copies ran while one was open for 8% -> 10% of each run, Pallas kernels for 51% -> 55%
where the time goes in v3:
time: 554 us; the launch traced here: 547 us
  Pallas kernels  334 us (60%)
  starting transfers between devices  83.6 us (15%)
  local copies, waits for them, and re-layouts  67.3 us (12%)
  waiting for transfers between devices  47.7 us (9%)
  other arithmetic  11.8 us (2%)
    pallas_call x64, Pallas kernels, call(): pl.pallas_call(run, grid_spec=spec, out_shape=[jax.ShapeDtypeStruct(s, d)...  334 us
    ppermute x56, starting transfers between devices, swap(): return lax.ppermute(x, axis, [(i, i ^ mask) for i in range(size)])  47.3 us
    unnamed x151, local copies, waits for them, and re-layouts  31.6 us
    all_to_all x6, starting transfers between devices, over_seq(): return lax.all_to_all(v, 'seq', 0, 0, tiled=True)  26.5 us
    ppermute x56, waiting for transfers between devices, swap(): return lax.ppermute(x, axis, [(i, i ^ mask) for i in range(size)])  25.7 us
    ppermute x8, waiting for transfers between devices, rolled(): return lax.ppermute(x, 'seq', perm) if step % nb else x  12.3 us
    transpose x1, local copies, waits for them, and re-layouts, some_pages(): jnp.transpose(lax.dynamic_slice_in_dim(enc_t, at, pages, 1), (1, 0, 2))  11.2 us
  transfers between devices with their start and end apart: 70, of which 11 were waited for; matrix products, arithmetic and copies ran while one was open for 10% of the time, Pallas kernels for 55%

profile of v3, /device:TPU:0, one launch (start us, length us, event | category | flops | bytes accessed | tf_op | source)
XLA Modules:
  0.0 547.3 jit_solution(14511878726801075855)
XLA Ops:
  1.3 4.0 collective-permute-start.1
  5.3 8.1 %constant_dynamic-slice_fusion.3 = (bf16[3,324,768]{2,0,1:T(4,128)(2,1)S(1)}, bf16[3,324,768]{2,0,1:T(4,128)(2,1)S(1)}) fusion(bf16[24,324,768]{2,0,1:T(8,128)(2,1)} %param.21, s32[]{:T(128)S(6)} %add.95, s32[]{:T(128)S(6)} %select_n.51), kind=kLoop, calls=%fused_computation.25 | loop fusion | bytes 5971976 | tf_op jit(solution)/shard_map/slice | solution.py:1183
  20.3 10.7 %shard_map.331 = (bf16[6,128,768]{2,1,0:T(8,128)(2,1)}, bf16[6,128,768]{2,1,0:T(8,128)(2,1)}, bf16[6,128,1152]{2,1,0:T(8,128)(2,1)}, bf16[6,128,384]{2,1,0:T(8,1...) custom-call(s32[7]{0:T(128)} %stack.43.refs_0_, s32[6]{0:T(128)} %reduce_sum.63.refs_1_, ...), custom_call_target="tpu_custom_call" | custom-call | flops 99999997952 | tf_op jit(solution)/shard_map/pallas_call | solution.py:55
  37.1 4.2 shard_map.332
  43.8 11.2 %constant_dynamic-slice_fusion.1 = (bf16[6,324,768]{2,0,1:T(8,128)(2,1)}, bf16[6,324,768]{2,0,1:T(8,128)(2,1)}) fusion(bf16[24,324,768]{2,0,1:T(8,128)(2,1)} %param.21, s32[]{:T(128)S(6)} %select_n.55, s32[]{:T(128)S(6)} %select_n.53), kind=kLoop, calls=%fused_computation.23 | loop fusion | bytes 11943944 | tf_op jit(solution)/shard_map/transpose | solution.py:1179
  55.0 4.3 copy_dynamic-update-slice_fusion.1
  59.3 7.8 %collective-permute-done.5.refs_0_ = bf16[3,324,768]{2,1,0:T(8,128)(2,1)S(1)} collective-permute-done((bf16[3,324,768]{2,1,0:T(8,128)(2,1)S(1)}, bf16[3,324,768]{2,1,0:T(8,128)(2,1)S(1)}, u32[]{:S(2)}, u32[]{:S(2)}) %collective-permute-start.5) | collective-permute-done | bytes 1493024 | tf_op jit(solution)/shard_map/ppermute | solution.py:862
  68.2 4.3 copy_dynamic-update-slice_fusion.refs_1_.refs_2_
  72.6 9.8 %shard_map.333.refs_3_.refs_4_ = bf16[12,324,768]{2,1,0:T(8,128)(2,1)} custom-call(s32[7]{0:T(128)} %stack.43.refs_0_, bf16[12,324,768]{2,1,0:T(8,128)(2,1)} %copy_dynamic-update-slice_fusion.refs_1_.refs_2_, bf16[768,768]{1,0:T(8,128)(2,1)} %constant_dynamic-update-slice_fusion.refs_2_.refs_3_, s32[8,128]{1,0:T(8,128)} %get-tuple-element.157.refs_3_.refs_1_), custom_call_target="tpu_custom_call" | custom-call | flops 108000002048 | tf_op jit(solution)/shard_map/pallas_call | solution.py:55
  82.3 5.6 %shard_map.335 = (bf16[12,324,768]{2,1,0:T(8,128)(2,1)}, bf16[12,324,768]{2,1,0:T(8,128)(2,1)}) custom-call(s32[7]{0:T(128)} %stack.43.refs_0_, bf16[3,324,768]{2,1,0:T(8,128)(2,1)} %shard_map.334.refs_1_, bf16[768,768]{1,0:T(8,128)(2,1)} %constant_dynamic-update-slice_fusion.refs_2_.refs_3_, bf16[12,324,768]{2,1,0:T(8,128)(2,1)} %shard_map.333.refs_3_.refs_4_), custom_call_target="tpu_custom_call" | custom-call | flops 27000000512 | tf_op jit(solution)/shard_map/pallas_call | solution.py:55
  89.0 5.6 %shard_map.336 = (bf16[12,324,768]{2,1,0:T(8,128)(2,1)}, bf16[12,324,768]{2,1,0:T(8,128)(2,1)}) custom-call(s32[7]{0:T(128)} %stack.43.refs_0_, bf16[3,324,768]{2,1,0:T(8,128)(2,1)} %copy-done.30, bf16[768,768]{1,0:T(8,128)(2,1)} %constant_dynamic-update-slice_fusion.refs_2_.refs_3_, ...), custom_call_target="tpu_custom_call", output_to_operand_aliasing={{0}: (3, {}), {1}: (4, {})} | custom-call | flops 27000000512 | tf_op jit(solution)/shard_map/pallas_call | solution.py:55
  94.6 6.1 %shard_map.337.refs_1_.refs_5_.refs_0_ = bf16[3,416,128]{2,1,0:T(8,128)(2,1)} custom-call(s32[7]{0:T(128)} %stack.43.refs_0_, s32[6]{0:T(128)} %refs_1_.9, bf16[6,128,384]{2,1,0:T(8,128)(2,1)} %get-tuple-element.156.refs_2_, bf16[12,324,768]{2,1,0:T(8,128)(2,1)} %shard_map.333.refs_3_.refs_4_, bf16[12,324,768]{2,1,0:T(8,128)(2,1)} %get-tuple-element.160.refs_4_.refs_3_), custom_call_target="tpu_custom_call" | custom-call | flops 48000000000 | tf_op jit(solution)/shard_map/pallas_call | solution.py:55
  100.7 11.1 %collective-permute-done.4.refs_0_ = bf16[3,324,768]{2,1,0:T(8,128)(2,1)} collective-permute-done((bf16[3,324,768]{2,1,0:T(8,128)(2,1)}, bf16[3,324,768]{2,1,0:T(8,128)(2,1)}, u32[]{:S(2)}, u32[]{:S(2)}) %collective-permute-start.4) | collective-permute-done | bytes 1493024 | tf_op jit(solution)/shard_map/ppermute | solution.py:862
  111.8 5.6 %shard_map.339 = (bf16[12,324,768]{2,1,0:T(8,128)(2,1)}, bf16[12,324,768]{2,1,0:T(8,128)(2,1)}) custom-call(s32[7]{0:T(128)} %stack.43.refs_0_, bf16[3,324,768]{2,1,0:T(8,128)(2,1)} %shard_map.338.refs_1_, bf16[768,768]{1,0:T(8,128)(2,1)} %constant_dynamic-update-slice_fusion.refs_2_.refs_3_, ...), custom_call_target="tpu_custom_call", output_to_operand_aliasing={{0}: (3, {}), {1}: (4, {})} | custom-call | flops 27000000512 | tf_op jit(solution)/shard_map/pallas_call | solution.py:55
  118.5 5.6 %shard_map.340 = (bf16[12,324,768]{2,1,0:T(8,128)(2,1)}, bf16[12,324,768]{2,1,0:T(8,128)(2,1)}) custom-call(s32[7]{0:T(128)} %stack.43.refs_0_, bf16[3,324,768]{2,1,0:T(8,128)(2,1)} %copy-done.31, bf16[768,768]{1,0:T(8,128)(2,1)} %constant_dynamic-update-slice_fusion.refs_2_.refs_3_, ...), custom_call_target="tpu_custom_call", output_to_operand_aliasing={{0}: (3, {}), {1}: (4, {})} | custom-call | flops 27000000512 | tf_op jit(solution)/shard_map/pallas_call | solution.py:55
  124.1 6.5 %shard_map.341.refs_5_ = bf16[3,416,128]{2,1,0:T(8,128)(2,1)} custom-call(s32[7]{0:T(128)} %stack.43.refs_0_, s32[6]{0:T(128)} %copy-done.70, bf16[6,128,384]{2,1,0:T(8,128)(2,1)} %collective-permute-done.8.refs_2_, bf16[12,324,768]{2,1,0:T(8,128)(2,1)} %shard_map.333.refs_3_.refs_4_, bf16[12,324,768]{2,1,0:T(8,128)(2,1)} %get-tuple-element.164.refs_4_.refs_5_), custom_call_target="tpu_custom_call" | custom-call | flops 48000000000 | tf_op jit(solution)/shard_map/pallas_call | solution.py:55
  130.7 6.1 %shard_map.342.refs_5_ = bf16[3,416,128]{2,1,0:T(8,128)(2,1)} custom-call(s32[7]{0:T(128)} %stack.43.refs_0_, s32[6]{0:T(128)} %copy-done.70, bf16[6,128,384]{2,1,0:T(8,128)(2,1)} %collective-permute-done.8.refs_2_, bf16[12,324,768]{2,1,0:T(8,128)(2,1)} %shard_map.333.refs_3_.refs_4_, bf16[12,324,768]{2,1,0:T(8,128)(2,1)} %get-tuple-element.164.refs_4_.refs_5_, ...), custom_call_target="tpu_custom_call" | custom-call | flops 48000000000 | tf_op jit(solution)/shard_map/pallas_call | solution.py:55
  136.8 6.1 %shard_map.343.refs_3_.refs_0_ = bf16[3,416,128]{2,1,0:T(8,128)(2,1)} custom-call(s32[7]{0:T(128)} %stack.43.refs_0_, s32[6]{0:T(128)} %refs_1_.9, bf16[6,128,384]{2,1,0:T(8,128)(2,1)} %get-tuple-element.156.refs_2_, bf16[12,324,768]{2,1,0:T(8,128)(2,1)} %shard_map.333.refs_3_.refs_4_, bf16[12,324,768]{2,1,0:T(8,128)(2,1)} %get-tuple-element.164.refs_4_.refs_5_, ...), custom_call_target="tpu_custom_call" | custom-call | flops 48000000000 | tf_op jit(solution)/shard_map/pallas_call | solution.py:55
  142.9 4.7 collective-permute-done.10.refs_1_
  154.0 8.3 %shard_map.345 = (f32[3,128,768]{2,1,0:T(8,128)}, bf16[3,128,768]{2,1,0:T(8,128)(2,1)}, bf16[3,128,1536]{2,1,0:T(8,128)(2,1)}, bf16[3,128,1536]{2,1,0:T(8,128)(2,1)}, bf16[3,128,768]{2,1,0:T(8,128)(2,1)}) custom-call(f32[6,128,768]{2,1,0:T(8,128)} %get-tuple-element.155.refs_0_.refs_2_, bf16[3,128,768]{2,1,0:T(8,128)(2,1)} %get-tuple-element.165.refs_1_.refs_7_, ...), custom_call_target="tpu_custom_call" | custom-call | flops 120000004096 | tf_op jit(solution)/shard_map/pallas_call | solution.py:55
  162.4 7.5 %collective-permute-done.9.refs_1_ = bf16[3,416,128]{2,1,0:T(8,128)(2,1)S(1)} collective-permute-done((bf16[3,416,128]{2,1,0:T(8,128)(2,1)S(1)}, bf16[3,416,128]{2,1,0:T(8,128)(2,1)S(1)}, u32[]{:S(2)}, u32[]{:S(2)}) %collective-permute-start.9) | collective-permute-done | bytes 319520 | tf_op jit(solution)/shard_map/ppermute | solution.py:1167
  170.6 2.7 shard_map.346
  174.2 4.8 shard_map.347
  179.8 8.4 %shard_map.348 = (f32[3,128,768]{2,1,0:T(8,128)}, bf16[3,128,768]{2,1,0:T(8,128)(2,1)}, bf16[3,128,1536]{2,1,0:T(8,128)(2,1)}, bf16[3,128,1536]{2,1,0:T(8,128)(2,1)}, bf16[3,128,768]{2,1,0:T(8,128)(2,1)}) custom-call(f32[6,128,768]{2,1,0:T(8,128)} %get-tuple-element.155.refs_0_.refs_2_, bf16[3,128,768]{2,1,0:T(8,128)(2,1)} %get-tuple-element.168.refs_1_.refs_7_, ...), custom_call_target="tpu_custom_call" | custom-call | flops 120000004096 | tf_op jit(solution)/shard_map/pallas_call | solution.py:55
  188.6 12.0 %shard_map.349 = (bf16[768,768]{1,0:T(8,128)(2,1)}, bf16[768,768]{1,0:T(8,128)(2,1)}, bf16[768,768]{1,0:T(8,128)(2,1)}, bf16[768,768]{1,0:T(8,128)(2,1)}) custom-call(s32[7]{0:T(128)} %stack.43.refs_0_, bf16[384,1536]{1,0:T(8,128)(2,1)} %bitcast.45, bf16[384,1536]{1,0:T(8,128)(2,1)} %bitcast.47, bf16[384,768]{1,0:T(8,128)(2,1)} %bitcast.55, ...), custom_call_target="tpu_custom_call" | custom-call | flops 99999997952 | tf_op jit(solution)/shard_map/pallas_call | solution.py:55
  204.5 4.8 shard_map.350
  209.3 8.7 %shard_map.351 = (bf16[3,384,128]{2,1,0:T(8,128)(2,1)}, bf16[12,324,768]{2,1,0:T(8,128)(2,1)}, bf16[12,324,768]{2,1,0:T(8,128)(2,1)}) custom-call(s32[7]{0:T(128)} %stack.43.refs_0_, s32[6]{0:T(128)} %refs_1_.9, bf16[6,128,384]{2,1,0:T(8,128)(2,1)} %get-tuple-element.156.refs_2_, bf16[3,160,384]{2,1,0:T(8,128)(2,1)} %get-tuple-element.176.refs_3_, ...), custom_call_target="tpu_custom_call" | custom-call | flops 71999995904 | tf_op jit(solution)/shard_map/pallas_call | solution.py:55
  218.0 2.9 collective-permute-start.17
  220.9 8.7 %shard_map.352 = (bf16[3,384,128]{2,1,0:T(8,128)(2,1)}, bf16[12,324,768]{2,1,0:T(8,128)(2,1)}, bf16[12,324,768]{2,1,0:T(8,128)(2,1)}) custom-call(s32[7]{0:T(128)} %stack.43.refs_0_, s32[6]{0:T(128)} %copy-done.70, bf16[6,128,384]{2,1,0:T(8,128)(2,1)} %collective-permute-done.8.refs_2_, ...), custom_call_target="tpu_custom_call", output_to_operand_aliasing={{1}: (6, {}), {2}: (7, {})} | custom-call | flops 71999995904 | tf_op jit(solution)/shard_map/pallas_call | solution.py:55
  229.7 9.2 %shard_map.353 = (bf16[3,384,128]{2,1,0:T(8,128)(2,1)}, bf16[12,324,768]{2,1,0:T(8,128)(2,1)}, bf16[12,324,768]{2,1,0:T(8,128)(2,1)}) custom-call(s32[7]{0:T(128)} %stack.43.refs_0_, s32[6]{0:T(128)} %refs_1_.9, bf16[6,128,384]{2,1,0:T(8,128)(2,1)} %get-tuple-element.156.refs_2_, ...), custom_call_target="tpu_custom_call", output_to_operand_aliasing={{1}: (6, {}), {2}: (7, {})} | custom-call | flops 71999995904 | tf_op jit(solution)/shard_map/pallas_call | solution.py:55
  239.5 4.7 shard_map.354
  244.9 8.7 %shard_map.355 = (bf16[3,384,128]{2,1,0:T(8,128)(2,1)}, bf16[12,324,768]{2,1,0:T(8,128)(2,1)}, bf16[12,324,768]{2,1,0:T(8,128)(2,1)}) custom-call(s32[7]{0:T(128)} %stack.43.refs_0_, s32[6]{0:T(128)} %copy-done.70, bf16[6,128,384]{2,1,0:T(8,128)(2,1)} %collective-permute-done.8.refs_2_, ...), custom_call_target="tpu_custom_call", output_to_operand_aliasing={{1}: (6, {}), {2}: (7, {})} | custom-call | flops 71999995904 | tf_op jit(solution)/shard_map/pallas_call | solution.py:55
  253.6 2.8 collective-permute-start.23
  258.5 18.3 %shard_map.356 = (bf16[12,324,384]{2,1,0:T(8,128)(2,1)}, bf16[12,324,384]{2,1,0:T(8,128)(2,1)}, f32[768,768]{1,0:T(8,128)}) custom-call(s32[7]{0:T(128)} %stack.43.refs_0_, bf16[12,324,768]{2,1,0:T(8,128)(2,1)} %get-tuple-element.199.refs_1_, bf16[12,324,768]{2,1,0:T(8,128)(2,1)} %get-tuple-element.200.refs_2_, ...), custom_call_target="tpu_custom_call" | custom-call | flops 204000002048 | tf_op jit(solution)/shard_map/pallas_call | solution.py:55
  282.6 2.9 shard_map.359.refs_6_
  285.5 4.3 all-to-all-start
  291.4 18.3 %shard_map.360 = (bf16[12,324,384]{2,1,0:T(8,128)(2,1)}, bf16[12,324,384]{2,1,0:T(8,128)(2,1)}, f32[768,768]{1,0:T(8,128)}) custom-call(s32[7]{0:T(128)} %stack.43.refs_0_, bf16[12,324,768]{2,1,0:T(8,128)(2,1)} %get-tuple-element.212.refs_1_, bf16[12,324,768]{2,1,0:T(8,128)(2,1)} %copy_dynamic-update-slice_fusion.refs_1_.refs_2_, ...), custom_call_target="tpu_custom_call" | custom-call | flops 204000002048 | tf_op jit(solution)/shard_map/pallas_call | solution.py:55
  309.7 2.9 shard_map.361.refs_9_
  314.6 5.8 %shard_map.362 = (bf16[768,384]{1,0:T(8,128)(2,1)}, bf16[768,384]{1,0:T(8,128)(2,1)}, bf16[768,384]{1,0:T(8,128)(2,1)}, bf16[768,384]{1,0:T(8,128)(2,1)}) custom-call(s32[7]{0:T(128)} %stack.43.refs_0_, bf16[768,768]{1,0:T(8,128)(2,1)} %bitcast.46, f32[768,768]{1,0:T(8,128)} %get-tuple-element.214.refs_2_, bf16[384,384]{1,0:T(8,128)(2,1)} %bitcast.62, ...), custom_call_target="tpu_custom_call" | custom-call | flops 60000002048 | tf_op jit(solution)/shard_map/pallas_call | solution.py:55
  325.8 4.4 all-to-all-start.1
  330.2 10.5 %shard_map.364 = (f32[3,64,768]{2,1,0:T(8,128)}, bf16[3,128,768]{2,1,0:T(8,128)(2,1)}, bf16[3,128,384]{2,1,0:T(8,128)(2,1)}, bf16[3,128,384]{2,1,0:T(8,128)(2,1)...) custom-call(s32[7]{0:T(128)} %stack.43.refs_0_, ...), custom_call_target="tpu_custom_call" | custom-call | flops 83999997952 | tf_op jit(solution)/shard_map/pallas_call | solution.py:55
  342.2 3.4 shard_map.365
  346.7 10.4 %shard_map.366 = (f32[3,64,768]{2,1,0:T(8,128)}, bf16[3,128,768]{2,1,0:T(8,128)(2,1)}, bf16[3,128,384]{2,1,0:T(8,128)(2,1)}, bf16[3,128,384]{2,1,0:T(8,128)(2,1)...) custom-call(s32[7]{0:T(128)} %stack.43.refs_0_, ...), custom_call_target="tpu_custom_call" | custom-call | flops 83999997952 | tf_op jit(solution)/shard_map/pallas_call | solution.py:55
  367.5 6.5 %shard_map.369 = (bf16[768,384]{1,0:T(8,128)(2,1)}, bf16[768,384]{1,0:T(8,128)(2,1)}, bf16[768,384]{1,0:T(8,128)(2,1)}, bf16[768,384]{1,0:T(8,128)(2,1)}) custom-call(s32[7]{0:T(128)} %stack.43.refs_0_, bf16[768,768]{1,0:T(8,128)(2,1)} %bitcast.44, bf16[768,384]{1,0:T(8,128)(2,1)} %bitcast.50, bf16[384,384]{1,0:T(8,128)(2,1)} %bitcast.59, ...), custom_call_target="tpu_custom_call" | custom-call | flops 70000001024 | tf_op jit(solution)/shard_map/pallas_call | solution.py:55
  377.8 6.1 %shard_map.370 = (bf16[6,64,768]{2,1,0:T(8,128)(2,1)}, bf16[6,64,768]{2,1,0:T(8,128)(2,1)}) custom-call(s32[7]{0:T(128)} %stack.43.refs_0_, bf16[3,128,1536]{2,1,0:T(8,128)(2,1)} %get-tuple-element.174.refs_1_, bf16[3,128,1536]{2,1,0:T(8,128)(2,1)} %get-tuple-element.175.refs_2_, bf16[1536,768]{1,0:T(8,128)(2,1)} %refs_3_.1, bf16[3,64,768]{2,1,0:T(8,128)(2,1)} %copy-done.47, ...), custom_call_target="tpu_custom_call" | custom-call | flops 70000001024 | tf_op jit(solution)/shard_map/pallas_call | solution.py:55
  383.8 5.7 %shard_map.371.refs_2_ = bf16[24,324,384]{2,1,0:T(8,128)(2,1)} custom-call(s32[7]{0:T(128)} %stack.43.refs_0_, bf16[12,324,384]{2,1,0:T(8,128)(2,1)} %get-tuple-element.251.refs_1_, bf16[12,324,384]{2,1,0:T(8,128)(2,1)} %copy-done.29, bf16[6,64,768]{2,1,0:T(8,128)(2,1)} %get-tuple-element.246.refs_3_), custom_call_target="tpu_custom_call" | custom-call | flops 40000000000 | tf_op jit(solution)/shard_map/pallas_call | solution.py:55
  389.6 3.0 shard_map.372.refs_5_.refs_2_
  393.6 3.5 shard_map.373
  398.1 3.6 all-to-all-start.3
  417.8 4.4 all-to-all-start.2
  424.2 5.1 shard_map.379.refs_2_
  429.3 5.1 shard_map.380.refs_3_
  437.7 2.7 shard_map.381.refs_1_.refs_2_
  442.4 5.1 all-to-all-start.5
  453.9 4.5 shard_map.384
  458.4 4.6 shard_map.385
  464.2 7.0 %shard_map.386 = (f32[1536,768]{1,0:T(8,128)}, f32[768,1536]{1,0:T(8,128)}) custom-call(s32[7]{0:T(128)} %stack.43.refs_0_, bf16[384,768]{1,0:T(8,128)(2,1)} %get-tuple-element.260.refs_5_.refs_1_, bf16[384,768]{1,0:T(8,128)(2,1)} %collective-permute-done.42.refs_2_, bf16[384,768]{1,0:T(8,128)(2,1)} %collective-permute-done.43.refs_3_, ...), custom_call_target="tpu_custom_call" | custom-call | flops 60000002048 | tf_op jit(solution)/shard_map/pallas_call | solution.py:55
  471.2 4.7 all-to-all-start.4
  481.9 8.1 %all-to-all-done.4.refs_0_ = bf16[4,192,384]{2,1,0:T(8,128)(2,1)S(1)} async-done(((bf16[4,192,384]{2,1,0:T(8,128)(2,1)}), bf16[4,192,384]{2,1,0:T(8,128)(2,1)S(1)}, u32[]{:S(2)}, u32[]{:S(2)}) %all-to-all-start.4) | async-done | bytes 589856 | tf_op jit(solution)/shard_map/all_to_all | solution.py:1010
  504.1 2.7 shard_map.391.refs_2_
  506.8 5.4 collective-permute-done.49.refs_1_
  518.6 5.5 shard_map.393
  528.0 5.3 copy_convert_fusion
  541.6 5.4 shard_map.396
  (331 shorter events, 137.6 us)
Async XLA Ops:
  0.7 18.1 %collective-permute-start.2 = (bf16[6,64,768]{2,1,0:T(8,128)(2,1)}, bf16[6,64,768]{2,1,0:T(8,128)(2,1)S(1)}, u32[]{:S(2)}, u32[]{:S(2)}) collective-permute-start(bf16[6,64,768]{2,1,0:T(8,128)(2,1)} %param.39), channel_id=1, source_target_pairs={{0,1},{1,0},{2,3},{3,2},{4,5},{5,4},{6,7},{7,6},{8,9},{9,8},{10,11... | collective-permute-start | bytes 1769480 | tf_op jit(solution)/shard_map/ppermute | solution.py:862
  1.2 17.6 %collective-permute-start = (bf16[6,64,768]{2,1,0:T(8,128)(2,1)}, bf16[6,64,768]{2,1,0:T(8,128)(2,1)S(1)}, u32[]{:S(2)}, u32[]{:S(2)}) collective-permute-start(bf16[6,64,768]{2,1,0:T(8,128)(2,1)} %refs_0_.3), channel_id=1, source_target_pairs={{0,1},{1,0},{2,3},{3,2},{4,5},{5,4},{6,7},{7,6},{8,9},{9,8},{10,11... | collective-permute-start | bytes 1769480 | tf_op jit(solution)/shard_map/ppermute | solution.py:862
  1.3 17.4 %collective-permute-start.1 = (s32[6]{0:T(128)}, s32[6]{0:T(128)S(1)}, u32[]{:S(2)}, u32[]{:S(2)}) collective-permute-start(s32[6]{0:T(128)} %refs_1_.9), channel_id=1, source_target_pairs={{0,4},{2,6},{4,0},{6,2},{1,5},{3,7},{5,1},{7,3},{8,12},{10,14},{12... | collective-permute-start | bytes 80 | tf_op jit(solution)/shard_map/ppermute | solution.py:1167
  31.2 36.0 %collective-permute-start.5 = (bf16[3,324,768]{2,1,0:T(8,128)(2,1)S(1)}, bf16[3,324,768]{2,1,0:T(8,128)(2,1)S(1)}, u32[]{:S(2)}, u32[]{:S(2)}) collective-permute-start(bf16[3,324,768]{2,1,0:T(8,128)(2,1)S(1)} %copy-done), channel_id=1, source_target_pairs={{0,2},{2,0},{4,6},{6,4},{1,3},{3,1},{5,7},{7,5},{8,10},{10,8},{12,... | collective-permute-start | bytes 4478984 | tf_op jit(solution)/shard_map/ppermute | solution.py:862
  32.8 79.0 %collective-permute-start.4 = (bf16[3,324,768]{2,1,0:T(8,128)(2,1)}, bf16[3,324,768]{2,1,0:T(8,128)(2,1)}, u32[]{:S(2)}, u32[]{:S(2)}) collective-permute-start(bf16[3,324,768]{2,1,0:T(8,128)(2,1)} %copy.69.refs_12_), channel_id=1, source_target_pairs={{0,2},{2,0},{4,6},{6,4},{1,3},{3,1},{5,7},{7,5},{8,10},{10,8},{12,... | collective-permute-start | bytes 4478984 | tf_op jit(solution)/shard_map/ppermute | solution.py:862
  68.2 19.7 %collective-permute-start.6 = (bf16[3,324,768]{2,1,0:T(8,128)(2,1)}, bf16[3,324,768]{2,1,0:T(8,128)(2,1)S(1)}, u32[]{:S(2)}, u32[]{:S(2)}) collective-permute-start(bf16[3,324,768]{2,1,0:T(8,128)(2,1)} %shard_map.334.refs_1_), channel_id=1, source_target_pairs={{0,1},{1,0},{2,3},{3,2},{4,5},{5,4},{6,7},{7,6},{8,9},{9,8},{10,11... | collective-permute-start | bytes 4478984 | tf_op jit(solution)/shard_map/ppermute | solution.py:862
  68.2 55.9 %collective-permute-start.8 = (bf16[6,128,384]{2,1,0:T(8,128)(2,1)}, bf16[6,128,384]{2,1,0:T(8,128)(2,1)}, u32[]{:S(2)}, u32[]{:S(2)}) collective-permute-start(bf16[6,128,384]{2,1,0:T(8,128)(2,1)} %get-tuple-element.156.refs_2_), channel_id=1, source_target_pairs={{0,4},{2,6},{4,0},{6,2},{1,5},{3,7},{5,1},{7,3},{8,12},{10,14},{12... | collective-permute-start | bytes 1769480 | tf_op jit(solution)/shard_map/ppermute | solution.py:1167
  130.7 16.9 %collective-permute-start.10 = (bf16[3,416,128]{2,1,0:T(8,128)(2,1)}, bf16[3,416,128]{2,1,0:T(8,128)(2,1)S(1)}, u32[]{:S(2)}, u32[]{:S(2)}) collective-permute-start(bf16[3,416,128]{2,1,0:T(8,128)(2,1)} %shard_map.341.refs_5_), channel_id=1, source_target_pairs={{0,4},{2,6},{4,0},{6,2},{1,5},{3,7},{5,1},{7,3},{8,12},{10,14},{12... | collective-permute-start | bytes 958472 | tf_op jit(solution)/shard_map/ppermute | solution.py:1167
  152.7 17.2 %collective-permute-start.9 = (bf16[3,416,128]{2,1,0:T(8,128)(2,1)S(1)}, bf16[3,416,128]{2,1,0:T(8,128)(2,1)S(1)}, u32[]{:S(2)}, u32[]{:S(2)}) collective-permute-start(bf16[3,416,128]{2,1,0:T(8,128)(2,1)S(1)} %copy-done.44), channel_id=1, source_target_pairs={{0,4},{2,6},{4,0},{6,2},{1,5},{3,7},{5,1},{7,3},{8,12},{10,14},{12... | collective-permute-start | bytes 958472 | tf_op jit(solution)/shard_map/ppermute | solution.py:1167
  162.3 11.1 %collective-permute-start.13 = (bf16[3,128,768]{2,1,0:T(8,128)(2,1)}, bf16[3,128,768]{2,1,0:T(8,128)(2,1)S(1)}, u32[]{:S(2)}, u32[]{:S(2)}) collective-permute-start(bf16[3,128,768]{2,1,0:T(8,128)(2,1)} %get-tuple-element.169.refs_2_), channel_id=1, source_target_pairs={{0,1},{1,0},{2,3},{3,2},{4,5},{5,4},{6,7},{7,6},{8,9},{9,8},{10,11... | collective-permute-start | bytes 1769480 | tf_op jit(solution)/shard_map/ppermute | solution.py:862
  188.2 15.5 %collective-permute-start.14 = (bf16[3,128,768]{2,1,0:T(8,128)(2,1)}, bf16[3,128,768]{2,1,0:T(8,128)(2,1)S(1)}, u32[]{:S(2)}, u32[]{:S(2)}) collective-permute-start(bf16[3,128,768]{2,1,0:T(8,128)(2,1)} %get-tuple-element.177.refs_2_), channel_id=1, source_target_pairs={{0,1},{1,0},{2,3},{3,2},{4,5},{5,4},{6,7},{7,6},{8,9},{9,8},{10,11... | collective-permute-start | bytes 1769480 | tf_op jit(solution)/shard_map/ppermute | solution.py:862
  188.6 32.3 %collective-permute-start.15 = (bf16[3,160,384]{2,1,0:T(8,128)(2,1)}, bf16[3,160,384]{2,1,0:T(8,128)(2,1)}, u32[]{:S(2)}, u32[]{:S(2)}) collective-permute-start(bf16[3,160,384]{2,1,0:T(8,128)(2,1)} %get-tuple-element.176.refs_3_), channel_id=1, source_target_pairs={{0,4},{2,6},{4,0},{6,2},{1,5},{3,7},{5,1},{7,3},{8,12},{10,14},{12... | collective-permute-start | bytes 1105928 | tf_op jit(solution)/shard_map/ppermute | solution.py:1167
  200.6 38.9 %collective-permute-start.18 = (bf16[768,768]{1,0:T(8,128)(2,1)}, bf16[768,768]{1,0:T(8,128)(2,1)}, u32[]{:S(2)}, u32[]{:S(2)}) collective-permute-start(bf16[768,768]{1,0:T(8,128)(2,1)} %get-tuple-element.183.refs_9_), channel_id=1, source_target_pairs={{0,8},{8,0},{16,24},{24,16},{1,9},{9,1},{17,25},{25,17},{2,10},{10... | collective-permute-start | bytes 3538952 | tf_op jit(solution)/shard_map/ppermute | solution.py:862
  202.1 37.4 %collective-permute-start.19 = (bf16[768,768]{1,0:T(8,128)(2,1)}, bf16[768,768]{1,0:T(8,128)(2,1)}, u32[]{:S(2)}, u32[]{:S(2)}) collective-permute-start(bf16[768,768]{1,0:T(8,128)(2,1)} %get-tuple-element.196), channel_id=1, source_target_pairs={{0,16},{8,24},{16,0},{24,8},{1,17},{9,25},{17,1},{25,9},{2,18},{10... | collective-permute-start | bytes 3538952 | tf_op jit(solution)/shard_map/ppermute | solution.py:862
  218.0 26.9 %collective-permute-start.17 = (bf16[3,160,384]{2,1,0:T(8,128)(2,1)}, bf16[3,160,384]{2,1,0:T(8,128)(2,1)}, u32[]{:S(2)}, u32[]{:S(2)}) collective-permute-start(bf16[3,160,384]{2,1,0:T(8,128)(2,1)} %get-tuple-element.189.refs_3_), channel_id=1, source_target_pairs={{0,4},{2,6},{4,0},{6,2},{1,5},{3,7},{5,1},{7,3},{8,12},{10,14},{12... | collective-permute-start | bytes 1105928 | tf_op jit(solution)/shard_map/ppermute | solution.py:1167
  229.6 47.3 %collective-permute-start.16 = (bf16[3,384,128]{2,1,0:T(8,128)(2,1)}, bf16[3,384,128]{2,1,0:T(8,128)(2,1)}, u32[]{:S(2)}, u32[]{:S(2)}) collective-permute-start(bf16[3,384,128]{2,1,0:T(8,128)(2,1)} %get-tuple-element.188.refs_8_), channel_id=1, source_target_pairs={{0,4},{2,6},{4,0},{6,2},{1,5},{3,7},{5,1},{7,3},{8,12},{10,14},{12... | collective-permute-start | bytes 884744 | tf_op jit(solution)/shard_map/ppermute | solution.py:1167
  244.3 38.4 %collective-permute-start.21 = (bf16[384,768]{1,0:T(8,128)(2,1)}, bf16[384,768]{1,0:T(8,128)(2,1)}, u32[]{:S(2)}, u32[]{:S(2)}) collective-permute-start(bf16[384,768]{1,0:T(8,128)(2,1)} %get-tuple-element.198.refs_8_), channel_id=1, source_target_pairs={{0,16},{8,24},{16,0},{24,8},{1,17},{9,25},{17,1},{25,9},{2,18},{10... | collective-permute-start | bytes 1769480 | tf_op jit(solution)/shard_map/ppermute | solution.py:862
  253.6 26.4 %collective-permute-start.23 = (bf16[3,384,128]{2,1,0:T(8,128)(2,1)}, bf16[3,384,128]{2,1,0:T(8,128)(2,1)}, u32[]{:S(2)}, u32[]{:S(2)}) collective-permute-start(bf16[3,384,128]{2,1,0:T(8,128)(2,1)} %get-tuple-element.201.refs_5_), channel_id=1, source_target_pairs={{0,4},{2,6},{4,0},{6,2},{1,5},{3,7},{5,1},{7,3},{8,12},{10,14},{12... | collective-permute-start | bytes 884744 | tf_op jit(solution)/shard_map/ppermute | solution.py:1167
  256.4 26.2 %collective-permute-start.22 = (bf16[384,768]{1,0:T(8,128)(2,1)}, bf16[384,768]{1,0:T(8,128)(2,1)}, u32[]{:S(2)}, u32[]{:S(2)}) collective-permute-start(bf16[384,768]{1,0:T(8,128)(2,1)} %get-tuple-element.208), channel_id=1, source_target_pairs={{0,8},{8,0},{16,24},{24,16},{1,9},{9,1},{17,25},{25,17},{2,10},{10... | collective-permute-start | bytes 1769480 | tf_op jit(solution)/shard_map/ppermute | solution.py:862
  276.8 12.9 %collective-permute-start.24 = (bf16[12,324,384]{2,1,0:T(8,128)(2,1)}, bf16[12,324,384]{2,1,0:T(8,128)(2,1)S(1)}, u32[]{:S(2)}, u32[]{:S(2)}) collective-permute-start(bf16[12,324,384]{2,1,0:T(8,128)(2,1)} %get-tuple-element.213), channel_id=1, source_target_pairs={{0,1},{1,0},{2,3},{3,2},{4,5},{5,4},{6,7},{7,6},{8,9},{9,8},{10,11... | collective-permute-start | bytes 8957960 | tf_op jit(solution)/shard_map/ppermute | solution.py:862
  279.5 50.7 %collective-permute-start.20 = (bf16[3,128,768]{2,1,0:T(8,128)(2,1)}, bf16[3,128,768]{2,1,0:T(8,128)(2,1)}, u32[]{:S(2)}, u32[]{:S(2)}) collective-permute-start(bf16[3,128,768]{2,1,0:T(8,128)(2,1)} %get-tuple-element.203.refs_3_), channel_id=1, source_target_pairs={{0,1},{1,0},{2,3},{3,2},{4,5},{5,4},{6,7},{7,6},{8,9},{9,8},{10,11... | collective-permute-start | bytes 1769480 | tf_op jit(solution)/shard_map/ppermute | solution.py:862
  282.6 63.5 %collective-permute-start.26 = (bf16[3,128,768]{2,1,0:T(8,128)(2,1)}, bf16[3,128,768]{2,1,0:T(8,128)(2,1)}, u32[]{:S(2)}, u32[]{:S(2)}) collective-permute-start(bf16[3,128,768]{2,1,0:T(8,128)(2,1)} %get-tuple-element.222.refs_3_), channel_id=1, source_target_pairs={{0,1},{1,0},{2,3},{3,2},{4,5},{5,4},{6,7},{7,6},{8,9},{9,8},{10,11... | collective-permute-start | bytes 1769480 | tf_op jit(solution)/shard_map/ppermute | solution.py:862
  285.5 37.9 %all-to-all-start = ((bf16[4,192,768]{2,1,0:T(8,128)(2,1)}), bf16[4,192,768]{2,1,0:T(8,128)(2,1)}, u32[]{:S(2)}, u32[]{:S(2)}) async-start(bf16[4,192,768]{2,1,0:T(8,128)(2,1)} %shard_map.359.refs_6_), calls=%async_computation | async-start | bytes 2359296 | tf_op jit(solution)/shard_map/all_to_all | solution.py:1010
  312.6 77.0 %collective-permute-start.36 = (bf16[6,324,384]{2,1,0:T(8,128)(2,1)}, bf16[6,324,384]{2,1,0:T(8,128)(2,1)}, u32[]{:S(2)}, u32[]{:S(2)}) collective-permute-start(bf16[6,324,384]{2,1,0:T(8,128)(2,1)} %shard_map.361.refs_9_), channel_id=1, source_target_pairs={{0,2},{2,0},{4,6},{6,4},{1,3},{3,1},{5,7},{7,5},{8,10},{10,8},{12,... | collective-permute-start | bytes 4478984 | tf_op jit(solution)/shard_map/ppermute | solution.py:862
  320.3 20.5 %collective-permute-start.27 = (bf16[768,384]{1,0:T(8,128)(2,1)}, bf16[768,384]{1,0:T(8,128)(2,1)S(1)}, u32[]{:S(2)}, u32[]{:S(2)}) collective-permute-start(bf16[768,384]{1,0:T(8,128)(2,1)} %get-tuple-element.220.refs_1_), channel_id=1, source_target_pairs={{0,8},{8,0},{16,24},{24,16},{1,9},{9,1},{17,25},{25,17},{2,10},{10... | collective-permute-start | bytes 1769480 | tf_op jit(solution)/shard_map/ppermute | solution.py:862
  321.8 19.6 %collective-permute-start.28 = (bf16[768,384]{1,0:T(8,128)(2,1)}, bf16[768,384]{1,0:T(8,128)(2,1)S(1)}, u32[]{:S(2)}, u32[]{:S(2)}) collective-permute-start(bf16[768,384]{1,0:T(8,128)(2,1)} %get-tuple-element.226), channel_id=1, source_target_pairs={{0,16},{8,24},{16,0},{24,8},{1,17},{9,25},{17,1},{25,9},{2,18},{10... | collective-permute-start | bytes 1769480 | tf_op jit(solution)/shard_map/ppermute | solution.py:862
  325.8 72.3 %all-to-all-start.1 = ((bf16[4,192,768]{2,1,0:T(8,128)(2,1)}), bf16[4,192,768]{2,1,0:T(8,128)(2,1)}, u32[]{:S(2)}, u32[]{:S(2)}) async-start(bf16[4,192,768]{2,1,0:T(8,128)(2,1)} %shard_map.363.refs_15_), calls=%async_computation.1 | async-start | bytes 2359296 | tf_op jit(solution)/shard_map/all_to_all | solution.py:1010
  340.7 25.1 %collective-permute-start.25 = (bf16[3,64,768]{2,1,0:T(8,128)(2,1)}, bf16[3,64,768]{2,1,0:T(8,128)(2,1)S(1)}, u32[]{:S(2)}, u32[]{:S(2)}) collective-permute-start(bf16[3,64,768]{2,1,0:T(8,128)(2,1)} %get-tuple-element.221), channel_id=1, source_target_pairs={{0,1},{1,0},{2,3},{3,2},{4,5},{5,4},{6,7},{7,6},{8,9},{9,8},{10,11... | collective-permute-start | bytes 884744 | tf_op jit(solution)/shard_map/ppermute | solution.py:862
  340.8 25.0 %collective-permute-start.30 = (bf16[12,324,384]{2,1,0:T(8,128)(2,1)S(1)}, bf16[12,324,384]{2,1,0:T(8,128)(2,1)S(1)}, u32[]{:S(2)}, u32[]{:S(2)}) collective-permute-start(bf16[12,324,384]{2,1,0:T(8,128)(2,1)S(1)} %copy-done.28), channel_id=1, source_target_pairs={{0,1},{1,0},{2,3},{3,2},{4,5},{5,4},{6,7},{7,6},{8,9},{9,8},{10,11... | collective-permute-start | bytes 8957960 | tf_op jit(solution)/shard_map/ppermute | solution.py:862
  345.6 12.8 %collective-permute-start.31 = (bf16[384,384]{1,0:T(8,128)(2,1)}, bf16[384,384]{1,0:T(8,128)(2,1)S(1)}, u32[]{:S(2)}, u32[]{:S(2)}) collective-permute-start(bf16[384,384]{1,0:T(8,128)(2,1)} %get-tuple-element.228.refs_15_), channel_id=1, source_target_pairs={{0,16},{8,24},{16,0},{24,8},{1,17},{9,25},{17,1},{25,9},{2,18},{10... | collective-permute-start | bytes 884744 | tf_op jit(solution)/shard_map/ppermute | solution.py:862
  346.1 12.4 %collective-permute-start.32 = (bf16[384,384]{1,0:T(8,128)(2,1)}, bf16[384,384]{1,0:T(8,128)(2,1)S(1)}, u32[]{:S(2)}, u32[]{:S(2)}) collective-permute-start(bf16[384,384]{1,0:T(8,128)(2,1)} %get-tuple-element.243), channel_id=1, source_target_pairs={{0,8},{8,0},{16,24},{24,16},{1,9},{9,1},{17,25},{25,17},{2,10},{10... | collective-permute-start | bytes 884744 | tf_op jit(solution)/shard_map/ppermute | solution.py:862
  358.4 18.6 %collective-permute-start.29 = (bf16[3,64,768]{2,1,0:T(8,128)(2,1)}, bf16[3,64,768]{2,1,0:T(8,128)(2,1)S(1)}, u32[]{:S(2)}, u32[]{:S(2)}) collective-permute-start(bf16[3,64,768]{2,1,0:T(8,128)(2,1)} %get-tuple-element.229), channel_id=1, source_target_pairs={{0,1},{1,0},{2,3},{3,2},{4,5},{5,4},{6,7},{7,6},{8,9},{9,8},{10,11... | collective-permute-start | bytes 884744 | tf_op jit(solution)/shard_map/ppermute | solution.py:862
  363.8 72.4 %collective-permute-start.39 = (bf16[3,324,384]{2,1,0:T(8,128)(2,1)}, bf16[3,324,384]{2,1,0:T(8,128)(2,1)}, u32[]{:S(2)}, u32[]{:S(2)}) collective-permute-start(bf16[3,324,384]{2,1,0:T(8,128)(2,1)} %shard_map.368.refs_13_), channel_id=1, source_target_pairs={{0,2},{2,0},{4,6},{6,4},{1,3},{3,1},{5,7},{7,5},{8,10},{10,8},{12,... | collective-permute-start | bytes 2239496 | tf_op jit(solution)/shard_map/ppermute | solution.py:862
  374.0 18.5 %collective-permute-start.34 = (bf16[768,384]{1,0:T(8,128)(2,1)}, bf16[768,384]{1,0:T(8,128)(2,1)S(1)}, u32[]{:S(2)}, u32[]{:S(2)}) collective-permute-start(bf16[768,384]{1,0:T(8,128)(2,1)} %get-tuple-element.245.refs_6_), channel_id=1, source_target_pairs={{0,8},{8,0},{16,24},{24,16},{1,9},{9,1},{17,25},{25,17},{2,10},{10... | collective-permute-start | bytes 1769480 | tf_op jit(solution)/shard_map/ppermute | solution.py:862
  375.5 17.1 %collective-permute-start.35 = (bf16[768,384]{1,0:T(8,128)(2,1)}, bf16[768,384]{1,0:T(8,128)(2,1)S(1)}, u32[]{:S(2)}, u32[]{:S(2)}) collective-permute-start(bf16[768,384]{1,0:T(8,128)(2,1)} %get-tuple-element.250), channel_id=1, source_target_pairs={{0,16},{8,24},{16,0},{24,8},{1,17},{9,25},{17,1},{25,9},{2,18},{10... | collective-permute-start | bytes 1769480 | tf_op jit(solution)/shard_map/ppermute | solution.py:862
  383.8 68.0 %collective-permute-start.33 = (bf16[6,64,768]{2,1,0:T(8,128)(2,1)}, bf16[6,64,768]{2,1,0:T(8,128)(2,1)}, u32[]{:S(2)}, u32[]{:S(2)}) collective-permute-start(bf16[6,64,768]{2,1,0:T(8,128)(2,1)} %get-tuple-element.247), channel_id=1, source_target_pairs={{0,1},{1,0},{2,3},{3,2},{4,5},{5,4},{6,7},{7,6},{8,9},{9,8},{10,11... | collective-permute-start | bytes 1769480 | tf_op jit(solution)/shard_map/ppermute | solution.py:862
  397.0 14.7 %collective-permute-start.37 = (bf16[384,384]{1,0:T(8,128)(2,1)}, bf16[384,384]{1,0:T(8,128)(2,1)S(1)}, u32[]{:S(2)}, u32[]{:S(2)}) collective-permute-start(bf16[384,384]{1,0:T(8,128)(2,1)} %get-tuple-element.253.refs_1_), channel_id=1, source_target_pairs={{0,16},{8,24},{16,0},{24,8},{1,17},{9,25},{17,1},{25,9},{2,18},{10... | collective-permute-start | bytes 884744 | tf_op jit(solution)/shard_map/ppermute | solution.py:862
  397.5 15.8 %collective-permute-start.38 = (bf16[384,384]{1,0:T(8,128)(2,1)}, bf16[384,384]{1,0:T(8,128)(2,1)S(1)}, u32[]{:S(2)}, u32[]{:S(2)}) collective-permute-start(bf16[384,384]{1,0:T(8,128)(2,1)} %get-tuple-element.255), channel_id=1, source_target_pairs={{0,8},{8,0},{16,24},{24,16},{1,9},{9,1},{17,25},{25,17},{2,10},{10... | collective-permute-start | bytes 884744 | tf_op jit(solution)/shard_map/ppermute | solution.py:862
  398.1 19.7 %all-to-all-start.3 = ((bf16[4,192,384]{2,1,0:T(8,128)(2,1)}), bf16[4,192,384]{2,1,0:T(8,128)(2,1)S(1)}, u32[]{:S(2)}, u32[]{:S(2)}) async-start(bf16[4,192,384]{2,1,0:T(8,128)(2,1)} %shard_map.367.refs_2_), calls=%async_computation.3 | async-start | bytes 1179648 | tf_op jit(solution)/shard_map/all_to_all | solution.py:1010
  404.1 36.3 %collective-permute-start.42 = (bf16[384,768]{1,0:T(8,128)(2,1)}, bf16[384,768]{1,0:T(8,128)(2,1)}, u32[]{:S(2)}, u32[]{:S(2)}) collective-permute-start(bf16[384,768]{1,0:T(8,128)(2,1)} %get-tuple-element.260.refs_5_.refs_1_), channel_id=1, source_target_pairs={{0,16},{8,24},{16,0},{24,8},{1,17},{9,25},{17,1},{25,9},{2,18},{10... | collective-permute-start | bytes 1769480 | tf_op jit(solution)/shard_map/ppermute | solution.py:862
  411.8 51.3 %collective-permute-start.43 = (bf16[384,768]{1,0:T(8,128)(2,1)}, bf16[384,768]{1,0:T(8,128)(2,1)}, u32[]{:S(2)}, u32[]{:S(2)}) collective-permute-start(bf16[384,768]{1,0:T(8,128)(2,1)} %get-tuple-element.260.refs_5_.refs_1_), channel_id=1, source_target_pairs={{0,8},{8,0},{16,24},{24,16},{1,9},{9,1},{17,25},{25,17},{2,10},{10... | collective-permute-start | bytes 1769480 | tf_op jit(solution)/shard_map/ppermute | solution.py:862
  413.3 28.6 %collective-permute-start.45 = (bf16[384,768]{1,0:T(8,128)(2,1)}, bf16[384,768]{1,0:T(8,128)(2,1)}, u32[]{:S(2)}, u32[]{:S(2)}) collective-permute-start(bf16[384,768]{1,0:T(8,128)(2,1)} %get-tuple-element.271.refs_5_), channel_id=1, source_target_pairs={{0,8},{8,0},{16,24},{24,16},{1,9},{9,1},{17,25},{25,17},{2,10},{10... | collective-permute-start | bytes 1769480 | tf_op jit(solution)/shard_map/ppermute | solution.py:862
  417.8 24.6 %all-to-all-start.2 = ((bf16[4,192,384]{2,1,0:T(8,128)(2,1)}), bf16[4,192,384]{2,1,0:T(8,128)(2,1)}, u32[]{:S(2)}, u32[]{:S(2)}) async-start(bf16[4,192,384]{2,1,0:T(8,128)(2,1)} %shard_map.377.refs_1_), calls=%async_computation.2 | async-start | bytes 1179648 | tf_op jit(solution)/shard_map/all_to_all | solution.py:1010
  436.2 26.8 %collective-permute-start.46 = (bf16[384,768]{1,0:T(8,128)(2,1)}, bf16[384,768]{1,0:T(8,128)(2,1)S(1)}, u32[]{:S(2)}, u32[]{:S(2)}) collective-permute-start(bf16[384,768]{1,0:T(8,128)(2,1)} %get-tuple-element.271.refs_5_), channel_id=1, source_target_pairs={{0,16},{8,24},{16,0},{24,8},{1,17},{9,25},{17,1},{25,9},{2,18},{10... | collective-permute-start | bytes 1769480 | tf_op jit(solution)/shard_map/ppermute | solution.py:862
  440.4 22.7 %collective-permute-start.44 = (bf16[384,768]{1,0:T(8,128)(2,1)}, bf16[384,768]{1,0:T(8,128)(2,1)S(1)}, u32[]{:S(2)}, u32[]{:S(2)}) collective-permute-start(bf16[384,768]{1,0:T(8,128)(2,1)} %collective-permute-done.42.refs_2_), channel_id=1, source_target_pairs={{0,8},{8,0},{16,24},{24,16},{1,9},{9,1},{17,25},{25,17},{2,10},{10... | collective-permute-start | bytes 1769480 | tf_op jit(solution)/shard_map/ppermute | solution.py:862
  441.9 21.4 %collective-permute-start.47 = (bf16[384,768]{1,0:T(8,128)(2,1)}, bf16[384,768]{1,0:T(8,128)(2,1)S(1)}, u32[]{:S(2)}, u32[]{:S(2)}) collective-permute-start(bf16[384,768]{1,0:T(8,128)(2,1)} %collective-permute-done.45.refs_6_), channel_id=1, source_target_pairs={{0,16},{8,24},{16,0},{24,8},{1,17},{9,25},{17,1},{25,9},{2,18},{10... | collective-permute-start | bytes 1769480 | tf_op jit(solution)/shard_map/ppermute | solution.py:862
  442.4 28.8 %all-to-all-start.5 = ((bf16[4,192,384]{2,1,0:T(8,128)(2,1)}), bf16[4,192,384]{2,1,0:T(8,128)(2,1)}, u32[]{:S(2)}, u32[]{:S(2)}) async-start(bf16[4,192,384]{2,1,0:T(8,128)(2,1)} %shard_map.378.refs_2_), calls=%async_computation.5 | async-start | bytes 1179648 | tf_op jit(solution)/shard_map/all_to_all | solution.py:1010
  451.8 50.7 %collective-permute-start.40 = (bf16[3,324,384]{2,1,0:T(8,128)(2,1)}, bf16[3,324,384]{2,1,0:T(8,128)(2,1)}, u32[]{:S(2)}, u32[]{:S(2)}) collective-permute-start(bf16[3,324,384]{2,1,0:T(8,128)(2,1)} %shard_map.383.refs_9_), channel_id=1, source_target_pairs={{0,2},{2,0},{4,6},{6,4},{1,3},{3,1},{5,7},{7,5},{8,10},{10,8},{12,... | collective-permute-start | bytes 2239496 | tf_op jit(solution)/shard_map/ppermute | solution.py:862
  471.2 18.8 %all-to-all-start.4 = ((bf16[4,192,384]{2,1,0:T(8,128)(2,1)}), bf16[4,192,384]{2,1,0:T(8,128)(2,1)S(1)}, u32[]{:S(2)}, u32[]{:S(2)}) async-start(bf16[4,192,384]{2,1,0:T(8,128)(2,1)} %shard_map.382.refs_2_), calls=%async_computation.4 | async-start | bytes 1179648 | tf_op jit(solution)/shard_map/all_to_all | solution.py:1010
  478.0 20.5 %collective-permute-start.51 = (bf16[384,384]{1,0:T(8,128)(2,1)}, bf16[384,384]{1,0:T(8,128)(2,1)S(1)}, u32[]{:S(2)}, u32[]{:S(2)}) collective-permute-start(bf16[384,384]{1,0:T(8,128)(2,1)} %get-tuple-element.273.refs_1_), channel_id=1, source_target_pairs={{0,16},{8,24},{16,0},{24,8},{1,17},{9,25},{17,1},{25,9},{2,18},{10... | collective-permute-start | bytes 884744 | tf_op jit(solution)/shard_map/ppermute | solution.py:862
  479.5 35.8 %collective-permute-start.52 = (bf16[384,384]{1,0:T(8,128)(2,1)}, bf16[384,384]{1,0:T(8,128)(2,1)S(1)}, u32[]{:S(2)}, u32[]{:S(2)}) collective-permute-start(bf16[384,384]{1,0:T(8,128)(2,1)} %get-tuple-element.273.refs_1_), channel_id=1, source_target_pairs={{0,8},{8,0},{16,24},{24,16},{1,9},{9,1},{17,25},{25,17},{2,10},{10... | collective-permute-start | bytes 884744 | tf_op jit(solution)/shard_map/ppermute | solution.py:862
  481.2 11.5 %collective-permute-start.41 = (f32[4,768]{1,0:T(4,128)S(1)}, f32[4,768]{1,0:T(4,128)S(1)}, u32[]{:S(2)}, u32[]{:S(2)}) collective-permute-start(f32[4,768]{1,0:T(4,128)S(1)} %select_maximum_fusion.1.refs_0_), channel_id=1, source_target_pairs={{0,1},{1,0},{2,3},{3,2},{4,5},{5,4},{6,7},{7,6},{8,9},{9,8},{10,11... | collective-permute-start | bytes 36872 | tf_op jit(solution)/shard_map/ppermute | solution.py:862
  481.3 18.8 %collective-permute-start.54 = (bf16[384,384]{1,0:T(8,128)(2,1)}, bf16[384,384]{1,0:T(8,128)(2,1)S(1)}, u32[]{:S(2)}, u32[]{:S(2)}) collective-permute-start(bf16[384,384]{1,0:T(8,128)(2,1)} %get-tuple-element.275.refs_5_), channel_id=1, source_target_pairs={{0,8},{8,0},{16,24},{24,16},{1,9},{9,1},{17,25},{25,17},{2,10},{10... | collective-permute-start | bytes 884744 | tf_op jit(solution)/shard_map/ppermute | solution.py:862
  498.5 17.2 %collective-permute-start.55 = (bf16[384,384]{1,0:T(8,128)(2,1)S(1)}, bf16[384,384]{1,0:T(8,128)(2,1)S(1)}, u32[]{:S(2)}, u32[]{:S(2)}) collective-permute-start(bf16[384,384]{1,0:T(8,128)(2,1)S(1)} %copy-done.50), channel_id=1, source_target_pairs={{0,16},{8,24},{16,0},{24,8},{1,17},{9,25},{17,1},{25,9},{2,18},{10... | collective-permute-start | bytes 884744 | tf_op jit(solution)/shard_map/ppermute | solution.py:862
  500.1 17.9 %collective-permute-start.53 = (bf16[384,384]{1,0:T(8,128)(2,1)S(1)}, bf16[384,384]{1,0:T(8,128)(2,1)}, u32[]{:S(2)}, u32[]{:S(2)}) collective-permute-start(bf16[384,384]{1,0:T(8,128)(2,1)S(1)} %collective-permute-done.51.refs_2_), channel_id=1, source_target_pairs={{0,8},{8,0},{16,24},{24,16},{1,9},{9,1},{17,25},{25,17},{2,10},{10... | collective-permute-start | bytes 884744 | tf_op jit(solution)/shard_map/ppermute | solution.py:862
  500.6 18.0 %collective-permute-start.56 = (bf16[384,384]{1,0:T(8,128)(2,1)S(1)}, bf16[384,384]{1,0:T(8,128)(2,1)}, u32[]{:S(2)}, u32[]{:S(2)}) collective-permute-start(bf16[384,384]{1,0:T(8,128)(2,1)S(1)} %collective-permute-done.54.refs_6_), channel_id=1, source_target_pairs={{0,16},{8,24},{16,0},{24,8},{1,17},{9,25},{17,1},{25,9},{2,18},{10... | collective-permute-start | bytes 884744 | tf_op jit(solution)/shard_map/ppermute | solution.py:862
  502.6 9.6 %collective-permute-start.49 = (f32[4,768]{1,0:T(4,128)}, f32[4,768]{1,0:T(4,128)S(1)}, u32[]{:S(2)}, u32[]{:S(2)}) collective-permute-start(f32[4,768]{1,0:T(4,128)} %shard_map.390.refs_3_.refs_0_), channel_id=1, source_target_pairs={{0,16},{8,24},{16,0},{24,8},{1,17},{9,25},{17,1},{25,9},{2,18},{10... | collective-permute-start | bytes 36872 | tf_op jit(solution)/shard_map/ppermute | solution.py:862
  512.2 21.1 %collective-permute-start.58 = (bf16[384,384]{1,0:T(8,128)(2,1)S(1)}, bf16[384,384]{1,0:T(8,128)(2,1)S(1)}, u32[]{:S(2)}, u32[]{:S(2)}) collective-permute-start(bf16[384,384]{1,0:T(8,128)(2,1)S(1)} %copy-done.48), channel_id=1, source_target_pairs={{0,16},{8,24},{16,0},{24,8},{1,17},{9,25},{17,1},{25,9},{2,18},{10... | collective-permute-start | bytes 884744 | tf_op jit(solution)/shard_map/ppermute | solution.py:862
  515.3 24.8 %collective-permute-start.59 = (bf16[384,384]{1,0:T(8,128)(2,1)S(1)}, bf16[384,384]{1,0:T(8,128)(2,1)}, u32[]{:S(2)}, u32[]{:S(2)}) collective-permute-start(bf16[384,384]{1,0:T(8,128)(2,1)S(1)} %copy-done.48), channel_id=1, source_target_pairs={{0,8},{8,0},{16,24},{24,16},{1,9},{9,1},{17,25},{25,17},{2,10},{10... | collective-permute-start | bytes 884744 | tf_op jit(solution)/shard_map/ppermute | solution.py:862
  516.5 17.4 %collective-permute-start.61 = (bf16[384,384]{1,0:T(8,128)(2,1)S(1)}, bf16[384,384]{1,0:T(8,128)(2,1)S(1)}, u32[]{:S(2)}, u32[]{:S(2)}) collective-permute-start(bf16[384,384]{1,0:T(8,128)(2,1)S(1)} %copy-done.49), channel_id=1, source_target_pairs={{0,8},{8,0},{16,24},{24,16},{1,9},{9,1},{17,25},{25,17},{2,10},{10... | collective-permute-start | bytes 884744 | tf_op jit(solution)/shard_map/ppermute | solution.py:862
  518.0 22.0 %collective-permute-start.62 = (bf16[384,384]{1,0:T(8,128)(2,1)S(1)}, bf16[384,384]{1,0:T(8,128)(2,1)S(1)}, u32[]{:S(2)}, u32[]{:S(2)}) collective-permute-start(bf16[384,384]{1,0:T(8,128)(2,1)S(1)} %copy-done.49), channel_id=1, source_target_pairs={{0,16},{8,24},{16,0},{24,8},{1,17},{9,25},{17,1},{25,9},{2,18},{10... | collective-permute-start | bytes 884744 | tf_op jit(solution)/shard_map/ppermute | solution.py:862
  526.0 9.3 %collective-permute-start.57 = (f32[4,768]{1,0:T(4,128)}, f32[4,768]{1,0:T(4,128)S(1)}, u32[]{:S(2)}, u32[]{:S(2)}) collective-permute-start(f32[4,768]{1,0:T(4,128)} %shard_map.394.refs_0_), channel_id=1, source_target_pairs={{0,4},{2,6},{4,0},{6,2},{1,5},{3,7},{5,1},{7,3},{8,12},{10,14},{12... | collective-permute-start | bytes 36872 | tf_op jit(solution)/shard_map/ppermute | solution.py:862
  533.4 6.7 %collective-permute-start.60 = (bf16[384,384]{1,0:T(8,128)(2,1)S(1)}, bf16[384,384]{1,0:T(8,128)(2,1)S(1)}, u32[]{:S(2)}, u32[]{:S(2)}) collective-permute-start(bf16[384,384]{1,0:T(8,128)(2,1)S(1)} %collective-permute-done.58.refs_2_), channel_id=1, source_target_pairs={{0,8},{8,0},{16,24},{24,16},{1,9},{9,1},{17,25},{25,17},{2,10},{10... | collective-permute-start | bytes 884744 | tf_op jit(solution)/shard_map/ppermute | solution.py:862
  533.9 6.7 %collective-permute-start.63 = (bf16[384,384]{1,0:T(8,128)(2,1)S(1)}, bf16[384,384]{1,0:T(8,128)(2,1)S(1)}, u32[]{:S(2)}, u32[]{:S(2)}) collective-permute-start(bf16[384,384]{1,0:T(8,128)(2,1)S(1)} %collective-permute-done.61.refs_6_), channel_id=1, source_target_pairs={{0,16},{8,24},{16,0},{24,8},{1,17},{9,25},{17,1},{25,9},{2,18},{10... | collective-permute-start | bytes 884744 | tf_op jit(solution)/shard_map/ppermute | solution.py:862
  (79 other events, 278.0 us)

commit v4 on v3

--- a/solution.py
+++ b/solution.py
@@ -1,4 +1,5 @@
 import functools
+import math
 
 import jax
 import jax.numpy as jnp
@@ -17,7 +18,7 @@
 BF = jnp.bfloat16
 F32 = jnp.float32
 SCALE = HEAD_DIM ** (-0.5)
-VMEM = 56 * 1024 * 1024
+ROOM = 14 * 1024 * 1024
 PAIR = 2 * HEAD_DIM
 
 
@@ -52,12 +53,15 @@
         out_specs=[pl.BlockSpec(b, m) for _, _, b, m in outs],
         scratch_shapes=list(scratch),
     )
+    blocks = [(b, a.dtype) for a, b, _ in ins] + [(b, t) for _, t, b, _ in outs]
+    held = sum(2 * math.prod(b) * jnp.dtype(t).itemsize for b, t in blocks)
+    held += sum(math.prod(v.shape) * jnp.dtype(v.dtype).itemsize for v in scratch)
     results = pl.pallas_call(
         run,
         grid_spec=spec,
         out_shape=[jax.ShapeDtypeStruct(s, d) for s, d, _, _ in outs],
         compiler_params=pltpu.CompilerParams(
-            vmem_limit_bytes=VMEM, dimension_semantics=("arbitrary",) * len(grid)
+            vmem_limit_bytes=max(held + ROOM, 46 * 1024 * 1024), dimension_semantics=("arbitrary",) * len(grid)
         ),
         cost_estimate=pl.CostEstimate(flops=int(us * 1e10), bytes_accessed=0, transcendentals=0),
         input_output_aliases=aliases,
@@ -599,44 +603,43 @@
 
 def output_kernel(at, head, lens, h2, f_a, f_b, a_a, a_b, c_a, c_b, *refs):
     out, stats = refs[-2:]
-    page = pl.program_id(0)
-    first = head[0] == 0
     half = f_a.shape[1]
-
-    def mine(ref):
-        v = ref[0].astype(F32)
-        return jnp.where(first, v[:half], v[half:])
-
-    f = f_a[0].astype(F32) + f_b[0].astype(F32)
-    y = mine(h2) + f
-    out[0] = y.astype(BF)
-    a = mine(a_a) + mine(a_b)
-    c = mine(c_a) + mine(c_b)
-    row = lax.broadcasted_iota(jnp.int32, (half, 1), 0) + head[0] * half
-    valid = (row < lens[page + at]).astype(F32)
-    stats[0] = jnp.concatenate(
-        [jnp.sum(v * v * valid, axis=0, keepdims=True) for v in (y, a, c, f)]
-        + [jnp.zeros((4, y.shape[1]), F32)],
-        axis=0,
-    )
+    for i in range(f_a.shape[0]):
+        f, a, c = (
+            u[i].astype(F32) + v[i].astype(F32) for u, v in ((f_a, f_b), (a_a, a_b), (c_a, c_b))
+        )
+        y = h2[i] + f
+        out[i] = y.astype(BF)
+        row = lax.broadcasted_iota(jnp.int32, (half, 1), 0) + head[0] * half
+        valid = (row < lens[at + i]).astype(F32)
+        stats[i] = jnp.concatenate(
+            [jnp.sum(v * v * valid, axis=0, keepdims=True) for v in (y, a, c, f)]
+            + [jnp.zeros((4, y.shape[1]), F32)],
+            axis=0,
+        )
 
 
 def output_rows(at, head, lens, h2, f_a, f_b, a_a, a_b, c_a, c_b, prev=None, after=()):
     pages, rows, d = h2.shape
+    half = rows // 2
+
+    def mine(a, first):
+        return (a, (pages, half, d), lambda i, p, n: (first // pages, p[0], 0))
+
     return call(
         functools.partial(output_kernel, at),
-        (pages,),
-        [paged(a) for a in (h2, (f_a, at), (f_b, at), (a_a, at), (a_b, at), c_a, c_b)]
+        (1,),
+        [
+            mine(h2, 0), paged((f_a, at), pages), paged((f_b, at), pages), mine(a_a, at),
+            mine(a_b, at), mine(c_a, 0), mine(c_b, 0),
+        ]
         + ([] if prev is None else [kept(prev)]),
         [
-            (
-                (a_a.shape[0], rows // 2, d), BF, (1, rows // 2, d),
-                lambda i, *_: (i + at, 0, 0),
-            ),
-            out_paged((pages, 8, d), F32),
+            ((a_a.shape[0], half, d), BF, (pages, half, d), lambda i, *_: (at // pages, 0, 0)),
+            out_paged((pages, 8, d), F32, pages),
         ],
         scalars=(head, lens),
-        us=1.5 * pages,
+        us=3,
         after=after,
         aliases={} if prev is None else {9: 0},
     )

time: 554 us -> 513 us (0.926)
  Pallas kernels: 334 us -> 255 us
  local copies, waits for them, and re-layouts: 67.3 us -> 98.1 us
  waiting for transfers between devices: 47.7 us -> 62.3 us
    pallas_call x64, Pallas kernels: 334 us -> 255 us  [call(): pl.pallas_call(run, grid_spec=spec, out_shape=[jax.ShapeDtypeStruct(s, d)...]
    unnamed x151 -> x319, local copies, waits for them, and re-layouts: 31.6 us -> 68.6 us
    ppermute x56, waiting for transfers between devices: 25.7 us -> 35.1 us  [swap(): return lax.ppermute(x, axis, [(i, i ^ mask) for i in range(size)])]
  transfers between devices with their start and end apart: 70 -> 70, of which waited for: 11 -> 12; matrix products, arithmetic and copies ran while one was open for 10% -> 9% of each run, Pallas kernels for 55% -> 45%
where the time goes in v4:
time: 513 us; the launch traced here: 507 us
  Pallas kernels  255 us (50%)
  local copies, waits for them, and re-layouts  98.1 us (19%)
  starting transfers between devices  81.1 us (16%)
  waiting for transfers between devices  62.3 us (12%)
  other arithmetic  6.7 us (1%)
    pallas_call x64, Pallas kernels, call(): pl.pallas_call(run, grid_spec=spec, out_shape=[jax.ShapeDtypeStruct(s, d)...  255 us
    unnamed x319, local copies, waits for them, and re-layouts  68.6 us
    ppermute x56, starting transfers between devices, swap(): return lax.ppermute(x, axis, [(i, i ^ mask) for i in range(size)])  47.3 us
    ppermute x56, waiting for transfers between devices, swap(): return lax.ppermute(x, axis, [(i, i ^ mask) for i in range(size)])  35.1 us
    all_to_all x6, starting transfers between devices, over_seq(): return lax.all_to_all(v, 'seq', 0, 0, tiled=True)  25.5 us
    ppermute x8, waiting for transfers between devices, rolled(): return lax.ppermute(x, 'seq', perm) if step % nb else x  16.1 us
    transpose x1, local copies, waits for them, and re-layouts, some_pages(): jnp.transpose(lax.dynamic_slice_in_dim(enc_t, at, pages, 1), (1, 0, 2))  11.2 us
    all_to_all x6, waiting for transfers between devices, over_seq(): return lax.all_to_all(v, 'seq', 0, 0, tiled=True)  11.1 us
  transfers between devices with their start and end apart: 70, of which 12 were waited for; matrix products, arithmetic and copies ran while one was open for 9% of the time, Pallas kernels for 45%

profile of v4, /device:TPU:0, one launch (start us, length us, event | category | flops | bytes accessed | tf_op | source)
XLA Modules:
  0.0 507.3 jit_solution(7735984151438863993)
XLA Ops:
  1.3 4.0 collective-permute-start.1
  5.3 8.1 %constant_dynamic-slice_fusion.3 = (bf16[3,324,768]{2,0,1:T(4,128)(2,1)S(1)}, bf16[3,324,768]{2,0,1:T(4,128)(2,1)S(1)}) fusion(bf16[24,324,768]{2,0,1:T(8,128)(2,1)} %param.21, s32[]{:T(128)S(6)} %add.95, s32[]{:T(128)S(6)} %select_n.51), kind=kLoop, calls=%fused_computation.25 | loop fusion | bytes 5971976 | tf_op jit(solution)/shard_map/slice | solution.py:1186
  18.1 9.4 %shard_map.331 = (bf16[6,128,768]{2,1,0:T(8,128)(2,1)S(1)}, bf16[6,128,768]{2,1,0:T(8,128)(2,1)S(1)}, bf16[6,128,1152]{2,1,0:T(8,128)(2,1)}, bf16[6,128,384]{2,1...) custom-call(s32[7]{0:T(128)S(1)} %stack.43.refs_0_, s32[6]{0:T(128)S(1)} %reduce_sum.63.refs_1_, ...), custom_call_target="tpu_custom_call" | custom-call | flops 99999997952 | tf_op jit(solution)/shard_map/pallas_call | solution.py:59
  43.8 11.2 %constant_dynamic-slice_fusion.1 = (bf16[6,324,768]{2,0,1:T(8,128)(2,1)}, bf16[6,324,768]{2,0,1:T(8,128)(2,1)}) fusion(bf16[24,324,768]{2,0,1:T(8,128)(2,1)} %param.21, s32[]{:T(128)S(6)} %select_n.55, s32[]{:T(128)S(6)} %select_n.53), kind=kLoop, calls=%fused_computation.23 | loop fusion | bytes 11943944 | tf_op jit(solution)/shard_map/transpose | solution.py:1182
  55.0 4.3 copy_dynamic-update-slice_fusion.1
  59.3 7.1 %collective-permute-done.5.refs_0_ = bf16[3,324,768]{2,1,0:T(8,128)(2,1)S(1)} collective-permute-done((bf16[3,324,768]{2,1,0:T(8,128)(2,1)}, bf16[3,324,768]{2,1,0:T(8,128)(2,1)S(1)}, u32[]{:S(2)}, u32[]{:S(2)}) %collective-permute-start.5) | collective-permute-done | bytes 1493024 | tf_op jit(solution)/shard_map/ppermute | solution.py:865
  67.7 4.3 copy_dynamic-update-slice_fusion.refs_1_.refs_2_
  72.1 7.5 %shard_map.333.refs_3_.refs_4_ = bf16[12,324,768]{2,1,0:T(8,128)(2,1)S(1)} custom-call(s32[7]{0:T(128)S(1)} %stack.43.refs_0_, bf16[12,324,768]{2,1,0:T(8,128)(2,1)} %copy_dynamic-update-slice_fusion.refs_1_.refs_2_, bf16[768,768]{1,0:T(8,128)(2,1)S(1)} %constant_dynamic-update-slice_fusion.refs_2_.refs_3_, s32[8,128]{1,0:T(8,128)S(1)} %copy-done.16), custom_call_target="tpu_custom_call" | custom-call | flops 108000002048 | tf_op jit(solution)/shard_map/pallas_call | solution.py:59
  79.6 2.6 copy-done.90
  82.2 3.6 shard_map.335
  85.8 4.6 shard_map.336
  90.4 5.0 shard_map.337.refs_1_.refs_5_.refs_0_
  96.2 15.1 %collective-permute-done.4.refs_0_ = bf16[3,324,768]{2,1,0:T(8,128)(2,1)} collective-permute-done((bf16[3,324,768]{2,1,0:T(8,128)(2,1)}, bf16[3,324,768]{2,1,0:T(8,128)(2,1)}, u32[]{:S(2)}, u32[]{:S(2)}) %collective-permute-start.4) | collective-permute-done | bytes 1493024 | tf_op jit(solution)/shard_map/ppermute | solution.py:865
  112.2 5.3 %shard_map.339 = (bf16[12,324,768]{2,1,0:T(8,128)(2,1)}, bf16[12,324,768]{2,1,0:T(8,128)(2,1)}) custom-call(s32[7]{0:T(128)S(1)} %stack.43.refs_0_, bf16[3,324,768]{2,1,0:T(8,128)(2,1)} %shard_map.338.refs_1_, bf16[768,768]{1,0:T(8,128)(2,1)S(1)} %constant_dynamic-update-slice_fusion.refs_2_.refs_3_, ...), custom_call_target="tpu_custom_call", output_to_operand_aliasing={{0}: (3, {}), {1}: (4, {})} | custom-call | flops 27000000512 | tf_op jit(solution)/shard_map/pallas_call | solution.py:59
  117.6 4.3 shard_map.340
  121.9 5.5 %shard_map.341.refs_5_ = bf16[3,416,128]{2,1,0:T(8,128)(2,1)S(1)} custom-call(s32[7]{0:T(128)S(1)} %stack.43.refs_0_, s32[6]{0:T(128)S(1)} %collective-permute-done.1.refs_13_.refs_1_, bf16[6,128,384]{2,1,0:T(8,128)(2,1)} %collective-permute-done.8.refs_2_, bf16[12,324,768]{2,1,0:T(8,128)(2,1)S(1)} %bitcast.66, ...), custom_call_target="tpu_custom_call" | custom-call | flops 48000000000 | tf_op jit(solution)/shard_map/pallas_call | solution.py:59
  127.5 5.1 %shard_map.342.refs_5_ = bf16[3,416,128]{2,1,0:T(8,128)(2,1)S(1)} custom-call(s32[7]{0:T(128)S(1)} %stack.43.refs_0_, s32[6]{0:T(128)S(1)} %collective-permute-done.1.refs_13_.refs_1_, bf16[6,128,384]{2,1,0:T(8,128)(2,1)} %collective-permute-done.8.refs_2_, bf16[12,324,768]{2,1,0:T(8,128)(2,1)S(1)} %bitcast.66, ...), custom_call_target="tpu_custom_call" | custom-call | flops 48000000000 | tf_op jit(solution)/shard_map/pallas_call | solution.py:59
  132.6 5.0 shard_map.343.refs_3_.refs_0_
  137.7 5.7 %collective-permute-done.10.refs_1_ = bf16[3,416,128]{2,1,0:T(8,128)(2,1)S(1)} collective-permute-done((bf16[3,416,128]{2,1,0:T(8,128)(2,1)S(1)}, bf16[3,416,128]{2,1,0:T(8,128)(2,1)S(1)}, u32[]{:S(2)}, u32[]{:S(2)}) %collective-permute-start.10) | collective-permute-done | bytes 319520 | tf_op jit(solution)/shard_map/ppermute | solution.py:1170
  146.7 6.7 %shard_map.345 = (f32[3,128,768]{2,1,0:T(8,128)S(1)}, bf16[3,128,768]{2,1,0:T(8,128)(2,1)S(1)}, bf16[3,128,1536]{2,1,0:T(8,128)(2,1)S(1)}, bf16[3,128,1536]{2,1,0:T(8,128)(2,1)S(1)}, bf16[3,128,768]{2,1,0:T(8,128)(2,1)S(1)}) custom-call(f32[6,128,768]{2,1,0:T(8,128)} %copy-done.104, bf16[3,128,768]{2,1,0:T(8,128)(2,1)S(1)} %get-tuple-element.165.refs_1_.refs_7_, ...), custom_call_target="tpu_custom_call" | custom-call | flops 120000004096 | tf_op jit(solution)/shard_map/pallas_call | solution.py:59
  154.6 8.2 %collective-permute-done.9.refs_1_ = bf16[3,416,128]{2,1,0:T(8,128)(2,1)S(1)} collective-permute-done((bf16[3,416,128]{2,1,0:T(8,128)(2,1)S(1)}, bf16[3,416,128]{2,1,0:T(8,128)(2,1)S(1)}, u32[]{:S(2)}, u32[]{:S(2)}) %collective-permute-start.9) | collective-permute-done | bytes 319520 | tf_op jit(solution)/shard_map/ppermute | solution.py:1170
  164.2 2.8 shard_map.347
  168.0 6.9 %shard_map.348 = (f32[3,128,768]{2,1,0:T(8,128)S(1)}, bf16[3,128,768]{2,1,0:T(8,128)(2,1)S(1)}, bf16[3,128,1536]{2,1,0:T(8,128)(2,1)S(1)}, bf16[3,128,1536]{2,1,0:T(8,128)(2,1)S(1)}, bf16[3,128,768]{2,1,0:T(8,128)(2,1)S(1)}) custom-call(f32[6,128,768]{2,1,0:T(8,128)} %copy-done.104, bf16[3,128,768]{2,1,0:T(8,128)(2,1)S(1)} %get-tuple-element.168.refs_1_.refs_7_, ...), custom_call_target="tpu_custom_call" | custom-call | flops 120000004096 | tf_op jit(solution)/shard_map/pallas_call | solution.py:59
  177.5 10.7 %shard_map.349 = (bf16[768,768]{1,0:T(8,128)(2,1)}, bf16[768,768]{1,0:T(8,128)(2,1)S(1)}, bf16[768,768]{1,0:T(8,128)(2,1)}, bf16[768,768]{1,0:T(8,128)(2,1)S(1)}) custom-call(s32[7]{0:T(128)S(1)} %stack.43.refs_0_, bf16[384,1536]{1,0:T(8,128)(2,1)S(1)} %bitcast.43, bf16[384,1536]{1,0:T(8,128)(2,1)S(1)} %bitcast.45, bf16[384,768]{1,0:T(8,128)(2,1)S(1)} %bitcast.53, ...), custom_call_target="tpu_custom_call" | custom-call | flops 99999997952 | tf_op jit(solution)/shard_map/pallas_call | solution.py:59
  192.3 2.8 shard_map.350
  195.1 8.3 %shard_map.351 = (bf16[3,384,128]{2,1,0:T(8,128)(2,1)S(1)}, bf16[12,324,768]{2,1,0:T(8,128)(2,1)S(1)}, bf16[12,324,768]{2,1,0:T(8,128)(2,1)}) custom-call(s32[7]{0:T(128)S(1)} %stack.43.refs_0_, s32[6]{0:T(128)S(1)} %copy-done.59, bf16[6,128,384]{2,1,0:T(8,128)(2,1)S(1)} %copy-done.50, bf16[3,160,384]{2,1,0:T(8,128)(2,1)} %get-tuple-element.176.refs_3_, ...), custom_call_target="tpu_custom_call" | custom-call | flops 71999995904 | tf_op jit(solution)/shard_map/pallas_call | solution.py:59
  203.4 3.0 collective-permute-start.17
  206.4 8.4 %shard_map.352 = (bf16[3,384,128]{2,1,0:T(8,128)(2,1)}, bf16[12,324,768]{2,1,0:T(8,128)(2,1)S(1)}, bf16[12,324,768]{2,1,0:T(8,128)(2,1)}) custom-call(s32[7]{0:T(128)S(1)} %stack.43.refs_0_, s32[6]{0:T(128)S(1)} %collective-permute-done.1.refs_13_.refs_1_, ...), custom_call_target="tpu_custom_call", output_to_operand_aliasing={{1}: (6, {}), {2}: (7, {})} | custom-call | flops 71999995904 | tf_op jit(solution)/shard_map/pallas_call | solution.py:59
  214.9 8.7 %shard_map.353 = (bf16[3,384,128]{2,1,0:T(8,128)(2,1)S(1)}, bf16[12,324,768]{2,1,0:T(8,128)(2,1)S(1)}, bf16[12,324,768]{2,1,0:T(8,128)(2,1)}) custom-call(s32[7]{0:T(128)S(1)} %stack.43.refs_0_, s32[6]{0:T(128)S(1)} %copy-done.59, bf16[6,128,384]{2,1,0:T(8,128)(2,1)S(1)} %copy-done.50, ...), custom_call_target="tpu_custom_call", output_to_operand_aliasing={{1}: (6, {}), {2}: (7, {})} | custom-call | flops 71999995904 | tf_op jit(solution)/shard_map/pallas_call | solution.py:59
  224.2 3.6 shard_map.354
  230.3 8.4 %shard_map.355 = (bf16[3,384,128]{2,1,0:T(8,128)(2,1)}, bf16[12,324,768]{2,1,0:T(8,128)(2,1)S(1)}, bf16[12,324,768]{2,1,0:T(8,128)(2,1)}) custom-call(s32[7]{0:T(128)S(1)} %stack.43.refs_0_, s32[6]{0:T(128)S(1)} %collective-permute-done.1.refs_13_.refs_1_, ...), custom_call_target="tpu_custom_call", output_to_operand_aliasing={{1}: (6, {}), {2}: (7, {})} | custom-call | flops 71999995904 | tf_op jit(solution)/shard_map/pallas_call | solution.py:59
  240.4 16.3 %shard_map.356 = (bf16[12,324,384]{2,1,0:T(8,128)(2,1)}, bf16[12,324,384]{2,1,0:T(8,128)(2,1)}, f32[768,768]{1,0:T(8,128)S(1)}) custom-call(s32[7]{0:T(128)S(1)} %stack.43.refs_0_, bf16[12,324,768]{2,1,0:T(8,128)(2,1)} %get-tuple-element.199.refs_1_, bf16[12,324,768]{2,1,0:T(8,128)(2,1)} %get-tuple-element.200.refs_2_, ...), custom_call_target="tpu_custom_call" | custom-call | flops 204000002048 | tf_op jit(solution)/shard_map/pallas_call | solution.py:59
  256.8 2.5 shard_map.357
  265.4 4.3 all-to-all-start
  271.4 16.6 %shard_map.360 = (bf16[12,324,384]{2,1,0:T(8,128)(2,1)}, bf16[12,324,384]{2,1,0:T(8,128)(2,1)}, f32[768,768]{1,0:T(8,128)S(1)}) custom-call(s32[7]{0:T(128)S(1)} %stack.43.refs_0_, bf16[12,324,768]{2,1,0:T(8,128)(2,1)} %copy-done.111, bf16[12,324,768]{2,1,0:T(8,128)(2,1)} %copy_dynamic-update-slice_fusion.refs_1_.refs_2_, ...), custom_call_target="tpu_custom_call" | custom-call | flops 204000002048 | tf_op jit(solution)/shard_map/pallas_call | solution.py:59
  288.0 3.3 shard_map.361.refs_9_
  293.4 4.1 shard_map.362
  304.5 4.6 all-to-all-start.1
  309.2 8.3 %shard_map.364 = (f32[3,64,768]{2,1,0:T(8,128)S(1)}, bf16[3,128,768]{2,1,0:T(8,128)(2,1)S(1)}, bf16[3,128,384]{2,1,0:T(8,128)(2,1)S(1)}, bf16[3,128,384]{2,1,0:T...) custom-call(s32[7]{0:T(128)S(1)} %stack.43.refs_0_, ...), custom_call_target="tpu_custom_call" | custom-call | flops 83999997952 | tf_op jit(solution)/shard_map/pallas_call | solution.py:59
  324.0 8.3 %shard_map.366 = (f32[3,64,768]{2,1,0:T(8,128)S(1)}, bf16[3,128,768]{2,1,0:T(8,128)(2,1)S(1)}, bf16[3,128,384]{2,1,0:T(8,128)(2,1)S(1)}, bf16[3,128,384]{2,1,0:T...) custom-call(s32[7]{0:T(128)S(1)} %stack.43.refs_0_, ...), custom_call_target="tpu_custom_call" | custom-call | flops 83999997952 | tf_op jit(solution)/shard_map/pallas_call | solution.py:59
  346.9 3.1 shard_map.369
  353.8 3.5 shard_map.370
  360.1 3.0 shard_map.371.refs_2_
  363.0 2.7 copy-done
  367.8 2.6 copy-done.1
  373.9 3.6 all-to-all-start.3
  388.2 5.2 %all-to-all-done.3.refs_0_ = bf16[4,192,384]{2,1,0:T(8,128)(2,1)S(1)} async-done(((bf16[4,192,384]{2,1,0:T(8,128)(2,1)}), bf16[4,192,384]{2,1,0:T(8,128)(2,1)S(1)}, u32[]{:S(2)}, u32[]{:S(2)}) %all-to-all-start.3) | async-done | bytes 589856 | tf_op jit(solution)/shard_map/all_to_all | solution.py:1013
  393.4 4.4 all-to-all-start.2
  399.1 3.5 shard_map.379.refs_2_
  402.6 3.5 shard_map.380.refs_3_
  408.5 2.7 copy-done.2
  413.0 2.6 copy-done.3
  417.6 5.1 all-to-all-start.5
  422.6 2.7 copy-done.4
  432.0 2.5 shard_map.384
  434.5 2.5 shard_map.385
  437.1 6.3 %shard_map.386 = (f32[1536,768]{1,0:T(8,128)}, f32[768,1536]{1,0:T(8,128)}) custom-call(s32[7]{0:T(128)S(1)} %stack.43.refs_0_, bf16[384,768]{1,0:T(8,128)(2,1)} %get-tuple-element.260.refs_5_.refs_1_, bf16[384,768]{1,0:T(8,128)(2,1)} %collective-permute-done.42.refs_2_, bf16[384,768]{1,0:T(8,128)(2,1)} %collective-permute-done.43.refs_3_, ...), custom_call_target="tpu_custom_call" | custom-call | flops 60000002048 | tf_op jit(solution)/shard_map/pallas_call | solution.py:59
  443.4 3.6 all-to-all-start.4
  454.5 5.9 %all-to-all-done.4.refs_0_ = bf16[4,192,384]{2,1,0:T(8,128)(2,1)S(1)} async-done(((bf16[4,192,384]{2,1,0:T(8,128)(2,1)}), bf16[4,192,384]{2,1,0:T(8,128)(2,1)S(1)}, u32[]{:S(2)}, u32[]{:S(2)}) %all-to-all-start.4) | async-done | bytes 589856 | tf_op jit(solution)/shard_map/all_to_all | solution.py:1013
  469.8 6.2 %collective-permute-done.49.refs_1_ = f32[4,768]{1,0:T(4,128)S(1)} collective-permute-done((f32[4,768]{1,0:T(4,128)S(1)}, f32[4,768]{1,0:T(4,128)S(1)}, u32[]{:S(2)}, u32[]{:S(2)}) %collective-permute-start.49) | collective-permute-done | bytes 12320 | tf_op jit(solution)/shard_map/ppermute | solution.py:865
  480.4 4.8 shard_map.393
  488.4 5.3 %copy_convert_fusion = f32[24,324,384]{2,0,1:T(8,128)} fusion(bf16[24,324,384]{2,1,0:T(8,128)(2,1)S(1)} %shard_map.391.refs_2_), kind=kLoop, calls=%fused_computation | loop fusion | flops 2985984 | bytes 17915904 | tf_op jit(solution)/shard_map/convert_element_type | solution.py:1403
  498.0 2.7 collective-permute-done.60.refs_4_
  502.1 5.0 shard_map.396
  (500 shorter events, 146.0 us)
Async XLA Ops:
  0.7 15.8 %collective-permute-start.2 = (bf16[6,64,768]{2,1,0:T(8,128)(2,1)}, bf16[6,64,768]{2,1,0:T(8,128)(2,1)S(1)}, u32[]{:S(2)}, u32[]{:S(2)}) collective-permute-start(bf16[6,64,768]{2,1,0:T(8,128)(2,1)} %param.39), channel_id=1, source_target_pairs={{0,1},{1,0},{2,3},{3,2},{4,5},{5,4},{6,7},{7,6},{8,9},{9,8},{10,11... | collective-permute-start | bytes 1769480 | tf_op jit(solution)/shard_map/ppermute | solution.py:865
  1.2 15.3 %collective-permute-start = (bf16[6,64,768]{2,1,0:T(8,128)(2,1)}, bf16[6,64,768]{2,1,0:T(8,128)(2,1)}, u32[]{:S(2)}, u32[]{:S(2)}) collective-permute-start(bf16[6,64,768]{2,1,0:T(8,128)(2,1)} %refs_0_.3), channel_id=1, source_target_pairs={{0,1},{1,0},{2,3},{3,2},{4,5},{5,4},{6,7},{7,6},{8,9},{9,8},{10,11... | collective-permute-start | bytes 1769480 | tf_op jit(solution)/shard_map/ppermute | solution.py:865
  1.3 15.2 %collective-permute-start.1 = (s32[6]{0:T(128)}, s32[6]{0:T(128)S(1)}, u32[]{:S(2)}, u32[]{:S(2)}) collective-permute-start(s32[6]{0:T(128)} %refs_1_.9), channel_id=1, source_target_pairs={{0,4},{2,6},{4,0},{6,2},{1,5},{3,7},{5,1},{7,3},{8,12},{10,14},{12... | collective-permute-start | bytes 80 | tf_op jit(solution)/shard_map/ppermute | solution.py:1170
  30.4 36.1 %collective-permute-start.5 = (bf16[3,324,768]{2,1,0:T(8,128)(2,1)}, bf16[3,324,768]{2,1,0:T(8,128)(2,1)S(1)}, u32[]{:S(2)}, u32[]{:S(2)}) collective-permute-start(bf16[3,324,768]{2,1,0:T(8,128)(2,1)} %copy.68.refs_11_), channel_id=1, source_target_pairs={{0,2},{2,0},{4,6},{6,4},{1,3},{3,1},{5,7},{7,5},{8,10},{10,8},{12,... | collective-permute-start | bytes 4478984 | tf_op jit(solution)/shard_map/ppermute | solution.py:865
  32.1 79.1 %collective-permute-start.4 = (bf16[3,324,768]{2,1,0:T(8,128)(2,1)}, bf16[3,324,768]{2,1,0:T(8,128)(2,1)}, u32[]{:S(2)}, u32[]{:S(2)}) collective-permute-start(bf16[3,324,768]{2,1,0:T(8,128)(2,1)} %copy.69.refs_12_), channel_id=1, source_target_pairs={{0,2},{2,0},{4,6},{6,4},{1,3},{3,1},{5,7},{7,5},{8,10},{10,8},{12,... | collective-permute-start | bytes 4478984 | tf_op jit(solution)/shard_map/ppermute | solution.py:865
  67.6 18.2 %collective-permute-start.6 = (bf16[3,324,768]{2,1,0:T(8,128)(2,1)}, bf16[3,324,768]{2,1,0:T(8,128)(2,1)S(1)}, u32[]{:S(2)}, u32[]{:S(2)}) collective-permute-start(bf16[3,324,768]{2,1,0:T(8,128)(2,1)} %shard_map.334.refs_1_), channel_id=1, source_target_pairs={{0,1},{1,0},{2,3},{3,2},{4,5},{5,4},{6,7},{7,6},{8,9},{9,8},{10,11... | collective-permute-start | bytes 4478984 | tf_op jit(solution)/shard_map/ppermute | solution.py:865
  67.6 54.3 %collective-permute-start.8 = (bf16[6,128,384]{2,1,0:T(8,128)(2,1)}, bf16[6,128,384]{2,1,0:T(8,128)(2,1)}, u32[]{:S(2)}, u32[]{:S(2)}) collective-permute-start(bf16[6,128,384]{2,1,0:T(8,128)(2,1)} %copy-done.49), channel_id=1, source_target_pairs={{0,4},{2,6},{4,0},{6,2},{1,5},{3,7},{5,1},{7,3},{8,12},{10,14},{12... | collective-permute-start | bytes 1769480 | tf_op jit(solution)/shard_map/ppermute | solution.py:1170
  127.4 16.0 %collective-permute-start.10 = (bf16[3,416,128]{2,1,0:T(8,128)(2,1)S(1)}, bf16[3,416,128]{2,1,0:T(8,128)(2,1)S(1)}, u32[]{:S(2)}, u32[]{:S(2)}) collective-permute-start(bf16[3,416,128]{2,1,0:T(8,128)(2,1)S(1)} %shard_map.341.refs_5_), channel_id=1, source_target_pairs={{0,4},{2,6},{4,0},{6,2},{1,5},{3,7},{5,1},{7,3},{8,12},{10,14},{12... | collective-permute-start | bytes 958472 | tf_op jit(solution)/shard_map/ppermute | solution.py:1170
  145.6 17.3 %collective-permute-start.9 = (bf16[3,416,128]{2,1,0:T(8,128)(2,1)S(1)}, bf16[3,416,128]{2,1,0:T(8,128)(2,1)S(1)}, u32[]{:S(2)}, u32[]{:S(2)}) collective-permute-start(bf16[3,416,128]{2,1,0:T(8,128)(2,1)S(1)} %shard_map.342.refs_5_), channel_id=1, source_target_pairs={{0,4},{2,6},{4,0},{6,2},{1,5},{3,7},{5,1},{7,3},{8,12},{10,14},{12... | collective-permute-start | bytes 958472 | tf_op jit(solution)/shard_map/ppermute | solution.py:1170
  154.5 9.7 %collective-permute-start.13 = (bf16[3,128,768]{2,1,0:T(8,128)(2,1)S(1)}, bf16[3,128,768]{2,1,0:T(8,128)(2,1)S(1)}, u32[]{:S(2)}, u32[]{:S(2)}) collective-permute-start(bf16[3,128,768]{2,1,0:T(8,128)(2,1)S(1)} %get-tuple-element.169.refs_2_), channel_id=1, source_target_pairs={{0,1},{1,0},{2,3},{3,2},{4,5},{5,4},{6,7},{7,6},{8,9},{9,8},{10,11... | collective-permute-start | bytes 1769480 | tf_op jit(solution)/shard_map/ppermute | solution.py:865
  177.0 15.3 %collective-permute-start.14 = (bf16[3,128,768]{2,1,0:T(8,128)(2,1)S(1)}, bf16[3,128,768]{2,1,0:T(8,128)(2,1)S(1)}, u32[]{:S(2)}, u32[]{:S(2)}) collective-permute-start(bf16[3,128,768]{2,1,0:T(8,128)(2,1)S(1)} %get-tuple-element.177.refs_2_), channel_id=1, source_target_pairs={{0,1},{1,0},{2,3},{3,2},{4,5},{5,4},{6,7},{7,6},{8,9},{9,8},{10,11... | collective-permute-start | bytes 1769480 | tf_op jit(solution)/shard_map/ppermute | solution.py:865
  177.5 28.9 %collective-permute-start.15 = (bf16[3,160,384]{2,1,0:T(8,128)(2,1)}, bf16[3,160,384]{2,1,0:T(8,128)(2,1)}, u32[]{:S(2)}, u32[]{:S(2)}) collective-permute-start(bf16[3,160,384]{2,1,0:T(8,128)(2,1)} %get-tuple-element.176.refs_3_), channel_id=1, source_target_pairs={{0,4},{2,6},{4,0},{6,2},{1,5},{3,7},{5,1},{7,3},{8,12},{10,14},{12... | collective-permute-start | bytes 1105928 | tf_op jit(solution)/shard_map/ppermute | solution.py:1170
  189.3 34.9 %collective-permute-start.18 = (bf16[768,768]{1,0:T(8,128)(2,1)}, bf16[768,768]{1,0:T(8,128)(2,1)}, u32[]{:S(2)}, u32[]{:S(2)}) collective-permute-start(bf16[768,768]{1,0:T(8,128)(2,1)} %get-tuple-element.183.refs_9_), channel_id=1, source_target_pairs={{0,8},{8,0},{16,24},{24,16},{1,9},{9,1},{17,25},{25,17},{2,10},{10... | collective-permute-start | bytes 3538952 | tf_op jit(solution)/shard_map/ppermute | solution.py:865
  190.7 33.4 %collective-permute-start.19 = (bf16[768,768]{1,0:T(8,128)(2,1)}, bf16[768,768]{1,0:T(8,128)(2,1)}, u32[]{:S(2)}, u32[]{:S(2)}) collective-permute-start(bf16[768,768]{1,0:T(8,128)(2,1)} %get-tuple-element.196), channel_id=1, source_target_pairs={{0,16},{8,24},{16,0},{24,8},{1,17},{9,25},{17,1},{25,9},{2,18},{10... | collective-permute-start | bytes 3538952 | tf_op jit(solution)/shard_map/ppermute | solution.py:865
  203.4 27.0 %collective-permute-start.17 = (bf16[3,160,384]{2,1,0:T(8,128)(2,1)}, bf16[3,160,384]{2,1,0:T(8,128)(2,1)}, u32[]{:S(2)}, u32[]{:S(2)}) collective-permute-start(bf16[3,160,384]{2,1,0:T(8,128)(2,1)} %get-tuple-element.189.refs_3_), channel_id=1, source_target_pairs={{0,4},{2,6},{4,0},{6,2},{1,5},{3,7},{5,1},{7,3},{8,12},{10,14},{12... | collective-permute-start | bytes 1105928 | tf_op jit(solution)/shard_map/ppermute | solution.py:1170
  214.8 42.0 %collective-permute-start.16 = (bf16[3,384,128]{2,1,0:T(8,128)(2,1)}, bf16[3,384,128]{2,1,0:T(8,128)(2,1)}, u32[]{:S(2)}, u32[]{:S(2)}) collective-permute-start(bf16[3,384,128]{2,1,0:T(8,128)(2,1)} %get-tuple-element.188.refs_8_), channel_id=1, source_target_pairs={{0,4},{2,6},{4,0},{6,2},{1,5},{3,7},{5,1},{7,3},{8,12},{10,14},{12... | collective-permute-start | bytes 884744 | tf_op jit(solution)/shard_map/ppermute | solution.py:1170
  227.7 34.4 %collective-permute-start.21 = (bf16[384,768]{1,0:T(8,128)(2,1)}, bf16[384,768]{1,0:T(8,128)(2,1)}, u32[]{:S(2)}, u32[]{:S(2)}) collective-permute-start(bf16[384,768]{1,0:T(8,128)(2,1)} %get-tuple-element.198.refs_8_), channel_id=1, source_target_pairs={{0,16},{8,24},{16,0},{24,8},{1,17},{9,25},{17,1},{25,9},{2,18},{10... | collective-permute-start | bytes 1769480 | tf_op jit(solution)/shard_map/ppermute | solution.py:865
  238.8 20.8 %collective-permute-start.23 = (bf16[3,384,128]{2,1,0:T(8,128)(2,1)}, bf16[3,384,128]{2,1,0:T(8,128)(2,1)}, u32[]{:S(2)}, u32[]{:S(2)}) collective-permute-start(bf16[3,384,128]{2,1,0:T(8,128)(2,1)} %get-tuple-element.201.refs_5_), channel_id=1, source_target_pairs={{0,4},{2,6},{4,0},{6,2},{1,5},{3,7},{5,1},{7,3},{8,12},{10,14},{12... | collective-permute-start | bytes 884744 | tf_op jit(solution)/shard_map/ppermute | solution.py:1170
  239.6 22.5 %collective-permute-start.22 = (bf16[384,768]{1,0:T(8,128)(2,1)}, bf16[384,768]{1,0:T(8,128)(2,1)}, u32[]{:S(2)}, u32[]{:S(2)}) collective-permute-start(bf16[384,768]{1,0:T(8,128)(2,1)} %get-tuple-element.208), channel_id=1, source_target_pairs={{0,8},{8,0},{16,24},{24,16},{1,9},{9,1},{17,25},{25,17},{2,10},{10... | collective-permute-start | bytes 1769480 | tf_op jit(solution)/shard_map/ppermute | solution.py:865
  256.7 13.0 %collective-permute-start.24 = (bf16[12,324,384]{2,1,0:T(8,128)(2,1)}, bf16[12,324,384]{2,1,0:T(8,128)(2,1)}, u32[]{:S(2)}, u32[]{:S(2)}) collective-permute-start(bf16[12,324,384]{2,1,0:T(8,128)(2,1)} %get-tuple-element.213), channel_id=1, source_target_pairs={{0,1},{1,0},{2,3},{3,2},{4,5},{5,4},{6,7},{7,6},{8,9},{9,8},{10,11... | collective-permute-start | bytes 8957960 | tf_op jit(solution)/shard_map/ppermute | solution.py:865
  259.4 49.8 %collective-permute-start.20 = (bf16[3,128,768]{2,1,0:T(8,128)(2,1)}, bf16[3,128,768]{2,1,0:T(8,128)(2,1)}, u32[]{:S(2)}, u32[]{:S(2)}) collective-permute-start(bf16[3,128,768]{2,1,0:T(8,128)(2,1)} %get-tuple-element.203.refs_3_), channel_id=1, source_target_pairs={{0,1},{1,0},{2,3},{3,2},{4,5},{5,4},{6,7},{7,6},{8,9},{9,8},{10,11... | collective-permute-start | bytes 1769480 | tf_op jit(solution)/shard_map/ppermute | solution.py:865
  261.9 61.5 %collective-permute-start.26 = (bf16[3,128,768]{2,1,0:T(8,128)(2,1)}, bf16[3,128,768]{2,1,0:T(8,128)(2,1)}, u32[]{:S(2)}, u32[]{:S(2)}) collective-permute-start(bf16[3,128,768]{2,1,0:T(8,128)(2,1)} %get-tuple-element.222.refs_3_), channel_id=1, source_target_pairs={{0,1},{1,0},{2,3},{3,2},{4,5},{5,4},{6,7},{7,6},{8,9},{9,8},{10,11... | collective-permute-start | bytes 1769480 | tf_op jit(solution)/shard_map/ppermute | solution.py:865
  265.4 36.6 %all-to-all-start = ((bf16[4,192,768]{2,1,0:T(8,128)(2,1)}), bf16[4,192,768]{2,1,0:T(8,128)(2,1)}, u32[]{:S(2)}, u32[]{:S(2)}) async-start(bf16[4,192,768]{2,1,0:T(8,128)(2,1)} %shard_map.359.refs_6_), calls=%async_computation | async-start | bytes 2359296 | tf_op jit(solution)/shard_map/all_to_all | solution.py:1013
  291.4 71.7 %collective-permute-start.36 = (bf16[6,324,384]{2,1,0:T(8,128)(2,1)}, bf16[6,324,384]{2,1,0:T(8,128)(2,1)}, u32[]{:S(2)}, u32[]{:S(2)}) collective-permute-start(bf16[6,324,384]{2,1,0:T(8,128)(2,1)} %shard_map.361.refs_9_), channel_id=1, source_target_pairs={{0,2},{2,0},{4,6},{6,4},{1,3},{3,1},{5,7},{7,5},{8,10},{10,8},{12,... | collective-permute-start | bytes 4478984 | tf_op jit(solution)/shard_map/ppermute | solution.py:865
  299.1 21.0 %collective-permute-start.27 = (bf16[768,384]{1,0:T(8,128)(2,1)}, bf16[768,384]{1,0:T(8,128)(2,1)}, u32[]{:S(2)}, u32[]{:S(2)}) collective-permute-start(bf16[768,384]{1,0:T(8,128)(2,1)} %get-tuple-element.220.refs_1_), channel_id=1, source_target_pairs={{0,8},{8,0},{16,24},{24,16},{1,9},{9,1},{17,25},{25,17},{2,10},{10... | collective-permute-start | bytes 1769480 | tf_op jit(solution)/shard_map/ppermute | solution.py:865
  300.5 20.1 %collective-permute-start.28 = (bf16[768,384]{1,0:T(8,128)(2,1)S(1)}, bf16[768,384]{1,0:T(8,128)(2,1)}, u32[]{:S(2)}, u32[]{:S(2)}) collective-permute-start(bf16[768,384]{1,0:T(8,128)(2,1)S(1)} %get-tuple-element.226), channel_id=1, source_target_pairs={{0,16},{8,24},{16,0},{24,8},{1,17},{9,25},{17,1},{25,9},{2,18},{10... | collective-permute-start | bytes 1769480 | tf_op jit(solution)/shard_map/ppermute | solution.py:865
  304.5 69.4 %all-to-all-start.1 = ((bf16[4,192,768]{2,1,0:T(8,128)(2,1)}), bf16[4,192,768]{2,1,0:T(8,128)(2,1)}, u32[]{:S(2)}, u32[]{:S(2)}) async-start(bf16[4,192,768]{2,1,0:T(8,128)(2,1)} %shard_map.363.refs_15_), calls=%async_computation.1 | async-start | bytes 2359296 | tf_op jit(solution)/shard_map/all_to_all | solution.py:1013
  320.1 23.1 %collective-permute-start.25 = (bf16[3,64,768]{2,1,0:T(8,128)(2,1)S(1)}, bf16[3,64,768]{2,1,0:T(8,128)(2,1)S(1)}, u32[]{:S(2)}, u32[]{:S(2)}) collective-permute-start(bf16[3,64,768]{2,1,0:T(8,128)(2,1)S(1)} %get-tuple-element.221), channel_id=1, source_target_pairs={{0,1},{1,0},{2,3},{3,2},{4,5},{5,4},{6,7},{7,6},{8,9},{9,8},{10,11... | collective-permute-start | bytes 884744 | tf_op jit(solution)/shard_map/ppermute | solution.py:865
  320.1 23.1 %collective-permute-start.30 = (bf16[12,324,384]{2,1,0:T(8,128)(2,1)}, bf16[12,324,384]{2,1,0:T(8,128)(2,1)S(1)}, u32[]{:S(2)}, u32[]{:S(2)}) collective-permute-start(bf16[12,324,384]{2,1,0:T(8,128)(2,1)} %get-tuple-element.240), channel_id=1, source_target_pairs={{0,1},{1,0},{2,3},{3,2},{4,5},{5,4},{6,7},{7,6},{8,9},{9,8},{10,11... | collective-permute-start | bytes 8957960 | tf_op jit(solution)/shard_map/ppermute | solution.py:865
  322.8 13.3 %collective-permute-start.31 = (bf16[384,384]{1,0:T(8,128)(2,1)S(1)}, bf16[384,384]{1,0:T(8,128)(2,1)S(1)}, u32[]{:S(2)}, u32[]{:S(2)}) collective-permute-start(bf16[384,384]{1,0:T(8,128)(2,1)S(1)} %get-tuple-element.228.refs_15_), channel_id=1, source_target_pairs={{0,16},{8,24},{16,0},{24,8},{1,17},{9,25},{17,1},{25,9},{2,18},{10... | collective-permute-start | bytes 884744 | tf_op jit(solution)/shard_map/ppermute | solution.py:865
  323.4 12.7 %collective-permute-start.32 = (bf16[384,384]{1,0:T(8,128)(2,1)S(1)}, bf16[384,384]{1,0:T(8,128)(2,1)S(1)}, u32[]{:S(2)}, u32[]{:S(2)}) collective-permute-start(bf16[384,384]{1,0:T(8,128)(2,1)S(1)} %get-tuple-element.243), channel_id=1, source_target_pairs={{0,8},{8,0},{16,24},{24,16},{1,9},{9,1},{17,25},{25,17},{2,10},{10... | collective-permute-start | bytes 884744 | tf_op jit(solution)/shard_map/ppermute | solution.py:865
  336.0 17.7 %collective-permute-start.29 = (bf16[3,64,768]{2,1,0:T(8,128)(2,1)S(1)}, bf16[3,64,768]{2,1,0:T(8,128)(2,1)S(1)}, u32[]{:S(2)}, u32[]{:S(2)}) collective-permute-start(bf16[3,64,768]{2,1,0:T(8,128)(2,1)S(1)} %get-tuple-element.229), channel_id=1, source_target_pairs={{0,1},{1,0},{2,3},{3,2},{4,5},{5,4},{6,7},{7,6},{8,9},{9,8},{10,11... | collective-permute-start | bytes 884744 | tf_op jit(solution)/shard_map/ppermute | solution.py:865
  341.2 65.9 %collective-permute-start.39 = (bf16[3,324,384]{2,1,0:T(8,128)(2,1)}, bf16[3,324,384]{2,1,0:T(8,128)(2,1)}, u32[]{:S(2)}, u32[]{:S(2)}) collective-permute-start(bf16[3,324,384]{2,1,0:T(8,128)(2,1)} %shard_map.368.refs_13_), channel_id=1, source_target_pairs={{0,2},{2,0},{4,6},{6,4},{1,3},{3,1},{5,7},{7,5},{8,10},{10,8},{12,... | collective-permute-start | bytes 2239496 | tf_op jit(solution)/shard_map/ppermute | solution.py:865
  350.8 19.5 %collective-permute-start.34 = (bf16[768,384]{1,0:T(8,128)(2,1)S(1)}, bf16[768,384]{1,0:T(8,128)(2,1)S(1)}, u32[]{:S(2)}, u32[]{:S(2)}) collective-permute-start(bf16[768,384]{1,0:T(8,128)(2,1)S(1)} %get-tuple-element.245.refs_6_), channel_id=1, source_target_pairs={{0,8},{8,0},{16,24},{24,16},{1,9},{9,1},{17,25},{25,17},{2,10},{10... | collective-permute-start | bytes 1769480 | tf_op jit(solution)/shard_map/ppermute | solution.py:865
  352.3 18.1 %collective-permute-start.35 = (bf16[768,384]{1,0:T(8,128)(2,1)S(1)}, bf16[768,384]{1,0:T(8,128)(2,1)S(1)}, u32[]{:S(2)}, u32[]{:S(2)}) collective-permute-start(bf16[768,384]{1,0:T(8,128)(2,1)S(1)} %get-tuple-element.250), channel_id=1, source_target_pairs={{0,16},{8,24},{16,0},{24,8},{1,17},{9,25},{17,1},{25,9},{2,18},{10... | collective-permute-start | bytes 1769480 | tf_op jit(solution)/shard_map/ppermute | solution.py:865
  358.0 71.9 %collective-permute-start.33 = (bf16[6,64,768]{2,1,0:T(8,128)(2,1)}, bf16[6,64,768]{2,1,0:T(8,128)(2,1)}, u32[]{:S(2)}, u32[]{:S(2)}) collective-permute-start(bf16[6,64,768]{2,1,0:T(8,128)(2,1)} %get-tuple-element.247), channel_id=1, source_target_pairs={{0,1},{1,0},{2,3},{3,2},{4,5},{5,4},{6,7},{7,6},{8,9},{9,8},{10,11... | collective-permute-start | bytes 1769480 | tf_op jit(solution)/shard_map/ppermute | solution.py:865
  372.8 12.5 %collective-permute-start.37 = (bf16[384,384]{1,0:T(8,128)(2,1)S(1)}, bf16[384,384]{1,0:T(8,128)(2,1)S(1)}, u32[]{:S(2)}, u32[]{:S(2)}) collective-permute-start(bf16[384,384]{1,0:T(8,128)(2,1)S(1)} %get-tuple-element.253.refs_1_), channel_id=1, source_target_pairs={{0,16},{8,24},{16,0},{24,8},{1,17},{9,25},{17,1},{25,9},{2,18},{10... | collective-permute-start | bytes 884744 | tf_op jit(solution)/shard_map/ppermute | solution.py:865
  373.3 13.4 %collective-permute-start.38 = (bf16[384,384]{1,0:T(8,128)(2,1)S(1)}, bf16[384,384]{1,0:T(8,128)(2,1)S(1)}, u32[]{:S(2)}, u32[]{:S(2)}) collective-permute-start(bf16[384,384]{1,0:T(8,128)(2,1)S(1)} %get-tuple-element.255), channel_id=1, source_target_pairs={{0,8},{8,0},{16,24},{24,16},{1,9},{9,1},{17,25},{25,17},{2,10},{10... | collective-permute-start | bytes 884744 | tf_op jit(solution)/shard_map/ppermute | solution.py:865
  373.9 19.5 %all-to-all-start.3 = ((bf16[4,192,384]{2,1,0:T(8,128)(2,1)}), bf16[4,192,384]{2,1,0:T(8,128)(2,1)S(1)}, u32[]{:S(2)}, u32[]{:S(2)}) async-start(bf16[4,192,384]{2,1,0:T(8,128)(2,1)} %shard_map.367.refs_2_), calls=%async_computation.3 | async-start | bytes 1179648 | tf_op jit(solution)/shard_map/all_to_all | solution.py:1013
  380.0 35.6 %collective-permute-start.42 = (bf16[384,768]{1,0:T(8,128)(2,1)}, bf16[384,768]{1,0:T(8,128)(2,1)}, u32[]{:S(2)}, u32[]{:S(2)}) collective-permute-start(bf16[384,768]{1,0:T(8,128)(2,1)} %get-tuple-element.260.refs_5_.refs_1_), channel_id=1, source_target_pairs={{0,16},{8,24},{16,0},{24,8},{1,17},{9,25},{17,1},{25,9},{2,18},{10... | collective-permute-start | bytes 1769480 | tf_op jit(solution)/shard_map/ppermute | solution.py:865
  385.2 51.8 %collective-permute-start.43 = (bf16[384,768]{1,0:T(8,128)(2,1)}, bf16[384,768]{1,0:T(8,128)(2,1)}, u32[]{:S(2)}, u32[]{:S(2)}) collective-permute-start(bf16[384,768]{1,0:T(8,128)(2,1)} %get-tuple-element.260.refs_5_.refs_1_), channel_id=1, source_target_pairs={{0,8},{8,0},{16,24},{24,16},{1,9},{9,1},{17,25},{25,17},{2,10},{10... | collective-permute-start | bytes 1769480 | tf_op jit(solution)/shard_map/ppermute | solution.py:865
  386.7 30.4 %collective-permute-start.45 = (bf16[384,768]{1,0:T(8,128)(2,1)}, bf16[384,768]{1,0:T(8,128)(2,1)}, u32[]{:S(2)}, u32[]{:S(2)}) collective-permute-start(bf16[384,768]{1,0:T(8,128)(2,1)} %get-tuple-element.271.refs_5_), channel_id=1, source_target_pairs={{0,8},{8,0},{16,24},{24,16},{1,9},{9,1},{17,25},{25,17},{2,10},{10... | collective-permute-start | bytes 1769480 | tf_op jit(solution)/shard_map/ppermute | solution.py:865
  393.4 24.1 %all-to-all-start.2 = ((bf16[4,192,384]{2,1,0:T(8,128)(2,1)}), bf16[4,192,384]{2,1,0:T(8,128)(2,1)}, u32[]{:S(2)}, u32[]{:S(2)}) async-start(bf16[4,192,384]{2,1,0:T(8,128)(2,1)} %shard_map.377.refs_1_), calls=%async_computation.2 | async-start | bytes 1179648 | tf_op jit(solution)/shard_map/all_to_all | solution.py:1013
  407.0 30.0 %collective-permute-start.46 = (bf16[384,768]{1,0:T(8,128)(2,1)}, bf16[384,768]{1,0:T(8,128)(2,1)S(1)}, u32[]{:S(2)}, u32[]{:S(2)}) collective-permute-start(bf16[384,768]{1,0:T(8,128)(2,1)} %get-tuple-element.271.refs_5_), channel_id=1, source_target_pairs={{0,16},{8,24},{16,0},{24,8},{1,17},{9,25},{17,1},{25,9},{2,18},{10... | collective-permute-start | bytes 1769480 | tf_op jit(solution)/shard_map/ppermute | solution.py:865
  415.6 21.5 %collective-permute-start.44 = (bf16[384,768]{1,0:T(8,128)(2,1)}, bf16[384,768]{1,0:T(8,128)(2,1)S(1)}, u32[]{:S(2)}, u32[]{:S(2)}) collective-permute-start(bf16[384,768]{1,0:T(8,128)(2,1)} %collective-permute-done.42.refs_2_), channel_id=1, source_target_pairs={{0,8},{8,0},{16,24},{24,16},{1,9},{9,1},{17,25},{25,17},{2,10},{10... | collective-permute-start | bytes 1769480 | tf_op jit(solution)/shard_map/ppermute | solution.py:865
  417.0 20.0 %collective-permute-start.47 = (bf16[384,768]{1,0:T(8,128)(2,1)}, bf16[384,768]{1,0:T(8,128)(2,1)S(1)}, u32[]{:S(2)}, u32[]{:S(2)}) collective-permute-start(bf16[384,768]{1,0:T(8,128)(2,1)} %collective-permute-done.45.refs_6_), channel_id=1, source_target_pairs={{0,16},{8,24},{16,0},{24,8},{1,17},{9,25},{17,1},{25,9},{2,18},{10... | collective-permute-start | bytes 1769480 | tf_op jit(solution)/shard_map/ppermute | solution.py:865
  417.6 25.8 %all-to-all-start.5 = ((bf16[4,192,384]{2,1,0:T(8,128)(2,1)}), bf16[4,192,384]{2,1,0:T(8,128)(2,1)}, u32[]{:S(2)}, u32[]{:S(2)}) async-start(bf16[4,192,384]{2,1,0:T(8,128)(2,1)} %shard_map.378.refs_2_), calls=%async_computation.5 | async-start | bytes 1179648 | tf_op jit(solution)/shard_map/all_to_all | solution.py:1013
  429.8 36.7 %collective-permute-start.40 = (bf16[3,324,384]{2,1,0:T(8,128)(2,1)}, bf16[3,324,384]{2,1,0:T(8,128)(2,1)}, u32[]{:S(2)}, u32[]{:S(2)}) collective-permute-start(bf16[3,324,384]{2,1,0:T(8,128)(2,1)} %shard_map.383.refs_9_), channel_id=1, source_target_pairs={{0,2},{2,0},{4,6},{6,4},{1,3},{3,1},{5,7},{7,5},{8,10},{10,8},{12,... | collective-permute-start | bytes 2239496 | tf_op jit(solution)/shard_map/ppermute | solution.py:865
  443.4 16.9 %all-to-all-start.4 = ((bf16[4,192,384]{2,1,0:T(8,128)(2,1)}), bf16[4,192,384]{2,1,0:T(8,128)(2,1)S(1)}, u32[]{:S(2)}, u32[]{:S(2)}) async-start(bf16[4,192,384]{2,1,0:T(8,128)(2,1)} %shard_map.382.refs_2_), calls=%async_computation.4 | async-start | bytes 1179648 | tf_op jit(solution)/shard_map/all_to_all | solution.py:1013
  450.5 12.1 %collective-permute-start.51 = (bf16[384,384]{1,0:T(8,128)(2,1)S(1)}, bf16[384,384]{1,0:T(8,128)(2,1)S(1)}, u32[]{:S(2)}, u32[]{:S(2)}) collective-permute-start(bf16[384,384]{1,0:T(8,128)(2,1)S(1)} %get-tuple-element.273.refs_1_), channel_id=1, source_target_pairs={{0,16},{8,24},{16,0},{24,8},{1,17},{9,25},{17,1},{25,9},{2,18},{10... | collective-permute-start | bytes 884744 | tf_op jit(solution)/shard_map/ppermute | solution.py:865
  452.1 25.5 %collective-permute-start.52 = (bf16[384,384]{1,0:T(8,128)(2,1)S(1)}, bf16[384,384]{1,0:T(8,128)(2,1)}, u32[]{:S(2)}, u32[]{:S(2)}) collective-permute-start(bf16[384,384]{1,0:T(8,128)(2,1)S(1)} %get-tuple-element.273.refs_1_), channel_id=1, source_target_pairs={{0,8},{8,0},{16,24},{24,16},{1,9},{9,1},{17,25},{25,17},{2,10},{10... | collective-permute-start | bytes 884744 | tf_op jit(solution)/shard_map/ppermute | solution.py:865
  452.9 7.5 %collective-permute-start.41 = (f32[4,768]{1,0:T(4,128)S(1)}, f32[4,768]{1,0:T(4,128)S(1)}, u32[]{:S(2)}, u32[]{:S(2)}) collective-permute-start(f32[4,768]{1,0:T(4,128)S(1)} %select_maximum_fusion.1.refs_0_), channel_id=1, source_target_pairs={{0,1},{1,0},{2,3},{3,2},{4,5},{5,4},{6,7},{7,6},{8,9},{9,8},{10,11... | collective-permute-start | bytes 36872 | tf_op jit(solution)/shard_map/ppermute | solution.py:865
  453.0 12.5 %collective-permute-start.54 = (bf16[384,384]{1,0:T(8,128)(2,1)S(1)}, bf16[384,384]{1,0:T(8,128)(2,1)}, u32[]{:S(2)}, u32[]{:S(2)}) collective-permute-start(bf16[384,384]{1,0:T(8,128)(2,1)S(1)} %get-tuple-element.275.refs_5_), channel_id=1, source_target_pairs={{0,8},{8,0},{16,24},{24,16},{1,9},{9,1},{17,25},{25,17},{2,10},{10... | collective-permute-start | bytes 884744 | tf_op jit(solution)/shard_map/ppermute | solution.py:865
  462.6 15.8 %collective-permute-start.55 = (bf16[384,384]{1,0:T(8,128)(2,1)S(1)}, bf16[384,384]{1,0:T(8,128)(2,1)S(1)}, u32[]{:S(2)}, u32[]{:S(2)}) collective-permute-start(bf16[384,384]{1,0:T(8,128)(2,1)S(1)} %get-tuple-element.275.refs_5_), channel_id=1, source_target_pairs={{0,16},{8,24},{16,0},{24,8},{1,17},{9,25},{17,1},{25,9},{2,18},{10... | collective-permute-start | bytes 884744 | tf_op jit(solution)/shard_map/ppermute | solution.py:865
  465.4 14.2 %collective-permute-start.53 = (bf16[384,384]{1,0:T(8,128)(2,1)S(1)}, bf16[384,384]{1,0:T(8,128)(2,1)S(1)}, u32[]{:S(2)}, u32[]{:S(2)}) collective-permute-start(bf16[384,384]{1,0:T(8,128)(2,1)S(1)} %collective-permute-done.51.refs_2_), channel_id=1, source_target_pairs={{0,8},{8,0},{16,24},{24,16},{1,9},{9,1},{17,25},{25,17},{2,10},{10... | collective-permute-start | bytes 884744 | tf_op jit(solution)/shard_map/ppermute | solution.py:865
  466.0 14.1 %collective-permute-start.56 = (bf16[384,384]{1,0:T(8,128)(2,1)}, bf16[384,384]{1,0:T(8,128)(2,1)S(1)}, u32[]{:S(2)}, u32[]{:S(2)}) collective-permute-start(bf16[384,384]{1,0:T(8,128)(2,1)} %collective-permute-done.54.refs_6_), channel_id=1, source_target_pairs={{0,16},{8,24},{16,0},{24,8},{1,17},{9,25},{17,1},{25,9},{2,18},{10... | collective-permute-start | bytes 884744 | tf_op jit(solution)/shard_map/ppermute | solution.py:865
  466.5 9.5 %collective-permute-start.49 = (f32[4,768]{1,0:T(4,128)S(1)}, f32[4,768]{1,0:T(4,128)S(1)}, u32[]{:S(2)}, u32[]{:S(2)}) collective-permute-start(f32[4,768]{1,0:T(4,128)S(1)} %shard_map.390.refs_3_.refs_0_), channel_id=1, source_target_pairs={{0,16},{8,24},{16,0},{24,8},{1,17},{9,25},{17,1},{25,9},{2,18},{10... | collective-permute-start | bytes 36872 | tf_op jit(solution)/shard_map/ppermute | solution.py:865
  476.0 17.8 %collective-permute-start.58 = (bf16[384,384]{1,0:T(8,128)(2,1)S(1)}, bf16[384,384]{1,0:T(8,128)(2,1)}, u32[]{:S(2)}, u32[]{:S(2)}) collective-permute-start(bf16[384,384]{1,0:T(8,128)(2,1)S(1)} %get-tuple-element.274.refs_2_.refs_1_), channel_id=1, source_target_pairs={{0,16},{8,24},{16,0},{24,8},{1,17},{9,25},{17,1},{25,9},{2,18},{10... | collective-permute-start | bytes 884744 | tf_op jit(solution)/shard_map/ppermute | solution.py:865
  477.6 20.3 %collective-permute-start.59 = (bf16[384,384]{1,0:T(8,128)(2,1)S(1)}, bf16[384,384]{1,0:T(8,128)(2,1)}, u32[]{:S(2)}, u32[]{:S(2)}) collective-permute-start(bf16[384,384]{1,0:T(8,128)(2,1)S(1)} %get-tuple-element.274.refs_2_.refs_1_), channel_id=1, source_target_pairs={{0,8},{8,0},{16,24},{24,16},{1,9},{9,1},{17,25},{25,17},{2,10},{10... | collective-permute-start | bytes 884744 | tf_op jit(solution)/shard_map/ppermute | solution.py:865
  478.5 16.7 %collective-permute-start.61 = (bf16[384,384]{1,0:T(8,128)(2,1)S(1)}, bf16[384,384]{1,0:T(8,128)(2,1)}, u32[]{:S(2)}, u32[]{:S(2)}) collective-permute-start(bf16[384,384]{1,0:T(8,128)(2,1)S(1)} %get-tuple-element.277.refs_5_), channel_id=1, source_target_pairs={{0,8},{8,0},{16,24},{24,16},{1,9},{9,1},{17,25},{25,17},{2,10},{10... | collective-permute-start | bytes 884744 | tf_op jit(solution)/shard_map/ppermute | solution.py:865
  479.7 18.3 %collective-permute-start.62 = (bf16[384,384]{1,0:T(8,128)(2,1)S(1)}, bf16[384,384]{1,0:T(8,128)(2,1)}, u32[]{:S(2)}, u32[]{:S(2)}) collective-permute-start(bf16[384,384]{1,0:T(8,128)(2,1)S(1)} %get-tuple-element.277.refs_5_), channel_id=1, source_target_pairs={{0,16},{8,24},{16,0},{24,8},{1,17},{9,25},{17,1},{25,9},{2,18},{10... | collective-permute-start | bytes 884744 | tf_op jit(solution)/shard_map/ppermute | solution.py:865
  486.4 10.2 %collective-permute-start.57 = (f32[4,768]{1,0:T(4,128)S(1)}, f32[4,768]{1,0:T(4,128)S(1)}, u32[]{:S(2)}, u32[]{:S(2)}) collective-permute-start(f32[4,768]{1,0:T(4,128)S(1)} %shard_map.394.refs_0_), channel_id=1, source_target_pairs={{0,4},{2,6},{4,0},{6,2},{1,5},{3,7},{5,1},{7,3},{8,12},{10,14},{12... | collective-permute-start | bytes 36872 | tf_op jit(solution)/shard_map/ppermute | solution.py:865
  493.8 6.9 %collective-permute-start.60 = (bf16[384,384]{1,0:T(8,128)(2,1)}, bf16[384,384]{1,0:T(8,128)(2,1)S(1)}, u32[]{:S(2)}, u32[]{:S(2)}) collective-permute-start(bf16[384,384]{1,0:T(8,128)(2,1)} %collective-permute-done.58.refs_2_), channel_id=1, source_target_pairs={{0,8},{8,0},{16,24},{24,16},{1,9},{9,1},{17,25},{25,17},{2,10},{10... | collective-permute-start | bytes 884744 | tf_op jit(solution)/shard_map/ppermute | solution.py:865
  495.2 6.9 %collective-permute-start.63 = (bf16[384,384]{1,0:T(8,128)(2,1)}, bf16[384,384]{1,0:T(8,128)(2,1)S(1)}, u32[]{:S(2)}, u32[]{:S(2)}) collective-permute-start(bf16[384,384]{1,0:T(8,128)(2,1)} %collective-permute-done.61.refs_6_), channel_id=1, source_target_pairs={{0,16},{8,24},{16,0},{24,8},{1,17},{9,25},{17,1},{25,9},{2,18},{10... | collective-permute-start | bytes 884744 | tf_op jit(solution)/shard_map/ppermute | solution.py:865
  (163 other events, 773.2 us)
